TPU v7x, 32 devices: a whole 2x2x4 slice. The times are simulated.
32 devices in a mesh: corpus: 2 (over x), rows: 8 (over z, y), feat: 2 (over core).
Axes of the slice: x: 2, y: 2, z: 4, core: 2. Of those that a mesh axis runs over, the one named last changes fastest.
Arguments:
- queries: bfloat16 [1024, 4096], P('rows', 'feat'), may hold values from -6 to 6
- kernel: bfloat16 [8192, 4096], P(('corpus', 'feat'), 'rows'), parts along dimension 0, may hold values from -0.09375 to 0.09375
- train_feats: bfloat16 [65536, 4096], P(('corpus', 'rows', 'feat')), parts along dimension 0, may hold values from -6 to 6
Outputs:
- scores: bfloat16 [1024, 65536], P(('rows', 'feat'), 'corpus'), parts along dimension 1
There are 2 independent parts, one for each index of `corpus`. A program takes and returns all parts, laid end to end along the dimension named above; an argument that names none is the same for every part. Nothing has to cross between parts.
All inputs are finite; a program needn't handle non-finite values.
Results may differ from a plain program's by a relative error of at most 0.005.
Values may be sent and summed in bfloat16 or wider, within the bound.
No kernel may reach another device: no remote copies, remote signals or barrier semaphores. Data moves between devices by JAX's collectives and lax.ppermute only.
A program may use at most 128 MiB of HBM per device.

v0:
```python
import jax
import jax.numpy as jnp
from jax import lax
from jax.sharding import PartitionSpec as P

epsilon = 1e-06


def per_device(queries, kernel, train_feats):
    partial_pq = jnp.dot(
        lax.all_gather(queries, "rows", axis=0, tiled=True),
        kernel,
        preferred_element_type=jnp.float32,
    )
    precond = lax.psum(partial_pq, "feat").astype(jnp.bfloat16)
    gathered = lax.all_gather(precond, "rows", axis=1, tiled=True)
    widened = gathered.astype(jnp.float32)
    lengths = jnp.sqrt(jnp.sum(widened * widened, axis=1) + epsilon)
    running = lax.dot_general(
        gathered, train_feats, (((1,), (1,)), ((), ())), preferred_element_type=jnp.float32
    )
    local_scores = (running / lengths[:, None]).astype(jnp.bfloat16)
    return lax.all_to_all(local_scores, ("rows", "feat"), split_axis=0, concat_axis=1, tiled=True)


def solution(mesh):
    placed = (P("rows", "feat"), P(("corpus", "feat"), "rows"), P(("corpus", "rows", "feat"), None))
    return jax.shard_map(
        per_device,
        mesh=mesh,
        in_specs=placed,
        out_specs=P(("rows", "feat"), "corpus"),
        check_vma=False,
    )
```

profile of v0, /device:TPU:1, one launch (start us, length us, event | category | flops | bytes accessed | tf_op | source)
XLA Modules:
  0.0 355.8 jit_solution(16181787974725921309)
XLA Ops:
  6.5 0.0 copy-start
  6.5 0.0 all-gather.3.cloned.1.call-start
  6.5 0.7 all-gather.3.cloned.1.call-update
  7.3 0.0 all-gather.5.cloned.1.call-start
  7.3 76.5 %all-gather.3.cloned.1.call-done = bf16[1024,2048]{1,0:T(8,128)(2,1)} async-done(((bf16[128,2048]{1,0:T(8,128)(2,1)}), bf16[1024,2048]{1,0:T(8,128)(2,1)}) %all-gather.3.cloned.1.call-update) | async-done | bytes 4194320 | tf_op jit(solution)/shard_map/all_gather | solution.py:11
  83.8 0.0 copy-done
  83.8 5.8 %fusion = f32[1024,512]{1,0:T(8,128)} fusion(bf16[1024,2048]{1,0:T(8,128)(2,1)} %all-gather.3.cloned.1.call-done, bf16[2048,512]{1,0:T(8,128)(2,1)S(1)} %copy-done), kind=kOutput, calls=%fused_computation.3 | convolution fusion | flops 2147483648 | bytes 8388608 | tf_op jit(solution)/shard_map/dot_general | solution.py:10
  89.6 11.6 %all-reduce.1 = bf16[1024,512]{1,0:T(8,128)(2,1)} all-reduce(f32[1024,512]{1,0:T(8,128)} %fusion), channel_id=1, replica_groups=mesh['corpus'=2,'rows'=8,'feat'=2] {'feat'}, use_global_device_ids=true, to_apply=%region_0.0 | all-reduce | flops 524288 | bytes 3145728 | tf_op jit(solution)/shard_map/psum | solution.py:15
  101.3 0.0 all-gather.5.cloned.1.call-update
  101.3 122.9 %all-gather.5.cloned.1.call-done = bf16[1024,4096]{1,0:T(8,128)(2,1)} async-done(((bf16[1024,512]{1,0:T(8,128)(2,1)}), bf16[1024,4096]{1,0:T(8,128)(2,1)}) %all-gather.5.cloned.1.call-update) | async-done | bytes 8388624 | tf_op jit(solution)/shard_map/all_gather | solution.py:16
  224.2 0.0 copy-start.1
  224.2 5.2 %multiply_reduce_fusion = f32[1024]{0:T(1024)S(1)} fusion(bf16[1024,4096]{1,0:T(8,128)(2,1)} %all-gather.5.cloned.1.call-done), kind=kLoop, calls=%fused_computation | loop fusion | flops 12581888 | bytes 8392704 | tf_op jit(solution)/shard_map/reduce_sum | solution.py:18
  229.4 0.5 copy-done.1
  229.9 20.3 %divide_convert_fusion = bf16[1024,2048]{1,0:T(8,128)(2,1)S(1)} fusion(bf16[1024,4096]{1,0:T(8,128)(2,1)S(1)} %copy-done.1, bf16[2048,4096]{1,0:T(8,128)(2,1)} %param.5, f32[1024]{0:T(1024)S(1)} %add_sqrt_fusion), kind=kOutput, calls=%fused_computation.1 | convolution fusion | flops 17184063488 | bytes 29364224 | tf_op jit(solution)/shard_map/dot_general | solution.py:19
  250.2 96.3 %all_to_all.19 = bf16[16,64,2048]{2,1,0:T(8,128)(2,1)S(1)} all-to-all(bf16[16,64,2048]{2,1,0:T(8,128)(2,1)S(1)} %bitcast.9), channel_id=1, replica_groups=mesh['corpus'=2,'rows'=8,'feat'=2] {'rows','feat'}, dimensions={0} | all-to-all | bytes 8388608 | tf_op jit(solution)/shard_map/all_to_all | solution.py:23
  346.6 2.3 copy.5
  (1 shorter events, 0.0 us)
Async XLA Ops:
  6.5 77.3 %copy-start = (bf16[2048,512]{1,0:T(8,128)(2,1)S(1)}, bf16[2048,512]{1,0:T(8,128)(2,1)}, u32[]{:S(2)}) copy-start(bf16[2048,512]{1,0:T(8,128)(2,1)} %param.4) | copy-start | bytes 6291460
  6.5 77.3 %all-gather.3.cloned.1.call-start = ((), (), s32[]{:S(2)}) async-start(), calls=%async_computation.1 | async-start | bytes 4718592 | tf_op jit(solution)/shard_map/all_gather | solution.py:11
  7.3 216.9 %all-gather.5.cloned.1.call-start = ((), (), s32[]{:S(2)}) async-start(), calls=%async_computation.2 | async-start | bytes 9437184 | tf_op jit(solution)/shard_map/all_gather | solution.py:16
  224.2 5.8 %copy-start.1 = (bf16[1024,4096]{1,0:T(8,128)(2,1)S(1)}, bf16[1024,4096]{1,0:T(8,128)(2,1)}, u32[]{:S(2)}) copy-start(bf16[1024,4096]{1,0:T(8,128)(2,1)} %all-gather.5.cloned.1.call-done) | copy-start | bytes 25165828
Sparse Core Ops, SparseCore 0:
  9.5 74.2 all-gather.2
  101.4 122.6 all-gather.4
where the time goes:
time: 356 us
  waiting for transfers between devices  200 us (56%)
  blocking collectives  108 us (30%)
  matrix products  26.1 us (7%)
  between operations  13.4 us (4%)
  other arithmetic  5.23 us (1%)
    all_gather x1, waiting for transfers between devices, per_device(): gathered = lax.all_gather(precond, 'rows', axis=1, tiled=True)  123 us
    all_to_all x1, blocking collectives, per_device(): lax.all_to_all(local_scores, ('rows', 'feat'), split_axis=0, concat_axis=...  96.3 us
    all_gather x1, waiting for transfers between devices, per_device(): lax.all_gather(queries, 'rows', axis=0, tiled=True)  76.5 us
    dot_general x1, matrix products, per_device(): lax.dot_general(gathered, train_feats, (((1,), (1,)), ((), ())), preferre...  20.3 us
    psum x1, blocking collectives, per_device(): precond = lax.psum(partial_pq, 'feat').astype(jnp.bfloat16)  11.6 us
  transfers between devices with their start and end apart: 2, of which 2 were waited for; matrix products, arithmetic and copies ran while one was open for 0% of the time, Pallas kernels for 0%

commit v1 on v0

v1 whole, which is shorter than its diff:
```python
import functools

import jax
import jax.numpy as jnp
from jax import lax
from jax.sharding import PartitionSpec as P

epsilon = 1e-06


def ring_order(n):
    if n == 8:
        return [0, 2, 4, 6, 7, 5, 3, 1]
    return list(range(n))


def walk(block, n, order):
    ahead = [(order[i], order[(i + 1) % n]) for i in range(n)]
    back = [(b, a) for a, b in ahead]
    place = jnp.array([order.index(i) for i in range(n)])[lax.axis_index("rows")]
    ring = jnp.array(order)
    yield [(ring[place], 0, block)]
    forward = backward = block
    for step in range(1, n // 2):
        forward = lax.ppermute(forward, "rows", ahead)
        backward = lax.ppermute(backward, "rows", back)
        yield [(ring[(place - step) % n], 0, forward), (ring[(place + step) % n], 0, backward)]
    half = block.shape[0] // 2
    owner = ring[(place + n // 2) % n]
    top = lax.ppermute(forward[:half], "rows", ahead)
    bottom = lax.ppermute(backward[half:], "rows", back)
    yield [(owner, 0, top), (owner, half, bottom)]


def per_device(n, queries, kernel, train_feats):
    order = ring_order(n)
    feat = lax.axis_index("feat")
    me = lax.axis_index("rows") * 2 + feat
    swap = [(0, 1), (1, 0)]
    count = queries.shape[0]
    width = kernel.shape[1]
    half = width // 2
    total = count * n

    mine = jnp.zeros((total, half), jnp.bfloat16)
    for arrived in walk(queries, n, order):
        for owner, first, block in arrived:
            partial = jnp.dot(block, kernel, preferred_element_type=jnp.float32)
            keep = lax.dynamic_slice_in_dim(partial, feat * half, half, 1)
            give = lax.dynamic_slice_in_dim(partial, (1 - feat) * half, half, 1)
            piece = (keep + lax.ppermute(give, "feat", swap)).astype(jnp.bfloat16)
            mine = lax.dynamic_update_slice(mine, piece, (owner * count + first, 0))

    whole = jnp.zeros((total, width * n), jnp.bfloat16)
    squares = jnp.zeros((total,), jnp.float32)
    for arrived in walk(mine, n, order):
        for owner, first, block in arrived:
            other = lax.ppermute(block, "feat", swap)
            for part, at in ((block, feat), (other, 1 - feat)):
                whole = lax.dynamic_update_slice(whole, part, (first, owner * width + at * half))
                wide = part.astype(jnp.float32)
                squares = squares.at[first : first + part.shape[0]].add(jnp.sum(wide * wide, axis=1))
    lengths = jnp.sqrt(squares + epsilon)

    owned = count // 2
    devices = 2 * n
    group = max(1, 256 // owned)
    groups = devices // group
    columns = train_feats.shape[0]
    scores = jnp.zeros((owned, devices * columns), jnp.bfloat16)
    at_group, at_place = me // group, me % group
    for shift in [groups // 2] + [k for k in range(1, groups) if k != groups // 2] + [0]:
        target = (at_group + shift) % groups
        start = target * group * owned
        rows = lax.dynamic_slice_in_dim(whole, start, group * owned, 0)
        raw = lax.dot_general(rows, train_feats, (((1,), (1,)), ((), ())), preferred_element_type=jnp.float32)
        span = lax.dynamic_slice_in_dim(lengths, start, group * owned, 0)
        tile = (raw / span[:, None]).astype(jnp.bfloat16)
        for turn in range(group):
            pairs = []
            for i in range(devices):
                pairs.append((i, (i // group + shift) % groups * group + (i + turn) % group))
            block = lax.dynamic_slice_in_dim(tile, (at_place + turn) % group * owned, owned, 0)
            if shift or turn:
                block = lax.ppermute(block, ("rows", "feat"), pairs)
            source = (at_group - shift) % groups * group + (at_place - turn) % group
            scores = lax.dynamic_update_slice(scores, block, (0, source * columns))
    return scores


def solution(mesh):
    placed = (P("rows", "feat"), P(("corpus", "feat"), "rows"), P(("corpus", "rows", "feat"), None))
    return jax.shard_map(
        functools.partial(per_device, mesh.shape["rows"]),
        mesh=mesh,
        in_specs=placed,
        out_specs=P(("rows", "feat"), "corpus"),
        check_vma=False,
    )
```

time: 356 us -> 262 us (0.74)
  blocking collectives: 108 us -> 0 us
  waiting for transfers between devices: 200 us -> 101 us
  local copies, waits for them, and re-layouts: 2.86 us -> 45.8 us
  starting transfers between devices: 0.04 us -> 39.1 us
  matrix products: 26.1 us -> 50.9 us
  between operations: 13.4 us -> 17.8 us
    all_gather x2 -> x0, waiting for transfers between devices: 199 us -> none  [the longest x1 123 us: per_device(): gathered = lax.all_gather(precond, 'rows', axis=1, tiled=True)]
    ppermute x0 -> x49, waiting for transfers between devices: none -> 101 us  [the longest x15 58.6 us: per_device(): block = lax.ppermute(block, ('rows', 'feat'), pairs)]
    all_to_all x1 -> x0, blocking collectives: 96.3 us -> none  [per_device(): lax.all_to_all(local_scores, ('rows', 'feat'), split_axis=0, concat_axis=...]
    ppermute x0 -> x49, starting transfers between devices: none -> 39.1 us  [the longest x15 10 us: per_device(): block = lax.ppermute(block, ('rows', 'feat'), pairs)]
    dynamic_update_slice x0 -> x33, local copies, waits for them, and re-layouts: none -> 33.2 us  [the longest x18 17.5 us: per_device(): lax.dynamic_update_slice(whole, part, (first, owner * width + at * half))]
    dot_general x2 -> x13, matrix products: 26.1 us -> 50.9 us  [the longest x4 44.8 us: per_device(): lax.dot_general(rows, train_feats, (((1,), (1,)), ((), ())), preferred_el...]
    psum x1 -> x0, blocking collectives: 11.6 us -> none  [per_device(): precond = lax.psum(partial_pq, 'feat').astype(jnp.bfloat16)]
    broadcast_in_dim x0 -> x3, local copies, waits for them, and re-layouts: none -> 6.59 us  [the longest x1 4.26 us: per_device(): whole = jnp.zeros((total, width * n), jnp.bfloat16)]
  transfers between devices with their start and end apart: 2 -> 49, of which waited for: 2 -> 19; matrix products, arithmetic and copies ran while one was open for 0% -> 28% of each run, Pallas kernels for 0% -> 0%
where the time goes in v1:
time: 262 us; the launch traced here: 260 us
  waiting for transfers between devices  101 us (39%)
  matrix products  50.9 us (19%)
  local copies, waits for them, and re-layouts  45.8 us (17%)
  starting transfers between devices  39.1 us (15%)
  between operations  17.8 us (7%)
  other arithmetic  5.85 us (2%)
    ppermute x15, waiting for transfers between devices, per_device(): block = lax.ppermute(block, ('rows', 'feat'), pairs)  58.6 us
    dot_general x4, matrix products, per_device(): lax.dot_general(rows, train_feats, (((1,), (1,)), ((), ())), preferred_el...  44.8 us
    ppermute x6, waiting for transfers between devices, walk(): forward = lax.ppermute(forward, 'rows', ahead)  32.2 us
    dynamic_update_slice x18, local copies, waits for them, and re-layouts, per_device(): lax.dynamic_update_slice(whole, part, (first, owner * width + at * half))  17.5 us
    dynamic_update_slice x15, local copies, waits for them, and re-layouts, per_device(): scores = lax.dynamic_update_slice(scores, block, (0, source * columns))  15.6 us
    ppermute x15, starting transfers between devices, per_device(): block = lax.ppermute(block, ('rows', 'feat'), pairs)  10 us
    ppermute x9, starting transfers between devices, per_device(): other = lax.ppermute(block, 'feat', swap)  7.5 us
    ppermute x9, starting transfers between devices, per_device(): piece = (keep + lax.ppermute(give, 'feat', swap)).astype(jnp.bfloat16)  7.44 us
  transfers between devices with their start and end apart: 49, of which 19 were waited for; matrix products, arithmetic and copies ran while one was open for 28% of the time, Pallas kernels for 0%

profile of v1, /device:TPU:1, one launch (start us, length us, event | category | flops | bytes accessed | tf_op | source)
XLA Modules:
  0.0 259.9 jit_solution(2648894374698521577)
XLA Ops:
  0.0 2.1 collective-permute-start.1
  2.1 1.5 fusion.23
  3.7 1.0 collective-permute-start
  4.7 1.2 collective-permute-start.3
  5.9 1.2 dynamic_slice.182
  13.8 1.6 fusion.22
  21.7 1.5 fusion.25
  23.7 1.2 collective-permute-start.7
  25.0 9.8 %collective-permute-done.5 = bf16[128,2048]{1,0:T(8,128)(2,1)S(1)} collective-permute-done((bf16[128,2048]{1,0:T(8,128)(2,1)S(1)}, bf16[128,2048]{1,0:T(8,128)(2,1)S(1)}, u32[]{:S(2)}, u32[]{:S(2)}) %collective-permute-start.5) | collective-permute-done | bytes 524320 | tf_op jit(solution)/shard_map/ppermute | solution.py:25
  35.3 1.0 collective-permute-start.6
  37.9 0.9 collective-permute-start.8
  38.8 1.2 collective-permute-start.11
  40.1 9.7 %collective-permute-done.9 = bf16[128,2048]{1,0:T(8,128)(2,1)S(1)} collective-permute-done((bf16[128,2048]{1,0:T(8,128)(2,1)S(1)}, bf16[128,2048]{1,0:T(8,128)(2,1)S(1)}, u32[]{:S(2)}, u32[]{:S(2)}) %collective-permute-start.9) | collective-permute-done | bytes 524320 | tf_op jit(solution)/shard_map/ppermute | solution.py:25
  50.3 0.9 collective-permute-start.10
  51.2 1.1 collective-permute-done.11
  52.8 0.9 collective-permute-start.12
  53.7 1.4 collective-permute-start.13
  55.4 6.3 %collective-permute-done.13 = bf16[64,2048]{1,0:T(8,128)(2,1)S(1)} collective-permute-done((bf16[64,2048]{1,0:T(8,128)(2,1)S(1)}, bf16[64,2048]{1,0:T(8,128)(2,1)S(1)}, u32[]{:S(2)}, u32[]{:S(2)}) %collective-permute-start.13) | collective-permute-done | bytes 262176 | tf_op jit(solution)/shard_map/ppermute | solution.py:30
  65.4 1.3 collective-permute-start.18
  66.9 0.9 collective-permute-start.17
  73.4 4.3 %broadcast_in_dim.7 = bf16[1024,4096]{1,0:T(8,128)(2,1)} broadcast(bf16[]{:T(256)} %constant.748.clone.1), dimensions={} | broadcast | bytes 8388610 | tf_op jit(solution)/shard_map/broadcast_in_dim | solution.py:54
  78.7 1.1 collective-permute-start.19
  79.9 1.3 collective-permute-start.22
  81.9 1.9 constant_dynamic-update-slice_fusion.29
  83.8 1.3 multiply_reduce_fusion.11
  85.0 1.9 constant_dynamic-update-slice_fusion.27
  87.0 1.3 multiply_reduce_fusion.12
  88.2 5.4 %collective-permute-done.22 = bf16[1024,256]{1,0:T(8,128)(2,1)S(1)} collective-permute-done((bf16[1024,256]{1,0:T(8,128)(2,1)}, bf16[1024,256]{1,0:T(8,128)(2,1)S(1)}, u32[]{:S(2)}, u32[]{:S(2)}) %collective-permute-start.22) | collective-permute-done | bytes 524320 | tf_op jit(solution)/shard_map/ppermute | solution.py:25
  94.4 1.3 collective-permute-start.26
  96.9 0.9 constant_dynamic-update-slice_fusion.26
  98.9 0.9 constant_dynamic-update-slice_fusion.23
  99.8 0.9 constant_dynamic-update-slice_fusion.22
  100.7 7.3 %collective-permute-done.26 = bf16[1024,256]{1,0:T(8,128)(2,1)S(1)} collective-permute-done((bf16[1024,256]{1,0:T(8,128)(2,1)S(1)}, bf16[1024,256]{1,0:T(8,128)(2,1)S(1)}, u32[]{:S(2)}, u32[]{:S(2)}) %collective-permute-start.26) | collective-permute-done | bytes 524320 | tf_op jit(solution)/shard_map/ppermute | solution.py:25
  108.0 1.3 collective-permute-start.30
  110.2 1.3 collective-permute-start.27
  113.2 0.9 constant_dynamic-update-slice_fusion.20
  116.8 2.0 collective-permute-start.33
  119.6 0.9 constant_dynamic-update-slice_fusion.15
  121.4 0.9 constant_dynamic-update-slice_fusion.12
  125.8 12.0 %fusion = bf16[256,2048]{1,0:T(8,128)(2,1)} fusion(bf16[2048,4096]{1,0:T(8,128)(2,1)} %param.73, bf16[1024,4096]{1,0:T(8,128)(2,1)} %constant_dynamic-update-slice_fusion.34, s32[]{:T(128)S(6)} %select_n.531, f32[256]{0:T(256)S(1)} %get-tuple-element.349), kind=kOutput, calls=%fused_computation.1 | convolution fusion | flops 4296015872 | bytes 19923972 | tf_op jit(solution)/shard_map/dot_general | solution.py:76
  137.7 10.9 %fusion.3 = bf16[256,2048]{1,0:T(8,128)(2,1)S(1)} fusion(bf16[2048,4096]{1,0:T(8,128)(2,1)} %param.73, bf16[1024,4096]{1,0:T(8,128)(2,1)} %constant_dynamic-update-slice_fusion.34, s32[]{:T(128)S(6)} %select_n.498, f32[256]{0:T(256)S(1)} %get-tuple-element.352), kind=kOutput, calls=%fused_computation.7 | convolution fusion | flops 4296015872 | bytes 19923972 | tf_op jit(solution)/shard_map/dot_general | solution.py:76
  148.7 1.0 constant_dynamic-slice_fusion.4
  149.7 2.2 collective-permute-start.34
  152.1 3.2 %collective-permute-start.36 = (bf16[64,2048]{1,0:T(8,128)(2,1)}, bf16[64,2048]{1,0:T(8,128)(2,1)}, u32[]{:S(2)}, u32[]{:S(2)}) collective-permute-start(bf16[64,2048]{1,0:T(8,128)(2,1)} %get-tuple-element.346), channel_id=1, source_target_pairs={{0,10},{1,11},{2,8},{3,9},{4,14},{5,15},{6,12},{7,13},{8,2},{9,3},... | collective-permute-start | bytes 786440 | tf_op jit(solution)/shard_map/ppermute | solution.py:85
  155.3 10.9 %fusion.2 = bf16[256,2048]{1,0:T(8,128)(2,1)S(1)} fusion(bf16[2048,4096]{1,0:T(8,128)(2,1)} %param.73, bf16[1024,4096]{1,0:T(8,128)(2,1)} %constant_dynamic-update-slice_fusion.34, s32[]{:T(128)S(6)} %select_n.517, f32[256]{0:T(256)S(1)} %get-tuple-element.351), kind=kOutput, calls=%fused_computation.5 | convolution fusion | flops 4296015872 | bytes 19923972 | tf_op jit(solution)/shard_map/dot_general | solution.py:76
  166.2 0.9 constant_dynamic-slice_fusion
  168.0 10.9 %fusion.1 = bf16[256,2048]{1,0:T(8,128)(2,1)S(1)} fusion(bf16[2048,4096]{1,0:T(8,128)(2,1)} %param.73, bf16[1024,4096]{1,0:T(8,128)(2,1)} %constant_dynamic-update-slice_fusion.34, s32[]{:T(128)S(6)} %select_n.524, f32[256]{0:T(256)S(1)} %get-tuple-element.350), kind=kOutput, calls=%fused_computation.3 | convolution fusion | flops 4296015872 | bytes 19923972 | tf_op jit(solution)/shard_map/dot_general | solution.py:76
  179.0 7.9 %collective-permute-done.34 = bf16[64,2048]{1,0:T(8,128)(2,1)} collective-permute-done((bf16[64,2048]{1,0:T(8,128)(2,1)}, bf16[64,2048]{1,0:T(8,128)(2,1)}, u32[]{:S(2)}, u32[]{:S(2)}) %collective-permute-start.34) | collective-permute-done | bytes 262176 | tf_op jit(solution)/shard_map/ppermute | solution.py:85
  187.0 2.3 broadcast_in_dim.6
  189.3 1.8 constant_dynamic-update-slice_fusion.6
  191.0 7.8 %collective-permute-done.35 = bf16[64,2048]{1,0:T(8,128)(2,1)} collective-permute-done((bf16[64,2048]{1,0:T(8,128)(2,1)}, bf16[64,2048]{1,0:T(8,128)(2,1)}, u32[]{:S(2)}, u32[]{:S(2)}) %collective-permute-start.35) | collective-permute-done | bytes 262176 | tf_op jit(solution)/shard_map/ppermute | solution.py:85
  198.8 1.7 constant_dynamic-update-slice_fusion.5
  200.5 3.0 %collective-permute-done.36 = bf16[64,2048]{1,0:T(8,128)(2,1)} collective-permute-done((bf16[64,2048]{1,0:T(8,128)(2,1)}, bf16[64,2048]{1,0:T(8,128)(2,1)}, u32[]{:S(2)}, u32[]{:S(2)}) %collective-permute-start.36) | collective-permute-done | bytes 262176 | tf_op jit(solution)/shard_map/ppermute | solution.py:85
  203.6 1.7 constant_dynamic-update-slice_fusion.4
  205.2 15.5 %collective-permute-done.37 = bf16[64,2048]{1,0:T(8,128)(2,1)} collective-permute-done((bf16[64,2048]{1,0:T(8,128)(2,1)}, bf16[64,2048]{1,0:T(8,128)(2,1)}, u32[]{:S(2)}, u32[]{:S(2)}) %collective-permute-start.37) | collective-permute-done | bytes 262176 | tf_op jit(solution)/shard_map/ppermute | solution.py:85
  220.8 1.7 constant_dynamic-update-slice_fusion.3
  222.4 1.1 collective-permute-start.43
  223.6 1.7 constant_dynamic-update-slice_fusion.2
  228.5 3.7 %collective-permute-done.43 = bf16[64,2048]{1,0:T(8,128)(2,1)S(1)} collective-permute-done((bf16[64,2048]{1,0:T(8,128)(2,1)S(1)}, bf16[64,2048]{1,0:T(8,128)(2,1)S(1)}, u32[]{:S(2)}, u32[]{:S(2)}) %collective-permute-start.43) | collective-permute-done | bytes 262176 | tf_op jit(solution)/shard_map/ppermute | solution.py:85
  232.9 4.9 %collective-permute-done.44 = bf16[64,2048]{1,0:T(8,128)(2,1)S(1)} collective-permute-done((bf16[64,2048]{1,0:T(8,128)(2,1)S(1)}, bf16[64,2048]{1,0:T(8,128)(2,1)S(1)}, u32[]{:S(2)}, u32[]{:S(2)}) %collective-permute-start.44) | collective-permute-done | bytes 262176 | tf_op jit(solution)/shard_map/ppermute | solution.py:85
  238.5 4.4 %collective-permute-done.45 = bf16[64,2048]{1,0:T(8,128)(2,1)S(1)} collective-permute-done((bf16[64,2048]{1,0:T(8,128)(2,1)S(1)}, bf16[64,2048]{1,0:T(8,128)(2,1)S(1)}, u32[]{:S(2)}, u32[]{:S(2)}) %collective-permute-start.45) | collective-permute-done | bytes 262176 | tf_op jit(solution)/shard_map/ppermute | solution.py:85
  244.4 2.5 collective-permute-start.47
  246.9 2.0 collective-permute-done.46
  249.6 8.9 %collective-permute-done.47 = bf16[64,2048]{1,0:T(8,128)(2,1)S(1)} collective-permute-done((bf16[64,2048]{1,0:T(8,128)(2,1)S(1)}, bf16[64,2048]{1,0:T(8,128)(2,1)S(1)}, u32[]{:S(2)}, u32[]{:S(2)}) %collective-permute-start.47) | collective-permute-done | bytes 262176 | tf_op jit(solution)/shard_map/ppermute | solution.py:85
  (144 shorter events, 33.4 us)
Async XLA Ops:
  0.0 2.1 copy-start
  0.0 20.6 %collective-permute-start.1 = (bf16[128,2048]{1,0:T(8,128)(2,1)}, bf16[128,2048]{1,0:T(8,128)(2,1)S(1)}, u32[]{:S(2)}, u32[]{:S(2)}) collective-permute-start(bf16[128,2048]{1,0:T(8,128)(2,1)} %param.71), channel_id=1, source_target_pairs={{0,4},{4,8},{8,12},{12,14},{14,10},{10,6},{6,2},{2,0},{1,5},{5,9},... | collective-permute-start | bytes 1572872 | tf_op jit(solution)/shard_map/ppermute | solution.py:25
  3.7 16.8 %collective-permute-start = (f32[128,256]{1,0:T(8,128)S(1)}, f32[128,256]{1,0:T(8,128)S(1)}, u32[]{:S(2)}, u32[]{:S(2)}) collective-permute-start(f32[128,256]{1,0:T(8,128)S(1)} %constant_dynamic-slice_fusion.23), channel_id=1, source_target_pairs={{0,1},{1,0},{2,3},{3,2},{4,5},{5,4},{6,7},{7,6},{8,9},{9,8},{10,11... | collective-permute-start | bytes 393224 | tf_op jit(solution)/shard_map/ppermute | solution.py:51
  4.7 17.0 %collective-permute-start.3 = (bf16[128,2048]{1,0:T(8,128)(2,1)}, bf16[128,2048]{1,0:T(8,128)(2,1)}, u32[]{:S(2)}, u32[]{:S(2)}) collective-permute-start(bf16[128,2048]{1,0:T(8,128)(2,1)} %param.71), channel_id=1, source_target_pairs={{4,0},{8,4},{12,8},{14,12},{10,14},{6,10},{2,6},{0,2},{5,1},{9,5},... | collective-permute-start | bytes 1572872 | tf_op jit(solution)/shard_map/ppermute | solution.py:26
  21.1 3.9 %collective-permute-start.2 = (f32[128,256]{1,0:T(8,128)S(1)}, f32[128,256]{1,0:T(8,128)S(1)}, u32[]{:S(2)}, u32[]{:S(2)}) collective-permute-start(f32[128,256]{1,0:T(8,128)S(1)} %constant_dynamic-slice_fusion.21), channel_id=1, source_target_pairs={{0,1},{1,0},{2,3},{3,2},{4,5},{5,4},{6,7},{7,6},{8,9},{9,8},{10,11... | collective-permute-start | bytes 393224 | tf_op jit(solution)/shard_map/ppermute | solution.py:51
  21.5 13.4 %collective-permute-start.5 = (bf16[128,2048]{1,0:T(8,128)(2,1)S(1)}, bf16[128,2048]{1,0:T(8,128)(2,1)S(1)}, u32[]{:S(2)}, u32[]{:S(2)}) collective-permute-start(bf16[128,2048]{1,0:T(8,128)(2,1)S(1)} %collective-permute-done.1), channel_id=1, source_target_pairs={{0,4},{4,8},{8,12},{12,14},{14,10},{10,6},{6,2},{2,0},{1,5},{5,9},... | collective-permute-start | bytes 1572872 | tf_op jit(solution)/shard_map/ppermute | solution.py:25
  23.2 1.8 collective-permute-start.4
  23.7 13.7 %collective-permute-start.7 = (bf16[128,2048]{1,0:T(8,128)(2,1)}, bf16[128,2048]{1,0:T(8,128)(2,1)S(1)}, u32[]{:S(2)}, u32[]{:S(2)}) collective-permute-start(bf16[128,2048]{1,0:T(8,128)(2,1)} %collective-permute-done.3), channel_id=1, source_target_pairs={{4,0},{8,4},{12,8},{14,12},{10,14},{6,10},{2,6},{0,2},{5,1},{9,5},... | collective-permute-start | bytes 1572872 | tf_op jit(solution)/shard_map/ppermute | solution.py:26
  35.3 4.7 %collective-permute-start.6 = (f32[128,256]{1,0:T(8,128)S(1)}, f32[128,256]{1,0:T(8,128)S(1)}, u32[]{:S(2)}, u32[]{:S(2)}) collective-permute-start(f32[128,256]{1,0:T(8,128)S(1)} %constant_dynamic-slice_fusion.19), channel_id=1, source_target_pairs={{0,1},{1,0},{2,3},{3,2},{4,5},{5,4},{6,7},{7,6},{8,9},{9,8},{10,11... | collective-permute-start | bytes 393224 | tf_op jit(solution)/shard_map/ppermute | solution.py:51
  36.3 13.5 %collective-permute-start.9 = (bf16[128,2048]{1,0:T(8,128)(2,1)S(1)}, bf16[128,2048]{1,0:T(8,128)(2,1)S(1)}, u32[]{:S(2)}, u32[]{:S(2)}) collective-permute-start(bf16[128,2048]{1,0:T(8,128)(2,1)S(1)} %collective-permute-done.5), channel_id=1, source_target_pairs={{0,4},{4,8},{8,12},{12,14},{14,10},{10,6},{6,2},{2,0},{1,5},{5,9},... | collective-permute-start | bytes 1572872 | tf_op jit(solution)/shard_map/ppermute | solution.py:25
  37.9 2.2 collective-permute-start.8
  38.8 13.5 %collective-permute-start.11 = (bf16[128,2048]{1,0:T(8,128)(2,1)S(1)}, bf16[128,2048]{1,0:T(8,128)(2,1)S(1)}, u32[]{:S(2)}, u32[]{:S(2)}) collective-permute-start(bf16[128,2048]{1,0:T(8,128)(2,1)S(1)} %collective-permute-done.7), channel_id=1, source_target_pairs={{4,0},{8,4},{12,8},{14,12},{10,14},{6,10},{2,6},{0,2},{5,1},{9,5},... | collective-permute-start | bytes 1572872 | tf_op jit(solution)/shard_map/ppermute | solution.py:26
  50.3 5.0 %collective-permute-start.10 = (f32[128,256]{1,0:T(8,128)S(1)}, f32[128,256]{1,0:T(8,128)S(1)}, u32[]{:S(2)}, u32[]{:S(2)}) collective-permute-start(f32[128,256]{1,0:T(8,128)S(1)} %constant_dynamic-slice_fusion.17), channel_id=1, source_target_pairs={{0,1},{1,0},{2,3},{3,2},{4,5},{5,4},{6,7},{7,6},{8,9},{9,8},{10,11... | collective-permute-start | bytes 393224 | tf_op jit(solution)/shard_map/ppermute | solution.py:51
  52.8 2.6 collective-permute-start.12
  53.7 8.0 %collective-permute-start.13 = (bf16[64,2048]{1,0:T(8,128)(2,1)S(1)}, bf16[64,2048]{1,0:T(8,128)(2,1)S(1)}, u32[]{:S(2)}, u32[]{:S(2)}) collective-permute-start(bf16[64,2048]{1,0:T(8,128)(2,1)S(1)} %slice.196), channel_id=1, source_target_pairs={{0,4},{4,8},{8,12},{12,14},{14,10},{10,6},{6,2},{2,0},{1,5},{5,9},... | collective-permute-start | bytes 786440 | tf_op jit(solution)/shard_map/ppermute | solution.py:30
  55.1 8.0 %collective-permute-start.15 = (bf16[64,2048]{1,0:T(8,128)(2,1)S(1)}, bf16[64,2048]{1,0:T(8,128)(2,1)S(1)}, u32[]{:S(2)}, u32[]{:S(2)}) collective-permute-start(bf16[64,2048]{1,0:T(8,128)(2,1)S(1)} %slice.197), channel_id=1, source_target_pairs={{4,0},{8,4},{12,8},{14,12},{10,14},{6,10},{2,6},{0,2},{5,1},{9,5},... | collective-permute-start | bytes 786440 | tf_op jit(solution)/shard_map/ppermute | solution.py:31
  62.2 2.2 collective-permute-start.14
  63.6 1.8 collective-permute-start.16
  65.4 13.3 %collective-permute-start.18 = (bf16[1024,256]{1,0:T(8,128)(2,1)S(1)}, bf16[1024,256]{1,0:T(8,128)(2,1)}, u32[]{:S(2)}, u32[]{:S(2)}) collective-permute-start(bf16[1024,256]{1,0:T(8,128)(2,1)S(1)} %fusion.16), channel_id=1, source_target_pairs={{0,4},{4,8},{8,12},{12,14},{14,10},{10,6},{6,2},{2,0},{1,5},{5,9},... | collective-permute-start | bytes 1572872 | tf_op jit(solution)/shard_map/ppermute | solution.py:25
  66.7 14.4 %collective-permute-start.20 = (bf16[1024,256]{1,0:T(8,128)(2,1)S(1)}, bf16[1024,256]{1,0:T(8,128)(2,1)S(1)}, u32[]{:S(2)}, u32[]{:S(2)}) collective-permute-start(bf16[1024,256]{1,0:T(8,128)(2,1)S(1)} %fusion.16), channel_id=1, source_target_pairs={{4,0},{8,4},{12,8},{14,12},{10,14},{6,10},{2,6},{0,2},{5,1},{9,5},... | collective-permute-start | bytes 1572872 | tf_op jit(solution)/shard_map/ppermute | solution.py:26
  66.9 15.0 %collective-permute-start.17 = (bf16[1024,256]{1,0:T(8,128)(2,1)S(1)}, bf16[1024,256]{1,0:T(8,128)(2,1)}, u32[]{:S(2)}, u32[]{:S(2)}) collective-permute-start(bf16[1024,256]{1,0:T(8,128)(2,1)S(1)} %fusion.16), channel_id=1, source_target_pairs={{0,1},{1,0},{2,3},{3,2},{4,5},{5,4},{6,7},{7,6},{8,9},{9,8},{10,11... | collective-permute-start | bytes 1572872 | tf_op jit(solution)/shard_map/ppermute | solution.py:58
  78.7 17.7 %collective-permute-start.19 = (bf16[1024,256]{1,0:T(8,128)(2,1)}, bf16[1024,256]{1,0:T(8,128)(2,1)S(1)}, u32[]{:S(2)}, u32[]{:S(2)}) collective-permute-start(bf16[1024,256]{1,0:T(8,128)(2,1)} %collective-permute-done.18), channel_id=1, source_target_pairs={{0,1},{1,0},{2,3},{3,2},{4,5},{5,4},{6,7},{7,6},{8,9},{9,8},{10,11... | collective-permute-start | bytes 1572872 | tf_op jit(solution)/shard_map/ppermute | solution.py:58
  79.9 13.8 %collective-permute-start.22 = (bf16[1024,256]{1,0:T(8,128)(2,1)}, bf16[1024,256]{1,0:T(8,128)(2,1)S(1)}, u32[]{:S(2)}, u32[]{:S(2)}) collective-permute-start(bf16[1024,256]{1,0:T(8,128)(2,1)} %collective-permute-done.18), channel_id=1, source_target_pairs={{0,4},{4,8},{8,12},{12,14},{14,10},{10,6},{6,2},{2,0},{1,5},{5,9},... | collective-permute-start | bytes 1572872 | tf_op jit(solution)/shard_map/ppermute | solution.py:25
  81.2 17.5 %collective-permute-start.21 = (bf16[1024,256]{1,0:T(8,128)(2,1)S(1)}, bf16[1024,256]{1,0:T(8,128)(2,1)S(1)}, u32[]{:S(2)}, u32[]{:S(2)}) collective-permute-start(bf16[1024,256]{1,0:T(8,128)(2,1)S(1)} %collective-permute-done.20), channel_id=1, source_target_pairs={{0,1},{1,0},{2,3},{3,2},{4,5},{5,4},{6,7},{7,6},{8,9},{9,8},{10,11... | collective-permute-start | bytes 1572872 | tf_op jit(solution)/shard_map/ppermute | solution.py:58
  81.5 14.3 %collective-permute-start.24 = (bf16[1024,256]{1,0:T(8,128)(2,1)S(1)}, bf16[1024,256]{1,0:T(8,128)(2,1)S(1)}, u32[]{:S(2)}, u32[]{:S(2)}) collective-permute-start(bf16[1024,256]{1,0:T(8,128)(2,1)S(1)} %collective-permute-done.20), channel_id=1, source_target_pairs={{4,0},{8,4},{12,8},{14,12},{10,14},{6,10},{2,6},{0,2},{5,1},{9,5},... | collective-permute-start | bytes 1572872 | tf_op jit(solution)/shard_map/ppermute | solution.py:26
  93.6 18.7 %collective-permute-start.23 = (bf16[1024,256]{1,0:T(8,128)(2,1)S(1)}, bf16[1024,256]{1,0:T(8,128)(2,1)S(1)}, u32[]{:S(2)}, u32[]{:S(2)}) collective-permute-start(bf16[1024,256]{1,0:T(8,128)(2,1)S(1)} %collective-permute-done.22), channel_id=1, source_target_pairs={{0,1},{1,0},{2,3},{3,2},{4,5},{5,4},{6,7},{7,6},{8,9},{9,8},{10,11... | collective-permute-start | bytes 1572872 | tf_op jit(solution)/shard_map/ppermute | solution.py:58
  94.4 13.6 %collective-permute-start.26 = (bf16[1024,256]{1,0:T(8,128)(2,1)S(1)}, bf16[1024,256]{1,0:T(8,128)(2,1)S(1)}, u32[]{:S(2)}, u32[]{:S(2)}) collective-permute-start(bf16[1024,256]{1,0:T(8,128)(2,1)S(1)} %collective-permute-done.22), channel_id=1, source_target_pairs={{0,4},{4,8},{8,12},{12,14},{14,10},{10,6},{6,2},{2,0},{1,5},{5,9},... | collective-permute-start | bytes 1572872 | tf_op jit(solution)/shard_map/ppermute | solution.py:25
  95.7 16.3 %collective-permute-start.25 = (bf16[1024,256]{1,0:T(8,128)(2,1)S(1)}, bf16[1024,256]{1,0:T(8,128)(2,1)S(1)}, u32[]{:S(2)}, u32[]{:S(2)}) collective-permute-start(bf16[1024,256]{1,0:T(8,128)(2,1)S(1)} %collective-permute-done.24), channel_id=1, source_target_pairs={{0,1},{1,0},{2,3},{3,2},{4,5},{5,4},{6,7},{7,6},{8,9},{9,8},{10,11... | collective-permute-start | bytes 1572872 | tf_op jit(solution)/shard_map/ppermute | solution.py:58
  96.4 13.3 %collective-permute-start.28 = (bf16[1024,256]{1,0:T(8,128)(2,1)S(1)}, bf16[1024,256]{1,0:T(8,128)(2,1)S(1)}, u32[]{:S(2)}, u32[]{:S(2)}) collective-permute-start(bf16[1024,256]{1,0:T(8,128)(2,1)S(1)} %collective-permute-done.24), channel_id=1, source_target_pairs={{4,0},{8,4},{12,8},{14,12},{10,14},{6,10},{2,6},{0,2},{5,1},{9,5},... | collective-permute-start | bytes 1572872 | tf_op jit(solution)/shard_map/ppermute | solution.py:26
  108.0 8.0 %collective-permute-start.30 = (bf16[512,256]{1,0:T(8,128)(2,1)S(1)}, bf16[512,256]{1,0:T(8,128)(2,1)S(1)}, u32[]{:S(2)}, u32[]{:S(2)}) collective-permute-start(bf16[512,256]{1,0:T(8,128)(2,1)S(1)} %slice.198), channel_id=1, source_target_pairs={{0,4},{4,8},{8,12},{12,14},{14,10},{10,6},{6,2},{2,0},{1,5},{5,9},... | collective-permute-start | bytes 786440 | tf_op jit(solution)/shard_map/ppermute | solution.py:30
  109.8 7.0 %collective-permute-start.32 = (bf16[512,256]{1,0:T(8,128)(2,1)S(1)}, bf16[512,256]{1,0:T(8,128)(2,1)S(1)}, u32[]{:S(2)}, u32[]{:S(2)}) collective-permute-start(bf16[512,256]{1,0:T(8,128)(2,1)S(1)} %slice.199), channel_id=1, source_target_pairs={{4,0},{8,4},{12,8},{14,12},{10,14},{6,10},{2,6},{0,2},{5,1},{9,5},... | collective-permute-start | bytes 786440 | tf_op jit(solution)/shard_map/ppermute | solution.py:31
  110.2 9.1 %collective-permute-start.27 = (bf16[1024,256]{1,0:T(8,128)(2,1)S(1)}, bf16[1024,256]{1,0:T(8,128)(2,1)S(1)}, u32[]{:S(2)}, u32[]{:S(2)}) collective-permute-start(bf16[1024,256]{1,0:T(8,128)(2,1)S(1)} %collective-permute-done.26), channel_id=1, source_target_pairs={{0,1},{1,0},{2,3},{3,2},{4,5},{5,4},{6,7},{7,6},{8,9},{9,8},{10,11... | collective-permute-start | bytes 1572872 | tf_op jit(solution)/shard_map/ppermute | solution.py:58
  112.0 7.1 %collective-permute-start.29 = (bf16[1024,256]{1,0:T(8,128)(2,1)S(1)}, bf16[1024,256]{1,0:T(8,128)(2,1)S(1)}, u32[]{:S(2)}, u32[]{:S(2)}) collective-permute-start(bf16[1024,256]{1,0:T(8,128)(2,1)S(1)} %collective-permute-done.28), channel_id=1, source_target_pairs={{0,1},{1,0},{2,3},{3,2},{4,5},{5,4},{6,7},{7,6},{8,9},{9,8},{10,11... | collective-permute-start | bytes 1572872 | tf_op jit(solution)/shard_map/ppermute | solution.py:58
  116.0 7.0 %collective-permute-start.31 = (bf16[512,256]{1,0:T(8,128)(2,1)S(1)}, bf16[512,256]{1,0:T(8,128)(2,1)S(1)}, u32[]{:S(2)}, u32[]{:S(2)}) collective-permute-start(bf16[512,256]{1,0:T(8,128)(2,1)S(1)} %collective-permute-done.30), channel_id=1, source_target_pairs={{0,1},{1,0},{2,3},{3,2},{4,5},{5,4},{6,7},{7,6},{8,9},{9,8},{10,11... | collective-permute-start | bytes 786440 | tf_op jit(solution)/shard_map/ppermute | solution.py:58
  116.8 6.4 %collective-permute-start.33 = (bf16[512,256]{1,0:T(8,128)(2,1)S(1)}, bf16[512,256]{1,0:T(8,128)(2,1)S(1)}, u32[]{:S(2)}, u32[]{:S(2)}) collective-permute-start(bf16[512,256]{1,0:T(8,128)(2,1)S(1)} %collective-permute-done.32), channel_id=1, source_target_pairs={{0,1},{1,0},{2,3},{3,2},{4,5},{5,4},{6,7},{7,6},{8,9},{9,8},{10,11... | collective-permute-start | bytes 786440 | tf_op jit(solution)/shard_map/ppermute | solution.py:58
  149.7 37.3 %collective-permute-start.34 = (bf16[64,2048]{1,0:T(8,128)(2,1)}, bf16[64,2048]{1,0:T(8,128)(2,1)}, u32[]{:S(2)}, u32[]{:S(2)}) collective-permute-start(bf16[64,2048]{1,0:T(8,128)(2,1)} %get-tuple-element.348), channel_id=1, source_target_pairs={{0,8},{1,9},{2,10},{3,11},{4,12},{5,13},{6,14},{7,15},{8,0},{9,1},... | collective-permute-start | bytes 786440 | tf_op jit(solution)/shard_map/ppermute | solution.py:85
  151.9 47.0 %collective-permute-start.35 = (bf16[64,2048]{1,0:T(8,128)(2,1)}, bf16[64,2048]{1,0:T(8,128)(2,1)}, u32[]{:S(2)}, u32[]{:S(2)}) collective-permute-start(bf16[64,2048]{1,0:T(8,128)(2,1)} %get-tuple-element.347), channel_id=1, source_target_pairs={{0,9},{1,10},{2,11},{3,8},{4,13},{5,14},{6,15},{7,12},{8,1},{9,2},... | collective-permute-start | bytes 786440 | tf_op jit(solution)/shard_map/ppermute | solution.py:85
  152.1 51.5 %collective-permute-start.36 = (bf16[64,2048]{1,0:T(8,128)(2,1)}, bf16[64,2048]{1,0:T(8,128)(2,1)}, u32[]{:S(2)}, u32[]{:S(2)}) collective-permute-start(bf16[64,2048]{1,0:T(8,128)(2,1)} %get-tuple-element.346), channel_id=1, source_target_pairs={{0,10},{1,11},{2,8},{3,9},{4,14},{5,15},{6,12},{7,13},{8,2},{9,3},... | collective-permute-start | bytes 786440 | tf_op jit(solution)/shard_map/ppermute | solution.py:85
  155.3 65.5 %collective-permute-start.37 = (bf16[64,2048]{1,0:T(8,128)(2,1)}, bf16[64,2048]{1,0:T(8,128)(2,1)}, u32[]{:S(2)}, u32[]{:S(2)}) collective-permute-start(bf16[64,2048]{1,0:T(8,128)(2,1)} %get-tuple-element.345), channel_id=1, source_target_pairs={{0,11},{1,8},{2,9},{3,10},{4,15},{5,12},{6,13},{7,14},{8,3},{9,0},... | collective-permute-start | bytes 786440 | tf_op jit(solution)/shard_map/ppermute | solution.py:85
  167.2 55.3 %collective-permute-start.38 = (bf16[64,2048]{1,0:T(8,128)(2,1)}, bf16[64,2048]{1,0:T(8,128)(2,1)}, u32[]{:S(2)}, u32[]{:S(2)}) collective-permute-start(bf16[64,2048]{1,0:T(8,128)(2,1)} %get-tuple-element.344), channel_id=1, source_target_pairs={{0,4},{1,5},{2,6},{3,7},{4,8},{5,9},{6,10},{7,11},{8,12},{9,13},{1... | collective-permute-start | bytes 786440 | tf_op jit(solution)/shard_map/ppermute | solution.py:85
  178.9 19.9 %copy-start.2 = (bf16[64,2048]{1,0:T(8,128)(2,1)S(1)}, bf16[64,2048]{1,0:T(8,128)(2,1)}, u32[]{:S(2)}) copy-start(bf16[64,2048]{1,0:T(8,128)(2,1)} %get-tuple-element.342) | copy-start | bytes 786436
  187.0 38.2 %collective-permute-start.39 = (bf16[64,2048]{1,0:T(8,128)(2,1)}, bf16[64,2048]{1,0:T(8,128)(2,1)S(1)}, u32[]{:S(2)}, u32[]{:S(2)}) collective-permute-start(bf16[64,2048]{1,0:T(8,128)(2,1)} %get-tuple-element.343), channel_id=1, source_target_pairs={{0,5},{1,6},{2,7},{3,4},{4,9},{5,10},{6,11},{7,8},{8,13},{9,14},{1... | collective-permute-start | bytes 786440 | tf_op jit(solution)/shard_map/ppermute | solution.py:85
  189.3 54.4 %copy-start.1 = (bf16[256,2048]{1,0:T(8,128)(2,1)S(1)}, bf16[256,2048]{1,0:T(8,128)(2,1)}, u32[]{:S(2)}) copy-start(bf16[256,2048]{1,0:T(8,128)(2,1)} %fusion) | copy-start | bytes 3145732
  198.8 27.1 %collective-permute-start.40 = (bf16[64,2048]{1,0:T(8,128)(2,1)S(1)}, bf16[64,2048]{1,0:T(8,128)(2,1)S(1)}, u32[]{:S(2)}, u32[]{:S(2)}) collective-permute-start(bf16[64,2048]{1,0:T(8,128)(2,1)S(1)} %copy-done.2), channel_id=1, source_target_pairs={{0,6},{1,7},{2,4},{3,5},{4,10},{5,11},{6,8},{7,9},{8,14},{9,15},{1... | collective-permute-start | bytes 786440 | tf_op jit(solution)/shard_map/ppermute | solution.py:85
  203.6 23.1 %collective-permute-start.41 = (bf16[64,2048]{1,0:T(8,128)(2,1)S(1)}, bf16[64,2048]{1,0:T(8,128)(2,1)S(1)}, u32[]{:S(2)}, u32[]{:S(2)}) collective-permute-start(bf16[64,2048]{1,0:T(8,128)(2,1)S(1)} %get-tuple-element.341), channel_id=1, source_target_pairs={{0,7},{1,4},{2,5},{3,6},{4,11},{5,8},{6,9},{7,10},{8,15},{9,12},{1... | collective-permute-start | bytes 786440 | tf_op jit(solution)/shard_map/ppermute | solution.py:85
  220.8 7.0 %collective-permute-start.42 = (bf16[64,2048]{1,0:T(8,128)(2,1)S(1)}, bf16[64,2048]{1,0:T(8,128)(2,1)S(1)}, u32[]{:S(2)}, u32[]{:S(2)}) collective-permute-start(bf16[64,2048]{1,0:T(8,128)(2,1)S(1)} %get-tuple-element.340), channel_id=1, source_target_pairs={{0,12},{1,13},{2,14},{3,15},{4,0},{5,1},{6,2},{7,3},{8,4},{9,5},{1... | collective-permute-start | bytes 786440 | tf_op jit(solution)/shard_map/ppermute | solution.py:85
  222.4 9.7 %collective-permute-start.43 = (bf16[64,2048]{1,0:T(8,128)(2,1)S(1)}, bf16[64,2048]{1,0:T(8,128)(2,1)S(1)}, u32[]{:S(2)}, u32[]{:S(2)}) collective-permute-start(bf16[64,2048]{1,0:T(8,128)(2,1)S(1)} %get-tuple-element.339), channel_id=1, source_target_pairs={{0,13},{1,14},{2,15},{3,12},{4,1},{5,2},{6,3},{7,0},{8,5},{9,6},{1... | collective-permute-start | bytes 786440 | tf_op jit(solution)/shard_map/ppermute | solution.py:85
  225.2 12.6 %collective-permute-start.44 = (bf16[64,2048]{1,0:T(8,128)(2,1)S(1)}, bf16[64,2048]{1,0:T(8,128)(2,1)S(1)}, u32[]{:S(2)}, u32[]{:S(2)}) collective-permute-start(bf16[64,2048]{1,0:T(8,128)(2,1)S(1)} %get-tuple-element.338), channel_id=1, source_target_pairs={{0,14},{1,15},{2,12},{3,13},{4,2},{5,3},{6,0},{7,1},{8,6},{9,7},{1... | collective-permute-start | bytes 786440 | tf_op jit(solution)/shard_map/ppermute | solution.py:85
  226.0 17.0 %collective-permute-start.45 = (bf16[64,2048]{1,0:T(8,128)(2,1)S(1)}, bf16[64,2048]{1,0:T(8,128)(2,1)S(1)}, u32[]{:S(2)}, u32[]{:S(2)}) collective-permute-start(bf16[64,2048]{1,0:T(8,128)(2,1)S(1)} %get-tuple-element.337), channel_id=1, source_target_pairs={{0,15},{1,12},{2,13},{3,14},{4,3},{5,0},{6,1},{7,2},{8,7},{9,4},{1... | collective-permute-start | bytes 786440 | tf_op jit(solution)/shard_map/ppermute | solution.py:85
  244.4 4.5 %collective-permute-start.46 = (bf16[64,2048]{1,0:T(8,128)(2,1)S(1)}, bf16[64,2048]{1,0:T(8,128)(2,1)S(1)}, u32[]{:S(2)}, u32[]{:S(2)}) collective-permute-start(bf16[64,2048]{1,0:T(8,128)(2,1)S(1)} %get-tuple-element.335), channel_id=1, source_target_pairs={{0,1},{1,2},{2,3},{3,0},{4,5},{5,6},{6,7},{7,4},{8,9},{9,10},{10,1... | collective-permute-start | bytes 786440 | tf_op jit(solution)/shard_map/ppermute | solution.py:85
  244.4 14.1 %collective-permute-start.47 = (bf16[64,2048]{1,0:T(8,128)(2,1)S(1)}, bf16[64,2048]{1,0:T(8,128)(2,1)S(1)}, u32[]{:S(2)}, u32[]{:S(2)}) collective-permute-start(bf16[64,2048]{1,0:T(8,128)(2,1)S(1)} %get-tuple-element.334), channel_id=1, source_target_pairs={{0,2},{1,3},{2,0},{3,1},{4,6},{5,7},{6,4},{7,5},{8,10},{9,11},{10,... | collective-permute-start | bytes 786440 | tf_op jit(solution)/shard_map/ppermute | solution.py:85
  246.9 12.4 %collective-permute-start.48 = (bf16[64,2048]{1,0:T(8,128)(2,1)S(1)}, bf16[64,2048]{1,0:T(8,128)(2,1)S(1)}, u32[]{:S(2)}, u32[]{:S(2)}) collective-permute-start(bf16[64,2048]{1,0:T(8,128)(2,1)S(1)} %get-tuple-element.333), channel_id=1, source_target_pairs={{0,3},{1,0},{2,1},{3,2},{4,7},{5,4},{6,5},{7,6},{8,11},{9,8},{10,9... | collective-permute-start | bytes 786440 | tf_op jit(solution)/shard_map/ppermute | solution.py:85

commit v2 on v0

v2 whole, which is shorter than its diff:
```python
import functools

import jax
import jax.numpy as jnp
from jax import lax
from jax.experimental import pallas as pl
from jax.experimental.pallas import tpu as pltpu
from jax.sharding import PartitionSpec as P

epsilon = 1e-06


def snake(n):
    if n == 8:
        return (lambda r: jnp.where(r % 2 == 0, r // 2, n - 1 - r // 2),
                lambda p: jnp.where(p < n // 2, 2 * p, 2 * (n - 1 - p) + 1),
                [0, 2, 4, 6, 7, 5, 3, 1])
    return (lambda r: r), (lambda p: p), list(range(n))


def tile_rows(owners, shifts, span, where, *refs):
    n_near = 2 * (owners - 1)
    near, (top, top_other, bottom, bottom_other, train) = refs[:n_near], refs[n_near : n_near + 5]
    scores, left, held, lengths, piece_sems, train_sems = refs[n_near + 5 :]
    width = top.shape[1]
    upper = top.shape[0]
    tile = held.shape[1]
    steps = train.shape[0] // tile

    def stream(j):
        return pltpu.make_async_copy(train.at[pl.ds(pl.multiple_of(j * tile, tile), tile), :], held.at[j % 2], train_sems.at[j % 2])

    def lay(source, first, number, k):
        columns = pl.ds(pl.multiple_of(where[k] * width, width), width)
        return pltpu.make_async_copy(
            source.at[pl.ds(pl.multiple_of(first, span), span), :],
            left.at[pl.ds(number * span, span), columns],
            piece_sems.at[number, k],
        )

    stream(0).start()
    for number in range(len(shifts)):
        first = where[2 * owners + number] * span
        for k, piece in enumerate(near):
            lay(piece, first, number, k).start()

        @pl.when(first < upper)
        def _():
            lay(top, first, number, n_near).start()
            lay(top_other, first, number, n_near + 1).start()

        @pl.when(first >= upper)
        def _():
            lay(bottom, first - upper, number, n_near).start()
            lay(bottom_other, first - upper, number, n_near + 1).start()

    for number in range(len(shifts)):
        for k in range(2 * owners):
            lay(top, 0, number, k).wait()

    sums = 0.0
    for at in range(0, left.shape[1], 128):
        wide = left[:, at : at + 128].astype(jnp.float32)
        sums = sums + wide * wide
    lengths[...] = jnp.broadcast_to(jnp.sqrt(jnp.sum(sums, axis=1, keepdims=True) + epsilon), lengths.shape)

    def step(j, carry):
        @pl.when(j + 1 < steps)
        def _():
            stream(j + 1).start()

        stream(j).wait()
        across = (((1,), (1,)), ((), ()))
        if left.shape[0] < tile:
            raw = lax.dot_general(held[j % 2], left[...], across, preferred_element_type=jnp.float32).T
        else:
            raw = lax.dot_general(left[...], held[j % 2], across, preferred_element_type=jnp.float32)
        for at in range(0, tile, 128):
            columns = pl.ds(pl.multiple_of(j * tile + at, 128), 128)
            scores[:, columns] = (raw[:, at : at + 128] / lengths[...]).astype(scores.dtype)
        return carry

    lax.fori_loop(0, steps, step, 0)


def group_scores(near, far, where, targets, train_feats, span):
    owners = len(near) // 2 + 1
    columns, depth = train_feats.shape
    rows = span * len(targets)
    where = jnp.stack(list(where) + list(targets)).astype(jnp.int32)
    tile = 512
    anywhere = pl.BlockSpec(memory_space=pl.ANY)
    return pl.pallas_call(
        functools.partial(tile_rows, owners, tuple(range(len(targets))), span),
        out_shape=jax.ShapeDtypeStruct((rows, columns), jnp.bfloat16),
        in_specs=[pl.BlockSpec(memory_space=pltpu.SMEM)] + [anywhere] * (len(near) + len(far) + 1),
        out_specs=pl.BlockSpec(memory_space=pltpu.VMEM),
        scratch_shapes=[
            pltpu.VMEM((rows, depth), jnp.bfloat16),
            pltpu.VMEM((2, tile, depth), jnp.bfloat16),
            pltpu.VMEM((rows, 128), jnp.float32),
            pltpu.SemaphoreType.DMA((len(targets), 2 * owners)),
            pltpu.SemaphoreType.DMA((2,)),
        ],
        compiler_params=pltpu.CompilerParams(vmem_limit_bytes=VMEM_LIMIT),
        cost_estimate=pl.CostEstimate(flops=2 * rows * columns * depth, bytes_accessed=2 * columns * depth, transcendentals=0),
    )(where, *near, *far, train_feats)


VMEM_LIMIT = 58 * 2**20
IN_FLIGHT = 5


def per_device(n, queries, kernel, train_feats):
    to_place, to_owner, order = snake(n)
    ahead = [(order[i], order[(i + 1) % n]) for i in range(n)]
    back = [(b, a) for a, b in ahead]
    swap = [(0, 1), (1, 0)]
    row = lax.axis_index("rows")
    feat = lax.axis_index("feat")
    me = row * 2 + feat
    place = to_place(row)
    before = lambda step: to_owner((place + n - step) % n)
    after = lambda step: to_owner((place + step) % n)
    count = queries.shape[0]
    width = kernel.shape[1]
    half = width // 2
    total = count * n

    def product(block):
        partial = jnp.dot(block, kernel, preferred_element_type=jnp.float32)
        return (lax.dynamic_slice_in_dim(partial, feat * half, half, 1),
                lax.dynamic_slice_in_dim(partial, (1 - feat) * half, half, 1))

    blocks = [(row, queries)]
    forward = backward = queries
    for step in range(1, n // 2):
        forward = lax.ppermute(forward, "rows", ahead)
        backward = lax.ppermute(backward, "rows", back)
        blocks += [(before(step), forward), (after(step), backward)]
    top = lax.ppermute(forward[: count // 2], "rows", ahead)
    bottom = lax.ppermute(backward[count // 2 :], "rows", back)
    keep = jnp.zeros((total, half), jnp.float32)
    give = jnp.zeros((total, half), jnp.float32)
    for owner, block in blocks:
        a, b = product(block)
        keep = lax.dynamic_update_slice(keep, a, (owner * count, 0))
        give = lax.dynamic_update_slice(give, b, (owner * count, 0))
    mine = (keep + lax.ppermute(give, "feat", swap)).astype(jnp.bfloat16)
    a, b = product(jnp.concatenate([top, bottom]))
    mine = lax.dynamic_update_slice(
        mine, (a + lax.ppermute(b, "feat", swap)).astype(jnp.bfloat16), (before(n // 2) * count, 0)
    )

    near, where = [mine, lax.ppermute(mine, "feat", swap)], [me, row * 2 + 1 - feat]
    forward = backward = mine
    for step in range(1, n // 2):
        forward = lax.ppermute(forward, "rows", ahead)
        backward = lax.ppermute(backward, "rows", back)
        for owner, block in ((before(step), forward), (after(step), backward)):
            near += [block, lax.ppermute(block, "feat", swap)]
            where += [owner * 2 + feat, owner * 2 + 1 - feat]
    top = lax.ppermute(forward[: total // 2], "rows", ahead)
    bottom = lax.ppermute(backward[total // 2 :], "rows", back)
    far = [top, lax.ppermute(top, "feat", swap), bottom, lax.ppermute(bottom, "feat", swap)]
    where += [before(n // 2) * 2 + feat, before(n // 2) * 2 + 1 - feat]

    owned = count // 2
    devices = 2 * n
    columns = train_feats.shape[0]
    group = 256 // owned
    groups = devices // group
    span = group * owned
    at_group, at_place = me // group, me % group
    shifts = [groups // 2] + [k for k in range(1, groups) if k != groups // 2] + [0]
    target = lambda shift: (at_group + shift) % groups
    first = group_scores(near, far, where, [target(shifts[0])], train_feats, span)
    rest = group_scores(near, far, where, [target(k) for k in shifts[1:]], train_feats, span)
    scores = jnp.zeros((owned, devices * columns), jnp.bfloat16)
    order = [(0, turn) for turn in range(group)]
    for turn in range(group):
        order += [(number, turn) for number in range(1, groups)]
    going, sources = [], []
    for number, turn in order:
        shift = shifts[number]
        tiles, offset = (first, 0) if number == 0 else (rest, (number - 1) * span)
        block = lax.dynamic_slice_in_dim(tiles, offset + (at_place + turn) % group * owned, owned, 0)
        source = (at_group + groups - shift) % groups * group + (at_place + group - turn) % group
        if shift or turn:
            pairs = [(i, (i // group + shift) % groups * group + (i + turn) % group) for i in range(devices)]
            if len(going) >= IN_FLIGHT:
                block, going[-IN_FLIGHT] = lax.optimization_barrier((block, going[-IN_FLIGHT]))
            going.append(lax.ppermute(block, ("rows", "feat"), pairs))
            sources.append(source)
        else:
            own = (block, source)
    for block, source in [own] + list(zip(going, sources)):
        scores = lax.dynamic_update_slice(scores, block, (0, source * columns))
    return scores


def solution(mesh):
    placed = (P("rows", "feat"), P(("corpus", "feat"), "rows"), P(("corpus", "rows", "feat"), None))
    return jax.shard_map(
        functools.partial(per_device, mesh.shape["rows"]),
        mesh=mesh,
        in_specs=placed,
        out_specs=P(("rows", "feat"), "corpus"),
        check_vma=False,
    )
```

time: 356 us -> 227 us (0.64)
  blocking collectives: 108 us -> 0 us
  waiting for transfers between devices: 200 us -> 107 us
  starting transfers between devices: 0.04 us -> 47.9 us
  Pallas kernels: 0 us -> 33.6 us
  local copies, waits for them, and re-layouts: 2.86 us -> 29 us
  matrix products: 26.1 us -> 7.81 us
  between operations: 13.4 us -> 0.29 us
  other arithmetic: 5.23 us -> 1.35 us
    all_gather x2 -> x0, waiting for transfers between devices: 199 us -> none  [the longest x1 123 us: per_device(): gathered = lax.all_gather(precond, 'rows', axis=1, tiled=True)]
    ppermute x0 -> x42, waiting for transfers between devices: none -> 107 us  [the longest x6 39.7 us: per_device(): backward = lax.ppermute(backward, 'rows', back)]
    all_to_all x1 -> x0, blocking collectives: 96.3 us -> none  [per_device(): lax.all_to_all(local_scores, ('rows', 'feat'), split_axis=0, concat_axis=...]
    ppermute x0 -> x42, starting transfers between devices: none -> 47.9 us  [the longest x15 21.3 us: per_device(): going.append(lax.ppermute(block, ('rows', 'feat'), pairs))]
    pallas_call x0 -> x2, Pallas kernels: none -> 33.6 us  [group_scores(): pl.pallas_call(functools.partial(tile_rows, owners, tuple(range(len(targe...]
    dynamic_update_slice x0 -> x23, local copies, waits for them, and re-layouts: none -> 19.4 us  [the longest x15 14.6 us: per_device(): scores = lax.dynamic_update_slice(scores, block, (0, source * columns))]
    dot_general x2 -> x8, matrix products: 26.1 us -> 7.81 us  [product(): partial = jnp.dot(block, kernel, preferred_element_type=jnp.float32)]
    psum x1 -> x0, blocking collectives: 11.6 us -> none  [per_device(): precond = lax.psum(partial_pq, 'feat').astype(jnp.bfloat16)]
  transfers between devices with their start and end apart: 2 -> 42, of which waited for: 2 -> 19; matrix products, arithmetic and copies ran while one was open for 0% -> 15% of each run, Pallas kernels for 0% -> 9%
where the time goes in v2:
time: 227 us
  waiting for transfers between devices  107 us (47%)
  starting transfers between devices  47.9 us (21%)
  Pallas kernels  33.6 us (15%)
  local copies, waits for them, and re-layouts  29 us (13%)
  matrix products  7.81 us (3%)
    ppermute x6, waiting for transfers between devices, per_device(): backward = lax.ppermute(backward, 'rows', back)  39.7 us
    ppermute x15, waiting for transfers between devices, per_device(): going.append(lax.ppermute(block, ('rows', 'feat'), pairs))  36.9 us
    pallas_call x2, Pallas kernels, group_scores(): pl.pallas_call(functools.partial(tile_rows, owners, tuple(range(len(targe...  33.6 us
    ppermute x15, starting transfers between devices, per_device(): going.append(lax.ppermute(block, ('rows', 'feat'), pairs))  21.3 us
    ppermute x6, waiting for transfers between devices, per_device(): forward = lax.ppermute(forward, 'rows', ahead)  15.4 us
    dynamic_update_slice x15, local copies, waits for them, and re-layouts, per_device(): scores = lax.dynamic_update_slice(scores, block, (0, source * columns))  14.6 us
    ppermute x6, starting transfers between devices, per_device(): backward = lax.ppermute(backward, 'rows', back)  7.91 us
    dot_general x8, matrix products, product(): partial = jnp.dot(block, kernel, preferred_element_type=jnp.float32)  7.81 us
  transfers between devices with their start and end apart: 42, of which 19 were waited for; matrix products, arithmetic and copies ran while one was open for 15% of the time, Pallas kernels for 9%

profile of v2, /device:TPU:1, one launch (start us, length us, event | category | flops | bytes accessed | tf_op | source)
XLA Modules:
  0.0 226.8 jit_solution(2338173847354368838)
XLA Ops:
  0.0 2.1 collective-permute-start.1
  2.2 1.5 fusion.6
  3.7 1.0 broadcast.30.clone
  5.5 8.6 %collective-permute-done.1 = bf16[128,2048]{1,0:T(8,128)(2,1)} collective-permute-done((bf16[128,2048]{1,0:T(8,128)(2,1)}, bf16[128,2048]{1,0:T(8,128)(2,1)}, u32[]{:S(2)}, u32[]{:S(2)}) %collective-permute-start.1) | collective-permute-done | bytes 524320 | tf_op jit(solution)/shard_map/ppermute | solution.py:139
  14.1 1.1 collective-permute-start.3
  15.2 1.5 fusion.8
  17.1 1.5 fusion.7
  20.0 8.5 %collective-permute-done.2 = bf16[128,2048]{1,0:T(8,128)(2,1)S(1)} collective-permute-done((bf16[128,2048]{1,0:T(8,128)(2,1)}, bf16[128,2048]{1,0:T(8,128)(2,1)S(1)}, u32[]{:S(2)}, u32[]{:S(2)}) %collective-permute-start.2) | collective-permute-done | bytes 524320 | tf_op jit(solution)/shard_map/ppermute | solution.py:138
  29.7 0.8 collective-permute-start.5
  32.4 6.9 %collective-permute-done.4 = bf16[128,2048]{1,0:T(8,128)(2,1)S(1)} collective-permute-done((bf16[128,2048]{1,0:T(8,128)(2,1)S(1)}, bf16[128,2048]{1,0:T(8,128)(2,1)S(1)}, u32[]{:S(2)}, u32[]{:S(2)}) %collective-permute-start.4) | collective-permute-done | bytes 524320 | tf_op jit(solution)/shard_map/ppermute | solution.py:138
  41.6 3.6 %collective-permute-start.6 = (f32[1024,256]{1,0:T(8,128)}, f32[1024,256]{1,0:T(8,128)}, u32[]{:S(2)}, u32[]{:S(2)}) collective-permute-start(f32[1024,256]{1,0:T(8,128)} %get-tuple-element.61), channel_id=1, source_target_pairs={{0,1},{1,0},{2,3},{3,2},{4,5},{5,4},{6,7},{7,6},{8,9},{9,8},{10,11... | collective-permute-start | bytes 3145736 | tf_op jit(solution)/shard_map/ppermute | solution.py:149
  45.3 1.3 collective-permute-start.8
  46.6 0.7 slice.16
  47.5 5.9 %collective-permute-done.8 = bf16[64,2048]{1,0:T(8,128)(2,1)} collective-permute-done((bf16[64,2048]{1,0:T(8,128)(2,1)S(1)}, bf16[64,2048]{1,0:T(8,128)(2,1)}, u32[]{:S(2)}, u32[]{:S(2)}) %collective-permute-start.8) | collective-permute-done | bytes 262176 | tf_op jit(solution)/shard_map/ppermute | solution.py:142
  53.4 1.9 collective-permute-done.7
  55.2 1.5 fusion
  56.7 1.2 collective-permute-start.9
  57.9 1.3 add_convert_fusion
  59.3 1.3 collective-permute-start.13
  60.8 12.1 %collective-permute-done.13.refs_4_ = bf16[1024,256]{1,0:T(8,128)(2,1)S(1)} collective-permute-done((bf16[1024,256]{1,0:T(8,128)(2,1)S(1)}, bf16[1024,256]{1,0:T(8,128)(2,1)S(1)}, u32[]{:S(2)}, u32[]{:S(2)}) %collective-permute-start.13) | collective-permute-done | bytes 524320 | tf_op jit(solution)/shard_map/ppermute | solution.py:159
  72.9 1.3 collective-permute-start.17
  74.3 11.3 %collective-permute-done.17.refs_8_ = bf16[1024,256]{1,0:T(8,128)(2,1)S(1)} collective-permute-done((bf16[1024,256]{1,0:T(8,128)(2,1)S(1)}, bf16[1024,256]{1,0:T(8,128)(2,1)S(1)}, u32[]{:S(2)}, u32[]{:S(2)}) %collective-permute-start.17) | collective-permute-done | bytes 524320 | tf_op jit(solution)/shard_map/ppermute | solution.py:159
  85.6 1.3 collective-permute-start.21
  87.1 2.1 collective-permute-start.10
  89.8 7.7 %collective-permute-done.21.refs_12_ = bf16[1024,256]{1,0:T(8,128)(2,1)S(1)} collective-permute-done((bf16[1024,256]{1,0:T(8,128)(2,1)S(1)}, bf16[1024,256]{1,0:T(8,128)(2,1)S(1)}, u32[]{:S(2)}, u32[]{:S(2)}) %collective-permute-start.21) | collective-permute-done | bytes 524320 | tf_op jit(solution)/shard_map/ppermute | solution.py:159
  97.5 2.5 %collective-permute-start.18 = (bf16[1024,256]{1,0:T(8,128)(2,1)S(1)}, bf16[1024,256]{1,0:T(8,128)(2,1)S(1)}, u32[]{:S(2)}, u32[]{:S(2)}) collective-permute-start(bf16[1024,256]{1,0:T(8,128)(2,1)S(1)} %collective-permute-done.17.refs_8_), channel_id=1, source_target_pairs={{0,1},{1,0},{2,3},{3,2},{4,5},{5,4},{6,7},{7,6},{8,9},{9,8},{10,11... | collective-permute-start | bytes 1572872 | tf_op jit(solution)/shard_map/ppermute | solution.py:161
  100.0 1.5 collective-permute-start.16
  101.5 1.4 collective-permute-start.25
  103.7 5.9 %collective-permute-done.25.refs_16_ = bf16[512,256]{1,0:T(8,128)(2,1)S(1)} collective-permute-done((bf16[512,256]{1,0:T(8,128)(2,1)S(1)}, bf16[512,256]{1,0:T(8,128)(2,1)S(1)}, u32[]{:S(2)}, u32[]{:S(2)}) %collective-permute-start.25) | collective-permute-done | bytes 262176 | tf_op jit(solution)/shard_map/ppermute | solution.py:164
  110.3 1.0 collective-permute-done.23.refs_14_
  111.3 1.1 collective-permute-start.24
  113.9 12.2 %shard_map.38 = bf16[256,2048]{1,0:T(8,128)(2,1)} custom-call(s32[17]{0:T(128)} %stack.103.where, bf16[1024,256]{1,0:T(8,128)(2,1)} %copy-done.2, bf16[1024,256]{1,0:T(8,128)(2,1)} %copy-done.8, bf16[1024,256]{1,0:T(8,128)(2,1)} %copy-done.6, bf16[1024,256]{1,0:T(8,128)(2,1)} %copy-done.10, bf16[1024,256]{1,0:T(8,128)(2,1)} %copy-done.5, ...), custom_call_target="tpu_custom_call" | custom-call | flops 4294967296 | bytes 16777216 | tf_op jit(solution)/shard_map/pallas_call | solution.py:93
  126.1 1.3 constant_dynamic-slice_fusion.6
  127.5 3.2 %collective-permute-start.29 = (bf16[64,2048]{1,0:T(8,128)(2,1)S(1)}, bf16[64,2048]{1,0:T(8,128)(2,1)}, u32[]{:S(2)}, u32[]{:S(2)}) collective-permute-start(bf16[64,2048]{1,0:T(8,128)(2,1)S(1)} %get-tuple-element.58), channel_id=1, source_target_pairs={{0,10},{1,11},{2,8},{3,9},{4,14},{5,15},{6,12},{7,13},{8,2},{9,3},... | collective-permute-start | bytes 786440 | tf_op jit(solution)/shard_map/ppermute | solution.py:193
  131.4 2.9 %collective-permute-start.27 = (bf16[64,2048]{1,0:T(8,128)(2,1)S(1)}, bf16[64,2048]{1,0:T(8,128)(2,1)}, u32[]{:S(2)}, u32[]{:S(2)}) collective-permute-start(bf16[64,2048]{1,0:T(8,128)(2,1)S(1)} %get-tuple-element.60), channel_id=1, source_target_pairs={{0,8},{1,9},{2,10},{3,11},{4,12},{5,13},{6,14},{7,15},{8,0},{9,1},... | collective-permute-start | bytes 786440 | tf_op jit(solution)/shard_map/ppermute | solution.py:193
  134.2 21.4 %shard_map.37 = bf16[768,2048]{1,0:T(8,128)(2,1)} custom-call(s32[19]{0:T(128)} %stack.101.where, bf16[1024,256]{1,0:T(8,128)(2,1)} %copy-done.2, bf16[1024,256]{1,0:T(8,128)(2,1)} %copy-done.8, bf16[1024,256]{1,0:T(8,128)(2,1)} %copy-done.6, bf16[1024,256]{1,0:T(8,128)(2,1)} %copy-done.10, bf16[1024,256]{1,0:T(8,128)(2,1)} %copy-done.5, ...), custom_call_target="tpu_custom_call" | custom-call | flops 12884901888 | bytes 16777216 | tf_op jit(solution)/shard_map/pallas_call | solution.py:93
  155.6 2.4 %broadcast_in_dim.3 = bf16[64,32768]{1,0:T(8,128)(2,1)} broadcast(bf16[]{:T(256)} %constant.270.clone.1), dimensions={} | broadcast | bytes 4194306 | tf_op jit(solution)/shard_map/broadcast_in_dim | solution.py:179
  158.0 1.0 copy-done.1
  159.0 1.7 constant_dynamic-slice_fusion.15
  160.9 4.7 %collective-permute-done.29 = bf16[64,2048]{1,0:T(8,128)(2,1)} collective-permute-done((bf16[64,2048]{1,0:T(8,128)(2,1)S(1)}, bf16[64,2048]{1,0:T(8,128)(2,1)}, u32[]{:S(2)}, u32[]{:S(2)}) %collective-permute-start.29) | collective-permute-done | bytes 262176 | tf_op jit(solution)/shard_map/ppermute | solution.py:193
  165.6 10.7 %collective-permute-done.28 = bf16[64,2048]{1,0:T(8,128)(2,1)} collective-permute-done((bf16[64,2048]{1,0:T(8,128)(2,1)S(1)}, bf16[64,2048]{1,0:T(8,128)(2,1)}, u32[]{:S(2)}, u32[]{:S(2)}) %collective-permute-start.28) | collective-permute-done | bytes 262176 | tf_op jit(solution)/shard_map/ppermute | solution.py:193
  176.4 5.5 %collective-permute-done.27 = bf16[64,2048]{1,0:T(8,128)(2,1)} collective-permute-done((bf16[64,2048]{1,0:T(8,128)(2,1)S(1)}, bf16[64,2048]{1,0:T(8,128)(2,1)}, u32[]{:S(2)}, u32[]{:S(2)}) %collective-permute-start.27) | collective-permute-done | bytes 262176 | tf_op jit(solution)/shard_map/ppermute | solution.py:193
  181.8 2.7 %collective-permute-start.33 = (bf16[64,2048]{1,0:T(8,128)(2,1)}, bf16[64,2048]{1,0:T(8,128)(2,1)S(1)}, u32[]{:S(2)}, u32[]{:S(2)}) collective-permute-start(bf16[64,2048]{1,0:T(8,128)(2,1)} %get-tuple-element.32), channel_id=1, source_target_pairs={{0,5},{1,6},{2,7},{3,4},{4,9},{5,10},{6,11},{7,8},{8,13},{9,14},{1... | collective-permute-start | bytes 786440 | tf_op jit(solution)/shard_map/ppermute | solution.py:193
  184.6 1.5 collective-permute-start.34
  186.0 0.9 collective-permute-start.35
  187.5 1.7 constant_dynamic-update-slice_fusion.7
  189.2 1.7 constant_dynamic-update-slice_fusion.6
  190.8 1.7 constant_dynamic-update-slice_fusion.5
  192.5 0.7 constant_dynamic-update-slice_fusion.4
  193.2 1.7 constant_dynamic-update-slice_fusion.3
  194.9 3.6 %collective-permute-start.37 = (bf16[64,2048]{1,0:T(8,128)(2,1)}, bf16[64,2048]{1,0:T(8,128)(2,1)S(1)}, u32[]{:S(2)}, u32[]{:S(2)}) collective-permute-start(bf16[64,2048]{1,0:T(8,128)(2,1)} %get-tuple-element.40), channel_id=1, source_target_pairs={{0,14},{1,15},{2,12},{3,13},{4,2},{5,3},{6,0},{7,1},{8,6},{9,7},{1... | collective-permute-start | bytes 786440 | tf_op jit(solution)/shard_map/ppermute | solution.py:193
  198.5 0.9 collective-permute-start.38
  199.4 8.7 %collective-permute-done.34 = bf16[64,2048]{1,0:T(8,128)(2,1)S(1)} collective-permute-done((bf16[64,2048]{1,0:T(8,128)(2,1)}, bf16[64,2048]{1,0:T(8,128)(2,1)S(1)}, u32[]{:S(2)}, u32[]{:S(2)}) %collective-permute-start.34) | collective-permute-done | bytes 262176 | tf_op jit(solution)/shard_map/ppermute | solution.py:193
  208.1 4.2 %collective-permute-start.40 = (bf16[64,2048]{1,0:T(8,128)(2,1)}, bf16[64,2048]{1,0:T(8,128)(2,1)S(1)}, u32[]{:S(2)}, u32[]{:S(2)}) collective-permute-start(bf16[64,2048]{1,0:T(8,128)(2,1)} %get-tuple-element.43), channel_id=1, source_target_pairs={{0,15},{1,12},{2,13},{3,14},{4,3},{5,0},{6,1},{7,2},{8,7},{9,4},{1... | collective-permute-start | bytes 786440 | tf_op jit(solution)/shard_map/ppermute | solution.py:193
  212.3 0.7 constant_dynamic-update-slice_fusion.2
  213.0 0.7 constant_dynamic-update-slice_fusion.1
  215.9 0.7 constant_dynamic-update-slice_fusion.12
  216.6 4.5 %collective-permute-done.38 = bf16[64,2048]{1,0:T(8,128)(2,1)S(1)} collective-permute-done((bf16[64,2048]{1,0:T(8,128)(2,1)}, bf16[64,2048]{1,0:T(8,128)(2,1)S(1)}, u32[]{:S(2)}, u32[]{:S(2)}) %collective-permute-start.38) | collective-permute-done | bytes 262176 | tf_op jit(solution)/shard_map/ppermute | solution.py:193
  221.2 0.7 constant_dynamic-update-slice_fusion.11
  221.9 0.7 constant_dynamic-update-slice_fusion.10
  222.6 1.9 collective-permute-done.40
  224.5 0.7 constant_dynamic-update-slice_fusion.9
  225.2 0.9 collective-permute-done.41
  226.1 0.7 constant_dynamic-update-slice_fusion.8
  (93 shorter events, 16.1 us)
Async XLA Ops:
  0.0 2.2 copy-start
  0.0 14.1 %collective-permute-start.1 = (bf16[128,2048]{1,0:T(8,128)(2,1)}, bf16[128,2048]{1,0:T(8,128)(2,1)}, u32[]{:S(2)}, u32[]{:S(2)}) collective-permute-start(bf16[128,2048]{1,0:T(8,128)(2,1)} %param.3), channel_id=1, source_target_pairs={{4,0},{8,4},{12,8},{14,12},{10,14},{6,10},{2,6},{0,2},{5,1},{9,5},... | collective-permute-start | bytes 1572872 | tf_op jit(solution)/shard_map/ppermute | solution.py:139
  2.1 14.6 %collective-permute-start = (bf16[128,2048]{1,0:T(8,128)(2,1)}, bf16[128,2048]{1,0:T(8,128)(2,1)}, u32[]{:S(2)}, u32[]{:S(2)}) collective-permute-start(bf16[128,2048]{1,0:T(8,128)(2,1)} %param.3), channel_id=1, source_target_pairs={{0,4},{4,8},{8,12},{12,14},{14,10},{10,6},{6,2},{2,0},{1,5},{5,9},... | collective-permute-start | bytes 1572872 | tf_op jit(solution)/shard_map/ppermute | solution.py:138
  14.1 15.6 %collective-permute-start.3 = (bf16[128,2048]{1,0:T(8,128)(2,1)}, bf16[128,2048]{1,0:T(8,128)(2,1)S(1)}, u32[]{:S(2)}, u32[]{:S(2)}) collective-permute-start(bf16[128,2048]{1,0:T(8,128)(2,1)} %collective-permute-done.1), channel_id=1, source_target_pairs={{4,0},{8,4},{12,8},{14,12},{10,14},{6,10},{2,6},{0,2},{5,1},{9,5},... | collective-permute-start | bytes 1572872 | tf_op jit(solution)/shard_map/ppermute | solution.py:139
  16.7 11.9 %collective-permute-start.2 = (bf16[128,2048]{1,0:T(8,128)(2,1)}, bf16[128,2048]{1,0:T(8,128)(2,1)S(1)}, u32[]{:S(2)}, u32[]{:S(2)}) collective-permute-start(bf16[128,2048]{1,0:T(8,128)(2,1)} %collective-permute-done), channel_id=1, source_target_pairs={{0,4},{4,8},{8,12},{12,14},{14,10},{10,6},{6,2},{2,0},{1,5},{5,9},... | collective-permute-start | bytes 1572872 | tf_op jit(solution)/shard_map/ppermute | solution.py:138
  28.6 10.7 %collective-permute-start.4 = (bf16[128,2048]{1,0:T(8,128)(2,1)S(1)}, bf16[128,2048]{1,0:T(8,128)(2,1)S(1)}, u32[]{:S(2)}, u32[]{:S(2)}) collective-permute-start(bf16[128,2048]{1,0:T(8,128)(2,1)S(1)} %collective-permute-done.2), channel_id=1, source_target_pairs={{0,4},{4,8},{8,12},{12,14},{14,10},{10,6},{6,2},{2,0},{1,5},{5,9},... | collective-permute-start | bytes 1572872 | tf_op jit(solution)/shard_map/ppermute | solution.py:138
  29.7 10.8 %collective-permute-start.5 = (bf16[128,2048]{1,0:T(8,128)(2,1)S(1)}, bf16[128,2048]{1,0:T(8,128)(2,1)S(1)}, u32[]{:S(2)}, u32[]{:S(2)}) collective-permute-start(bf16[128,2048]{1,0:T(8,128)(2,1)S(1)} %collective-permute-done.3), channel_id=1, source_target_pairs={{4,0},{8,4},{12,8},{14,12},{10,14},{6,10},{2,6},{0,2},{5,1},{9,5},... | collective-permute-start | bytes 1572872 | tf_op jit(solution)/shard_map/ppermute | solution.py:139
  41.6 16.3 %collective-permute-start.6 = (f32[1024,256]{1,0:T(8,128)}, f32[1024,256]{1,0:T(8,128)}, u32[]{:S(2)}, u32[]{:S(2)}) collective-permute-start(f32[1024,256]{1,0:T(8,128)} %get-tuple-element.61), channel_id=1, source_target_pairs={{0,1},{1,0},{2,3},{3,2},{4,5},{5,4},{6,7},{7,6},{8,9},{9,8},{10,11... | collective-permute-start | bytes 3145736 | tf_op jit(solution)/shard_map/ppermute | solution.py:149
  45.3 8.1 %collective-permute-start.8 = (bf16[64,2048]{1,0:T(8,128)(2,1)S(1)}, bf16[64,2048]{1,0:T(8,128)(2,1)}, u32[]{:S(2)}, u32[]{:S(2)}) collective-permute-start(bf16[64,2048]{1,0:T(8,128)(2,1)S(1)} %slice.17), channel_id=1, source_target_pairs={{4,0},{8,4},{12,8},{14,12},{10,14},{6,10},{2,6},{0,2},{5,1},{9,5},... | collective-permute-start | bytes 786440 | tf_op jit(solution)/shard_map/ppermute | solution.py:142
  47.3 7.9 %collective-permute-start.7 = (bf16[64,2048]{1,0:T(8,128)(2,1)}, bf16[64,2048]{1,0:T(8,128)(2,1)}, u32[]{:S(2)}, u32[]{:S(2)}) collective-permute-start(bf16[64,2048]{1,0:T(8,128)(2,1)} %slice.16), channel_id=1, source_target_pairs={{0,4},{4,8},{8,12},{12,14},{14,10},{10,6},{6,2},{2,0},{1,5},{5,9},... | collective-permute-start | bytes 786440 | tf_op jit(solution)/shard_map/ppermute | solution.py:141
  56.7 2.5 %collective-permute-start.9 = (f32[128,256]{1,0:T(8,128)S(1)}, f32[128,256]{1,0:T(8,128)S(1)}, u32[]{:S(2)}, u32[]{:S(2)}) collective-permute-start(f32[128,256]{1,0:T(8,128)S(1)} %constant_dynamic-slice_fusion.14), channel_id=1, source_target_pairs={{0,1},{1,0},{2,3},{3,2},{4,5},{5,4},{6,7},{7,6},{8,9},{9,8},{10,11... | collective-permute-start | bytes 393224 | tf_op jit(solution)/shard_map/ppermute | solution.py:152
  59.3 27.8 %copy-start.2 = (bf16[1024,256]{1,0:T(8,128)(2,1)}, bf16[1024,256]{1,0:T(8,128)(2,1)S(1)}, u32[]{:S(2)}) copy-start(bf16[1024,256]{1,0:T(8,128)(2,1)S(1)} %fusion.4.refs_0_) | copy-start | bytes 1572868
  59.3 13.6 %collective-permute-start.13 = (bf16[1024,256]{1,0:T(8,128)(2,1)S(1)}, bf16[1024,256]{1,0:T(8,128)(2,1)S(1)}, u32[]{:S(2)}, u32[]{:S(2)}) collective-permute-start(bf16[1024,256]{1,0:T(8,128)(2,1)S(1)} %fusion.4.refs_0_), channel_id=1, source_target_pairs={{4,0},{8,4},{12,8},{14,12},{10,14},{6,10},{2,6},{0,2},{5,1},{9,5},... | collective-permute-start | bytes 1572872 | tf_op jit(solution)/shard_map/ppermute | solution.py:159
  60.6 13.5 %collective-permute-start.11 = (bf16[1024,256]{1,0:T(8,128)(2,1)S(1)}, bf16[1024,256]{1,0:T(8,128)(2,1)S(1)}, u32[]{:S(2)}, u32[]{:S(2)}) collective-permute-start(bf16[1024,256]{1,0:T(8,128)(2,1)S(1)} %fusion.4.refs_0_), channel_id=1, source_target_pairs={{0,4},{4,8},{8,12},{12,14},{14,10},{10,6},{6,2},{2,0},{1,5},{5,9},... | collective-permute-start | bytes 1572872 | tf_op jit(solution)/shard_map/ppermute | solution.py:158
  72.9 30.3 %copy-start.5 = (bf16[1024,256]{1,0:T(8,128)(2,1)}, bf16[1024,256]{1,0:T(8,128)(2,1)S(1)}, u32[]{:S(2)}) copy-start(bf16[1024,256]{1,0:T(8,128)(2,1)S(1)} %collective-permute-done.13.refs_4_) | copy-start | bytes 1572868
  72.9 12.8 %collective-permute-start.17 = (bf16[1024,256]{1,0:T(8,128)(2,1)S(1)}, bf16[1024,256]{1,0:T(8,128)(2,1)S(1)}, u32[]{:S(2)}, u32[]{:S(2)}) collective-permute-start(bf16[1024,256]{1,0:T(8,128)(2,1)S(1)} %collective-permute-done.13.refs_4_), channel_id=1, source_target_pairs={{4,0},{8,4},{12,8},{14,12},{10,14},{6,10},{2,6},{0,2},{5,1},{9,5},... | collective-permute-start | bytes 1572872 | tf_op jit(solution)/shard_map/ppermute | solution.py:159
  74.2 29.0 %copy-start.6 = (bf16[1024,256]{1,0:T(8,128)(2,1)}, bf16[1024,256]{1,0:T(8,128)(2,1)S(1)}, u32[]{:S(2)}) copy-start(bf16[1024,256]{1,0:T(8,128)(2,1)S(1)} %collective-permute-done.11.refs_2_) | copy-start | bytes 1572868
  74.2 12.8 %collective-permute-start.15 = (bf16[1024,256]{1,0:T(8,128)(2,1)S(1)}, bf16[1024,256]{1,0:T(8,128)(2,1)}, u32[]{:S(2)}, u32[]{:S(2)}) collective-permute-start(bf16[1024,256]{1,0:T(8,128)(2,1)S(1)} %collective-permute-done.11.refs_2_), channel_id=1, source_target_pairs={{0,4},{4,8},{8,12},{12,14},{14,10},{10,6},{6,2},{2,0},{1,5},{5,9},... | collective-permute-start | bytes 1572872 | tf_op jit(solution)/shard_map/ppermute | solution.py:158
  85.6 17.8 %copy-start.7 = (bf16[1024,256]{1,0:T(8,128)(2,1)}, bf16[1024,256]{1,0:T(8,128)(2,1)S(1)}, u32[]{:S(2)}) copy-start(bf16[1024,256]{1,0:T(8,128)(2,1)S(1)} %collective-permute-done.17.refs_8_) | copy-start | bytes 1572868
  85.6 11.8 %collective-permute-start.21 = (bf16[1024,256]{1,0:T(8,128)(2,1)S(1)}, bf16[1024,256]{1,0:T(8,128)(2,1)S(1)}, u32[]{:S(2)}, u32[]{:S(2)}) collective-permute-start(bf16[1024,256]{1,0:T(8,128)(2,1)S(1)} %collective-permute-done.17.refs_8_), channel_id=1, source_target_pairs={{4,0},{8,4},{12,8},{14,12},{10,14},{6,10},{2,6},{0,2},{5,1},{9,5},... | collective-permute-start | bytes 1572872 | tf_op jit(solution)/shard_map/ppermute | solution.py:159
  86.9 13.1 %collective-permute-start.19 = (bf16[1024,256]{1,0:T(8,128)(2,1)}, bf16[1024,256]{1,0:T(8,128)(2,1)S(1)}, u32[]{:S(2)}, u32[]{:S(2)}) collective-permute-start(bf16[1024,256]{1,0:T(8,128)(2,1)} %collective-permute-done.15.refs_6_), channel_id=1, source_target_pairs={{0,4},{4,8},{8,12},{12,14},{14,10},{10,6},{6,2},{2,0},{1,5},{5,9},... | collective-permute-start | bytes 1572872 | tf_op jit(solution)/shard_map/ppermute | solution.py:158
  87.1 14.4 %collective-permute-start.10 = (bf16[1024,256]{1,0:T(8,128)(2,1)S(1)}, bf16[1024,256]{1,0:T(8,128)(2,1)S(1)}, u32[]{:S(2)}, u32[]{:S(2)}) collective-permute-start(bf16[1024,256]{1,0:T(8,128)(2,1)S(1)} %fusion.4.refs_0_), channel_id=1, source_target_pairs={{0,1},{1,0},{2,3},{3,2},{4,5},{5,4},{6,7},{7,6},{8,9},{9,8},{10,11... | collective-permute-start | bytes 1572872 | tf_op jit(solution)/shard_map/ppermute | solution.py:155
  89.2 13.6 %collective-permute-start.14 = (bf16[1024,256]{1,0:T(8,128)(2,1)S(1)}, bf16[1024,256]{1,0:T(8,128)(2,1)S(1)}, u32[]{:S(2)}, u32[]{:S(2)}) collective-permute-start(bf16[1024,256]{1,0:T(8,128)(2,1)S(1)} %collective-permute-done.13.refs_4_), channel_id=1, source_target_pairs={{0,1},{1,0},{2,3},{3,2},{4,5},{5,4},{6,7},{7,6},{8,9},{9,8},{10,11... | collective-permute-start | bytes 1572872 | tf_op jit(solution)/shard_map/ppermute | solution.py:161
  89.2 13.9 %collective-permute-start.12 = (bf16[1024,256]{1,0:T(8,128)(2,1)S(1)}, bf16[1024,256]{1,0:T(8,128)(2,1)S(1)}, u32[]{:S(2)}, u32[]{:S(2)}) collective-permute-start(bf16[1024,256]{1,0:T(8,128)(2,1)S(1)} %collective-permute-done.11.refs_2_), channel_id=1, source_target_pairs={{0,1},{1,0},{2,3},{3,2},{4,5},{5,4},{6,7},{7,6},{8,9},{9,8},{10,11... | collective-permute-start | bytes 1572872 | tf_op jit(solution)/shard_map/ppermute | solution.py:161
  97.5 16.4 %copy-start.3 = (bf16[1024,256]{1,0:T(8,128)(2,1)}, bf16[1024,256]{1,0:T(8,128)(2,1)S(1)}, u32[]{:S(2)}) copy-start(bf16[1024,256]{1,0:T(8,128)(2,1)S(1)} %collective-permute-done.21.refs_12_) | copy-start | bytes 1572868
  97.5 6.0 %collective-permute-start.18 = (bf16[1024,256]{1,0:T(8,128)(2,1)S(1)}, bf16[1024,256]{1,0:T(8,128)(2,1)S(1)}, u32[]{:S(2)}, u32[]{:S(2)}) collective-permute-start(bf16[1024,256]{1,0:T(8,128)(2,1)S(1)} %collective-permute-done.17.refs_8_), channel_id=1, source_target_pairs={{0,1},{1,0},{2,3},{3,2},{4,5},{5,4},{6,7},{7,6},{8,9},{9,8},{10,11... | collective-permute-start | bytes 1572872 | tf_op jit(solution)/shard_map/ppermute | solution.py:161
  100.0 13.9 %copy-start.4 = (bf16[1024,256]{1,0:T(8,128)(2,1)}, bf16[1024,256]{1,0:T(8,128)(2,1)S(1)}, u32[]{:S(2)}) copy-start(bf16[1024,256]{1,0:T(8,128)(2,1)S(1)} %collective-permute-done.19.refs_10_) | copy-start | bytes 1572868
  100.0 13.7 %collective-permute-start.16 = (bf16[1024,256]{1,0:T(8,128)(2,1)}, bf16[1024,256]{1,0:T(8,128)(2,1)}, u32[]{:S(2)}, u32[]{:S(2)}) collective-permute-start(bf16[1024,256]{1,0:T(8,128)(2,1)} %collective-permute-done.15.refs_6_), channel_id=1, source_target_pairs={{0,1},{1,0},{2,3},{3,2},{4,5},{5,4},{6,7},{7,6},{8,9},{9,8},{10,11... | collective-permute-start | bytes 1572872 | tf_op jit(solution)/shard_map/ppermute | solution.py:161
  101.5 2.0 copy-start.8
  101.5 8.1 %collective-permute-start.25 = (bf16[512,256]{1,0:T(8,128)(2,1)S(1)}, bf16[512,256]{1,0:T(8,128)(2,1)S(1)}, u32[]{:S(2)}, u32[]{:S(2)}) collective-permute-start(bf16[512,256]{1,0:T(8,128)(2,1)S(1)} %slice.19), channel_id=1, source_target_pairs={{4,0},{8,4},{12,8},{14,12},{10,14},{6,10},{2,6},{0,2},{5,1},{9,5},... | collective-permute-start | bytes 786440 | tf_op jit(solution)/shard_map/ppermute | solution.py:164
  102.9 0.8 copy-start.9
  102.9 10.8 %collective-permute-start.22 = (bf16[1024,256]{1,0:T(8,128)(2,1)S(1)}, bf16[1024,256]{1,0:T(8,128)(2,1)}, u32[]{:S(2)}, u32[]{:S(2)}) collective-permute-start(bf16[1024,256]{1,0:T(8,128)(2,1)S(1)} %collective-permute-done.21.refs_12_), channel_id=1, source_target_pairs={{0,1},{1,0},{2,3},{3,2},{4,5},{5,4},{6,7},{7,6},{8,9},{9,8},{10,11... | collective-permute-start | bytes 1572872 | tf_op jit(solution)/shard_map/ppermute | solution.py:161
  103.2 6.4 %copy-start.10 = (bf16[1024,256]{1,0:T(8,128)(2,1)}, bf16[1024,256]{1,0:T(8,128)(2,1)S(1)}, u32[]{:S(2)}) copy-start(bf16[1024,256]{1,0:T(8,128)(2,1)S(1)} %collective-permute-done.12.refs_3_) | copy-start | bytes 1572868
  103.2 10.5 %collective-permute-start.20 = (bf16[1024,256]{1,0:T(8,128)(2,1)S(1)}, bf16[1024,256]{1,0:T(8,128)(2,1)}, u32[]{:S(2)}, u32[]{:S(2)}) collective-permute-start(bf16[1024,256]{1,0:T(8,128)(2,1)S(1)} %collective-permute-done.19.refs_10_), channel_id=1, source_target_pairs={{0,1},{1,0},{2,3},{3,2},{4,5},{5,4},{6,7},{7,6},{8,9},{9,8},{10,11... | collective-permute-start | bytes 1572872 | tf_op jit(solution)/shard_map/ppermute | solution.py:161
  103.5 6.8 %copy-start.11 = (bf16[1024,256]{1,0:T(8,128)(2,1)}, bf16[1024,256]{1,0:T(8,128)(2,1)S(1)}, u32[]{:S(2)}) copy-start(bf16[1024,256]{1,0:T(8,128)(2,1)S(1)} %collective-permute-done.18.refs_9_) | copy-start | bytes 1572868
  103.5 7.8 %collective-permute-start.23 = (bf16[512,256]{1,0:T(8,128)(2,1)S(1)}, bf16[512,256]{1,0:T(8,128)(2,1)}, u32[]{:S(2)}, u32[]{:S(2)}) collective-permute-start(bf16[512,256]{1,0:T(8,128)(2,1)S(1)} %slice.18), channel_id=1, source_target_pairs={{0,4},{4,8},{8,12},{12,14},{14,10},{10,6},{6,2},{2,0},{1,5},{5,9},... | collective-permute-start | bytes 786440 | tf_op jit(solution)/shard_map/ppermute | solution.py:163
  109.6 4.3 %copy-start.12 = (bf16[512,256]{1,0:T(8,128)(2,1)}, bf16[512,256]{1,0:T(8,128)(2,1)S(1)}, u32[]{:S(2)}) copy-start(bf16[512,256]{1,0:T(8,128)(2,1)S(1)} %collective-permute-done.25.refs_16_) | copy-start | bytes 786436
  109.6 4.1 %collective-permute-start.26 = (bf16[512,256]{1,0:T(8,128)(2,1)S(1)}, bf16[512,256]{1,0:T(8,128)(2,1)}, u32[]{:S(2)}, u32[]{:S(2)}) collective-permute-start(bf16[512,256]{1,0:T(8,128)(2,1)S(1)} %collective-permute-done.25.refs_16_), channel_id=1, source_target_pairs={{0,1},{1,0},{2,3},{3,2},{4,5},{5,4},{6,7},{7,6},{8,9},{9,8},{10,11... | collective-permute-start | bytes 786440 | tf_op jit(solution)/shard_map/ppermute | solution.py:165
  111.3 2.6 %collective-permute-start.24 = (bf16[512,256]{1,0:T(8,128)(2,1)}, bf16[512,256]{1,0:T(8,128)(2,1)}, u32[]{:S(2)}, u32[]{:S(2)}) collective-permute-start(bf16[512,256]{1,0:T(8,128)(2,1)} %collective-permute-done.23.refs_14_), channel_id=1, source_target_pairs={{0,1},{1,0},{2,3},{3,2},{4,5},{5,4},{6,7},{7,6},{8,9},{9,8},{10,11... | collective-permute-start | bytes 786440 | tf_op jit(solution)/shard_map/ppermute | solution.py:165
  127.4 33.5 %collective-permute-start.30 = (bf16[64,2048]{1,0:T(8,128)(2,1)S(1)}, bf16[64,2048]{1,0:T(8,128)(2,1)S(1)}, u32[]{:S(2)}, u32[]{:S(2)}) collective-permute-start(bf16[64,2048]{1,0:T(8,128)(2,1)S(1)} %get-tuple-element.57), channel_id=1, source_target_pairs={{0,11},{1,8},{2,9},{3,10},{4,15},{5,12},{6,13},{7,14},{8,3},{9,0},... | collective-permute-start | bytes 786440 | tf_op jit(solution)/shard_map/ppermute | solution.py:193
  127.5 38.1 %collective-permute-start.29 = (bf16[64,2048]{1,0:T(8,128)(2,1)S(1)}, bf16[64,2048]{1,0:T(8,128)(2,1)}, u32[]{:S(2)}, u32[]{:S(2)}) collective-permute-start(bf16[64,2048]{1,0:T(8,128)(2,1)S(1)} %get-tuple-element.58), channel_id=1, source_target_pairs={{0,10},{1,11},{2,8},{3,9},{4,14},{5,15},{6,12},{7,13},{8,2},{9,3},... | collective-permute-start | bytes 786440 | tf_op jit(solution)/shard_map/ppermute | solution.py:193
  130.7 45.7 %collective-permute-start.28 = (bf16[64,2048]{1,0:T(8,128)(2,1)S(1)}, bf16[64,2048]{1,0:T(8,128)(2,1)}, u32[]{:S(2)}, u32[]{:S(2)}) collective-permute-start(bf16[64,2048]{1,0:T(8,128)(2,1)S(1)} %get-tuple-element.59), channel_id=1, source_target_pairs={{0,9},{1,10},{2,11},{3,8},{4,13},{5,14},{6,15},{7,12},{8,1},{9,2},... | collective-permute-start | bytes 786440 | tf_op jit(solution)/shard_map/ppermute | solution.py:193
  131.4 50.5 %collective-permute-start.27 = (bf16[64,2048]{1,0:T(8,128)(2,1)S(1)}, bf16[64,2048]{1,0:T(8,128)(2,1)}, u32[]{:S(2)}, u32[]{:S(2)}) collective-permute-start(bf16[64,2048]{1,0:T(8,128)(2,1)S(1)} %get-tuple-element.60), channel_id=1, source_target_pairs={{0,8},{1,9},{2,10},{3,11},{4,12},{5,13},{6,14},{7,15},{8,0},{9,1},... | collective-permute-start | bytes 786440 | tf_op jit(solution)/shard_map/ppermute | solution.py:193
  155.6 3.4 %copy-start.1 = (bf16[768,2048]{1,0:T(8,128)(2,1)S(1)}, bf16[768,2048]{1,0:T(8,128)(2,1)}, u32[]{:S(2)}) copy-start(bf16[768,2048]{1,0:T(8,128)(2,1)} %shard_map.37) | copy-start | bytes 9437188
  160.7 26.2 %collective-permute-start.31 = (bf16[64,2048]{1,0:T(8,128)(2,1)}, bf16[64,2048]{1,0:T(8,128)(2,1)}, u32[]{:S(2)}, u32[]{:S(2)}) collective-permute-start(bf16[64,2048]{1,0:T(8,128)(2,1)} %get-tuple-element.50), channel_id=1, source_target_pairs={{0,4},{1,5},{2,6},{3,7},{4,8},{5,9},{6,10},{7,11},{8,12},{9,13},{1... | collective-permute-start | bytes 786440 | tf_op jit(solution)/shard_map/ppermute | solution.py:193
  181.8 13.1 %collective-permute-start.32 = (bf16[64,2048]{1,0:T(8,128)(2,1)}, bf16[64,2048]{1,0:T(8,128)(2,1)S(1)}, u32[]{:S(2)}, u32[]{:S(2)}) collective-permute-start(bf16[64,2048]{1,0:T(8,128)(2,1)} %get-tuple-element.30), channel_id=1, source_target_pairs={{0,12},{1,13},{2,14},{3,15},{4,0},{5,1},{6,2},{7,3},{8,4},{9,5},{1... | collective-permute-start | bytes 786440 | tf_op jit(solution)/shard_map/ppermute | solution.py:193
  181.8 16.7 %collective-permute-start.33 = (bf16[64,2048]{1,0:T(8,128)(2,1)}, bf16[64,2048]{1,0:T(8,128)(2,1)S(1)}, u32[]{:S(2)}, u32[]{:S(2)}) collective-permute-start(bf16[64,2048]{1,0:T(8,128)(2,1)} %get-tuple-element.32), channel_id=1, source_target_pairs={{0,5},{1,6},{2,7},{3,4},{4,9},{5,10},{6,11},{7,8},{8,13},{9,14},{1... | collective-permute-start | bytes 786440 | tf_op jit(solution)/shard_map/ppermute | solution.py:193
  184.6 23.6 %collective-permute-start.34 = (bf16[64,2048]{1,0:T(8,128)(2,1)}, bf16[64,2048]{1,0:T(8,128)(2,1)S(1)}, u32[]{:S(2)}, u32[]{:S(2)}) collective-permute-start(bf16[64,2048]{1,0:T(8,128)(2,1)} %get-tuple-element.34), channel_id=1, source_target_pairs={{0,13},{1,14},{2,15},{3,12},{4,1},{5,2},{6,3},{7,0},{8,5},{9,6},{1... | collective-permute-start | bytes 786440 | tf_op jit(solution)/shard_map/ppermute | solution.py:193
  186.0 22.1 %collective-permute-start.35 = (bf16[64,2048]{1,0:T(8,128)(2,1)}, bf16[64,2048]{1,0:T(8,128)(2,1)S(1)}, u32[]{:S(2)}, u32[]{:S(2)}) collective-permute-start(bf16[64,2048]{1,0:T(8,128)(2,1)} %get-tuple-element.36), channel_id=1, source_target_pairs={{0,1},{1,2},{2,3},{3,0},{4,5},{5,6},{6,7},{7,4},{8,9},{9,10},{10,1... | collective-permute-start | bytes 786440 | tf_op jit(solution)/shard_map/ppermute | solution.py:193
  186.9 25.4 %collective-permute-start.36 = (bf16[64,2048]{1,0:T(8,128)(2,1)}, bf16[64,2048]{1,0:T(8,128)(2,1)S(1)}, u32[]{:S(2)}, u32[]{:S(2)}) collective-permute-start(bf16[64,2048]{1,0:T(8,128)(2,1)} %get-tuple-element.38), channel_id=1, source_target_pairs={{0,6},{1,7},{2,4},{3,5},{4,10},{5,11},{6,8},{7,9},{8,14},{9,15},{1... | collective-permute-start | bytes 786440 | tf_op jit(solution)/shard_map/ppermute | solution.py:193
  194.9 21.0 %collective-permute-start.37 = (bf16[64,2048]{1,0:T(8,128)(2,1)}, bf16[64,2048]{1,0:T(8,128)(2,1)S(1)}, u32[]{:S(2)}, u32[]{:S(2)}) collective-permute-start(bf16[64,2048]{1,0:T(8,128)(2,1)} %get-tuple-element.40), channel_id=1, source_target_pairs={{0,14},{1,15},{2,12},{3,13},{4,2},{5,3},{6,0},{7,1},{8,6},{9,7},{1... | collective-permute-start | bytes 786440 | tf_op jit(solution)/shard_map/ppermute | solution.py:193
  198.5 22.7 %collective-permute-start.38 = (bf16[64,2048]{1,0:T(8,128)(2,1)}, bf16[64,2048]{1,0:T(8,128)(2,1)S(1)}, u32[]{:S(2)}, u32[]{:S(2)}) collective-permute-start(bf16[64,2048]{1,0:T(8,128)(2,1)} %get-tuple-element.41), channel_id=1, source_target_pairs={{0,2},{1,3},{2,0},{3,1},{4,6},{5,7},{6,4},{7,5},{8,10},{9,11},{10,... | collective-permute-start | bytes 786440 | tf_op jit(solution)/shard_map/ppermute | solution.py:193
  208.1 13.8 %collective-permute-start.39 = (bf16[64,2048]{1,0:T(8,128)(2,1)}, bf16[64,2048]{1,0:T(8,128)(2,1)S(1)}, u32[]{:S(2)}, u32[]{:S(2)}) collective-permute-start(bf16[64,2048]{1,0:T(8,128)(2,1)} %get-tuple-element.42), channel_id=1, source_target_pairs={{0,7},{1,4},{2,5},{3,6},{4,11},{5,8},{6,9},{7,10},{8,15},{9,12},{1... | collective-permute-start | bytes 786440 | tf_op jit(solution)/shard_map/ppermute | solution.py:193
  208.1 16.3 %collective-permute-start.40 = (bf16[64,2048]{1,0:T(8,128)(2,1)}, bf16[64,2048]{1,0:T(8,128)(2,1)S(1)}, u32[]{:S(2)}, u32[]{:S(2)}) collective-permute-start(bf16[64,2048]{1,0:T(8,128)(2,1)} %get-tuple-element.43), channel_id=1, source_target_pairs={{0,15},{1,12},{2,13},{3,14},{4,3},{5,0},{6,1},{7,2},{8,7},{9,4},{1... | collective-permute-start | bytes 786440 | tf_op jit(solution)/shard_map/ppermute | solution.py:193
  212.3 13.8 %collective-permute-start.41 = (bf16[64,2048]{1,0:T(8,128)(2,1)}, bf16[64,2048]{1,0:T(8,128)(2,1)S(1)}, u32[]{:S(2)}, u32[]{:S(2)}) collective-permute-start(bf16[64,2048]{1,0:T(8,128)(2,1)} %get-tuple-element.44), channel_id=1, source_target_pairs={{0,3},{1,0},{2,1},{3,2},{4,7},{5,4},{6,5},{7,6},{8,11},{9,8},{10,9... | collective-permute-start | bytes 786440 | tf_op jit(solution)/shard_map/ppermute | solution.py:193

commit v3 on v2

--- a/solution.py
+++ b/solution.py
@@ -18,7 +18,7 @@
     return (lambda r: r), (lambda p: p), list(range(n))
 
 
-def tile_rows(owners, shifts, span, where, *refs):
+def tile_rows(owners, skip, shifts, span, where, *refs):
     n_near = 2 * (owners - 1)
     near, (top, top_other, bottom, bottom_other, train) = refs[:n_near], refs[n_near : n_near + 5]
     scores, left, held, lengths, piece_sems, train_sems = refs[n_near + 5 :]
@@ -40,7 +40,7 @@
 
     stream(0).start()
     for number in range(len(shifts)):
-        first = where[2 * owners + number] * span
+        first = where[2 * owners + skip + number] * span
         for k, piece in enumerate(near):
             lay(piece, first, number, k).start()
 
@@ -83,15 +83,126 @@
     lax.fori_loop(0, steps, step, 0)
 
 
-def group_scores(near, far, where, targets, train_feats, span):
+def some_columns(count, base, group_at, far, span, where, *refs):
+    near, refs = refs[:count], refs[count:]
+    if far:
+        top, top_other, bottom, bottom_other, train, raw_in, squares_in = refs[:7]
+        scores, left, held, before, sums, piece_sems, train_sems, in_sems = refs[7:]
+    else:
+        train, raw_out, squares_out, left, held, piece_sems, train_sems = refs
+    total = count + (2 if far else 0)
+    width = (near[0] if near else top).shape[1]
+    tile = held.shape[1]
+    steps = train.shape[0] // tile
+    first = where[group_at] * span
+
+    def stream(j, k):
+        return pltpu.make_async_copy(
+            train.at[pl.ds(pl.multiple_of(j * tile, tile), tile), pl.ds(pl.multiple_of(where[base + k] * width, width), width)],
+            held.at[j % 2, :, pl.ds(k * width, width)],
+            train_sems.at[j % 2, k],
+        )
+
+    def earlier(j):
+        rows = pl.ds(pl.multiple_of(j * tile, tile), tile)
+        return pltpu.make_async_copy(raw_in.at[rows, :], before.at[rows, :], in_sems.at[j])
+
+    def lay(source, at, k):
+        return pltpu.make_async_copy(
+            source.at[pl.ds(pl.multiple_of(at, span), span), :], left.at[:, pl.ds(k * width, width)], piece_sems.at[k]
+        )
+
+    for k, piece in enumerate(near):
+        lay(piece, first, k).start()
+    if far:
+        upper = top.shape[0]
+
+        @pl.when(first < upper)
+        def _():
+            lay(top, first, count).start()
+            lay(top_other, first, count + 1).start()
+
+        @pl.when(first >= upper)
+        def _():
+            lay(bottom, first - upper, count).start()
+            lay(bottom_other, first - upper, count + 1).start()
+
+    for k in range(total):
+        stream(0, k).start()
+    if far:
+        for j in range(steps):
+            earlier(j).start()
+    for k in range(total):
+        lay(top if far else near[0], 0, k).wait()
+
+    squared = squares_in[...] if far else 0.0
+    for at in range(0, left.shape[1], 128):
+        wide = left[:, at : at + 128].astype(jnp.float32)
+        squared = squared + wide * wide
+    if far:
+        sums[...] = jnp.broadcast_to(jnp.sqrt(jnp.sum(squared, axis=1, keepdims=True) + epsilon), sums.shape)
+    else:
+        squares_out[...] = squared
+
+    def step(j, carry):
+        @pl.when(j + 1 < steps)
+        def _():
+            for k in range(total):
+                stream(j + 1, k).start()
+
+        for k in range(total):
+            stream(j, k).wait()
+        raw = lax.dot_general(held[j % 2], left[...], (((1,), (1,)), ((), ())), preferred_element_type=jnp.float32)
+        rows = pl.ds(pl.multiple_of(j * tile, tile), tile)
+        if not far:
+            raw_out[rows, :] = raw
+            return carry
+        earlier(j).wait()
+        raw = (before[rows, :] + raw).T
+        for at in range(0, tile, 128):
+            columns = pl.ds(pl.multiple_of(j * tile + at, 128), 128)
+            scores[:, columns] = (raw[:, at : at + 128] / sums[...]).astype(scores.dtype)
+        return carry
+
+    lax.fori_loop(0, steps, step, 0)
+
+
+def group_part(near, where, base, group_at, train_feats, span, far=(), earlier=()):
+    columns = train_feats.shape[0]
+    total = len(near) + len(far) // 2
+    depth = total * (list(near) + list(far))[0].shape[1]
+    tile = 512
+    anywhere, inside = pl.BlockSpec(memory_space=pl.ANY), pl.BlockSpec(memory_space=pltpu.VMEM)
+    in_specs = [pl.BlockSpec(memory_space=pltpu.SMEM)] + [anywhere] * (len(near) + len(far) + 1)
+    scratch = [pltpu.VMEM((span, depth), jnp.bfloat16), pltpu.VMEM((2, tile, depth), jnp.bfloat16)]
+    sems = [pltpu.SemaphoreType.DMA((total,)), pltpu.SemaphoreType.DMA((2, total))]
+    if far:
+        in_specs += [anywhere, inside]
+        out_shape, out_specs = jax.ShapeDtypeStruct((span, columns), jnp.bfloat16), inside
+        scratch += [pltpu.VMEM((columns, span), jnp.float32), pltpu.VMEM((span, 128), jnp.float32)]
+        sems += [pltpu.SemaphoreType.DMA((columns // tile,))]
+    else:
+        out_shape = (jax.ShapeDtypeStruct((columns, span), jnp.float32), jax.ShapeDtypeStruct((span, 128), jnp.float32))
+        out_specs = (inside, inside)
+    return pl.pallas_call(
+        functools.partial(some_columns, len(near), base, group_at, bool(far), span),
+        out_shape=out_shape,
+        in_specs=in_specs,
+        out_specs=out_specs,
+        scratch_shapes=scratch + sems,
+        compiler_params=pltpu.CompilerParams(vmem_limit_bytes=VMEM_LIMIT),
+        cost_estimate=pl.CostEstimate(flops=2 * span * columns * depth, bytes_accessed=2 * columns * depth, transcendentals=0),
+    )(where, *near, *far, train_feats, *earlier)
+
+
+def group_scores(near, far, where, skip, targets, train_feats, span):
     owners = len(near) // 2 + 1
     columns, depth = train_feats.shape
-    rows = span * len(targets)
-    where = jnp.stack(list(where) + list(targets)).astype(jnp.int32)
+    rows = span * targets
     tile = 512
     anywhere = pl.BlockSpec(memory_space=pl.ANY)
     return pl.pallas_call(
-        functools.partial(tile_rows, owners, tuple(range(len(targets))), span),
+        functools.partial(tile_rows, owners, skip, tuple(range(targets)), span),
         out_shape=jax.ShapeDtypeStruct((rows, columns), jnp.bfloat16),
         in_specs=[pl.BlockSpec(memory_space=pltpu.SMEM)] + [anywhere] * (len(near) + len(far) + 1),
         out_specs=pl.BlockSpec(memory_space=pltpu.VMEM),
@@ -99,7 +210,7 @@
             pltpu.VMEM((rows, depth), jnp.bfloat16),
             pltpu.VMEM((2, tile, depth), jnp.bfloat16),
             pltpu.VMEM((rows, 128), jnp.float32),
-            pltpu.SemaphoreType.DMA((len(targets), 2 * owners)),
+            pltpu.SemaphoreType.DMA((targets, 2 * owners)),
             pltpu.SemaphoreType.DMA((2,)),
         ],
         compiler_params=pltpu.CompilerParams(vmem_limit_bytes=VMEM_LIMIT),
@@ -132,12 +243,29 @@
         return (lax.dynamic_slice_in_dim(partial, feat * half, half, 1),
                 lax.dynamic_slice_in_dim(partial, (1 - feat) * half, half, 1))
 
+    devices = 2 * n
+    owned = count // 2
+    columns = train_feats.shape[0]
+    group = 256 // owned
+    groups = devices // group
+    span = group * owned
+    at_group, at_place = me // group, me % group
+    shifts = [groups // 2] + [k for k in range(1, groups) if k != groups // 2] + [0]
+
+    table = [me, row * 2 + 1 - feat]
+    for step in range(1, n // 2 + 1):
+        for owner in (before(step), after(step))[: 1 if 2 * step == n else 2]:
+            table += [owner * 2 + feat, owner * 2 + 1 - feat]
+    table = jnp.stack(table + [(at_group + shift) % groups for shift in shifts]).astype(jnp.int32)
+
     blocks = [(row, queries)]
     forward = backward = queries
     for step in range(1, n // 2):
         forward = lax.ppermute(forward, "rows", ahead)
         backward = lax.ppermute(backward, "rows", back)
         blocks += [(before(step), forward), (after(step), backward)]
+        if step == 1:
+            forward, table = lax.optimization_barrier((forward, table))
     top = lax.ppermute(forward[: count // 2], "rows", ahead)
     bottom = lax.ppermute(backward[count // 2 :], "rows", back)
     keep = jnp.zeros((total, half), jnp.float32)
@@ -152,30 +280,24 @@
         mine, (a + lax.ppermute(b, "feat", swap)).astype(jnp.bfloat16), (before(n // 2) * count, 0)
     )
 
-    near, where = [mine, lax.ppermute(mine, "feat", swap)], [me, row * 2 + 1 - feat]
+    near = [mine, lax.ppermute(mine, "feat", swap)]
     forward = backward = mine
     for step in range(1, n // 2):
         forward = lax.ppermute(forward, "rows", ahead)
         backward = lax.ppermute(backward, "rows", back)
-        for owner, block in ((before(step), forward), (after(step), backward)):
+        if step == n // 2 - 1:
+            early = len(near)
+            partial = group_part(near, table, 0, devices, train_feats, span)
+            forward, backward, squares = lax.optimization_barrier((forward, backward, partial[1]))
+            partial = (partial[0], squares)
+        for block in (forward, backward):
             near += [block, lax.ppermute(block, "feat", swap)]
-            where += [owner * 2 + feat, owner * 2 + 1 - feat]
     top = lax.ppermute(forward[: total // 2], "rows", ahead)
     bottom = lax.ppermute(backward[total // 2 :], "rows", back)
     far = [top, lax.ppermute(top, "feat", swap), bottom, lax.ppermute(bottom, "feat", swap)]
-    where += [before(n // 2) * 2 + feat, before(n // 2) * 2 + 1 - feat]
-
-    owned = count // 2
-    devices = 2 * n
-    columns = train_feats.shape[0]
-    group = 256 // owned
-    groups = devices // group
-    span = group * owned
-    at_group, at_place = me // group, me % group
-    shifts = [groups // 2] + [k for k in range(1, groups) if k != groups // 2] + [0]
-    target = lambda shift: (at_group + shift) % groups
-    first = group_scores(near, far, where, [target(shifts[0])], train_feats, span)
-    rest = group_scores(near, far, where, [target(k) for k in shifts[1:]], train_feats, span)
+
+    first = group_part(near[early:], table, early, devices, train_feats, span, far, partial)
+    rest = group_scores(near, far, table, 1, groups - 1, train_feats, span)
     scores = jnp.zeros((owned, devices * columns), jnp.bfloat16)
     order = [(0, turn) for turn in range(group)]
     for turn in range(group):

time: 227 us -> 223 us (0.982)
  waiting for transfers between devices: 107 us -> 94.8 us
  Pallas kernels: 33.6 us -> 40 us
    ppermute x6, waiting for transfers between devices: 39.7 us -> 22.9 us  [per_device(): backward = lax.ppermute(backward, 'rows', back)]
    pallas_call x2 -> x3, Pallas kernels: 33.6 us -> 40 us  [the longest x1 21.4 us: group_scores(): pl.pallas_call(functools.partial(tile_rows, owners, skip, tuple(range(tar...]
    ppermute x6, waiting for transfers between devices: 15.4 us -> 21.7 us  [per_device(): forward = lax.ppermute(forward, 'rows', ahead)]
    ppermute x6, starting transfers between devices: 7.91 us -> 1.87 us  [per_device(): backward = lax.ppermute(backward, 'rows', back)]
    ppermute x6, starting transfers between devices: 1.75 us -> 7.7 us  [per_device(): forward = lax.ppermute(forward, 'rows', ahead)]
    ppermute x1, waiting for transfers between devices: 1.85 us -> 5.84 us  [per_device(): top = lax.ppermute(forward[:count // 2], 'rows', ahead)]
    ppermute x1, waiting for transfers between devices: 5.85 us -> 1.92 us  [per_device(): bottom = lax.ppermute(backward[count // 2:], 'rows', back)]
    ppermute x15, starting transfers between devices: 21.3 us -> 24 us  [per_device(): going.append(lax.ppermute(block, ('rows', 'feat'), pairs))]
  transfers between devices with their start and end apart: 42 -> 42, of which waited for: 19 -> 21; matrix products, arithmetic and copies ran while one was open for 15% -> 15% of each run, Pallas kernels for 9% -> 14%
where the time goes in v3:
time: 223 us
  waiting for transfers between devices  94.8 us (43%)
  starting transfers between devices  48.4 us (22%)
  Pallas kernels  40 us (18%)
  local copies, waits for them, and re-layouts  29.9 us (13%)
  matrix products  7.77 us (3%)
    ppermute x15, waiting for transfers between devices, per_device(): going.append(lax.ppermute(block, ('rows', 'feat'), pairs))  34.4 us
    ppermute x15, starting transfers between devices, per_device(): going.append(lax.ppermute(block, ('rows', 'feat'), pairs))  24 us
    ppermute x6, waiting for transfers between devices, per_device(): backward = lax.ppermute(backward, 'rows', back)  22.9 us
    ppermute x6, waiting for transfers between devices, per_device(): forward = lax.ppermute(forward, 'rows', ahead)  21.7 us
    pallas_call x1, Pallas kernels, group_scores(): pl.pallas_call(functools.partial(tile_rows, owners, skip, tuple(range(tar...  21.4 us
    pallas_call x2, Pallas kernels, group_part(): pl.pallas_call(functools.partial(some_columns, len(near), base, group_at,...  18.6 us
    dynamic_update_slice x15, local copies, waits for them, and re-layouts, per_device(): scores = lax.dynamic_update_slice(scores, block, (0, source * columns))  14.6 us
    dot_general x8, matrix products, product(): partial = jnp.dot(block, kernel, preferred_element_type=jnp.float32)  7.77 us
  transfers between devices with their start and end apart: 42, of which 21 were waited for; matrix products, arithmetic and copies ran while one was open for 15% of the time, Pallas kernels for 14%

profile of v3, /device:TPU:1, one launch (start us, length us, event | category | flops | bytes accessed | tf_op | source)
XLA Modules:
  0.0 222.5 jit_solution(12725853090985952015)
XLA Ops:
  0.0 2.1 collective-permute-start
  2.8 1.5 fusion.6
  4.3 1.0 broadcast.30.clone
  6.1 7.9 %collective-permute-done = bf16[128,2048]{1,0:T(8,128)(2,1)} collective-permute-done((bf16[128,2048]{1,0:T(8,128)(2,1)}, bf16[128,2048]{1,0:T(8,128)(2,1)}, u32[]{:S(2)}, u32[]{:S(2)}) %collective-permute-start) | collective-permute-done | bytes 524320 | tf_op jit(solution)/shard_map/ppermute | solution.py:264
  14.0 1.2 collective-permute-start.2
  15.2 1.5 fusion.7
  17.1 1.5 fusion.8
  20.0 6.5 %collective-permute-done.2 = bf16[128,2048]{1,0:T(8,128)(2,1)S(1)} collective-permute-done((bf16[128,2048]{1,0:T(8,128)(2,1)}, bf16[128,2048]{1,0:T(8,128)(2,1)S(1)}, u32[]{:S(2)}, u32[]{:S(2)}) %collective-permute-start.2) | collective-permute-done | bytes 524320 | tf_op jit(solution)/shard_map/ppermute | solution.py:264
  26.4 0.9 collective-permute-start.4
  27.8 0.9 collective-permute-done.3
  31.0 6.7 %collective-permute-done.4 = bf16[128,2048]{1,0:T(8,128)(2,1)S(1)} collective-permute-done((bf16[128,2048]{1,0:T(8,128)(2,1)S(1)}, bf16[128,2048]{1,0:T(8,128)(2,1)S(1)}, u32[]{:S(2)}, u32[]{:S(2)}) %collective-permute-start.4) | collective-permute-done | bytes 524320 | tf_op jit(solution)/shard_map/ppermute | solution.py:264
  40.4 3.7 %collective-permute-start.6 = (f32[1024,256]{1,0:T(8,128)}, f32[1024,256]{1,0:T(8,128)}, u32[]{:S(2)}, u32[]{:S(2)}) collective-permute-start(f32[1024,256]{1,0:T(8,128)} %get-tuple-element.75), channel_id=1, source_target_pairs={{0,1},{1,0},{2,3},{3,2},{4,5},{5,4},{6,7},{7,6},{8,9},{9,8},{10,11... | collective-permute-start | bytes 3145736 | tf_op jit(solution)/shard_map/ppermute | solution.py:277
  44.1 1.3 collective-permute-start.7
  45.5 0.7 slice.17
  46.4 5.8 %collective-permute-done.7 = bf16[64,2048]{1,0:T(8,128)(2,1)} collective-permute-done((bf16[64,2048]{1,0:T(8,128)(2,1)S(1)}, bf16[64,2048]{1,0:T(8,128)(2,1)}, u32[]{:S(2)}, u32[]{:S(2)}) %collective-permute-start.7) | collective-permute-done | bytes 262176 | tf_op jit(solution)/shard_map/ppermute | solution.py:269
  52.2 1.9 collective-permute-done.8
  54.1 1.5 fusion
  55.6 1.2 collective-permute-start.9
  56.8 1.3 add_convert_fusion
  58.4 1.3 collective-permute-start.11
  59.7 12.1 %collective-permute-done.13.refs_4_ = bf16[1024,256]{1,0:T(8,128)(2,1)S(1)} collective-permute-done((bf16[1024,256]{1,0:T(8,128)(2,1)S(1)}, bf16[1024,256]{1,0:T(8,128)(2,1)S(1)}, u32[]{:S(2)}, u32[]{:S(2)}) %collective-permute-start.13) | collective-permute-done | bytes 524320 | tf_op jit(solution)/shard_map/ppermute | solution.py:287
  72.0 1.3 collective-permute-start.15
  73.3 1.4 collective-permute-start.10
  75.1 9.3 %collective-permute-done.17.refs_8_ = bf16[1024,256]{1,0:T(8,128)(2,1)S(1)} collective-permute-done((bf16[1024,256]{1,0:T(8,128)(2,1)S(1)}, bf16[1024,256]{1,0:T(8,128)(2,1)S(1)}, u32[]{:S(2)}, u32[]{:S(2)}) %collective-permute-start.17) | collective-permute-done | bytes 524320 | tf_op jit(solution)/shard_map/ppermute | solution.py:287
  84.4 1.7 collective-permute-start.18
  86.9 0.9 collective-permute-start.19
  87.8 0.8 copy-done.11
  88.6 0.9 copy-done.12
  89.5 9.8 %shard_map.37 = (f32[2048,256]{1,0:T(8,128)}, f32[256,128]{1,0:T(8,128)}) custom-call(s32[20]{0:T(128)} %stack.83.where, bf16[1024,256]{1,0:T(8,128)(2,1)} %copy-done.2, bf16[1024,256]{1,0:T(8,128)(2,1)} %copy-done.9, bf16[1024,256]{1,0:T(8,128)(2,1)} %copy-done.6, bf16[1024,256]{1,0:T(8,128)(2,1)} %copy-done.11, bf16[1024,256]{1,0:T(8,128)(2,1)} %copy-done.5, ...), custom_call_target="tpu_custom_call" | custom-call | flops 2684354560 | bytes 10485760 | tf_op jit(solution)/shard_map/pallas_call | solution.py:187
  100.1 1.2 collective-permute-start.21
  101.4 0.9 collective-permute-start.25
  103.2 6.3 %collective-permute-done.25.refs_16_.refs_6_ = bf16[512,256]{1,0:T(8,128)(2,1)S(1)} collective-permute-done((bf16[512,256]{1,0:T(8,128)(2,1)S(1)}, bf16[512,256]{1,0:T(8,128)(2,1)S(1)}, u32[]{:S(2)}, u32[]{:S(2)}) %collective-permute-start.25) | collective-permute-done | bytes 262176 | tf_op jit(solution)/shard_map/ppermute | solution.py:296
  110.3 1.0 collective-permute-start.24
  111.4 1.4 collective-permute-done.24.refs_15_.refs_5_
  112.9 8.8 %shard_map.39 = bf16[256,2048]{1,0:T(8,128)(2,1)} custom-call(s32[20]{0:T(128)} %stack.83.where, bf16[1024,256]{1,0:T(8,128)(2,1)} %copy-done.4, bf16[1024,256]{1,0:T(8,128)(2,1)} %collective-permute-done.21.refs_11_.refs_1_, bf16[1024,256]{1,0:T(8,128)(2,1)} %copy-done.3, bf16[1024,256]{1,0:T(8,128)(2,1)} %collective-permute-done.22.refs_13_.refs_3_, ...), custom_call_target="tpu_custom_call" | custom-call | flops 1610612736 | bytes 6291456 | tf_op jit(solution)/shard_map/pallas_call | solution.py:187
  121.7 1.3 constant_dynamic-slice_fusion.6
  123.0 1.2 collective-permute-start.30
  124.2 2.5 %collective-permute-start.29 = (bf16[64,2048]{1,0:T(8,128)(2,1)S(1)}, bf16[64,2048]{1,0:T(8,128)(2,1)}, u32[]{:S(2)}, u32[]{:S(2)}) collective-permute-start(bf16[64,2048]{1,0:T(8,128)(2,1)S(1)} %get-tuple-element.72), channel_id=1, source_target_pairs={{0,10},{1,11},{2,8},{3,9},{4,14},{5,15},{6,12},{7,13},{8,2},{9,3},... | collective-permute-start | bytes 786440 | tf_op jit(solution)/shard_map/ppermute | solution.py:315
  126.7 3.2 %collective-permute-start.28 = (bf16[64,2048]{1,0:T(8,128)(2,1)S(1)}, bf16[64,2048]{1,0:T(8,128)(2,1)}, u32[]{:S(2)}, u32[]{:S(2)}) collective-permute-start(bf16[64,2048]{1,0:T(8,128)(2,1)S(1)} %get-tuple-element.73), channel_id=1, source_target_pairs={{0,9},{1,10},{2,11},{3,8},{4,13},{5,14},{6,15},{7,12},{8,1},{9,2},... | collective-permute-start | bytes 786440 | tf_op jit(solution)/shard_map/ppermute | solution.py:315
  130.2 21.4 %shard_map.38 = bf16[768,2048]{1,0:T(8,128)(2,1)} custom-call(s32[20]{0:T(128)} %stack.83.where, bf16[1024,256]{1,0:T(8,128)(2,1)} %copy-done.2, bf16[1024,256]{1,0:T(8,128)(2,1)} %copy-done.9, bf16[1024,256]{1,0:T(8,128)(2,1)} %copy-done.6, bf16[1024,256]{1,0:T(8,128)(2,1)} %copy-done.11, bf16[1024,256]{1,0:T(8,128)(2,1)} %copy-done.5, ...), custom_call_target="tpu_custom_call" | custom-call | flops 12884901888 | bytes 16777216 | tf_op jit(solution)/shard_map/pallas_call | solution.py:204
  151.6 2.4 %broadcast_in_dim.3 = bf16[64,32768]{1,0:T(8,128)(2,1)} broadcast(bf16[]{:T(256)} %constant.268.clone.1), dimensions={} | broadcast | bytes 4194306 | tf_op jit(solution)/shard_map/broadcast_in_dim | solution.py:301
  154.1 1.0 copy-done.1
  155.0 1.7 constant_dynamic-slice_fusion.15
  156.7 1.3 collective-permute-start.31
  158.0 3.5 %collective-permute-done.29 = bf16[64,2048]{1,0:T(8,128)(2,1)} collective-permute-done((bf16[64,2048]{1,0:T(8,128)(2,1)S(1)}, bf16[64,2048]{1,0:T(8,128)(2,1)}, u32[]{:S(2)}, u32[]{:S(2)}) %collective-permute-start.29) | collective-permute-done | bytes 262176 | tf_op jit(solution)/shard_map/ppermute | solution.py:315
  161.5 10.9 %collective-permute-done.28 = bf16[64,2048]{1,0:T(8,128)(2,1)} collective-permute-done((bf16[64,2048]{1,0:T(8,128)(2,1)S(1)}, bf16[64,2048]{1,0:T(8,128)(2,1)}, u32[]{:S(2)}, u32[]{:S(2)}) %collective-permute-start.28) | collective-permute-done | bytes 262176 | tf_op jit(solution)/shard_map/ppermute | solution.py:315
  172.4 4.7 %collective-permute-done.27 = bf16[64,2048]{1,0:T(8,128)(2,1)} collective-permute-done((bf16[64,2048]{1,0:T(8,128)(2,1)S(1)}, bf16[64,2048]{1,0:T(8,128)(2,1)}, u32[]{:S(2)}, u32[]{:S(2)}) %collective-permute-start.27) | collective-permute-done | bytes 262176 | tf_op jit(solution)/shard_map/ppermute | solution.py:315
  177.1 3.5 %collective-permute-start.33 = (bf16[64,2048]{1,0:T(8,128)(2,1)}, bf16[64,2048]{1,0:T(8,128)(2,1)S(1)}, u32[]{:S(2)}, u32[]{:S(2)}) collective-permute-start(bf16[64,2048]{1,0:T(8,128)(2,1)} %get-tuple-element.46), channel_id=1, source_target_pairs={{0,5},{1,6},{2,7},{3,4},{4,9},{5,10},{6,11},{7,8},{8,13},{9,14},{1... | collective-permute-start | bytes 786440 | tf_op jit(solution)/shard_map/ppermute | solution.py:315
  180.6 1.3 collective-permute-start.34
  182.6 0.9 collective-permute-start.36
  183.5 1.7 constant_dynamic-update-slice_fusion.7
  185.2 1.7 constant_dynamic-update-slice_fusion.6
  186.9 1.7 constant_dynamic-update-slice_fusion.5
  189.3 1.7 constant_dynamic-update-slice_fusion.3
  190.9 3.2 %collective-permute-start.37 = (bf16[64,2048]{1,0:T(8,128)(2,1)}, bf16[64,2048]{1,0:T(8,128)(2,1)S(1)}, u32[]{:S(2)}, u32[]{:S(2)}) collective-permute-start(bf16[64,2048]{1,0:T(8,128)(2,1)} %get-tuple-element.54), channel_id=1, source_target_pairs={{0,14},{1,15},{2,12},{3,13},{4,2},{5,3},{6,0},{7,1},{8,6},{9,7},{1... | collective-permute-start | bytes 786440 | tf_op jit(solution)/shard_map/ppermute | solution.py:315
  194.2 1.3 collective-permute-start.38
  195.5 8.4 %collective-permute-done.34 = bf16[64,2048]{1,0:T(8,128)(2,1)S(1)} collective-permute-done((bf16[64,2048]{1,0:T(8,128)(2,1)}, bf16[64,2048]{1,0:T(8,128)(2,1)S(1)}, u32[]{:S(2)}, u32[]{:S(2)}) %collective-permute-start.34) | collective-permute-done | bytes 262176 | tf_op jit(solution)/shard_map/ppermute | solution.py:315
  203.9 4.5 %collective-permute-start.40 = (bf16[64,2048]{1,0:T(8,128)(2,1)}, bf16[64,2048]{1,0:T(8,128)(2,1)S(1)}, u32[]{:S(2)}, u32[]{:S(2)}) collective-permute-start(bf16[64,2048]{1,0:T(8,128)(2,1)} %get-tuple-element.57), channel_id=1, source_target_pairs={{0,15},{1,12},{2,13},{3,14},{4,3},{5,0},{6,1},{7,2},{8,7},{9,4},{1... | collective-permute-start | bytes 786440 | tf_op jit(solution)/shard_map/ppermute | solution.py:315
  208.4 0.7 constant_dynamic-update-slice_fusion.2
  212.0 0.7 constant_dynamic-update-slice_fusion.12
  212.7 3.5 %collective-permute-done.38 = bf16[64,2048]{1,0:T(8,128)(2,1)S(1)} collective-permute-done((bf16[64,2048]{1,0:T(8,128)(2,1)}, bf16[64,2048]{1,0:T(8,128)(2,1)S(1)}, u32[]{:S(2)}, u32[]{:S(2)}) %collective-permute-start.38) | collective-permute-done | bytes 262176 | tf_op jit(solution)/shard_map/ppermute | solution.py:315
  216.2 0.7 constant_dynamic-update-slice_fusion.11
  216.9 0.7 constant_dynamic-update-slice_fusion.10
  217.6 2.8 %collective-permute-done.40 = bf16[64,2048]{1,0:T(8,128)(2,1)S(1)} collective-permute-done((bf16[64,2048]{1,0:T(8,128)(2,1)}, bf16[64,2048]{1,0:T(8,128)(2,1)S(1)}, u32[]{:S(2)}, u32[]{:S(2)}) %collective-permute-start.40) | collective-permute-done | bytes 262176 | tf_op jit(solution)/shard_map/ppermute | solution.py:315
  (95 shorter events, 20.1 us)
Async XLA Ops:
  0.0 2.8 %copy-start = (bf16[2048,512]{1,0:T(8,128)(2,1)S(1)}, bf16[2048,512]{1,0:T(8,128)(2,1)}, u32[]{:S(2)}) copy-start(bf16[2048,512]{1,0:T(8,128)(2,1)} %param.4) | copy-start | bytes 6291460
  0.0 14.0 %collective-permute-start = (bf16[128,2048]{1,0:T(8,128)(2,1)}, bf16[128,2048]{1,0:T(8,128)(2,1)}, u32[]{:S(2)}, u32[]{:S(2)}) collective-permute-start(bf16[128,2048]{1,0:T(8,128)(2,1)} %param.3), channel_id=1, source_target_pairs={{0,4},{4,8},{8,12},{12,14},{14,10},{10,6},{6,2},{2,0},{1,5},{5,9},... | collective-permute-start | bytes 1572872 | tf_op jit(solution)/shard_map/ppermute | solution.py:264
  2.1 14.6 %collective-permute-start.1 = (bf16[128,2048]{1,0:T(8,128)(2,1)}, bf16[128,2048]{1,0:T(8,128)(2,1)}, u32[]{:S(2)}, u32[]{:S(2)}) collective-permute-start(bf16[128,2048]{1,0:T(8,128)(2,1)} %param.3), channel_id=1, source_target_pairs={{4,0},{8,4},{12,8},{14,12},{10,14},{6,10},{2,6},{0,2},{5,1},{9,5},... | collective-permute-start | bytes 1572872 | tf_op jit(solution)/shard_map/ppermute | solution.py:265
  14.0 12.4 %collective-permute-start.2 = (bf16[128,2048]{1,0:T(8,128)(2,1)}, bf16[128,2048]{1,0:T(8,128)(2,1)S(1)}, u32[]{:S(2)}, u32[]{:S(2)}) collective-permute-start(bf16[128,2048]{1,0:T(8,128)(2,1)} %collective-permute-done), channel_id=1, source_target_pairs={{0,4},{4,8},{8,12},{12,14},{14,10},{10,6},{6,2},{2,0},{1,5},{5,9},... | collective-permute-start | bytes 1572872 | tf_op jit(solution)/shard_map/ppermute | solution.py:264
  16.8 11.9 %collective-permute-start.3 = (bf16[128,2048]{1,0:T(8,128)(2,1)}, bf16[128,2048]{1,0:T(8,128)(2,1)S(1)}, u32[]{:S(2)}, u32[]{:S(2)}) collective-permute-start(bf16[128,2048]{1,0:T(8,128)(2,1)} %collective-permute-done.1), channel_id=1, source_target_pairs={{4,0},{8,4},{12,8},{14,12},{10,14},{6,10},{2,6},{0,2},{5,1},{9,5},... | collective-permute-start | bytes 1572872 | tf_op jit(solution)/shard_map/ppermute | solution.py:265
  26.4 11.3 %collective-permute-start.4 = (bf16[128,2048]{1,0:T(8,128)(2,1)S(1)}, bf16[128,2048]{1,0:T(8,128)(2,1)S(1)}, u32[]{:S(2)}, u32[]{:S(2)}) collective-permute-start(bf16[128,2048]{1,0:T(8,128)(2,1)S(1)} %collective-permute-done.2), channel_id=1, source_target_pairs={{0,4},{4,8},{8,12},{12,14},{14,10},{10,6},{6,2},{2,0},{1,5},{5,9},... | collective-permute-start | bytes 1572872 | tf_op jit(solution)/shard_map/ppermute | solution.py:264
  28.6 10.7 %collective-permute-start.5 = (bf16[128,2048]{1,0:T(8,128)(2,1)S(1)}, bf16[128,2048]{1,0:T(8,128)(2,1)S(1)}, u32[]{:S(2)}, u32[]{:S(2)}) collective-permute-start(bf16[128,2048]{1,0:T(8,128)(2,1)S(1)} %collective-permute-done.3), channel_id=1, source_target_pairs={{4,0},{8,4},{12,8},{14,12},{10,14},{6,10},{2,6},{0,2},{5,1},{9,5},... | collective-permute-start | bytes 1572872 | tf_op jit(solution)/shard_map/ppermute | solution.py:265
  40.4 16.4 %collective-permute-start.6 = (f32[1024,256]{1,0:T(8,128)}, f32[1024,256]{1,0:T(8,128)}, u32[]{:S(2)}, u32[]{:S(2)}) collective-permute-start(f32[1024,256]{1,0:T(8,128)} %get-tuple-element.75), channel_id=1, source_target_pairs={{0,1},{1,0},{2,3},{3,2},{4,5},{5,4},{6,7},{7,6},{8,9},{9,8},{10,11... | collective-permute-start | bytes 3145736 | tf_op jit(solution)/shard_map/ppermute | solution.py:277
  44.1 8.1 %collective-permute-start.7 = (bf16[64,2048]{1,0:T(8,128)(2,1)S(1)}, bf16[64,2048]{1,0:T(8,128)(2,1)}, u32[]{:S(2)}, u32[]{:S(2)}) collective-permute-start(bf16[64,2048]{1,0:T(8,128)(2,1)S(1)} %slice.16), channel_id=1, source_target_pairs={{0,4},{4,8},{8,12},{12,14},{14,10},{10,6},{6,2},{2,0},{1,5},{5,9},... | collective-permute-start | bytes 786440 | tf_op jit(solution)/shard_map/ppermute | solution.py:269
  46.2 7.9 %collective-permute-start.8 = (bf16[64,2048]{1,0:T(8,128)(2,1)}, bf16[64,2048]{1,0:T(8,128)(2,1)}, u32[]{:S(2)}, u32[]{:S(2)}) collective-permute-start(bf16[64,2048]{1,0:T(8,128)(2,1)} %slice.17), channel_id=1, source_target_pairs={{4,0},{8,4},{12,8},{14,12},{10,14},{6,10},{2,6},{0,2},{5,1},{9,5},... | collective-permute-start | bytes 786440 | tf_op jit(solution)/shard_map/ppermute | solution.py:270
  55.6 2.5 %collective-permute-start.9 = (f32[128,256]{1,0:T(8,128)S(1)}, f32[128,256]{1,0:T(8,128)S(1)}, u32[]{:S(2)}, u32[]{:S(2)}) collective-permute-start(f32[128,256]{1,0:T(8,128)S(1)} %constant_dynamic-slice_fusion.14), channel_id=1, source_target_pairs={{0,1},{1,0},{2,3},{3,2},{4,5},{5,4},{6,7},{7,6},{8,9},{9,8},{10,11... | collective-permute-start | bytes 393224 | tf_op jit(solution)/shard_map/ppermute | solution.py:280
  58.2 31.3 %copy-start.2 = (bf16[1024,256]{1,0:T(8,128)(2,1)}, bf16[1024,256]{1,0:T(8,128)(2,1)S(1)}, u32[]{:S(2)}) copy-start(bf16[1024,256]{1,0:T(8,128)(2,1)S(1)} %fusion.4.refs_0_) | copy-start | bytes 1572868
  58.2 13.6 %collective-permute-start.13 = (bf16[1024,256]{1,0:T(8,128)(2,1)S(1)}, bf16[1024,256]{1,0:T(8,128)(2,1)S(1)}, u32[]{:S(2)}, u32[]{:S(2)}) collective-permute-start(bf16[1024,256]{1,0:T(8,128)(2,1)S(1)} %fusion.4.refs_0_), channel_id=1, source_target_pairs={{4,0},{8,4},{12,8},{14,12},{10,14},{6,10},{2,6},{0,2},{5,1},{9,5},... | collective-permute-start | bytes 1572872 | tf_op jit(solution)/shard_map/ppermute | solution.py:287
  58.4 13.5 %collective-permute-start.11 = (bf16[1024,256]{1,0:T(8,128)(2,1)S(1)}, bf16[1024,256]{1,0:T(8,128)(2,1)S(1)}, u32[]{:S(2)}, u32[]{:S(2)}) collective-permute-start(bf16[1024,256]{1,0:T(8,128)(2,1)S(1)} %fusion.4.refs_0_), channel_id=1, source_target_pairs={{0,4},{4,8},{8,12},{12,14},{14,10},{10,6},{6,2},{2,0},{1,5},{5,9},... | collective-permute-start | bytes 1572872 | tf_op jit(solution)/shard_map/ppermute | solution.py:286
  71.8 17.7 %copy-start.5 = (bf16[1024,256]{1,0:T(8,128)(2,1)}, bf16[1024,256]{1,0:T(8,128)(2,1)S(1)}, u32[]{:S(2)}) copy-start(bf16[1024,256]{1,0:T(8,128)(2,1)S(1)} %collective-permute-done.13.refs_4_) | copy-start | bytes 1572868
  71.8 12.6 %collective-permute-start.17 = (bf16[1024,256]{1,0:T(8,128)(2,1)S(1)}, bf16[1024,256]{1,0:T(8,128)(2,1)S(1)}, u32[]{:S(2)}, u32[]{:S(2)}) collective-permute-start(bf16[1024,256]{1,0:T(8,128)(2,1)S(1)} %collective-permute-done.13.refs_4_), channel_id=1, source_target_pairs={{4,0},{8,4},{12,8},{14,12},{10,14},{6,10},{2,6},{0,2},{5,1},{9,5},... | collective-permute-start | bytes 1572872 | tf_op jit(solution)/shard_map/ppermute | solution.py:287
  72.0 17.5 %copy-start.6 = (bf16[1024,256]{1,0:T(8,128)(2,1)}, bf16[1024,256]{1,0:T(8,128)(2,1)S(1)}, u32[]{:S(2)}) copy-start(bf16[1024,256]{1,0:T(8,128)(2,1)S(1)} %collective-permute-done.11.refs_2_) | copy-start | bytes 1572868
  72.0 14.2 %collective-permute-start.15 = (bf16[1024,256]{1,0:T(8,128)(2,1)S(1)}, bf16[1024,256]{1,0:T(8,128)(2,1)S(1)}, u32[]{:S(2)}, u32[]{:S(2)}) collective-permute-start(bf16[1024,256]{1,0:T(8,128)(2,1)S(1)} %collective-permute-done.11.refs_2_), channel_id=1, source_target_pairs={{0,4},{4,8},{8,12},{12,14},{14,10},{10,6},{6,2},{2,0},{1,5},{5,9},... | collective-permute-start | bytes 1572872 | tf_op jit(solution)/shard_map/ppermute | solution.py:286
  73.3 13.0 %collective-permute-start.10 = (bf16[1024,256]{1,0:T(8,128)(2,1)S(1)}, bf16[1024,256]{1,0:T(8,128)(2,1)S(1)}, u32[]{:S(2)}, u32[]{:S(2)}) collective-permute-start(bf16[1024,256]{1,0:T(8,128)(2,1)S(1)} %fusion.4.refs_0_), channel_id=1, source_target_pairs={{0,1},{1,0},{2,3},{3,2},{4,5},{5,4},{6,7},{7,6},{8,9},{9,8},{10,11... | collective-permute-start | bytes 1572872 | tf_op jit(solution)/shard_map/ppermute | solution.py:283
  74.6 12.3 %collective-permute-start.14 = (bf16[1024,256]{1,0:T(8,128)(2,1)S(1)}, bf16[1024,256]{1,0:T(8,128)(2,1)S(1)}, u32[]{:S(2)}, u32[]{:S(2)}) collective-permute-start(bf16[1024,256]{1,0:T(8,128)(2,1)S(1)} %collective-permute-done.13.refs_4_), channel_id=1, source_target_pairs={{0,1},{1,0},{2,3},{3,2},{4,5},{5,4},{6,7},{7,6},{8,9},{9,8},{10,11... | collective-permute-start | bytes 1572872 | tf_op jit(solution)/shard_map/ppermute | solution.py:294
  74.6 13.2 %collective-permute-start.12 = (bf16[1024,256]{1,0:T(8,128)(2,1)S(1)}, bf16[1024,256]{1,0:T(8,128)(2,1)S(1)}, u32[]{:S(2)}, u32[]{:S(2)}) collective-permute-start(bf16[1024,256]{1,0:T(8,128)(2,1)S(1)} %collective-permute-done.11.refs_2_), channel_id=1, source_target_pairs={{0,1},{1,0},{2,3},{3,2},{4,5},{5,4},{6,7},{7,6},{8,9},{9,8},{10,11... | collective-permute-start | bytes 1572872 | tf_op jit(solution)/shard_map/ppermute | solution.py:294
  84.4 5.0 %copy-start.7 = (bf16[1024,256]{1,0:T(8,128)(2,1)}, bf16[1024,256]{1,0:T(8,128)(2,1)S(1)}, u32[]{:S(2)}) copy-start(bf16[1024,256]{1,0:T(8,128)(2,1)S(1)} %collective-permute-done.17.refs_8_) | copy-start | bytes 1572868
  84.4 3.3 %collective-permute-start.18 = (bf16[1024,256]{1,0:T(8,128)(2,1)S(1)}, bf16[1024,256]{1,0:T(8,128)(2,1)S(1)}, u32[]{:S(2)}, u32[]{:S(2)}) collective-permute-start(bf16[1024,256]{1,0:T(8,128)(2,1)S(1)} %collective-permute-done.17.refs_8_), channel_id=1, source_target_pairs={{0,1},{1,0},{2,3},{3,2},{4,5},{5,4},{6,7},{7,6},{8,9},{9,8},{10,11... | collective-permute-start | bytes 1572872 | tf_op jit(solution)/shard_map/ppermute | solution.py:294
  86.1 3.4 %copy-start.8 = (bf16[1024,256]{1,0:T(8,128)(2,1)}, bf16[1024,256]{1,0:T(8,128)(2,1)S(1)}, u32[]{:S(2)}) copy-start(bf16[1024,256]{1,0:T(8,128)(2,1)S(1)} %collective-permute-done.15.refs_6_) | copy-start | bytes 1572868
  86.1 3.3 %collective-permute-start.16 = (bf16[1024,256]{1,0:T(8,128)(2,1)S(1)}, bf16[1024,256]{1,0:T(8,128)(2,1)}, u32[]{:S(2)}, u32[]{:S(2)}) collective-permute-start(bf16[1024,256]{1,0:T(8,128)(2,1)S(1)} %collective-permute-done.15.refs_6_), channel_id=1, source_target_pairs={{0,1},{1,0},{2,3},{3,2},{4,5},{5,4},{6,7},{7,6},{8,9},{9,8},{10,11... | collective-permute-start | bytes 1572872 | tf_op jit(solution)/shard_map/ppermute | solution.py:294
  86.3 1.5 copy-start.9
  86.3 13.2 %collective-permute-start.20 = (bf16[1024,256]{1,0:T(8,128)(2,1)S(1)}, bf16[1024,256]{1,0:T(8,128)(2,1)S(1)}, u32[]{:S(2)}, u32[]{:S(2)}) collective-permute-start(bf16[1024,256]{1,0:T(8,128)(2,1)S(1)} %collective-permute-done.17.refs_8_), channel_id=1, source_target_pairs={{4,0},{8,4},{12,8},{14,12},{10,14},{6,10},{2,6},{0,2},{5,1},{9,5},... | collective-permute-start | bytes 1572872 | tf_op jit(solution)/shard_map/ppermute | solution.py:287
  86.9 0.9 copy-start.10
  86.9 13.2 %collective-permute-start.19 = (bf16[1024,256]{1,0:T(8,128)(2,1)S(1)}, bf16[1024,256]{1,0:T(8,128)(2,1)S(1)}, u32[]{:S(2)}, u32[]{:S(2)}) collective-permute-start(bf16[1024,256]{1,0:T(8,128)(2,1)S(1)} %collective-permute-done.15.refs_6_), channel_id=1, source_target_pairs={{0,4},{4,8},{8,12},{12,14},{14,10},{10,6},{6,2},{2,0},{1,5},{5,9},... | collective-permute-start | bytes 1572872 | tf_op jit(solution)/shard_map/ppermute | solution.py:286
  87.8 0.8 copy-start.11
  88.6 0.9 copy-start.12
  99.5 13.4 %copy-start.3 = (bf16[1024,256]{1,0:T(8,128)(2,1)}, bf16[1024,256]{1,0:T(8,128)(2,1)S(1)}, u32[]{:S(2)}) copy-start(bf16[1024,256]{1,0:T(8,128)(2,1)S(1)} %collective-permute-done.20.refs_12_.refs_2_) | copy-start | bytes 1572868
  100.1 12.8 %copy-start.4 = (bf16[1024,256]{1,0:T(8,128)(2,1)}, bf16[1024,256]{1,0:T(8,128)(2,1)S(1)}, u32[]{:S(2)}) copy-start(bf16[1024,256]{1,0:T(8,128)(2,1)S(1)} %collective-permute-done.19.refs_10_.refs_0_) | copy-start | bytes 1572868
  100.1 11.3 %collective-permute-start.21 = (bf16[1024,256]{1,0:T(8,128)(2,1)S(1)}, bf16[1024,256]{1,0:T(8,128)(2,1)}, u32[]{:S(2)}, u32[]{:S(2)}) collective-permute-start(bf16[1024,256]{1,0:T(8,128)(2,1)S(1)} %collective-permute-done.19.refs_10_.refs_0_), channel_id=1, source_target_pairs={{0,1},{1,0},{2,3},{3,2},{4,5},{5,4},{6,7},{7,6},{8,9},{9,8},{10,11... | collective-permute-start | bytes 1572872 | tf_op jit(solution)/shard_map/ppermute | solution.py:294
  101.4 8.1 %collective-permute-start.25 = (bf16[512,256]{1,0:T(8,128)(2,1)S(1)}, bf16[512,256]{1,0:T(8,128)(2,1)S(1)}, u32[]{:S(2)}, u32[]{:S(2)}) collective-permute-start(bf16[512,256]{1,0:T(8,128)(2,1)S(1)} %slice.15), channel_id=1, source_target_pairs={{4,0},{8,4},{12,8},{14,12},{10,14},{6,10},{2,6},{0,2},{5,1},{9,5},... | collective-permute-start | bytes 786440 | tf_op jit(solution)/shard_map/ppermute | solution.py:296
  102.2 9.1 %collective-permute-start.22 = (bf16[1024,256]{1,0:T(8,128)(2,1)S(1)}, bf16[1024,256]{1,0:T(8,128)(2,1)}, u32[]{:S(2)}, u32[]{:S(2)}) collective-permute-start(bf16[1024,256]{1,0:T(8,128)(2,1)S(1)} %collective-permute-done.20.refs_12_.refs_2_), channel_id=1, source_target_pairs={{0,1},{1,0},{2,3},{3,2},{4,5},{5,4},{6,7},{7,6},{8,9},{9,8},{10,11... | collective-permute-start | bytes 1572872 | tf_op jit(solution)/shard_map/ppermute | solution.py:294
  102.5 7.8 %collective-permute-start.23 = (bf16[512,256]{1,0:T(8,128)(2,1)S(1)}, bf16[512,256]{1,0:T(8,128)(2,1)}, u32[]{:S(2)}, u32[]{:S(2)}) collective-permute-start(bf16[512,256]{1,0:T(8,128)(2,1)S(1)} %slice.14), channel_id=1, source_target_pairs={{0,4},{4,8},{8,12},{12,14},{14,10},{10,6},{6,2},{2,0},{1,5},{5,9},... | collective-permute-start | bytes 786440 | tf_op jit(solution)/shard_map/ppermute | solution.py:295
  109.4 3.4 %copy-start.13 = (bf16[512,256]{1,0:T(8,128)(2,1)}, bf16[512,256]{1,0:T(8,128)(2,1)S(1)}, u32[]{:S(2)}) copy-start(bf16[512,256]{1,0:T(8,128)(2,1)S(1)} %collective-permute-done.25.refs_16_.refs_6_) | copy-start | bytes 786436
  109.4 2.0 collective-permute-start.26
  110.3 2.5 %collective-permute-start.24 = (bf16[512,256]{1,0:T(8,128)(2,1)}, bf16[512,256]{1,0:T(8,128)(2,1)}, u32[]{:S(2)}, u32[]{:S(2)}) collective-permute-start(bf16[512,256]{1,0:T(8,128)(2,1)} %collective-permute-done.23.refs_14_.refs_4_), channel_id=1, source_target_pairs={{0,1},{1,0},{2,3},{3,2},{4,5},{5,4},{6,7},{7,6},{8,9},{9,8},{10,11... | collective-permute-start | bytes 786440 | tf_op jit(solution)/shard_map/ppermute | solution.py:297
  123.0 35.0 %collective-permute-start.30 = (bf16[64,2048]{1,0:T(8,128)(2,1)S(1)}, bf16[64,2048]{1,0:T(8,128)(2,1)S(1)}, u32[]{:S(2)}, u32[]{:S(2)}) collective-permute-start(bf16[64,2048]{1,0:T(8,128)(2,1)S(1)} %get-tuple-element.71), channel_id=1, source_target_pairs={{0,11},{1,8},{2,9},{3,10},{4,15},{5,12},{6,13},{7,14},{8,3},{9,0},... | collective-permute-start | bytes 786440 | tf_op jit(solution)/shard_map/ppermute | solution.py:315
  124.2 37.3 %collective-permute-start.29 = (bf16[64,2048]{1,0:T(8,128)(2,1)S(1)}, bf16[64,2048]{1,0:T(8,128)(2,1)}, u32[]{:S(2)}, u32[]{:S(2)}) collective-permute-start(bf16[64,2048]{1,0:T(8,128)(2,1)S(1)} %get-tuple-element.72), channel_id=1, source_target_pairs={{0,10},{1,11},{2,8},{3,9},{4,14},{5,15},{6,12},{7,13},{8,2},{9,3},... | collective-permute-start | bytes 786440 | tf_op jit(solution)/shard_map/ppermute | solution.py:315
  126.7 45.8 %collective-permute-start.28 = (bf16[64,2048]{1,0:T(8,128)(2,1)S(1)}, bf16[64,2048]{1,0:T(8,128)(2,1)}, u32[]{:S(2)}, u32[]{:S(2)}) collective-permute-start(bf16[64,2048]{1,0:T(8,128)(2,1)S(1)} %get-tuple-element.73), channel_id=1, source_target_pairs={{0,9},{1,10},{2,11},{3,8},{4,13},{5,14},{6,15},{7,12},{8,1},{9,2},... | collective-permute-start | bytes 786440 | tf_op jit(solution)/shard_map/ppermute | solution.py:315
  129.9 47.2 %collective-permute-start.27 = (bf16[64,2048]{1,0:T(8,128)(2,1)S(1)}, bf16[64,2048]{1,0:T(8,128)(2,1)}, u32[]{:S(2)}, u32[]{:S(2)}) collective-permute-start(bf16[64,2048]{1,0:T(8,128)(2,1)S(1)} %get-tuple-element.74), channel_id=1, source_target_pairs={{0,8},{1,9},{2,10},{3,11},{4,12},{5,13},{6,14},{7,15},{8,0},{9,1},... | collective-permute-start | bytes 786440 | tf_op jit(solution)/shard_map/ppermute | solution.py:315
  151.6 3.4 %copy-start.1 = (bf16[768,2048]{1,0:T(8,128)(2,1)S(1)}, bf16[768,2048]{1,0:T(8,128)(2,1)}, u32[]{:S(2)}) copy-start(bf16[768,2048]{1,0:T(8,128)(2,1)} %shard_map.38) | copy-start | bytes 9437188
  156.7 25.9 %collective-permute-start.31 = (bf16[64,2048]{1,0:T(8,128)(2,1)}, bf16[64,2048]{1,0:T(8,128)(2,1)}, u32[]{:S(2)}, u32[]{:S(2)}) collective-permute-start(bf16[64,2048]{1,0:T(8,128)(2,1)} %get-tuple-element.64), channel_id=1, source_target_pairs={{0,4},{1,5},{2,6},{3,7},{4,8},{5,9},{6,10},{7,11},{8,12},{9,13},{1... | collective-permute-start | bytes 786440 | tf_op jit(solution)/shard_map/ppermute | solution.py:315
  177.1 13.8 %collective-permute-start.32 = (bf16[64,2048]{1,0:T(8,128)(2,1)}, bf16[64,2048]{1,0:T(8,128)(2,1)S(1)}, u32[]{:S(2)}, u32[]{:S(2)}) collective-permute-start(bf16[64,2048]{1,0:T(8,128)(2,1)} %get-tuple-element.44), channel_id=1, source_target_pairs={{0,12},{1,13},{2,14},{3,15},{4,0},{5,1},{6,2},{7,3},{8,4},{9,5},{1... | collective-permute-start | bytes 786440 | tf_op jit(solution)/shard_map/ppermute | solution.py:315
  177.1 17.1 %collective-permute-start.33 = (bf16[64,2048]{1,0:T(8,128)(2,1)}, bf16[64,2048]{1,0:T(8,128)(2,1)S(1)}, u32[]{:S(2)}, u32[]{:S(2)}) collective-permute-start(bf16[64,2048]{1,0:T(8,128)(2,1)} %get-tuple-element.46), channel_id=1, source_target_pairs={{0,5},{1,6},{2,7},{3,4},{4,9},{5,10},{6,11},{7,8},{8,13},{9,14},{1... | collective-permute-start | bytes 786440 | tf_op jit(solution)/shard_map/ppermute | solution.py:315
  180.6 23.3 %collective-permute-start.34 = (bf16[64,2048]{1,0:T(8,128)(2,1)}, bf16[64,2048]{1,0:T(8,128)(2,1)S(1)}, u32[]{:S(2)}, u32[]{:S(2)}) collective-permute-start(bf16[64,2048]{1,0:T(8,128)(2,1)} %get-tuple-element.48), channel_id=1, source_target_pairs={{0,13},{1,14},{2,15},{3,12},{4,1},{5,2},{6,3},{7,0},{8,5},{9,6},{1... | collective-permute-start | bytes 786440 | tf_op jit(solution)/shard_map/ppermute | solution.py:315
  181.9 22.0 %collective-permute-start.35 = (bf16[64,2048]{1,0:T(8,128)(2,1)}, bf16[64,2048]{1,0:T(8,128)(2,1)S(1)}, u32[]{:S(2)}, u32[]{:S(2)}) collective-permute-start(bf16[64,2048]{1,0:T(8,128)(2,1)} %get-tuple-element.50), channel_id=1, source_target_pairs={{0,1},{1,2},{2,3},{3,0},{4,5},{5,6},{6,7},{7,4},{8,9},{9,10},{10,1... | collective-permute-start | bytes 786440 | tf_op jit(solution)/shard_map/ppermute | solution.py:315
  182.6 25.8 %collective-permute-start.36 = (bf16[64,2048]{1,0:T(8,128)(2,1)}, bf16[64,2048]{1,0:T(8,128)(2,1)S(1)}, u32[]{:S(2)}, u32[]{:S(2)}) collective-permute-start(bf16[64,2048]{1,0:T(8,128)(2,1)} %get-tuple-element.52), channel_id=1, source_target_pairs={{0,6},{1,7},{2,4},{3,5},{4,10},{5,11},{6,8},{7,9},{8,14},{9,15},{1... | collective-permute-start | bytes 786440 | tf_op jit(solution)/shard_map/ppermute | solution.py:315
  190.9 21.0 %collective-permute-start.37 = (bf16[64,2048]{1,0:T(8,128)(2,1)}, bf16[64,2048]{1,0:T(8,128)(2,1)S(1)}, u32[]{:S(2)}, u32[]{:S(2)}) collective-permute-start(bf16[64,2048]{1,0:T(8,128)(2,1)} %get-tuple-element.54), channel_id=1, source_target_pairs={{0,14},{1,15},{2,12},{3,13},{4,2},{5,3},{6,0},{7,1},{8,6},{9,7},{1... | collective-permute-start | bytes 786440 | tf_op jit(solution)/shard_map/ppermute | solution.py:315
  194.2 22.0 %collective-permute-start.38 = (bf16[64,2048]{1,0:T(8,128)(2,1)}, bf16[64,2048]{1,0:T(8,128)(2,1)S(1)}, u32[]{:S(2)}, u32[]{:S(2)}) collective-permute-start(bf16[64,2048]{1,0:T(8,128)(2,1)} %get-tuple-element.55), channel_id=1, source_target_pairs={{0,2},{1,3},{2,0},{3,1},{4,6},{5,7},{6,4},{7,5},{8,10},{9,11},{10,... | collective-permute-start | bytes 786440 | tf_op jit(solution)/shard_map/ppermute | solution.py:315
  203.9 13.0 %collective-permute-start.39 = (bf16[64,2048]{1,0:T(8,128)(2,1)}, bf16[64,2048]{1,0:T(8,128)(2,1)S(1)}, u32[]{:S(2)}, u32[]{:S(2)}) collective-permute-start(bf16[64,2048]{1,0:T(8,128)(2,1)} %get-tuple-element.56), channel_id=1, source_target_pairs={{0,7},{1,4},{2,5},{3,6},{4,11},{5,8},{6,9},{7,10},{8,15},{9,12},{1... | collective-permute-start | bytes 786440 | tf_op jit(solution)/shard_map/ppermute | solution.py:315
  203.9 16.5 %collective-permute-start.40 = (bf16[64,2048]{1,0:T(8,128)(2,1)}, bf16[64,2048]{1,0:T(8,128)(2,1)S(1)}, u32[]{:S(2)}, u32[]{:S(2)}) collective-permute-start(bf16[64,2048]{1,0:T(8,128)(2,1)} %get-tuple-element.57), channel_id=1, source_target_pairs={{0,15},{1,12},{2,13},{3,14},{4,3},{5,0},{6,1},{7,2},{8,7},{9,4},{1... | collective-permute-start | bytes 786440 | tf_op jit(solution)/shard_map/ppermute | solution.py:315
  208.4 13.4 %collective-permute-start.41 = (bf16[64,2048]{1,0:T(8,128)(2,1)}, bf16[64,2048]{1,0:T(8,128)(2,1)S(1)}, u32[]{:S(2)}, u32[]{:S(2)}) collective-permute-start(bf16[64,2048]{1,0:T(8,128)(2,1)} %get-tuple-element.58), channel_id=1, source_target_pairs={{0,3},{1,0},{2,1},{3,2},{4,7},{5,4},{6,5},{7,6},{8,11},{9,8},{10,9... | collective-permute-start | bytes 786440 | tf_op jit(solution)/shard_map/ppermute | solution.py:315

commit v4 on v3

--- a/solution.py
+++ b/solution.py
@@ -83,18 +83,26 @@
     lax.fori_loop(0, steps, step, 0)
 
 
-def some_columns(count, base, group_at, far, span, where, *refs):
-    near, refs = refs[:count], refs[count:]
-    if far:
-        top, top_other, bottom, bottom_other, train, raw_in, squares_in = refs[:7]
-        scores, left, held, before, sums, piece_sems, train_sems, in_sems = refs[7:]
+def some_columns(count, base, group_at, last, more, owned, where, *refs):
+    near, refs = refs[: 4 if last else count], refs[4 if last else count :]
+    train, refs = refs[0], refs[1:]
+    if more:
+        raw_in, squares_in, refs = refs[0], refs[1], refs[2:]
+    if last:
+        outs = refs[: len(refs) - (7 if more else 5)]
+        refs = refs[len(outs) :]
     else:
-        train, raw_out, squares_out, left, held, piece_sems, train_sems = refs
-    total = count + (2 if far else 0)
-    width = (near[0] if near else top).shape[1]
+        raw_out, squares_out, refs = refs[0], refs[1], refs[2:]
+    left, held, piece_sems, train_sems = refs[:4]
+    if more:
+        before, in_sems = refs[4:6]
+    span = left.shape[0]
+    group = span // owned
+    width = near[0].shape[1]
     tile = held.shape[1]
     steps = train.shape[0] // tile
     first = where[group_at] * span
+    place = where[where.shape[0] - 1]
 
     def stream(j, k):
         return pltpu.make_async_copy(
@@ -104,95 +112,109 @@
         )
 
     def earlier(j):
-        rows = pl.ds(pl.multiple_of(j * tile, tile), tile)
-        return pltpu.make_async_copy(raw_in.at[rows, :], before.at[rows, :], in_sems.at[j])
-
-    def lay(source, at, k):
+        columns = pl.ds(pl.multiple_of(j * tile, tile), tile)
+        return pltpu.make_async_copy(raw_in.at[:, columns], before.at[:, columns], in_sems.at[j])
+
+    def lay(source, start, k, turn):
+        at = start + lax.rem(place + turn, group) * owned
         return pltpu.make_async_copy(
-            source.at[pl.ds(pl.multiple_of(at, span), span), :], left.at[:, pl.ds(k * width, width)], piece_sems.at[k]
+            source.at[pl.ds(pl.multiple_of(at, owned), owned), :],
+            left.at[pl.ds(turn * owned, owned), pl.ds(k * width, width)],
+            piece_sems.at[k, turn],
         )
 
-    for k, piece in enumerate(near):
-        lay(piece, first, k).start()
-    if far:
-        upper = top.shape[0]
-
-        @pl.when(first < upper)
-        def _():
-            lay(top, first, count).start()
-            lay(top_other, first, count + 1).start()
-
-        @pl.when(first >= upper)
-        def _():
-            lay(bottom, first - upper, count).start()
-            lay(bottom_other, first - upper, count + 1).start()
-
-    for k in range(total):
+    def lay_all(some, start):
+        for k, piece in enumerate(some):
+            for turn in range(group):
+                lay(piece, start, k, turn).start()
+
+    if last:
+        upper = near[0].shape[0]
+        pl.when(first < upper)(lambda: lay_all(near[:2], first))
+        pl.when(first >= upper)(lambda: lay_all(near[2:], first - upper))
+    else:
+        lay_all(near, first)
+    for k in range(count):
         stream(0, k).start()
-    if far:
+    if more:
         for j in range(steps):
             earlier(j).start()
-    for k in range(total):
-        lay(top if far else near[0], 0, k).wait()
-
-    squared = squares_in[...] if far else 0.0
+    for k in range(count):
+        for turn in range(group):
+            lay(near[0], 0, k, turn).wait()
+
+    squared = squares_in[...] if more else 0.0
     for at in range(0, left.shape[1], 128):
         wide = left[:, at : at + 128].astype(jnp.float32)
         squared = squared + wide * wide
-    if far:
-        sums[...] = jnp.broadcast_to(jnp.sqrt(jnp.sum(squared, axis=1, keepdims=True) + epsilon), sums.shape)
+    if last:
+        lengths = refs[-1]
+        lengths[...] = jnp.broadcast_to(jnp.sqrt(jnp.sum(squared, axis=1, keepdims=True) + epsilon), lengths.shape)
     else:
         squares_out[...] = squared
 
     def step(j, carry):
         @pl.when(j + 1 < steps)
         def _():
-            for k in range(total):
+            for k in range(count):
                 stream(j + 1, k).start()
 
-        for k in range(total):
+        for k in range(count):
             stream(j, k).wait()
-        raw = lax.dot_general(held[j % 2], left[...], (((1,), (1,)), ((), ())), preferred_element_type=jnp.float32)
-        rows = pl.ds(pl.multiple_of(j * tile, tile), tile)
-        if not far:
-            raw_out[rows, :] = raw
+        across = (((1,), (1,)), ((), ()))
+        if last:
+            raw = lax.dot_general(left[...], held[j % 2], across, preferred_element_type=jnp.float32)
+        else:
+            raw = lax.dot_general(held[j % 2], left[...], across, preferred_element_type=jnp.float32).T
+        columns = pl.ds(pl.multiple_of(j * tile, tile), tile)
+        if more:
+            earlier(j).wait()
+            raw = before[:, columns] + raw
+        if not last:
+            raw_out[:, columns] = raw
             return carry
-        earlier(j).wait()
-        raw = (before[rows, :] + raw).T
         for at in range(0, tile, 128):
-            columns = pl.ds(pl.multiple_of(j * tile + at, 128), 128)
-            scores[:, columns] = (raw[:, at : at + 128] / sums[...]).astype(scores.dtype)
+            part = (raw[:, at : at + 128] / lengths[...]).astype(outs[0].dtype)
+            for turn in range(group):
+                outs[turn][:, pl.ds(pl.multiple_of(j * tile + at, 128), 128)] = part[turn * owned : (turn + 1) * owned]
         return carry
 
     lax.fori_loop(0, steps, step, 0)
 
 
-def group_part(near, where, base, group_at, train_feats, span, far=(), earlier=()):
+def group_part(pieces, table, base, group_at, train_feats, span, owned, earlier=(), last=False):
     columns = train_feats.shape[0]
-    total = len(near) + len(far) // 2
-    depth = total * (list(near) + list(far))[0].shape[1]
+    count = len(pieces) // 2 if last else len(pieces)
+    depth = count * pieces[0].shape[1]
     tile = 512
+    group = span // owned
     anywhere, inside = pl.BlockSpec(memory_space=pl.ANY), pl.BlockSpec(memory_space=pltpu.VMEM)
-    in_specs = [pl.BlockSpec(memory_space=pltpu.SMEM)] + [anywhere] * (len(near) + len(far) + 1)
-    scratch = [pltpu.VMEM((span, depth), jnp.bfloat16), pltpu.VMEM((2, tile, depth), jnp.bfloat16)]
-    sems = [pltpu.SemaphoreType.DMA((total,)), pltpu.SemaphoreType.DMA((2, total))]
-    if far:
+    in_specs = [pl.BlockSpec(memory_space=pltpu.SMEM)] + [anywhere] * (len(pieces) + 1)
+    scratch = [
+        pltpu.VMEM((span, depth), jnp.bfloat16),
+        pltpu.VMEM((2, tile, depth), jnp.bfloat16),
+        pltpu.SemaphoreType.DMA((count, group)),
+        pltpu.SemaphoreType.DMA((2, count)),
+    ]
+    if earlier:
         in_specs += [anywhere, inside]
-        out_shape, out_specs = jax.ShapeDtypeStruct((span, columns), jnp.bfloat16), inside
-        scratch += [pltpu.VMEM((columns, span), jnp.float32), pltpu.VMEM((span, 128), jnp.float32)]
-        sems += [pltpu.SemaphoreType.DMA((columns // tile,))]
+        scratch += [pltpu.VMEM((span, columns), jnp.float32), pltpu.SemaphoreType.DMA((columns // tile,))]
+    if last:
+        scratch += [pltpu.VMEM((span, 128), jnp.float32)]
+        out_shape = (jax.ShapeDtypeStruct((owned, columns), jnp.bfloat16),) * group
+        out_specs = (inside,) * group
     else:
-        out_shape = (jax.ShapeDtypeStruct((columns, span), jnp.float32), jax.ShapeDtypeStruct((span, 128), jnp.float32))
+        out_shape = (jax.ShapeDtypeStruct((span, columns), jnp.float32), jax.ShapeDtypeStruct((span, 128), jnp.float32))
         out_specs = (inside, inside)
     return pl.pallas_call(
-        functools.partial(some_columns, len(near), base, group_at, bool(far), span),
+        functools.partial(some_columns, count, base, group_at, last, bool(earlier), owned),
         out_shape=out_shape,
         in_specs=in_specs,
         out_specs=out_specs,
-        scratch_shapes=scratch + sems,
+        scratch_shapes=scratch,
         compiler_params=pltpu.CompilerParams(vmem_limit_bytes=VMEM_LIMIT),
         cost_estimate=pl.CostEstimate(flops=2 * span * columns * depth, bytes_accessed=2 * columns * depth, transcendentals=0),
-    )(where, *near, *far, train_feats, *earlier)
+    )(table, *pieces, train_feats, *earlier)
 
 
 def group_scores(near, far, where, skip, targets, train_feats, span):
@@ -256,7 +278,7 @@
     for step in range(1, n // 2 + 1):
         for owner in (before(step), after(step))[: 1 if 2 * step == n else 2]:
             table += [owner * 2 + feat, owner * 2 + 1 - feat]
-    table = jnp.stack(table + [(at_group + shift) % groups for shift in shifts]).astype(jnp.int32)
+    table = jnp.stack(table + [(at_group + shift) % groups for shift in shifts] + [at_place]).astype(jnp.int32)
 
     blocks = [(row, queries)]
     forward = backward = queries
@@ -275,6 +297,7 @@
         keep = lax.dynamic_update_slice(keep, a, (owner * count, 0))
         give = lax.dynamic_update_slice(give, b, (owner * count, 0))
     mine = (keep + lax.ppermute(give, "feat", swap)).astype(jnp.bfloat16)
+    top, bottom, mine = lax.optimization_barrier((top, bottom, mine))
     a, b = product(jnp.concatenate([top, bottom]))
     mine = lax.dynamic_update_slice(
         mine, (a + lax.ppermute(b, "feat", swap)).astype(jnp.bfloat16), (before(n // 2) * count, 0)
@@ -287,16 +310,19 @@
         backward = lax.ppermute(backward, "rows", back)
         if step == n // 2 - 1:
             early = len(near)
-            partial = group_part(near, table, 0, devices, train_feats, span)
+            partial = group_part(near, table, 0, devices, train_feats, span, owned)
             forward, backward, squares = lax.optimization_barrier((forward, backward, partial[1]))
             partial = (partial[0], squares)
         for block in (forward, backward):
             near += [block, lax.ppermute(block, "feat", swap)]
     top = lax.ppermute(forward[: total // 2], "rows", ahead)
     bottom = lax.ppermute(backward[total // 2 :], "rows", back)
+    partial = group_part(near[early:], table, early, devices, train_feats, span, owned, partial)
+    top, bottom, squares = lax.optimization_barrier((top, bottom, partial[1]))
+    partial = (partial[0], squares)
     far = [top, lax.ppermute(top, "feat", swap), bottom, lax.ppermute(bottom, "feat", swap)]
 
-    first = group_part(near[early:], table, early, devices, train_feats, span, far, partial)
+    first = group_part(far, table, len(near), devices, train_feats, span, owned, partial, last=True)
     rest = group_scores(near, far, table, 1, groups - 1, train_feats, span)
     scores = jnp.zeros((owned, devices * columns), jnp.bfloat16)
     order = [(0, turn) for turn in range(group)]
@@ -305,8 +331,10 @@
     going, sources = [], []
     for number, turn in order:
         shift = shifts[number]
-        tiles, offset = (first, 0) if number == 0 else (rest, (number - 1) * span)
-        block = lax.dynamic_slice_in_dim(tiles, offset + (at_place + turn) % group * owned, owned, 0)
+        if number == 0:
+            block = first[turn]
+        else:
+            block = lax.dynamic_slice_in_dim(rest, (number - 1) * span + (at_place + turn) % group * owned, owned, 0)
         source = (at_group + groups - shift) % groups * group + (at_place + group - turn) % group
         if shift or turn:
             pairs = [(i, (i // group + shift) % groups * group + (i + turn) % group) for i in range(devices)]

time: 223 us -> 217 us (0.973)
  local copies, waits for them, and re-layouts: 29.9 us -> 20 us
  waiting for transfers between devices: 94.8 us -> 103 us
  starting transfers between devices: 48.4 us -> 41.5 us
  Pallas kernels: 40 us -> 46.2 us
  matrix products: 7.77 us -> 4.59 us
    ppermute x15, waiting for transfers between devices: 34.4 us -> 44.1 us  [per_device(): going.append(lax.ppermute(block, ('rows', 'feat'), pairs))]
    ppermute x6, waiting for transfers between devices: 21.7 us -> 28.4 us  [per_device(): forward = lax.ppermute(forward, 'rows', ahead)]
    ppermute x15, starting transfers between devices: 24 us -> 17.5 us  [per_device(): going.append(lax.ppermute(block, ('rows', 'feat'), pairs))]
    ppermute x1, waiting for transfers between devices: 6.26 us -> 0.01 us  [per_device(): bottom = lax.ppermute(backward[total // 2:], 'rows', back)]
    pallas_call x2 -> x3, Pallas kernels: 18.6 us -> 24.8 us  [group_part(): pl.pallas_call(functools.partial(some_columns, count, base, group_at, las...]
    dynamic_update_slice x7, local copies, waits for them, and re-layouts: 4.74 us -> 0.18 us  [per_device(): give = lax.dynamic_update_slice(give, b, (owner * count, 0))]
    dynamic_update_slice x15, local copies, waits for them, and re-layouts: 14.6 us -> 10.8 us  [per_device(): scores = lax.dynamic_update_slice(scores, block, (0, source * columns))]
    dot_general x8, matrix products: 7.77 us -> 4.59 us  [product(): partial = jnp.dot(block, kernel, preferred_element_type=jnp.float32)]
  transfers between devices with their start and end apart: 42 -> 42, of which waited for: 21 -> 20; matrix products, arithmetic and copies ran while one was open for 15% -> 9% of each run, Pallas kernels for 14% -> 18%
where the time goes in v4:
time: 217 us; the launch traced here: 216 us
  waiting for transfers between devices  103 us (47%)
  Pallas kernels  46.2 us (21%)
  starting transfers between devices  41.5 us (19%)
  local copies, waits for them, and re-layouts  20 us (9%)
  matrix products  4.59 us (2%)
    ppermute x15, waiting for transfers between devices, per_device(): going.append(lax.ppermute(block, ('rows', 'feat'), pairs))  44.1 us
    ppermute x6, waiting for transfers between devices, per_device(): forward = lax.ppermute(forward, 'rows', ahead)  28.4 us
    pallas_call x3, Pallas kernels, group_part(): pl.pallas_call(functools.partial(some_columns, count, base, group_at, las...  24.8 us
    pallas_call x1, Pallas kernels, group_scores(): pl.pallas_call(functools.partial(tile_rows, owners, skip, tuple(range(tar...  21.4 us
    ppermute x6, waiting for transfers between devices, per_device(): backward = lax.ppermute(backward, 'rows', back)  20.5 us
    ppermute x15, starting transfers between devices, per_device(): going.append(lax.ppermute(block, ('rows', 'feat'), pairs))  17.5 us
    dynamic_update_slice x15, local copies, waits for them, and re-layouts, per_device(): scores = lax.dynamic_update_slice(scores, block, (0, source * columns))  10.8 us
    ppermute x6, starting transfers between devices, per_device(): forward = lax.ppermute(forward, 'rows', ahead)  7.7 us
  transfers between devices with their start and end apart: 42, of which 20 were waited for; matrix products, arithmetic and copies ran while one was open for 9% of the time, Pallas kernels for 18%

profile of v4, /device:TPU:1, one launch (start us, length us, event | category | flops | bytes accessed | tf_op | source)
XLA Modules:
  0.0 216.4 jit_solution(7985934719556304068)
XLA Ops:
  0.0 2.1 collective-permute-start
  2.8 1.5 fusion.6
  4.5 9.5 %collective-permute-done = bf16[128,2048]{1,0:T(8,128)(2,1)S(1)} collective-permute-done((bf16[128,2048]{1,0:T(8,128)(2,1)}, bf16[128,2048]{1,0:T(8,128)(2,1)S(1)}, u32[]{:S(2)}, u32[]{:S(2)}) %collective-permute-start) | collective-permute-done | bytes 524320 | tf_op jit(solution)/shard_map/ppermute | solution.py:286
  13.9 1.2 collective-permute-start.1
  16.4 9.7 %collective-permute-done.1 = bf16[128,2048]{1,0:T(8,128)(2,1)S(1)} collective-permute-done((bf16[128,2048]{1,0:T(8,128)(2,1)S(1)}, bf16[128,2048]{1,0:T(8,128)(2,1)S(1)}, u32[]{:S(2)}, u32[]{:S(2)}) %collective-permute-start.1) | collective-permute-done | bytes 524320 | tf_op jit(solution)/shard_map/ppermute | solution.py:286
  26.1 0.9 collective-permute-start.2
  28.6 8.8 %collective-permute-done.2 = bf16[128,2048]{1,0:T(8,128)(2,1)S(1)} collective-permute-done((bf16[128,2048]{1,0:T(8,128)(2,1)S(1)}, bf16[128,2048]{1,0:T(8,128)(2,1)S(1)}, u32[]{:S(2)}, u32[]{:S(2)}) %collective-permute-start.2) | collective-permute-done | bytes 524320 | tf_op jit(solution)/shard_map/ppermute | solution.py:286
  38.7 3.7 %collective-permute-start.8 = (f32[1024,256]{1,0:T(8,128)S(1)}, f32[1024,256]{1,0:T(8,128)S(1)}, u32[]{:S(2)}, u32[]{:S(2)}) collective-permute-start(f32[1024,256]{1,0:T(8,128)S(1)} %get-tuple-element.95), channel_id=1, source_target_pairs={{0,1},{1,0},{2,3},{3,2},{4,5},{5,4},{6,7},{7,6},{8,9},{9,8},{10,11... | collective-permute-start | bytes 3145736 | tf_op jit(solution)/shard_map/ppermute | solution.py:299
  42.4 1.4 collective-permute-start.3
  44.0 0.7 collective-permute-done.8
  44.9 5.5 %collective-permute-done.3 = bf16[64,2048]{1,0:T(8,128)(2,1)S(1)} collective-permute-done((bf16[64,2048]{1,0:T(8,128)(2,1)S(1)}, bf16[64,2048]{1,0:T(8,128)(2,1)S(1)}, u32[]{:S(2)}, u32[]{:S(2)}) %collective-permute-start.3) | collective-permute-done | bytes 262176 | tf_op jit(solution)/shard_map/ppermute | solution.py:291
  50.4 1.1 collective-permute-done.7
  51.9 1.2 collective-permute-start.9
  53.1 1.0 collective-permute-done.9
  54.4 1.3 collective-permute-start.11
  55.7 11.7 %collective-permute-done.13.refs_4_ = bf16[1024,256]{1,0:T(8,128)(2,1)S(1)} collective-permute-done((bf16[1024,256]{1,0:T(8,128)(2,1)S(1)}, bf16[1024,256]{1,0:T(8,128)(2,1)S(1)}, u32[]{:S(2)}, u32[]{:S(2)}) %collective-permute-start.13) | collective-permute-done | bytes 524320 | tf_op jit(solution)/shard_map/ppermute | solution.py:310
  67.5 1.3 collective-permute-start.15
  68.8 1.8 collective-permute-start.10
  71.1 8.5 %collective-permute-done.17.refs_8_ = bf16[1024,256]{1,0:T(8,128)(2,1)S(1)} collective-permute-done((bf16[1024,256]{1,0:T(8,128)(2,1)S(1)}, bf16[1024,256]{1,0:T(8,128)(2,1)S(1)}, u32[]{:S(2)}, u32[]{:S(2)}) %collective-permute-start.17) | collective-permute-done | bytes 524320 | tf_op jit(solution)/shard_map/ppermute | solution.py:310
  79.6 2.1 collective-permute-start.18
  82.5 0.9 collective-permute-start.19
  83.4 0.8 copy-done.11
  84.1 0.8 copy-done.12
  85.0 10.1 %shard_map.37 = (f32[256,2048]{1,0:T(8,128)}, f32[256,128]{1,0:T(8,128)}) custom-call(s32[21]{0:T(128)} %stack.87.where, bf16[1024,256]{1,0:T(8,128)(2,1)} %copy-done.2, bf16[1024,256]{1,0:T(8,128)(2,1)} %copy-done.9, bf16[1024,256]{1,0:T(8,128)(2,1)} %copy-done.6, bf16[1024,256]{1,0:T(8,128)(2,1)} %copy-done.11, bf16[1024,256]{1,0:T(8,128)(2,1)} %copy-done.5, ...), custom_call_target="tpu_custom_call" | custom-call | flops 2684354560 | bytes 10485760 | tf_op jit(solution)/shard_map/pallas_call | solution.py:209
  95.6 1.2 collective-permute-start.21
  96.8 0.9 collective-permute-start.24
  98.4 0.7 collective-permute-done.22.refs_3_.refs_13_
  99.1 0.7 copy-done.14
  99.9 8.0 %shard_map.38 = (f32[256,2048]{1,0:T(8,128)}, f32[256,128]{1,0:T(8,128)}) custom-call(s32[21]{0:T(128)} %stack.87.where, bf16[1024,256]{1,0:T(8,128)(2,1)} %copy-done.4, bf16[1024,256]{1,0:T(8,128)(2,1)} %copy-done.13, bf16[1024,256]{1,0:T(8,128)(2,1)} %copy-done.3, bf16[1024,256]{1,0:T(8,128)(2,1)} %copy-done.14, bf16[2048,4096]{1,0:T(8,128)(2,1)} %refs_4_.3, ...), custom_call_target="tpu_custom_call" | custom-call | flops 1073741824 | bytes 4194304 | tf_op jit(solution)/shard_map/pallas_call | solution.py:209
  108.6 1.3 collective-permute-done.25.refs_15_.refs_1_
  110.8 6.6 %shard_map.40 = (bf16[64,2048]{1,0:T(8,128)(2,1)}, bf16[64,2048]{1,0:T(8,128)(2,1)}, bf16[64,2048]{1,0:T(8,128)(2,1)}, bf16[64,2048]{1,0:T(8,128)(2,1)}) custom-call(s32[21]{0:T(128)} %stack.87.where, bf16[512,256]{1,0:T(8,128)(2,1)} %collective-permute-done.23.refs_14_.refs_0_, bf16[512,256]{1,0:T(8,128)(2,1)} %copy-done.16, bf16[512,256]{1,0:T(8,128)(2,1)} %copy-done.15, ...), custom_call_target="tpu_custom_call" | custom-call | flops 536870912 | bytes 2097152 | tf_op jit(solution)/shard_map/pallas_call | solution.py:209
  117.5 1.6 collective-permute-start.27
  119.0 2.0 collective-permute-start.28
  121.0 1.8 collective-permute-start.29
  123.4 21.4 %shard_map.39 = bf16[768,2048]{1,0:T(8,128)(2,1)} custom-call(s32[21]{0:T(128)} %stack.87.where, bf16[1024,256]{1,0:T(8,128)(2,1)} %copy-done.2, bf16[1024,256]{1,0:T(8,128)(2,1)} %copy-done.9, bf16[1024,256]{1,0:T(8,128)(2,1)} %copy-done.6, bf16[1024,256]{1,0:T(8,128)(2,1)} %copy-done.11, bf16[1024,256]{1,0:T(8,128)(2,1)} %copy-done.5, ...), custom_call_target="tpu_custom_call" | custom-call | flops 12884901888 | bytes 16777216 | tf_op jit(solution)/shard_map/pallas_call | solution.py:226
  144.8 2.4 %broadcast_in_dim.3 = bf16[64,32768]{1,0:T(8,128)(2,1)} broadcast(bf16[]{:T(256)} %constant.260.clone.1), dimensions={} | broadcast | bytes 4194306 | tf_op jit(solution)/shard_map/broadcast_in_dim | solution.py:327
  147.2 1.0 copy-done.1
  148.2 1.7 constant_dynamic-slice_fusion.11
  149.8 1.3 collective-permute-start.31
  151.1 21.0 %collective-permute-done.30 = bf16[64,2048]{1,0:T(8,128)(2,1)S(1)} collective-permute-done((bf16[64,2048]{1,0:T(8,128)(2,1)}, bf16[64,2048]{1,0:T(8,128)(2,1)S(1)}, u32[]{:S(2)}, u32[]{:S(2)}) %collective-permute-start.30) | collective-permute-done | bytes 262176 | tf_op jit(solution)/shard_map/ppermute | solution.py:343
  172.2 1.5 collective-permute-start.33
  173.7 2.4 %collective-permute-start.34 = (bf16[64,2048]{1,0:T(8,128)(2,1)}, bf16[64,2048]{1,0:T(8,128)(2,1)S(1)}, u32[]{:S(2)}, u32[]{:S(2)}) collective-permute-start(bf16[64,2048]{1,0:T(8,128)(2,1)} %get-tuple-element.72), channel_id=1, source_target_pairs={{0,13},{1,14},{2,15},{3,12},{4,1},{5,2},{6,3},{7,0},{8,5},{9,6},{1... | collective-permute-start | bytes 786440 | tf_op jit(solution)/shard_map/ppermute | solution.py:343
  176.7 0.7 constant_dynamic-update-slice_fusion.7
  177.4 0.7 constant_dynamic-update-slice_fusion.6
  178.1 0.7 constant_dynamic-update-slice_fusion.5
  178.8 0.7 constant_dynamic-update-slice_fusion.4
  179.6 0.7 constant_dynamic-update-slice_fusion.3
  180.3 5.9 %collective-permute-done.32 = bf16[64,2048]{1,0:T(8,128)(2,1)S(1)} collective-permute-done((bf16[64,2048]{1,0:T(8,128)(2,1)}, bf16[64,2048]{1,0:T(8,128)(2,1)S(1)}, u32[]{:S(2)}, u32[]{:S(2)}) %collective-permute-start.32) | collective-permute-done | bytes 262176 | tf_op jit(solution)/shard_map/ppermute | solution.py:343
  186.2 0.8 collective-permute-start.38
  187.0 10.5 %collective-permute-done.34 = bf16[64,2048]{1,0:T(8,128)(2,1)S(1)} collective-permute-done((bf16[64,2048]{1,0:T(8,128)(2,1)}, bf16[64,2048]{1,0:T(8,128)(2,1)S(1)}, u32[]{:S(2)}, u32[]{:S(2)}) %collective-permute-start.34) | collective-permute-done | bytes 262176 | tf_op jit(solution)/shard_map/ppermute | solution.py:343
  197.4 4.0 %collective-permute-start.40 = (bf16[64,2048]{1,0:T(8,128)(2,1)}, bf16[64,2048]{1,0:T(8,128)(2,1)S(1)}, u32[]{:S(2)}, u32[]{:S(2)}) collective-permute-start(bf16[64,2048]{1,0:T(8,128)(2,1)} %get-tuple-element.81), channel_id=1, source_target_pairs={{0,15},{1,12},{2,13},{3,14},{4,3},{5,0},{6,1},{7,2},{8,7},{9,4},{1... | collective-permute-start | bytes 786440 | tf_op jit(solution)/shard_map/ppermute | solution.py:343
  201.5 1.0 collective-permute-start.41
  202.5 0.7 constant_dynamic-update-slice_fusion.2
  203.2 0.7 constant_dynamic-update-slice_fusion.1
  203.9 0.7 constant_dynamic-update-slice_fusion
  204.6 0.7 constant_dynamic-update-slice_fusion.14
  205.4 0.7 constant_dynamic-update-slice_fusion.13
  206.1 0.7 constant_dynamic-update-slice_fusion.12
  206.8 4.2 %collective-permute-done.38 = bf16[64,2048]{1,0:T(8,128)(2,1)S(1)} collective-permute-done((bf16[64,2048]{1,0:T(8,128)(2,1)}, bf16[64,2048]{1,0:T(8,128)(2,1)S(1)}, u32[]{:S(2)}, u32[]{:S(2)}) %collective-permute-start.38) | collective-permute-done | bytes 262176 | tf_op jit(solution)/shard_map/ppermute | solution.py:343
  211.0 0.7 constant_dynamic-update-slice_fusion.11
  211.8 0.7 constant_dynamic-update-slice_fusion.10
  212.5 2.0 collective-permute-done.40
  214.5 0.7 constant_dynamic-update-slice_fusion.9
  215.7 0.7 constant_dynamic-update-slice_fusion.8
  (103 shorter events, 11.8 us)
Async XLA Ops:
  0.0 2.8 %copy-start = (bf16[2048,512]{1,0:T(8,128)(2,1)S(1)}, bf16[2048,512]{1,0:T(8,128)(2,1)}, u32[]{:S(2)}) copy-start(bf16[2048,512]{1,0:T(8,128)(2,1)} %param.4) | copy-start | bytes 6291460
  0.0 13.9 %collective-permute-start = (bf16[128,2048]{1,0:T(8,128)(2,1)}, bf16[128,2048]{1,0:T(8,128)(2,1)S(1)}, u32[]{:S(2)}, u32[]{:S(2)}) collective-permute-start(bf16[128,2048]{1,0:T(8,128)(2,1)} %param.3), channel_id=1, source_target_pairs={{0,4},{4,8},{8,12},{12,14},{14,10},{10,6},{6,2},{2,0},{1,5},{5,9},... | collective-permute-start | bytes 1572872 | tf_op jit(solution)/shard_map/ppermute | solution.py:286
  2.1 13.5 %collective-permute-start.4 = (bf16[128,2048]{1,0:T(8,128)(2,1)}, bf16[128,2048]{1,0:T(8,128)(2,1)S(1)}, u32[]{:S(2)}, u32[]{:S(2)}) collective-permute-start(bf16[128,2048]{1,0:T(8,128)(2,1)} %param.3), channel_id=1, source_target_pairs={{4,0},{8,4},{12,8},{14,12},{10,14},{6,10},{2,6},{0,2},{5,1},{9,5},... | collective-permute-start | bytes 1572872 | tf_op jit(solution)/shard_map/ppermute | solution.py:287
  13.9 12.2 %collective-permute-start.1 = (bf16[128,2048]{1,0:T(8,128)(2,1)S(1)}, bf16[128,2048]{1,0:T(8,128)(2,1)S(1)}, u32[]{:S(2)}, u32[]{:S(2)}) collective-permute-start(bf16[128,2048]{1,0:T(8,128)(2,1)S(1)} %collective-permute-done), channel_id=1, source_target_pairs={{0,4},{4,8},{8,12},{12,14},{14,10},{10,6},{6,2},{2,0},{1,5},{5,9},... | collective-permute-start | bytes 1572872 | tf_op jit(solution)/shard_map/ppermute | solution.py:286
  15.6 11.9 %collective-permute-start.5 = (bf16[128,2048]{1,0:T(8,128)(2,1)S(1)}, bf16[128,2048]{1,0:T(8,128)(2,1)S(1)}, u32[]{:S(2)}, u32[]{:S(2)}) collective-permute-start(bf16[128,2048]{1,0:T(8,128)(2,1)S(1)} %collective-permute-done.4), channel_id=1, source_target_pairs={{4,0},{8,4},{12,8},{14,12},{10,14},{6,10},{2,6},{0,2},{5,1},{9,5},... | collective-permute-start | bytes 1572872 | tf_op jit(solution)/shard_map/ppermute | solution.py:287
  26.1 11.3 %collective-permute-start.2 = (bf16[128,2048]{1,0:T(8,128)(2,1)S(1)}, bf16[128,2048]{1,0:T(8,128)(2,1)S(1)}, u32[]{:S(2)}, u32[]{:S(2)}) collective-permute-start(bf16[128,2048]{1,0:T(8,128)(2,1)S(1)} %collective-permute-done.1), channel_id=1, source_target_pairs={{0,4},{4,8},{8,12},{12,14},{14,10},{10,6},{6,2},{2,0},{1,5},{5,9},... | collective-permute-start | bytes 1572872 | tf_op jit(solution)/shard_map/ppermute | solution.py:286
  27.5 10.7 %collective-permute-start.6 = (bf16[128,2048]{1,0:T(8,128)(2,1)S(1)}, bf16[128,2048]{1,0:T(8,128)(2,1)S(1)}, u32[]{:S(2)}, u32[]{:S(2)}) collective-permute-start(bf16[128,2048]{1,0:T(8,128)(2,1)S(1)} %collective-permute-done.5), channel_id=1, source_target_pairs={{4,0},{8,4},{12,8},{14,12},{10,14},{6,10},{2,6},{0,2},{5,1},{9,5},... | collective-permute-start | bytes 1572872 | tf_op jit(solution)/shard_map/ppermute | solution.py:287
  38.7 6.0 %collective-permute-start.8 = (f32[1024,256]{1,0:T(8,128)S(1)}, f32[1024,256]{1,0:T(8,128)S(1)}, u32[]{:S(2)}, u32[]{:S(2)}) collective-permute-start(f32[1024,256]{1,0:T(8,128)S(1)} %get-tuple-element.95), channel_id=1, source_target_pairs={{0,1},{1,0},{2,3},{3,2},{4,5},{5,4},{6,7},{7,6},{8,9},{9,8},{10,11... | collective-permute-start | bytes 3145736 | tf_op jit(solution)/shard_map/ppermute | solution.py:299
  42.4 8.0 %collective-permute-start.3 = (bf16[64,2048]{1,0:T(8,128)(2,1)S(1)}, bf16[64,2048]{1,0:T(8,128)(2,1)S(1)}, u32[]{:S(2)}, u32[]{:S(2)}) collective-permute-start(bf16[64,2048]{1,0:T(8,128)(2,1)S(1)} %slice.16), channel_id=1, source_target_pairs={{0,4},{4,8},{8,12},{12,14},{14,10},{10,6},{6,2},{2,0},{1,5},{5,9},... | collective-permute-start | bytes 786440 | tf_op jit(solution)/shard_map/ppermute | solution.py:291
  43.8 7.7 %collective-permute-start.7 = (bf16[64,2048]{1,0:T(8,128)(2,1)S(1)}, bf16[64,2048]{1,0:T(8,128)(2,1)S(1)}, u32[]{:S(2)}, u32[]{:S(2)}) collective-permute-start(bf16[64,2048]{1,0:T(8,128)(2,1)S(1)} %slice.17), channel_id=1, source_target_pairs={{4,0},{8,4},{12,8},{14,12},{10,14},{6,10},{2,6},{0,2},{5,1},{9,5},... | collective-permute-start | bytes 786440 | tf_op jit(solution)/shard_map/ppermute | solution.py:292
  51.9 2.2 %collective-permute-start.9 = (f32[128,256]{1,0:T(8,128)S(1)}, f32[128,256]{1,0:T(8,128)S(1)}, u32[]{:S(2)}, u32[]{:S(2)}) collective-permute-start(f32[128,256]{1,0:T(8,128)S(1)} %constant_dynamic-slice_fusion.10), channel_id=1, source_target_pairs={{0,1},{1,0},{2,3},{3,2},{4,5},{5,4},{6,7},{7,6},{8,9},{9,8},{10,11... | collective-permute-start | bytes 393224 | tf_op jit(solution)/shard_map/ppermute | solution.py:303
  54.1 30.8 %copy-start.2 = (bf16[1024,256]{1,0:T(8,128)(2,1)}, bf16[1024,256]{1,0:T(8,128)(2,1)S(1)}, u32[]{:S(2)}) copy-start(bf16[1024,256]{1,0:T(8,128)(2,1)S(1)} %fusion.4.refs_0_) | copy-start | bytes 1572868
  54.1 13.2 %collective-permute-start.13 = (bf16[1024,256]{1,0:T(8,128)(2,1)S(1)}, bf16[1024,256]{1,0:T(8,128)(2,1)S(1)}, u32[]{:S(2)}, u32[]{:S(2)}) collective-permute-start(bf16[1024,256]{1,0:T(8,128)(2,1)S(1)} %fusion.4.refs_0_), channel_id=1, source_target_pairs={{4,0},{8,4},{12,8},{14,12},{10,14},{6,10},{2,6},{0,2},{5,1},{9,5},... | collective-permute-start | bytes 1572872 | tf_op jit(solution)/shard_map/ppermute | solution.py:310
  54.4 13.2 %collective-permute-start.11 = (bf16[1024,256]{1,0:T(8,128)(2,1)S(1)}, bf16[1024,256]{1,0:T(8,128)(2,1)S(1)}, u32[]{:S(2)}, u32[]{:S(2)}) collective-permute-start(bf16[1024,256]{1,0:T(8,128)(2,1)S(1)} %fusion.4.refs_0_), channel_id=1, source_target_pairs={{0,4},{4,8},{8,12},{12,14},{14,10},{10,6},{6,2},{2,0},{1,5},{5,9},... | collective-permute-start | bytes 1572872 | tf_op jit(solution)/shard_map/ppermute | solution.py:309
  67.3 17.6 %copy-start.5 = (bf16[1024,256]{1,0:T(8,128)(2,1)}, bf16[1024,256]{1,0:T(8,128)(2,1)S(1)}, u32[]{:S(2)}) copy-start(bf16[1024,256]{1,0:T(8,128)(2,1)S(1)} %collective-permute-done.13.refs_4_) | copy-start | bytes 1572868
  67.3 12.2 %collective-permute-start.17 = (bf16[1024,256]{1,0:T(8,128)(2,1)S(1)}, bf16[1024,256]{1,0:T(8,128)(2,1)S(1)}, u32[]{:S(2)}, u32[]{:S(2)}) collective-permute-start(bf16[1024,256]{1,0:T(8,128)(2,1)S(1)} %collective-permute-done.13.refs_4_), channel_id=1, source_target_pairs={{4,0},{8,4},{12,8},{14,12},{10,14},{6,10},{2,6},{0,2},{5,1},{9,5},... | collective-permute-start | bytes 1572872 | tf_op jit(solution)/shard_map/ppermute | solution.py:310
  67.5 17.5 %copy-start.6 = (bf16[1024,256]{1,0:T(8,128)(2,1)}, bf16[1024,256]{1,0:T(8,128)(2,1)S(1)}, u32[]{:S(2)}) copy-start(bf16[1024,256]{1,0:T(8,128)(2,1)S(1)} %collective-permute-done.11.refs_2_) | copy-start | bytes 1572868
  67.5 14.2 %collective-permute-start.15 = (bf16[1024,256]{1,0:T(8,128)(2,1)S(1)}, bf16[1024,256]{1,0:T(8,128)(2,1)S(1)}, u32[]{:S(2)}, u32[]{:S(2)}) collective-permute-start(bf16[1024,256]{1,0:T(8,128)(2,1)S(1)} %collective-permute-done.11.refs_2_), channel_id=1, source_target_pairs={{0,4},{4,8},{8,12},{12,14},{14,10},{10,6},{6,2},{2,0},{1,5},{5,9},... | collective-permute-start | bytes 1572872 | tf_op jit(solution)/shard_map/ppermute | solution.py:309
  68.8 13.0 %collective-permute-start.10 = (bf16[1024,256]{1,0:T(8,128)(2,1)S(1)}, bf16[1024,256]{1,0:T(8,128)(2,1)S(1)}, u32[]{:S(2)}, u32[]{:S(2)}) collective-permute-start(bf16[1024,256]{1,0:T(8,128)(2,1)S(1)} %fusion.4.refs_0_), channel_id=1, source_target_pairs={{0,1},{1,0},{2,3},{3,2},{4,5},{5,4},{6,7},{7,6},{8,9},{9,8},{10,11... | collective-permute-start | bytes 1572872 | tf_op jit(solution)/shard_map/ppermute | solution.py:306
  70.6 11.9 %collective-permute-start.14 = (bf16[1024,256]{1,0:T(8,128)(2,1)S(1)}, bf16[1024,256]{1,0:T(8,128)(2,1)S(1)}, u32[]{:S(2)}, u32[]{:S(2)}) collective-permute-start(bf16[1024,256]{1,0:T(8,128)(2,1)S(1)} %collective-permute-done.13.refs_4_), channel_id=1, source_target_pairs={{0,1},{1,0},{2,3},{3,2},{4,5},{5,4},{6,7},{7,6},{8,9},{9,8},{10,11... | collective-permute-start | bytes 1572872 | tf_op jit(solution)/shard_map/ppermute | solution.py:317
  70.6 12.8 %collective-permute-start.12 = (bf16[1024,256]{1,0:T(8,128)(2,1)S(1)}, bf16[1024,256]{1,0:T(8,128)(2,1)S(1)}, u32[]{:S(2)}, u32[]{:S(2)}) collective-permute-start(bf16[1024,256]{1,0:T(8,128)(2,1)S(1)} %collective-permute-done.11.refs_2_), channel_id=1, source_target_pairs={{0,1},{1,0},{2,3},{3,2},{4,5},{5,4},{6,7},{7,6},{8,9},{9,8},{10,11... | collective-permute-start | bytes 1572872 | tf_op jit(solution)/shard_map/ppermute | solution.py:317
  79.6 5.4 %copy-start.7 = (bf16[1024,256]{1,0:T(8,128)(2,1)}, bf16[1024,256]{1,0:T(8,128)(2,1)S(1)}, u32[]{:S(2)}) copy-start(bf16[1024,256]{1,0:T(8,128)(2,1)S(1)} %collective-permute-done.17.refs_8_) | copy-start | bytes 1572868
  79.6 3.8 %collective-permute-start.18 = (bf16[1024,256]{1,0:T(8,128)(2,1)S(1)}, bf16[1024,256]{1,0:T(8,128)(2,1)S(1)}, u32[]{:S(2)}, u32[]{:S(2)}) collective-permute-start(bf16[1024,256]{1,0:T(8,128)(2,1)S(1)} %collective-permute-done.17.refs_8_), channel_id=1, source_target_pairs={{0,1},{1,0},{2,3},{3,2},{4,5},{5,4},{6,7},{7,6},{8,9},{9,8},{10,11... | collective-permute-start | bytes 1572872 | tf_op jit(solution)/shard_map/ppermute | solution.py:317
  81.7 3.3 %copy-start.8 = (bf16[1024,256]{1,0:T(8,128)(2,1)}, bf16[1024,256]{1,0:T(8,128)(2,1)S(1)}, u32[]{:S(2)}) copy-start(bf16[1024,256]{1,0:T(8,128)(2,1)S(1)} %collective-permute-done.15.refs_6_) | copy-start | bytes 1572868
  81.7 3.3 %collective-permute-start.16 = (bf16[1024,256]{1,0:T(8,128)(2,1)S(1)}, bf16[1024,256]{1,0:T(8,128)(2,1)}, u32[]{:S(2)}, u32[]{:S(2)}) collective-permute-start(bf16[1024,256]{1,0:T(8,128)(2,1)S(1)} %collective-permute-done.15.refs_6_), channel_id=1, source_target_pairs={{0,1},{1,0},{2,3},{3,2},{4,5},{5,4},{6,7},{7,6},{8,9},{9,8},{10,11... | collective-permute-start | bytes 1572872 | tf_op jit(solution)/shard_map/ppermute | solution.py:317
  81.9 1.5 copy-start.9
  81.9 13.3 %collective-permute-start.20 = (bf16[1024,256]{1,0:T(8,128)(2,1)S(1)}, bf16[1024,256]{1,0:T(8,128)(2,1)S(1)}, u32[]{:S(2)}, u32[]{:S(2)}) collective-permute-start(bf16[1024,256]{1,0:T(8,128)(2,1)S(1)} %collective-permute-done.17.refs_8_), channel_id=1, source_target_pairs={{4,0},{8,4},{12,8},{14,12},{10,14},{6,10},{2,6},{0,2},{5,1},{9,5},... | collective-permute-start | bytes 1572872 | tf_op jit(solution)/shard_map/ppermute | solution.py:310
  82.4 0.9 copy-start.10
  82.5 13.2 %collective-permute-start.19 = (bf16[1024,256]{1,0:T(8,128)(2,1)S(1)}, bf16[1024,256]{1,0:T(8,128)(2,1)S(1)}, u32[]{:S(2)}, u32[]{:S(2)}) collective-permute-start(bf16[1024,256]{1,0:T(8,128)(2,1)S(1)} %collective-permute-done.15.refs_6_), channel_id=1, source_target_pairs={{0,4},{4,8},{8,12},{12,14},{14,10},{10,6},{6,2},{2,0},{1,5},{5,9},... | collective-permute-start | bytes 1572872 | tf_op jit(solution)/shard_map/ppermute | solution.py:309
  83.3 0.8 copy-start.11
  84.1 0.8 copy-start.12
  95.1 3.9 %copy-start.3 = (bf16[1024,256]{1,0:T(8,128)(2,1)}, bf16[1024,256]{1,0:T(8,128)(2,1)S(1)}, u32[]{:S(2)}) copy-start(bf16[1024,256]{1,0:T(8,128)(2,1)S(1)} %collective-permute-done.20.refs_2_.refs_12_) | copy-start | bytes 1572868
  95.6 3.5 %copy-start.4 = (bf16[1024,256]{1,0:T(8,128)(2,1)}, bf16[1024,256]{1,0:T(8,128)(2,1)S(1)}, u32[]{:S(2)}) copy-start(bf16[1024,256]{1,0:T(8,128)(2,1)S(1)} %collective-permute-done.19.refs_0_.refs_10_) | copy-start | bytes 1572868
  95.6 2.7 %collective-permute-start.21 = (bf16[1024,256]{1,0:T(8,128)(2,1)S(1)}, bf16[1024,256]{1,0:T(8,128)(2,1)S(1)}, u32[]{:S(2)}, u32[]{:S(2)}) collective-permute-start(bf16[1024,256]{1,0:T(8,128)(2,1)S(1)} %collective-permute-done.19.refs_0_.refs_10_), channel_id=1, source_target_pairs={{0,1},{1,0},{2,3},{3,2},{4,5},{5,4},{6,7},{7,6},{8,9},{9,8},{10,11... | collective-permute-start | bytes 1572872 | tf_op jit(solution)/shard_map/ppermute | solution.py:317
  96.8 2.3 %collective-permute-start.22 = (bf16[1024,256]{1,0:T(8,128)(2,1)S(1)}, bf16[1024,256]{1,0:T(8,128)(2,1)S(1)}, u32[]{:S(2)}, u32[]{:S(2)}) collective-permute-start(bf16[1024,256]{1,0:T(8,128)(2,1)S(1)} %collective-permute-done.20.refs_2_.refs_12_), channel_id=1, source_target_pairs={{0,1},{1,0},{2,3},{3,2},{4,5},{5,4},{6,7},{7,6},{8,9},{9,8},{10,11... | collective-permute-start | bytes 1572872 | tf_op jit(solution)/shard_map/ppermute | solution.py:317
  96.8 11.1 %collective-permute-start.24 = (bf16[512,256]{1,0:T(8,128)(2,1)S(1)}, bf16[512,256]{1,0:T(8,128)(2,1)S(1)}, u32[]{:S(2)}, u32[]{:S(2)}) collective-permute-start(bf16[512,256]{1,0:T(8,128)(2,1)S(1)} %slice.15), channel_id=1, source_target_pairs={{4,0},{8,4},{12,8},{14,12},{10,14},{6,10},{2,6},{0,2},{5,1},{9,5},... | collective-permute-start | bytes 786440 | tf_op jit(solution)/shard_map/ppermute | solution.py:319
  97.7 10.2 %collective-permute-start.23 = (bf16[512,256]{1,0:T(8,128)(2,1)S(1)}, bf16[512,256]{1,0:T(8,128)(2,1)}, u32[]{:S(2)}, u32[]{:S(2)}) collective-permute-start(bf16[512,256]{1,0:T(8,128)(2,1)S(1)} %slice.14), channel_id=1, source_target_pairs={{0,4},{4,8},{8,12},{12,14},{14,10},{10,6},{6,2},{2,0},{1,5},{5,9},... | collective-permute-start | bytes 786440 | tf_op jit(solution)/shard_map/ppermute | solution.py:318
  98.4 0.8 copy-start.13
  99.1 0.8 copy-start.14
  107.9 2.2 %copy-start.15 = (bf16[512,256]{1,0:T(8,128)(2,1)}, bf16[512,256]{1,0:T(8,128)(2,1)S(1)}, u32[]{:S(2)}) copy-start(bf16[512,256]{1,0:T(8,128)(2,1)S(1)} %collective-permute-done.24.refs_16_.refs_2_) | copy-start | bytes 786436
  108.0 2.0 collective-permute-start.25
  108.6 1.5 collective-permute-start.26
  109.9 0.7 copy-start.16
  110.1 0.7 copy-start.17
  117.5 54.7 %collective-permute-start.27 = (bf16[64,2048]{1,0:T(8,128)(2,1)}, bf16[64,2048]{1,0:T(8,128)(2,1)S(1)}, u32[]{:S(2)}, u32[]{:S(2)}) collective-permute-start(bf16[64,2048]{1,0:T(8,128)(2,1)} %get-tuple-element.59), channel_id=1, source_target_pairs={{0,8},{1,9},{2,10},{3,11},{4,12},{5,13},{6,14},{7,15},{8,0},{9,1},... | collective-permute-start | bytes 786440 | tf_op jit(solution)/shard_map/ppermute | solution.py:343
  119.0 53.2 %collective-permute-start.28 = (bf16[64,2048]{1,0:T(8,128)(2,1)}, bf16[64,2048]{1,0:T(8,128)(2,1)S(1)}, u32[]{:S(2)}, u32[]{:S(2)}) collective-permute-start(bf16[64,2048]{1,0:T(8,128)(2,1)} %get-tuple-element.61), channel_id=1, source_target_pairs={{0,9},{1,10},{2,11},{3,8},{4,13},{5,14},{6,15},{7,12},{8,1},{9,2},... | collective-permute-start | bytes 786440 | tf_op jit(solution)/shard_map/ppermute | solution.py:343
  121.0 51.2 %collective-permute-start.29 = (bf16[64,2048]{1,0:T(8,128)(2,1)}, bf16[64,2048]{1,0:T(8,128)(2,1)S(1)}, u32[]{:S(2)}, u32[]{:S(2)}) collective-permute-start(bf16[64,2048]{1,0:T(8,128)(2,1)} %get-tuple-element.63), channel_id=1, source_target_pairs={{0,10},{1,11},{2,8},{3,9},{4,14},{5,15},{6,12},{7,13},{8,2},{9,3},... | collective-permute-start | bytes 786440 | tf_op jit(solution)/shard_map/ppermute | solution.py:343
  122.8 49.3 %collective-permute-start.30 = (bf16[64,2048]{1,0:T(8,128)(2,1)}, bf16[64,2048]{1,0:T(8,128)(2,1)S(1)}, u32[]{:S(2)}, u32[]{:S(2)}) collective-permute-start(bf16[64,2048]{1,0:T(8,128)(2,1)} %get-tuple-element.65), channel_id=1, source_target_pairs={{0,11},{1,8},{2,9},{3,10},{4,15},{5,12},{6,13},{7,14},{8,3},{9,0},... | collective-permute-start | bytes 786440 | tf_op jit(solution)/shard_map/ppermute | solution.py:343
  144.8 3.4 %copy-start.1 = (bf16[768,2048]{1,0:T(8,128)(2,1)S(1)}, bf16[768,2048]{1,0:T(8,128)(2,1)}, u32[]{:S(2)}) copy-start(bf16[768,2048]{1,0:T(8,128)(2,1)} %shard_map.39) | copy-start | bytes 9437188
  149.8 26.5 %collective-permute-start.31 = (bf16[64,2048]{1,0:T(8,128)(2,1)}, bf16[64,2048]{1,0:T(8,128)(2,1)S(1)}, u32[]{:S(2)}, u32[]{:S(2)}) collective-permute-start(bf16[64,2048]{1,0:T(8,128)(2,1)} %get-tuple-element.88), channel_id=1, source_target_pairs={{0,4},{1,5},{2,6},{3,7},{4,8},{5,9},{6,10},{7,11},{8,12},{9,13},{1... | collective-permute-start | bytes 786440 | tf_op jit(solution)/shard_map/ppermute | solution.py:343
  172.2 14.0 %collective-permute-start.32 = (bf16[64,2048]{1,0:T(8,128)(2,1)}, bf16[64,2048]{1,0:T(8,128)(2,1)S(1)}, u32[]{:S(2)}, u32[]{:S(2)}) collective-permute-start(bf16[64,2048]{1,0:T(8,128)(2,1)} %get-tuple-element.68), channel_id=1, source_target_pairs={{0,12},{1,13},{2,14},{3,15},{4,0},{5,1},{6,2},{7,3},{8,4},{9,5},{1... | collective-permute-start | bytes 786440 | tf_op jit(solution)/shard_map/ppermute | solution.py:343
  172.2 14.0 %collective-permute-start.33 = (bf16[64,2048]{1,0:T(8,128)(2,1)}, bf16[64,2048]{1,0:T(8,128)(2,1)S(1)}, u32[]{:S(2)}, u32[]{:S(2)}) collective-permute-start(bf16[64,2048]{1,0:T(8,128)(2,1)} %get-tuple-element.70), channel_id=1, source_target_pairs={{0,5},{1,6},{2,7},{3,4},{4,9},{5,10},{6,11},{7,8},{8,13},{9,14},{1... | collective-permute-start | bytes 786440 | tf_op jit(solution)/shard_map/ppermute | solution.py:343
  173.7 23.7 %collective-permute-start.34 = (bf16[64,2048]{1,0:T(8,128)(2,1)}, bf16[64,2048]{1,0:T(8,128)(2,1)S(1)}, u32[]{:S(2)}, u32[]{:S(2)}) collective-permute-start(bf16[64,2048]{1,0:T(8,128)(2,1)} %get-tuple-element.72), channel_id=1, source_target_pairs={{0,13},{1,14},{2,15},{3,12},{4,1},{5,2},{6,3},{7,0},{8,5},{9,6},{1... | collective-permute-start | bytes 786440 | tf_op jit(solution)/shard_map/ppermute | solution.py:343
  176.2 21.3 %collective-permute-start.35 = (bf16[64,2048]{1,0:T(8,128)(2,1)}, bf16[64,2048]{1,0:T(8,128)(2,1)S(1)}, u32[]{:S(2)}, u32[]{:S(2)}) collective-permute-start(bf16[64,2048]{1,0:T(8,128)(2,1)} %get-tuple-element.74), channel_id=1, source_target_pairs={{0,1},{1,2},{2,3},{3,0},{4,5},{5,6},{6,7},{7,4},{8,9},{9,10},{10,1... | collective-permute-start | bytes 786440 | tf_op jit(solution)/shard_map/ppermute | solution.py:343
  176.4 25.1 %collective-permute-start.36 = (bf16[64,2048]{1,0:T(8,128)(2,1)}, bf16[64,2048]{1,0:T(8,128)(2,1)S(1)}, u32[]{:S(2)}, u32[]{:S(2)}) collective-permute-start(bf16[64,2048]{1,0:T(8,128)(2,1)} %get-tuple-element.76), channel_id=1, source_target_pairs={{0,6},{1,7},{2,4},{3,5},{4,10},{5,11},{6,8},{7,9},{8,14},{9,15},{1... | collective-permute-start | bytes 786440 | tf_op jit(solution)/shard_map/ppermute | solution.py:343
  186.2 19.9 %collective-permute-start.37 = (bf16[64,2048]{1,0:T(8,128)(2,1)}, bf16[64,2048]{1,0:T(8,128)(2,1)S(1)}, u32[]{:S(2)}, u32[]{:S(2)}) collective-permute-start(bf16[64,2048]{1,0:T(8,128)(2,1)} %get-tuple-element.78), channel_id=1, source_target_pairs={{0,14},{1,15},{2,12},{3,13},{4,2},{5,3},{6,0},{7,1},{8,6},{9,7},{1... | collective-permute-start | bytes 786440 | tf_op jit(solution)/shard_map/ppermute | solution.py:343
  186.2 24.8 %collective-permute-start.38 = (bf16[64,2048]{1,0:T(8,128)(2,1)}, bf16[64,2048]{1,0:T(8,128)(2,1)S(1)}, u32[]{:S(2)}, u32[]{:S(2)}) collective-permute-start(bf16[64,2048]{1,0:T(8,128)(2,1)} %get-tuple-element.79), channel_id=1, source_target_pairs={{0,2},{1,3},{2,0},{3,1},{4,6},{5,7},{6,4},{7,5},{8,10},{9,11},{10,... | collective-permute-start | bytes 786440 | tf_op jit(solution)/shard_map/ppermute | solution.py:343
  197.4 14.3 %collective-permute-start.39 = (bf16[64,2048]{1,0:T(8,128)(2,1)}, bf16[64,2048]{1,0:T(8,128)(2,1)S(1)}, u32[]{:S(2)}, u32[]{:S(2)}) collective-permute-start(bf16[64,2048]{1,0:T(8,128)(2,1)} %get-tuple-element.80), channel_id=1, source_target_pairs={{0,7},{1,4},{2,5},{3,6},{4,11},{5,8},{6,9},{7,10},{8,15},{9,12},{1... | collective-permute-start | bytes 786440 | tf_op jit(solution)/shard_map/ppermute | solution.py:343
  197.4 17.1 %collective-permute-start.40 = (bf16[64,2048]{1,0:T(8,128)(2,1)}, bf16[64,2048]{1,0:T(8,128)(2,1)S(1)}, u32[]{:S(2)}, u32[]{:S(2)}) collective-permute-start(bf16[64,2048]{1,0:T(8,128)(2,1)} %get-tuple-element.81), channel_id=1, source_target_pairs={{0,15},{1,12},{2,13},{3,14},{4,3},{5,0},{6,1},{7,2},{8,7},{9,4},{1... | collective-permute-start | bytes 786440 | tf_op jit(solution)/shard_map/ppermute | solution.py:343
  201.5 14.2 %collective-permute-start.41 = (bf16[64,2048]{1,0:T(8,128)(2,1)}, bf16[64,2048]{1,0:T(8,128)(2,1)S(1)}, u32[]{:S(2)}, u32[]{:S(2)}) collective-permute-start(bf16[64,2048]{1,0:T(8,128)(2,1)} %get-tuple-element.82), channel_id=1, source_target_pairs={{0,3},{1,0},{2,1},{3,2},{4,7},{5,4},{6,5},{7,6},{8,11},{9,8},{10,9... | collective-permute-start | bytes 786440 | tf_op jit(solution)/shard_map/ppermute | solution.py:343

commit v5 on v4

--- a/solution.py
+++ b/solution.py
@@ -292,16 +292,18 @@
     bottom = lax.ppermute(backward[count // 2 :], "rows", back)
     keep = jnp.zeros((total, half), jnp.float32)
     give = jnp.zeros((total, half), jnp.float32)
-    for owner, block in blocks:
+    for owner, block in blocks[:-2]:
         a, b = product(block)
         keep = lax.dynamic_update_slice(keep, a, (owner * count, 0))
         give = lax.dynamic_update_slice(give, b, (owner * count, 0))
     mine = (keep + lax.ppermute(give, "feat", swap)).astype(jnp.bfloat16)
     top, bottom, mine = lax.optimization_barrier((top, bottom, mine))
-    a, b = product(jnp.concatenate([top, bottom]))
-    mine = lax.dynamic_update_slice(
-        mine, (a + lax.ppermute(b, "feat", swap)).astype(jnp.bfloat16), (before(n // 2) * count, 0)
-    )
+    late = [product(block) for _, block in blocks[-2:]] + [product(jnp.concatenate([top, bottom]))]
+    here = jnp.concatenate([a for a, _ in late])
+    there = lax.ppermute(jnp.concatenate([b for _, b in late]), "feat", swap)
+    late = (here + there).astype(jnp.bfloat16)
+    for k, owner in enumerate([owner for owner, _ in blocks[-2:]] + [before(n // 2)]):
+        mine = lax.dynamic_update_slice(mine, late[k * count : (k + 1) * count], (owner * count, 0))
 
     near = [mine, lax.ppermute(mine, "feat", swap)]
     forward = backward = mine
@@ -327,7 +329,7 @@
     scores = jnp.zeros((owned, devices * columns), jnp.bfloat16)
     order = [(0, turn) for turn in range(group)]
     for turn in range(group):
-        order += [(number, turn) for number in range(1, groups)]
+        order += [(number, turn) for number in (groups - 1, *range(1, groups - 1))]
     going, sources = [], []
     for number, turn in order:
         shift = shifts[number]

time: 217 us -> 215 us (level)
  waiting for transfers between devices: 103 us -> 93.3 us
  starting transfers between devices: 41.5 us -> 47.8 us
    ppermute x15, waiting for transfers between devices: 44.1 us -> 39.3 us  [per_device(): going.append(lax.ppermute(block, ('rows', 'feat'), pairs))]
    ppermute x15, starting transfers between devices: 17.5 us -> 21.3 us  [per_device(): going.append(lax.ppermute(block, ('rows', 'feat'), pairs))]
    ppermute x1, starting transfers between devices: 1.19 us -> 4.52 us  [per_device(): there = lax.ppermute(jnp.concatenate([b for _, b in late]), 'feat', swap)]
    ppermute x1, waiting for transfers between devices: 5.54 us -> 2.36 us  [per_device(): top = lax.ppermute(forward[:count // 2], 'rows', ahead)]
    ppermute x6, waiting for transfers between devices: 28.4 us -> 26.1 us  [per_device(): forward = lax.ppermute(forward, 'rows', ahead)]
  transfers between devices with their start and end apart: 42 -> 42, of which waited for: 20 -> 19; matrix products, arithmetic and copies ran while one was open for 9% -> 9% of each run, Pallas kernels for 18% -> 19%
where the time goes in v5:
time: 215 us; the launch traced here: 214 us
  waiting for transfers between devices  93.3 us (43%)
  starting transfers between devices  47.8 us (22%)
  Pallas kernels  46.2 us (21%)
  local copies, waits for them, and re-layouts  20.1 us (9%)
  matrix products  4.61 us (2%)
    ppermute x15, waiting for transfers between devices, per_device(): going.append(lax.ppermute(block, ('rows', 'feat'), pairs))  39.3 us
    ppermute x6, waiting for transfers between devices, per_device(): forward = lax.ppermute(forward, 'rows', ahead)  26.1 us
    pallas_call x3, Pallas kernels, group_part(): pl.pallas_call(functools.partial(some_columns, count, base, group_at, las...  24.8 us
    pallas_call x1, Pallas kernels, group_scores(): pl.pallas_call(functools.partial(tile_rows, owners, skip, tuple(range(tar...  21.4 us
    ppermute x15, starting transfers between devices, per_device(): going.append(lax.ppermute(block, ('rows', 'feat'), pairs))  21.3 us
    ppermute x6, waiting for transfers between devices, per_device(): backward = lax.ppermute(backward, 'rows', back)  20.3 us
    dynamic_update_slice x15, local copies, waits for them, and re-layouts, per_device(): scores = lax.dynamic_update_slice(scores, block, (0, source * columns))  10.8 us
    ppermute x6, starting transfers between devices, per_device(): forward = lax.ppermute(forward, 'rows', ahead)  6.95 us
  transfers between devices with their start and end apart: 42, of which 19 were waited for; matrix products, arithmetic and copies ran while one was open for 9% of the time, Pallas kernels for 19%

profile of v5, /device:TPU:1, one launch (start us, length us, event | category | flops | bytes accessed | tf_op | source)
XLA Modules:
  0.0 213.7 jit_solution(5760924743052871307)
XLA Ops:
  0.0 2.1 collective-permute-start
  2.8 1.5 fusion.6
  4.5 9.5 %collective-permute-done = bf16[128,2048]{1,0:T(8,128)(2,1)S(1)} collective-permute-done((bf16[128,2048]{1,0:T(8,128)(2,1)}, bf16[128,2048]{1,0:T(8,128)(2,1)S(1)}, u32[]{:S(2)}, u32[]{:S(2)}) %collective-permute-start) | collective-permute-done | bytes 524320 | tf_op jit(solution)/shard_map/ppermute | solution.py:286
  13.9 1.2 collective-permute-start.1
  16.4 9.7 %collective-permute-done.1 = bf16[128,2048]{1,0:T(8,128)(2,1)S(1)} collective-permute-done((bf16[128,2048]{1,0:T(8,128)(2,1)S(1)}, bf16[128,2048]{1,0:T(8,128)(2,1)S(1)}, u32[]{:S(2)}, u32[]{:S(2)}) %collective-permute-start.1) | collective-permute-done | bytes 524320 | tf_op jit(solution)/shard_map/ppermute | solution.py:286
  26.1 0.9 collective-permute-start.2
  28.6 2.8 %collective-permute-start.8 = (f32[1024,256]{1,0:T(8,128)S(1)}, f32[1024,256]{1,0:T(8,128)S(1)}, u32[]{:S(2)}, u32[]{:S(2)}) collective-permute-start(f32[1024,256]{1,0:T(8,128)S(1)} %get-tuple-element.101), channel_id=1, source_target_pairs={{0,1},{1,0},{2,3},{3,2},{4,5},{5,4},{6,7},{7,6},{8,9},{9,8},{10,11... | collective-permute-start | bytes 3145736 | tf_op jit(solution)/shard_map/ppermute | solution.py:299
  31.4 6.0 %collective-permute-done.2 = bf16[128,2048]{1,0:T(8,128)(2,1)S(1)} collective-permute-done((bf16[128,2048]{1,0:T(8,128)(2,1)S(1)}, bf16[128,2048]{1,0:T(8,128)(2,1)S(1)}, u32[]{:S(2)}, u32[]{:S(2)}) %collective-permute-start.2) | collective-permute-done | bytes 524320 | tf_op jit(solution)/shard_map/ppermute | solution.py:286
  38.2 1.0 collective-permute-start.7
  40.3 2.4 %collective-permute-done.3 = bf16[64,2048]{1,0:T(8,128)(2,1)S(1)} collective-permute-done((bf16[64,2048]{1,0:T(8,128)(2,1)S(1)}, bf16[64,2048]{1,0:T(8,128)(2,1)S(1)}, u32[]{:S(2)}, u32[]{:S(2)}) %collective-permute-start.3) | collective-permute-done | bytes 262176 | tf_op jit(solution)/shard_map/ppermute | solution.py:291
  42.7 1.6 collective-permute-done.7
  44.8 4.5 %collective-permute-start.9 = (f32[384,256]{1,0:T(8,128)S(1)}, f32[384,256]{1,0:T(8,128)}, u32[]{:S(2)}, u32[]{:S(2)}) collective-permute-start(f32[384,256]{1,0:T(8,128)S(1)} %pad_maximum_fusion), channel_id=1, source_target_pairs={{0,1},{1,0},{2,3},{3,2},{4,5},{5,4},{6,7},{7,6},{8,9},{9,8},{10,11... | collective-permute-start | bytes 1179656 | tf_op jit(solution)/shard_map/ppermute | solution.py:303
  49.3 1.5 collective-permute-done.9
  50.8 1.0 fusion.4
  52.2 1.2 collective-permute-start.11
  53.4 11.7 %collective-permute-done.13.refs_4_ = bf16[1024,256]{1,0:T(8,128)(2,1)S(1)} collective-permute-done((bf16[1024,256]{1,0:T(8,128)(2,1)S(1)}, bf16[1024,256]{1,0:T(8,128)(2,1)S(1)}, u32[]{:S(2)}, u32[]{:S(2)}) %collective-permute-start.13) | collective-permute-done | bytes 524320 | tf_op jit(solution)/shard_map/ppermute | solution.py:312
  65.4 1.2 collective-permute-start.15
  66.6 1.8 collective-permute-start.10
  68.8 8.5 %collective-permute-done.17.refs_8_ = bf16[1024,256]{1,0:T(8,128)(2,1)S(1)} collective-permute-done((bf16[1024,256]{1,0:T(8,128)(2,1)S(1)}, bf16[1024,256]{1,0:T(8,128)(2,1)S(1)}, u32[]{:S(2)}, u32[]{:S(2)}) %collective-permute-start.17) | collective-permute-done | bytes 524320 | tf_op jit(solution)/shard_map/ppermute | solution.py:312
  77.3 2.1 collective-permute-start.18
  79.7 1.1 collective-permute-start.20
  82.0 0.8 copy-done.12
  82.9 10.1 %shard_map.37 = (f32[256,2048]{1,0:T(8,128)}, f32[256,128]{1,0:T(8,128)}) custom-call(s32[21]{0:T(128)} %stack.87.where, bf16[1024,256]{1,0:T(8,128)(2,1)} %copy-done.2, bf16[1024,256]{1,0:T(8,128)(2,1)} %copy-done.9, bf16[1024,256]{1,0:T(8,128)(2,1)} %copy-done.6, bf16[1024,256]{1,0:T(8,128)(2,1)} %copy-done.11, bf16[1024,256]{1,0:T(8,128)(2,1)} %copy-done.5, ...), custom_call_target="tpu_custom_call" | custom-call | flops 2684354560 | bytes 10485760 | tf_op jit(solution)/shard_map/pallas_call | solution.py:209
  93.0 1.0 collective-permute-done.19.refs_0_.refs_10_
  94.0 1.2 collective-permute-start.21
  95.3 1.4 collective-permute-start.24
  97.6 0.7 copy-done.14
  98.3 8.0 %shard_map.38 = (f32[256,2048]{1,0:T(8,128)}, f32[256,128]{1,0:T(8,128)}) custom-call(s32[21]{0:T(128)} %stack.87.where, bf16[1024,256]{1,0:T(8,128)(2,1)} %copy-done.4, bf16[1024,256]{1,0:T(8,128)(2,1)} %copy-done.13, bf16[1024,256]{1,0:T(8,128)(2,1)} %copy-done.3, bf16[1024,256]{1,0:T(8,128)(2,1)} %copy-done.14, bf16[2048,4096]{1,0:T(8,128)(2,1)} %refs_4_.3, ...), custom_call_target="tpu_custom_call" | custom-call | flops 1073741824 | bytes 4194304 | tf_op jit(solution)/shard_map/pallas_call | solution.py:209
  107.0 1.3 collective-permute-done.25.refs_15_.refs_1_
  109.2 6.6 %shard_map.40 = (bf16[64,2048]{1,0:T(8,128)(2,1)}, bf16[64,2048]{1,0:T(8,128)(2,1)}, bf16[64,2048]{1,0:T(8,128)(2,1)}, bf16[64,2048]{1,0:T(8,128)(2,1)}) custom-call(s32[21]{0:T(128)} %stack.87.where, bf16[512,256]{1,0:T(8,128)(2,1)} %collective-permute-done.23.refs_14_.refs_0_, bf16[512,256]{1,0:T(8,128)(2,1)} %copy-done.16, bf16[512,256]{1,0:T(8,128)(2,1)} %copy-done.15, ...), custom_call_target="tpu_custom_call" | custom-call | flops 536870912 | bytes 2097152 | tf_op jit(solution)/shard_map/pallas_call | solution.py:209
  115.9 0.9 collective-permute-start.27
  116.8 3.1 %collective-permute-start.28 = (bf16[64,2048]{1,0:T(8,128)(2,1)}, bf16[64,2048]{1,0:T(8,128)(2,1)S(1)}, u32[]{:S(2)}, u32[]{:S(2)}) collective-permute-start(bf16[64,2048]{1,0:T(8,128)(2,1)} %get-tuple-element.61), channel_id=1, source_target_pairs={{0,9},{1,10},{2,11},{3,8},{4,13},{5,14},{6,15},{7,12},{8,1},{9,2},... | collective-permute-start | bytes 786440 | tf_op jit(solution)/shard_map/ppermute | solution.py:345
  120.6 1.7 collective-permute-start.30
  122.2 21.4 %shard_map.39 = bf16[768,2048]{1,0:T(8,128)(2,1)} custom-call(s32[21]{0:T(128)} %stack.87.where, bf16[1024,256]{1,0:T(8,128)(2,1)} %copy-done.2, bf16[1024,256]{1,0:T(8,128)(2,1)} %copy-done.9, bf16[1024,256]{1,0:T(8,128)(2,1)} %copy-done.6, bf16[1024,256]{1,0:T(8,128)(2,1)} %copy-done.11, bf16[1024,256]{1,0:T(8,128)(2,1)} %copy-done.5, ...), custom_call_target="tpu_custom_call" | custom-call | flops 12884901888 | bytes 16777216 | tf_op jit(solution)/shard_map/pallas_call | solution.py:226
  143.7 2.4 %broadcast_in_dim.3 = bf16[64,32768]{1,0:T(8,128)(2,1)} broadcast(bf16[]{:T(256)} %constant.260.clone.1), dimensions={} | broadcast | bytes 4194306 | tf_op jit(solution)/shard_map/broadcast_in_dim | solution.py:329
  146.1 1.0 copy-done.1
  147.0 1.7 constant_dynamic-slice_fusion
  148.7 1.3 collective-permute-start.31
  150.0 21.0 %collective-permute-done.30 = bf16[64,2048]{1,0:T(8,128)(2,1)S(1)} collective-permute-done((bf16[64,2048]{1,0:T(8,128)(2,1)}, bf16[64,2048]{1,0:T(8,128)(2,1)S(1)}, u32[]{:S(2)}, u32[]{:S(2)}) %collective-permute-start.30) | collective-permute-done | bytes 262176 | tf_op jit(solution)/shard_map/ppermute | solution.py:345
  171.2 1.6 collective-permute-start.34
  172.8 2.5 %collective-permute-start.35 = (bf16[64,2048]{1,0:T(8,128)(2,1)}, bf16[64,2048]{1,0:T(8,128)(2,1)S(1)}, u32[]{:S(2)}, u32[]{:S(2)}) collective-permute-start(bf16[64,2048]{1,0:T(8,128)(2,1)} %get-tuple-element.74), channel_id=1, source_target_pairs={{0,13},{1,14},{2,15},{3,12},{4,1},{5,2},{6,3},{7,0},{8,5},{9,6},{1... | collective-permute-start | bytes 786440 | tf_op jit(solution)/shard_map/ppermute | solution.py:345
  176.0 0.7 constant_dynamic-update-slice_fusion.8
  176.7 0.7 constant_dynamic-update-slice_fusion.7
  177.4 0.7 constant_dynamic-update-slice_fusion.6
  178.1 0.7 constant_dynamic-update-slice_fusion.5
  178.8 0.7 constant_dynamic-update-slice_fusion.4
  179.6 5.7 %collective-permute-done.32 = bf16[64,2048]{1,0:T(8,128)(2,1)S(1)} collective-permute-done((bf16[64,2048]{1,0:T(8,128)(2,1)}, bf16[64,2048]{1,0:T(8,128)(2,1)S(1)}, u32[]{:S(2)}, u32[]{:S(2)}) %collective-permute-start.32) | collective-permute-done | bytes 262176 | tf_op jit(solution)/shard_map/ppermute | solution.py:345
  185.3 4.2 %collective-permute-start.38 = (bf16[64,2048]{1,0:T(8,128)(2,1)}, bf16[64,2048]{1,0:T(8,128)(2,1)S(1)}, u32[]{:S(2)}, u32[]{:S(2)}) collective-permute-start(bf16[64,2048]{1,0:T(8,128)(2,1)} %get-tuple-element.79), channel_id=1, source_target_pairs={{0,14},{1,15},{2,12},{3,13},{4,2},{5,3},{6,0},{7,1},{8,6},{9,7},{1... | collective-permute-start | bytes 786440 | tf_op jit(solution)/shard_map/ppermute | solution.py:345
  189.4 1.0 collective-permute-start.39
  190.4 5.8 %collective-permute-done.35 = bf16[64,2048]{1,0:T(8,128)(2,1)S(1)} collective-permute-done((bf16[64,2048]{1,0:T(8,128)(2,1)}, bf16[64,2048]{1,0:T(8,128)(2,1)S(1)}, u32[]{:S(2)}, u32[]{:S(2)}) %collective-permute-start.35) | collective-permute-done | bytes 262176 | tf_op jit(solution)/shard_map/ppermute | solution.py:345
  196.2 3.6 %collective-permute-start.41 = (bf16[64,2048]{1,0:T(8,128)(2,1)}, bf16[64,2048]{1,0:T(8,128)(2,1)S(1)}, u32[]{:S(2)}, u32[]{:S(2)}) collective-permute-start(bf16[64,2048]{1,0:T(8,128)(2,1)} %get-tuple-element.82), channel_id=1, source_target_pairs={{0,15},{1,12},{2,13},{3,14},{4,3},{5,0},{6,1},{7,2},{8,7},{9,4},{1... | collective-permute-start | bytes 786440 | tf_op jit(solution)/shard_map/ppermute | solution.py:345
  199.8 0.7 constant_dynamic-update-slice_fusion.3
  200.5 0.7 constant_dynamic-update-slice_fusion.2
  201.2 0.7 constant_dynamic-update-slice_fusion.1
  201.9 0.7 constant_dynamic-update-slice_fusion
  202.6 0.7 constant_dynamic-update-slice_fusion.14
  203.4 0.7 constant_dynamic-update-slice_fusion.13
  204.1 0.7 constant_dynamic-update-slice_fusion.12
  204.8 1.6 collective-permute-done.39
  206.4 0.7 constant_dynamic-update-slice_fusion.11
  207.1 1.7 collective-permute-done.40
  208.8 0.7 constant_dynamic-update-slice_fusion.10
  209.5 3.5 %collective-permute-done.41 = bf16[64,2048]{1,0:T(8,128)(2,1)S(1)} collective-permute-done((bf16[64,2048]{1,0:T(8,128)(2,1)}, bf16[64,2048]{1,0:T(8,128)(2,1)S(1)}, u32[]{:S(2)}, u32[]{:S(2)}) %collective-permute-start.41) | collective-permute-done | bytes 262176 | tf_op jit(solution)/shard_map/ppermute | solution.py:345
  213.0 0.7 constant_dynamic-update-slice_fusion.9
  (107 shorter events, 12.7 us)
Async XLA Ops:
  0.0 2.8 %copy-start = (bf16[2048,512]{1,0:T(8,128)(2,1)S(1)}, bf16[2048,512]{1,0:T(8,128)(2,1)}, u32[]{:S(2)}) copy-start(bf16[2048,512]{1,0:T(8,128)(2,1)} %param.4) | copy-start | bytes 6291460
  0.0 13.9 %collective-permute-start = (bf16[128,2048]{1,0:T(8,128)(2,1)}, bf16[128,2048]{1,0:T(8,128)(2,1)S(1)}, u32[]{:S(2)}, u32[]{:S(2)}) collective-permute-start(bf16[128,2048]{1,0:T(8,128)(2,1)} %param.3), channel_id=1, source_target_pairs={{0,4},{4,8},{8,12},{12,14},{14,10},{10,6},{6,2},{2,0},{1,5},{5,9},... | collective-permute-start | bytes 1572872 | tf_op jit(solution)/shard_map/ppermute | solution.py:286
  2.1 13.5 %collective-permute-start.4 = (bf16[128,2048]{1,0:T(8,128)(2,1)}, bf16[128,2048]{1,0:T(8,128)(2,1)S(1)}, u32[]{:S(2)}, u32[]{:S(2)}) collective-permute-start(bf16[128,2048]{1,0:T(8,128)(2,1)} %param.3), channel_id=1, source_target_pairs={{4,0},{8,4},{12,8},{14,12},{10,14},{6,10},{2,6},{0,2},{5,1},{9,5},... | collective-permute-start | bytes 1572872 | tf_op jit(solution)/shard_map/ppermute | solution.py:287
  13.9 12.2 %collective-permute-start.1 = (bf16[128,2048]{1,0:T(8,128)(2,1)S(1)}, bf16[128,2048]{1,0:T(8,128)(2,1)S(1)}, u32[]{:S(2)}, u32[]{:S(2)}) collective-permute-start(bf16[128,2048]{1,0:T(8,128)(2,1)S(1)} %collective-permute-done), channel_id=1, source_target_pairs={{0,4},{4,8},{8,12},{12,14},{14,10},{10,6},{6,2},{2,0},{1,5},{5,9},... | collective-permute-start | bytes 1572872 | tf_op jit(solution)/shard_map/ppermute | solution.py:286
  15.6 11.9 %collective-permute-start.5 = (bf16[128,2048]{1,0:T(8,128)(2,1)S(1)}, bf16[128,2048]{1,0:T(8,128)(2,1)S(1)}, u32[]{:S(2)}, u32[]{:S(2)}) collective-permute-start(bf16[128,2048]{1,0:T(8,128)(2,1)S(1)} %collective-permute-done.4), channel_id=1, source_target_pairs={{4,0},{8,4},{12,8},{14,12},{10,14},{6,10},{2,6},{0,2},{5,1},{9,5},... | collective-permute-start | bytes 1572872 | tf_op jit(solution)/shard_map/ppermute | solution.py:287
  26.1 11.3 %collective-permute-start.2 = (bf16[128,2048]{1,0:T(8,128)(2,1)S(1)}, bf16[128,2048]{1,0:T(8,128)(2,1)S(1)}, u32[]{:S(2)}, u32[]{:S(2)}) collective-permute-start(bf16[128,2048]{1,0:T(8,128)(2,1)S(1)} %collective-permute-done.1), channel_id=1, source_target_pairs={{0,4},{4,8},{8,12},{12,14},{14,10},{10,6},{6,2},{2,0},{1,5},{5,9},... | collective-permute-start | bytes 1572872 | tf_op jit(solution)/shard_map/ppermute | solution.py:286
  27.5 10.7 %collective-permute-start.6 = (bf16[128,2048]{1,0:T(8,128)(2,1)S(1)}, bf16[128,2048]{1,0:T(8,128)(2,1)S(1)}, u32[]{:S(2)}, u32[]{:S(2)}) collective-permute-start(bf16[128,2048]{1,0:T(8,128)(2,1)S(1)} %collective-permute-done.5), channel_id=1, source_target_pairs={{4,0},{8,4},{12,8},{14,12},{10,14},{6,10},{2,6},{0,2},{5,1},{9,5},... | collective-permute-start | bytes 1572872 | tf_op jit(solution)/shard_map/ppermute | solution.py:287
  28.6 11.5 %collective-permute-start.8 = (f32[1024,256]{1,0:T(8,128)S(1)}, f32[1024,256]{1,0:T(8,128)S(1)}, u32[]{:S(2)}, u32[]{:S(2)}) collective-permute-start(f32[1024,256]{1,0:T(8,128)S(1)} %get-tuple-element.101), channel_id=1, source_target_pairs={{0,1},{1,0},{2,3},{3,2},{4,5},{5,4},{6,7},{7,6},{8,9},{9,8},{10,11... | collective-permute-start | bytes 3145736 | tf_op jit(solution)/shard_map/ppermute | solution.py:299
  37.4 5.3 %collective-permute-start.3 = (bf16[64,2048]{1,0:T(8,128)(2,1)S(1)}, bf16[64,2048]{1,0:T(8,128)(2,1)S(1)}, u32[]{:S(2)}, u32[]{:S(2)}) collective-permute-start(bf16[64,2048]{1,0:T(8,128)(2,1)S(1)} %slice.28), channel_id=1, source_target_pairs={{0,4},{4,8},{8,12},{12,14},{14,10},{10,6},{6,2},{2,0},{1,5},{5,9},... | collective-permute-start | bytes 786440 | tf_op jit(solution)/shard_map/ppermute | solution.py:291
  38.2 6.1 %collective-permute-start.7 = (bf16[64,2048]{1,0:T(8,128)(2,1)S(1)}, bf16[64,2048]{1,0:T(8,128)(2,1)S(1)}, u32[]{:S(2)}, u32[]{:S(2)}) collective-permute-start(bf16[64,2048]{1,0:T(8,128)(2,1)S(1)} %slice.29), channel_id=1, source_target_pairs={{4,0},{8,4},{12,8},{14,12},{10,14},{6,10},{2,6},{0,2},{5,1},{9,5},... | collective-permute-start | bytes 786440 | tf_op jit(solution)/shard_map/ppermute | solution.py:292
  44.8 6.0 %collective-permute-start.9 = (f32[384,256]{1,0:T(8,128)S(1)}, f32[384,256]{1,0:T(8,128)}, u32[]{:S(2)}, u32[]{:S(2)}) collective-permute-start(f32[384,256]{1,0:T(8,128)S(1)} %pad_maximum_fusion), channel_id=1, source_target_pairs={{0,1},{1,0},{2,3},{3,2},{4,5},{5,4},{6,7},{7,6},{8,9},{9,8},{10,11... | collective-permute-start | bytes 1179656 | tf_op jit(solution)/shard_map/ppermute | solution.py:303
  51.9 30.9 %copy-start.2 = (bf16[1024,256]{1,0:T(8,128)(2,1)}, bf16[1024,256]{1,0:T(8,128)(2,1)S(1)}, u32[]{:S(2)}) copy-start(bf16[1024,256]{1,0:T(8,128)(2,1)S(1)} %slice_dynamic-update-slice_fusion.refs_0_) | copy-start | bytes 1572868
  51.9 13.2 %collective-permute-start.13 = (bf16[1024,256]{1,0:T(8,128)(2,1)S(1)}, bf16[1024,256]{1,0:T(8,128)(2,1)S(1)}, u32[]{:S(2)}, u32[]{:S(2)}) collective-permute-start(bf16[1024,256]{1,0:T(8,128)(2,1)S(1)} %slice_dynamic-update-slice_fusion.refs_0_), channel_id=1, source_target_pairs={{4,0},{8,4},{12,8},{14,12},{10,14},{6,10},{2,6},{0,2},{5,1},{9,5},... | collective-permute-start | bytes 1572872 | tf_op jit(solution)/shard_map/ppermute | solution.py:312
  52.2 13.1 %collective-permute-start.11 = (bf16[1024,256]{1,0:T(8,128)(2,1)S(1)}, bf16[1024,256]{1,0:T(8,128)(2,1)S(1)}, u32[]{:S(2)}, u32[]{:S(2)}) collective-permute-start(bf16[1024,256]{1,0:T(8,128)(2,1)S(1)} %slice_dynamic-update-slice_fusion.refs_0_), channel_id=1, source_target_pairs={{0,4},{4,8},{8,12},{12,14},{14,10},{10,6},{6,2},{2,0},{1,5},{5,9},... | collective-permute-start | bytes 1572872 | tf_op jit(solution)/shard_map/ppermute | solution.py:311
  65.1 17.7 %copy-start.5 = (bf16[1024,256]{1,0:T(8,128)(2,1)}, bf16[1024,256]{1,0:T(8,128)(2,1)S(1)}, u32[]{:S(2)}) copy-start(bf16[1024,256]{1,0:T(8,128)(2,1)S(1)} %collective-permute-done.13.refs_4_) | copy-start | bytes 1572868
  65.1 12.2 %collective-permute-start.17 = (bf16[1024,256]{1,0:T(8,128)(2,1)S(1)}, bf16[1024,256]{1,0:T(8,128)(2,1)S(1)}, u32[]{:S(2)}, u32[]{:S(2)}) collective-permute-start(bf16[1024,256]{1,0:T(8,128)(2,1)S(1)} %collective-permute-done.13.refs_4_), channel_id=1, source_target_pairs={{4,0},{8,4},{12,8},{14,12},{10,14},{6,10},{2,6},{0,2},{5,1},{9,5},... | collective-permute-start | bytes 1572872 | tf_op jit(solution)/shard_map/ppermute | solution.py:312
  65.4 17.5 %copy-start.6 = (bf16[1024,256]{1,0:T(8,128)(2,1)}, bf16[1024,256]{1,0:T(8,128)(2,1)S(1)}, u32[]{:S(2)}) copy-start(bf16[1024,256]{1,0:T(8,128)(2,1)S(1)} %collective-permute-done.11.refs_2_) | copy-start | bytes 1572868
  65.4 14.1 %collective-permute-start.15 = (bf16[1024,256]{1,0:T(8,128)(2,1)S(1)}, bf16[1024,256]{1,0:T(8,128)(2,1)S(1)}, u32[]{:S(2)}, u32[]{:S(2)}) collective-permute-start(bf16[1024,256]{1,0:T(8,128)(2,1)S(1)} %collective-permute-done.11.refs_2_), channel_id=1, source_target_pairs={{0,4},{4,8},{8,12},{12,14},{14,10},{10,6},{6,2},{2,0},{1,5},{5,9},... | collective-permute-start | bytes 1572872 | tf_op jit(solution)/shard_map/ppermute | solution.py:311
  66.6 13.1 %collective-permute-start.10 = (bf16[1024,256]{1,0:T(8,128)(2,1)S(1)}, bf16[1024,256]{1,0:T(8,128)(2,1)S(1)}, u32[]{:S(2)}, u32[]{:S(2)}) collective-permute-start(bf16[1024,256]{1,0:T(8,128)(2,1)S(1)} %slice_dynamic-update-slice_fusion.refs_0_), channel_id=1, source_target_pairs={{0,1},{1,0},{2,3},{3,2},{4,5},{5,4},{6,7},{7,6},{8,9},{9,8},{10,11... | collective-permute-start | bytes 1572872 | tf_op jit(solution)/shard_map/ppermute | solution.py:308
  68.3 12.5 %collective-permute-start.14 = (bf16[1024,256]{1,0:T(8,128)(2,1)S(1)}, bf16[1024,256]{1,0:T(8,128)(2,1)S(1)}, u32[]{:S(2)}, u32[]{:S(2)}) collective-permute-start(bf16[1024,256]{1,0:T(8,128)(2,1)S(1)} %collective-permute-done.13.refs_4_), channel_id=1, source_target_pairs={{0,1},{1,0},{2,3},{3,2},{4,5},{5,4},{6,7},{7,6},{8,9},{9,8},{10,11... | collective-permute-start | bytes 1572872 | tf_op jit(solution)/shard_map/ppermute | solution.py:319
  68.3 12.9 %collective-permute-start.12 = (bf16[1024,256]{1,0:T(8,128)(2,1)S(1)}, bf16[1024,256]{1,0:T(8,128)(2,1)S(1)}, u32[]{:S(2)}, u32[]{:S(2)}) collective-permute-start(bf16[1024,256]{1,0:T(8,128)(2,1)S(1)} %collective-permute-done.11.refs_2_), channel_id=1, source_target_pairs={{0,1},{1,0},{2,3},{3,2},{4,5},{5,4},{6,7},{7,6},{8,9},{9,8},{10,11... | collective-permute-start | bytes 1572872 | tf_op jit(solution)/shard_map/ppermute | solution.py:319
  77.3 5.5 %copy-start.7 = (bf16[1024,256]{1,0:T(8,128)(2,1)}, bf16[1024,256]{1,0:T(8,128)(2,1)S(1)}, u32[]{:S(2)}) copy-start(bf16[1024,256]{1,0:T(8,128)(2,1)S(1)} %collective-permute-done.17.refs_8_) | copy-start | bytes 1572868
  77.3 3.9 %collective-permute-start.18 = (bf16[1024,256]{1,0:T(8,128)(2,1)S(1)}, bf16[1024,256]{1,0:T(8,128)(2,1)S(1)}, u32[]{:S(2)}, u32[]{:S(2)}) collective-permute-start(bf16[1024,256]{1,0:T(8,128)(2,1)S(1)} %collective-permute-done.17.refs_8_), channel_id=1, source_target_pairs={{0,1},{1,0},{2,3},{3,2},{4,5},{5,4},{6,7},{7,6},{8,9},{9,8},{10,11... | collective-permute-start | bytes 1572872 | tf_op jit(solution)/shard_map/ppermute | solution.py:319
  79.4 3.4 %copy-start.8 = (bf16[1024,256]{1,0:T(8,128)(2,1)}, bf16[1024,256]{1,0:T(8,128)(2,1)S(1)}, u32[]{:S(2)}) copy-start(bf16[1024,256]{1,0:T(8,128)(2,1)S(1)} %collective-permute-done.15.refs_6_) | copy-start | bytes 1572868
  79.4 3.4 %collective-permute-start.16 = (bf16[1024,256]{1,0:T(8,128)(2,1)S(1)}, bf16[1024,256]{1,0:T(8,128)(2,1)}, u32[]{:S(2)}, u32[]{:S(2)}) collective-permute-start(bf16[1024,256]{1,0:T(8,128)(2,1)S(1)} %collective-permute-done.15.refs_6_), channel_id=1, source_target_pairs={{0,1},{1,0},{2,3},{3,2},{4,5},{5,4},{6,7},{7,6},{8,9},{9,8},{10,11... | collective-permute-start | bytes 1572872 | tf_op jit(solution)/shard_map/ppermute | solution.py:319
  79.7 1.5 copy-start.9
  79.7 13.3 %collective-permute-start.20 = (bf16[1024,256]{1,0:T(8,128)(2,1)S(1)}, bf16[1024,256]{1,0:T(8,128)(2,1)S(1)}, u32[]{:S(2)}, u32[]{:S(2)}) collective-permute-start(bf16[1024,256]{1,0:T(8,128)(2,1)S(1)} %collective-permute-done.17.refs_8_), channel_id=1, source_target_pairs={{4,0},{8,4},{12,8},{14,12},{10,14},{6,10},{2,6},{0,2},{5,1},{9,5},... | collective-permute-start | bytes 1572872 | tf_op jit(solution)/shard_map/ppermute | solution.py:312
  80.9 0.8 copy-start.10
  80.9 13.2 %collective-permute-start.19 = (bf16[1024,256]{1,0:T(8,128)(2,1)S(1)}, bf16[1024,256]{1,0:T(8,128)(2,1)S(1)}, u32[]{:S(2)}, u32[]{:S(2)}) collective-permute-start(bf16[1024,256]{1,0:T(8,128)(2,1)S(1)} %collective-permute-done.15.refs_6_), channel_id=1, source_target_pairs={{0,4},{4,8},{8,12},{12,14},{14,10},{10,6},{6,2},{2,0},{1,5},{5,9},... | collective-permute-start | bytes 1572872 | tf_op jit(solution)/shard_map/ppermute | solution.py:311
  81.2 0.8 copy-start.11
  82.0 0.8 copy-start.12
  93.0 4.5 %copy-start.3 = (bf16[1024,256]{1,0:T(8,128)(2,1)}, bf16[1024,256]{1,0:T(8,128)(2,1)S(1)}, u32[]{:S(2)}) copy-start(bf16[1024,256]{1,0:T(8,128)(2,1)S(1)} %collective-permute-done.20.refs_2_.refs_12_) | copy-start | bytes 1572868
  94.0 3.5 %copy-start.4 = (bf16[1024,256]{1,0:T(8,128)(2,1)}, bf16[1024,256]{1,0:T(8,128)(2,1)S(1)}, u32[]{:S(2)}) copy-start(bf16[1024,256]{1,0:T(8,128)(2,1)S(1)} %collective-permute-done.19.refs_0_.refs_10_) | copy-start | bytes 1572868
  94.0 2.7 %collective-permute-start.21 = (bf16[1024,256]{1,0:T(8,128)(2,1)S(1)}, bf16[1024,256]{1,0:T(8,128)(2,1)S(1)}, u32[]{:S(2)}, u32[]{:S(2)}) collective-permute-start(bf16[1024,256]{1,0:T(8,128)(2,1)S(1)} %collective-permute-done.19.refs_0_.refs_10_), channel_id=1, source_target_pairs={{0,1},{1,0},{2,3},{3,2},{4,5},{5,4},{6,7},{7,6},{8,9},{9,8},{10,11... | collective-permute-start | bytes 1572872 | tf_op jit(solution)/shard_map/ppermute | solution.py:319
  95.2 2.3 %collective-permute-start.22 = (bf16[1024,256]{1,0:T(8,128)(2,1)S(1)}, bf16[1024,256]{1,0:T(8,128)(2,1)S(1)}, u32[]{:S(2)}, u32[]{:S(2)}) collective-permute-start(bf16[1024,256]{1,0:T(8,128)(2,1)S(1)} %collective-permute-done.20.refs_2_.refs_12_), channel_id=1, source_target_pairs={{0,1},{1,0},{2,3},{3,2},{4,5},{5,4},{6,7},{7,6},{8,9},{9,8},{10,11... | collective-permute-start | bytes 1572872 | tf_op jit(solution)/shard_map/ppermute | solution.py:319
  95.3 11.1 %collective-permute-start.24 = (bf16[512,256]{1,0:T(8,128)(2,1)S(1)}, bf16[512,256]{1,0:T(8,128)(2,1)S(1)}, u32[]{:S(2)}, u32[]{:S(2)}) collective-permute-start(bf16[512,256]{1,0:T(8,128)(2,1)S(1)} %slice.27), channel_id=1, source_target_pairs={{4,0},{8,4},{12,8},{14,12},{10,14},{6,10},{2,6},{0,2},{5,1},{9,5},... | collective-permute-start | bytes 786440 | tf_op jit(solution)/shard_map/ppermute | solution.py:321
  96.6 9.7 %collective-permute-start.23 = (bf16[512,256]{1,0:T(8,128)(2,1)S(1)}, bf16[512,256]{1,0:T(8,128)(2,1)}, u32[]{:S(2)}, u32[]{:S(2)}) collective-permute-start(bf16[512,256]{1,0:T(8,128)(2,1)S(1)} %slice.26), channel_id=1, source_target_pairs={{0,4},{4,8},{8,12},{12,14},{14,10},{10,6},{6,2},{2,0},{1,5},{5,9},... | collective-permute-start | bytes 786440 | tf_op jit(solution)/shard_map/ppermute | solution.py:320
  96.8 0.8 copy-start.13
  97.5 0.8 copy-start.14
  106.3 2.2 %copy-start.15 = (bf16[512,256]{1,0:T(8,128)(2,1)}, bf16[512,256]{1,0:T(8,128)(2,1)S(1)}, u32[]{:S(2)}) copy-start(bf16[512,256]{1,0:T(8,128)(2,1)S(1)} %collective-permute-done.24.refs_16_.refs_2_) | copy-start | bytes 786436
  106.4 2.0 collective-permute-start.25
  107.0 1.5 collective-permute-start.26
  108.3 0.7 copy-start.16
  108.5 0.7 copy-start.17
  115.9 55.2 %collective-permute-start.27 = (bf16[64,2048]{1,0:T(8,128)(2,1)}, bf16[64,2048]{1,0:T(8,128)(2,1)S(1)}, u32[]{:S(2)}, u32[]{:S(2)}) collective-permute-start(bf16[64,2048]{1,0:T(8,128)(2,1)} %get-tuple-element.59), channel_id=1, source_target_pairs={{0,8},{1,9},{2,10},{3,11},{4,12},{5,13},{6,14},{7,15},{8,0},{9,1},... | collective-permute-start | bytes 786440 | tf_op jit(solution)/shard_map/ppermute | solution.py:345
  116.8 54.3 %collective-permute-start.28 = (bf16[64,2048]{1,0:T(8,128)(2,1)}, bf16[64,2048]{1,0:T(8,128)(2,1)S(1)}, u32[]{:S(2)}, u32[]{:S(2)}) collective-permute-start(bf16[64,2048]{1,0:T(8,128)(2,1)} %get-tuple-element.61), channel_id=1, source_target_pairs={{0,9},{1,10},{2,11},{3,8},{4,13},{5,14},{6,15},{7,12},{8,1},{9,2},... | collective-permute-start | bytes 786440 | tf_op jit(solution)/shard_map/ppermute | solution.py:345
  119.9 51.2 %collective-permute-start.29 = (bf16[64,2048]{1,0:T(8,128)(2,1)}, bf16[64,2048]{1,0:T(8,128)(2,1)S(1)}, u32[]{:S(2)}, u32[]{:S(2)}) collective-permute-start(bf16[64,2048]{1,0:T(8,128)(2,1)} %get-tuple-element.63), channel_id=1, source_target_pairs={{0,10},{1,11},{2,8},{3,9},{4,14},{5,15},{6,12},{7,13},{8,2},{9,3},... | collective-permute-start | bytes 786440 | tf_op jit(solution)/shard_map/ppermute | solution.py:345
  120.6 50.5 %collective-permute-start.30 = (bf16[64,2048]{1,0:T(8,128)(2,1)}, bf16[64,2048]{1,0:T(8,128)(2,1)S(1)}, u32[]{:S(2)}, u32[]{:S(2)}) collective-permute-start(bf16[64,2048]{1,0:T(8,128)(2,1)} %get-tuple-element.65), channel_id=1, source_target_pairs={{0,11},{1,8},{2,9},{3,10},{4,15},{5,12},{6,13},{7,14},{8,3},{9,0},... | collective-permute-start | bytes 786440 | tf_op jit(solution)/shard_map/ppermute | solution.py:345
  143.6 3.4 %copy-start.1 = (bf16[768,2048]{1,0:T(8,128)(2,1)S(1)}, bf16[768,2048]{1,0:T(8,128)(2,1)}, u32[]{:S(2)}) copy-start(bf16[768,2048]{1,0:T(8,128)(2,1)} %shard_map.39) | copy-start | bytes 9437188
  148.7 26.6 %collective-permute-start.31 = (bf16[64,2048]{1,0:T(8,128)(2,1)}, bf16[64,2048]{1,0:T(8,128)(2,1)S(1)}, u32[]{:S(2)}, u32[]{:S(2)}) collective-permute-start(bf16[64,2048]{1,0:T(8,128)(2,1)} %get-tuple-element.88), channel_id=1, source_target_pairs={{0,4},{1,5},{2,6},{3,7},{4,8},{5,9},{6,10},{7,11},{8,12},{9,13},{1... | collective-permute-start | bytes 786440 | tf_op jit(solution)/shard_map/ppermute | solution.py:345
  171.0 14.2 %collective-permute-start.32 = (bf16[64,2048]{1,0:T(8,128)(2,1)}, bf16[64,2048]{1,0:T(8,128)(2,1)S(1)}, u32[]{:S(2)}, u32[]{:S(2)}) collective-permute-start(bf16[64,2048]{1,0:T(8,128)(2,1)} %get-tuple-element.68), channel_id=1, source_target_pairs={{0,12},{1,13},{2,14},{3,15},{4,0},{5,1},{6,2},{7,3},{8,4},{9,5},{1... | collective-permute-start | bytes 786440 | tf_op jit(solution)/shard_map/ppermute | solution.py:345
  171.1 14.1 %collective-permute-start.33 = (bf16[64,2048]{1,0:T(8,128)(2,1)}, bf16[64,2048]{1,0:T(8,128)(2,1)S(1)}, u32[]{:S(2)}, u32[]{:S(2)}) collective-permute-start(bf16[64,2048]{1,0:T(8,128)(2,1)} %get-tuple-element.70), channel_id=1, source_target_pairs={{0,1},{1,2},{2,3},{3,0},{4,5},{5,6},{6,7},{7,4},{8,9},{9,10},{10,1... | collective-permute-start | bytes 786440 | tf_op jit(solution)/shard_map/ppermute | solution.py:345
  171.2 18.2 %collective-permute-start.34 = (bf16[64,2048]{1,0:T(8,128)(2,1)}, bf16[64,2048]{1,0:T(8,128)(2,1)S(1)}, u32[]{:S(2)}, u32[]{:S(2)}) collective-permute-start(bf16[64,2048]{1,0:T(8,128)(2,1)} %get-tuple-element.72), channel_id=1, source_target_pairs={{0,5},{1,6},{2,7},{3,4},{4,9},{5,10},{6,11},{7,8},{8,13},{9,14},{1... | collective-permute-start | bytes 786440 | tf_op jit(solution)/shard_map/ppermute | solution.py:345
  172.8 23.4 %collective-permute-start.35 = (bf16[64,2048]{1,0:T(8,128)(2,1)}, bf16[64,2048]{1,0:T(8,128)(2,1)S(1)}, u32[]{:S(2)}, u32[]{:S(2)}) collective-permute-start(bf16[64,2048]{1,0:T(8,128)(2,1)} %get-tuple-element.74), channel_id=1, source_target_pairs={{0,13},{1,14},{2,15},{3,12},{4,1},{5,2},{6,3},{7,0},{8,5},{9,6},{1... | collective-permute-start | bytes 786440 | tf_op jit(solution)/shard_map/ppermute | solution.py:345
  175.3 20.9 %collective-permute-start.36 = (bf16[64,2048]{1,0:T(8,128)(2,1)}, bf16[64,2048]{1,0:T(8,128)(2,1)S(1)}, u32[]{:S(2)}, u32[]{:S(2)}) collective-permute-start(bf16[64,2048]{1,0:T(8,128)(2,1)} %get-tuple-element.76), channel_id=1, source_target_pairs={{0,2},{1,3},{2,0},{3,1},{4,6},{5,7},{6,4},{7,5},{8,10},{9,11},{10,... | collective-permute-start | bytes 786440 | tf_op jit(solution)/shard_map/ppermute | solution.py:345
  185.2 18.1 %collective-permute-start.37 = (bf16[64,2048]{1,0:T(8,128)(2,1)}, bf16[64,2048]{1,0:T(8,128)(2,1)S(1)}, u32[]{:S(2)}, u32[]{:S(2)}) collective-permute-start(bf16[64,2048]{1,0:T(8,128)(2,1)} %get-tuple-element.78), channel_id=1, source_target_pairs={{0,6},{1,7},{2,4},{3,5},{4,10},{5,11},{6,8},{7,9},{8,14},{9,15},{1... | collective-permute-start | bytes 786440 | tf_op jit(solution)/shard_map/ppermute | solution.py:345
  185.3 18.8 %collective-permute-start.38 = (bf16[64,2048]{1,0:T(8,128)(2,1)}, bf16[64,2048]{1,0:T(8,128)(2,1)S(1)}, u32[]{:S(2)}, u32[]{:S(2)}) collective-permute-start(bf16[64,2048]{1,0:T(8,128)(2,1)} %get-tuple-element.79), channel_id=1, source_target_pairs={{0,14},{1,15},{2,12},{3,13},{4,2},{5,3},{6,0},{7,1},{8,6},{9,7},{1... | collective-permute-start | bytes 786440 | tf_op jit(solution)/shard_map/ppermute | solution.py:345
  189.4 17.0 %collective-permute-start.39 = (bf16[64,2048]{1,0:T(8,128)(2,1)}, bf16[64,2048]{1,0:T(8,128)(2,1)S(1)}, u32[]{:S(2)}, u32[]{:S(2)}) collective-permute-start(bf16[64,2048]{1,0:T(8,128)(2,1)} %get-tuple-element.80), channel_id=1, source_target_pairs={{0,3},{1,0},{2,1},{3,2},{4,7},{5,4},{6,5},{7,6},{8,11},{9,8},{10,9... | collective-permute-start | bytes 786440 | tf_op jit(solution)/shard_map/ppermute | solution.py:345
  196.2 12.6 %collective-permute-start.40 = (bf16[64,2048]{1,0:T(8,128)(2,1)}, bf16[64,2048]{1,0:T(8,128)(2,1)S(1)}, u32[]{:S(2)}, u32[]{:S(2)}) collective-permute-start(bf16[64,2048]{1,0:T(8,128)(2,1)} %get-tuple-element.81), channel_id=1, source_target_pairs={{0,7},{1,4},{2,5},{3,6},{4,11},{5,8},{6,9},{7,10},{8,15},{9,12},{1... | collective-permute-start | bytes 786440 | tf_op jit(solution)/shard_map/ppermute | solution.py:345
  196.2 16.8 %collective-permute-start.41 = (bf16[64,2048]{1,0:T(8,128)(2,1)}, bf16[64,2048]{1,0:T(8,128)(2,1)S(1)}, u32[]{:S(2)}, u32[]{:S(2)}) collective-permute-start(bf16[64,2048]{1,0:T(8,128)(2,1)} %get-tuple-element.82), channel_id=1, source_target_pairs={{0,15},{1,12},{2,13},{3,14},{4,3},{5,0},{6,1},{7,2},{8,7},{9,4},{1... | collective-permute-start | bytes 786440 | tf_op jit(solution)/shard_map/ppermute | solution.py:345

commit v6 on v5

--- a/solution.py
+++ b/solution.py
@@ -104,11 +104,12 @@
     first = where[group_at] * span
     place = where[where.shape[0] - 1]
 
-    def stream(j, k):
+    def stream(j, pair):
+        columns = pl.ds(pl.multiple_of(where[base + 2 * pair] // 2 * (2 * width), 2 * width), 2 * width)
         return pltpu.make_async_copy(
-            train.at[pl.ds(pl.multiple_of(j * tile, tile), tile), pl.ds(pl.multiple_of(where[base + k] * width, width), width)],
-            held.at[j % 2, :, pl.ds(k * width, width)],
-            train_sems.at[j % 2, k],
+            train.at[pl.ds(pl.multiple_of(j * tile, tile), tile), columns],
+            held.at[j, :, pl.ds(pair * 2 * width, 2 * width)],
+            train_sems.at[j, pair],
         )
 
     def earlier(j):
@@ -119,7 +120,7 @@
         at = start + lax.rem(place + turn, group) * owned
         return pltpu.make_async_copy(
             source.at[pl.ds(pl.multiple_of(at, owned), owned), :],
-            left.at[pl.ds(turn * owned, owned), pl.ds(k * width, width)],
+            left.at[pl.ds(turn * owned, owned), pl.ds(pl.multiple_of(k // 2 * (2 * width) + where[base + k] % 2 * width, width), width)],
             piece_sems.at[k, turn],
         )
 
@@ -128,14 +129,17 @@
             for turn in range(group):
                 lay(piece, start, k, turn).start()
 
+    for pair in range(count // 2):
+        stream(0, pair).start()
     if last:
         upper = near[0].shape[0]
         pl.when(first < upper)(lambda: lay_all(near[:2], first))
         pl.when(first >= upper)(lambda: lay_all(near[2:], first - upper))
     else:
         lay_all(near, first)
-    for k in range(count):
-        stream(0, k).start()
+    for j in range(1, steps):
+        for pair in range(count // 2):
+            stream(j, pair).start()
     if more:
         for j in range(steps):
             earlier(j).start()
@@ -154,18 +158,10 @@
         squares_out[...] = squared
 
     def step(j, carry):
-        @pl.when(j + 1 < steps)
-        def _():
-            for k in range(count):
-                stream(j + 1, k).start()
-
-        for k in range(count):
-            stream(j, k).wait()
+        for pair in range(count // 2):
+            stream(j, pair).wait()
         across = (((1,), (1,)), ((), ()))
-        if last:
-            raw = lax.dot_general(left[...], held[j % 2], across, preferred_element_type=jnp.float32)
-        else:
-            raw = lax.dot_general(held[j % 2], left[...], across, preferred_element_type=jnp.float32).T
+        raw = lax.dot_general(left[...], held[j], across, preferred_element_type=jnp.float32)
         columns = pl.ds(pl.multiple_of(j * tile, tile), tile)
         if more:
             earlier(j).wait()
@@ -192,9 +188,9 @@
     in_specs = [pl.BlockSpec(memory_space=pltpu.SMEM)] + [anywhere] * (len(pieces) + 1)
     scratch = [
         pltpu.VMEM((span, depth), jnp.bfloat16),
-        pltpu.VMEM((2, tile, depth), jnp.bfloat16),
+        pltpu.VMEM((columns // tile, tile, depth), jnp.bfloat16),
         pltpu.SemaphoreType.DMA((count, group)),
-        pltpu.SemaphoreType.DMA((2, count)),
+        pltpu.SemaphoreType.DMA((columns // tile, count // 2)),
     ]
     if earlier:
         in_specs += [anywhere, inside]

time: 215 us -> 212 us (0.986)
  transfers between devices with their start and end apart: 42 -> 42, of which waited for: 19 -> 19; matrix products, arithmetic and copies ran while one was open for 9% -> 9% of each run, Pallas kernels for 19% -> 18%
where the time goes in v6:
time: 212 us; the launch traced here: 211 us
  waiting for transfers between devices  92.9 us (44%)
  starting transfers between devices  47.9 us (23%)
  Pallas kernels  44.3 us (21%)
  local copies, waits for them, and re-layouts  20.1 us (9%)
  matrix products  4.61 us (2%)
    ppermute x15, waiting for transfers between devices, per_device(): going.append(lax.ppermute(block, ('rows', 'feat'), pairs))  39.1 us
    ppermute x6, waiting for transfers between devices, per_device(): forward = lax.ppermute(forward, 'rows', ahead)  25.9 us
    pallas_call x3, Pallas kernels, group_part(): pl.pallas_call(functools.partial(some_columns, count, base, group_at, las...  22.9 us
    ppermute x15, starting transfers between devices, per_device(): going.append(lax.ppermute(block, ('rows', 'feat'), pairs))  21.4 us
    pallas_call x1, Pallas kernels, group_scores(): pl.pallas_call(functools.partial(tile_rows, owners, skip, tuple(range(tar...  21.4 us
    ppermute x6, waiting for transfers between devices, per_device(): backward = lax.ppermute(backward, 'rows', back)  20.3 us
    dynamic_update_slice x15, local copies, waits for them, and re-layouts, per_device(): scores = lax.dynamic_update_slice(scores, block, (0, source * columns))  10.8 us
    ppermute x6, starting transfers between devices, per_device(): forward = lax.ppermute(forward, 'rows', ahead)  6.95 us
  transfers between devices with their start and end apart: 42, of which 19 were waited for; matrix products, arithmetic and copies ran while one was open for 9% of the time, Pallas kernels for 18%

profile of v6, /device:TPU:1, one launch (start us, length us, event | category | flops | bytes accessed | tf_op | source)
XLA Modules:
  0.0 211.5 jit_solution(7413637436053407917)
XLA Ops:
  0.0 2.1 %collective-permute-start = (bf16[128,2048]{1,0:T(8,128)(2,1)}, bf16[128,2048]{1,0:T(8,128)(2,1)S(1)}, u32[]{:S(2)}, u32[]{:S(2)}) collective-permute-start(bf16[128,2048]{1,0:T(8,128)(2,1)} %param.3), channel_id=1, source_target_pairs={{0,4},{4,8},{8,12},{12,14},{14,10},{10,6},{6,2},{2,0},{1,5},{5,9},... | collective-permute-start | bytes 1572872 | tf_op jit(solution)/shard_map/ppermute | solution.py:282
  2.8 1.5 fusion.6
  4.5 9.5 %collective-permute-done = bf16[128,2048]{1,0:T(8,128)(2,1)S(1)} collective-permute-done((bf16[128,2048]{1,0:T(8,128)(2,1)}, bf16[128,2048]{1,0:T(8,128)(2,1)S(1)}, u32[]{:S(2)}, u32[]{:S(2)}) %collective-permute-start) | collective-permute-done | bytes 524320 | tf_op jit(solution)/shard_map/ppermute | solution.py:282
  13.9 1.2 collective-permute-start.1
  16.4 9.7 %collective-permute-done.1 = bf16[128,2048]{1,0:T(8,128)(2,1)S(1)} collective-permute-done((bf16[128,2048]{1,0:T(8,128)(2,1)S(1)}, bf16[128,2048]{1,0:T(8,128)(2,1)S(1)}, u32[]{:S(2)}, u32[]{:S(2)}) %collective-permute-start.1) | collective-permute-done | bytes 524320 | tf_op jit(solution)/shard_map/ppermute | solution.py:282
  26.1 0.9 collective-permute-start.2
  28.6 2.8 %collective-permute-start.8 = (f32[1024,256]{1,0:T(8,128)S(1)}, f32[1024,256]{1,0:T(8,128)S(1)}, u32[]{:S(2)}, u32[]{:S(2)}) collective-permute-start(f32[1024,256]{1,0:T(8,128)S(1)} %get-tuple-element.101), channel_id=1, source_target_pairs={{0,1},{1,0},{2,3},{3,2},{4,5},{5,4},{6,7},{7,6},{8,9},{9,8},{10,11... | collective-permute-start | bytes 3145736 | tf_op jit(solution)/shard_map/ppermute | solution.py:295
  31.4 6.0 %collective-permute-done.2 = bf16[128,2048]{1,0:T(8,128)(2,1)S(1)} collective-permute-done((bf16[128,2048]{1,0:T(8,128)(2,1)S(1)}, bf16[128,2048]{1,0:T(8,128)(2,1)S(1)}, u32[]{:S(2)}, u32[]{:S(2)}) %collective-permute-start.2) | collective-permute-done | bytes 524320 | tf_op jit(solution)/shard_map/ppermute | solution.py:282
  38.2 1.0 collective-permute-start.7
  40.3 2.4 %collective-permute-done.3 = bf16[64,2048]{1,0:T(8,128)(2,1)S(1)} collective-permute-done((bf16[64,2048]{1,0:T(8,128)(2,1)S(1)}, bf16[64,2048]{1,0:T(8,128)(2,1)S(1)}, u32[]{:S(2)}, u32[]{:S(2)}) %collective-permute-start.3) | collective-permute-done | bytes 262176 | tf_op jit(solution)/shard_map/ppermute | solution.py:287
  42.7 1.6 collective-permute-done.7
  44.8 4.5 %collective-permute-start.9 = (f32[384,256]{1,0:T(8,128)S(1)}, f32[384,256]{1,0:T(8,128)}, u32[]{:S(2)}, u32[]{:S(2)}) collective-permute-start(f32[384,256]{1,0:T(8,128)S(1)} %pad_maximum_fusion), channel_id=1, source_target_pairs={{0,1},{1,0},{2,3},{3,2},{4,5},{5,4},{6,7},{7,6},{8,9},{9,8},{10,11... | collective-permute-start | bytes 1179656 | tf_op jit(solution)/shard_map/ppermute | solution.py:299
  49.3 1.5 collective-permute-done.9
  50.8 1.0 fusion.4
  52.2 1.2 collective-permute-start.11
  53.4 11.7 %collective-permute-done.13.refs_4_ = bf16[1024,256]{1,0:T(8,128)(2,1)S(1)} collective-permute-done((bf16[1024,256]{1,0:T(8,128)(2,1)S(1)}, bf16[1024,256]{1,0:T(8,128)(2,1)S(1)}, u32[]{:S(2)}, u32[]{:S(2)}) %collective-permute-start.13) | collective-permute-done | bytes 524320 | tf_op jit(solution)/shard_map/ppermute | solution.py:308
  65.4 1.2 collective-permute-start.15
  66.6 1.8 collective-permute-start.10
  68.8 8.5 %collective-permute-done.17.refs_8_ = bf16[1024,256]{1,0:T(8,128)(2,1)S(1)} collective-permute-done((bf16[1024,256]{1,0:T(8,128)(2,1)S(1)}, bf16[1024,256]{1,0:T(8,128)(2,1)S(1)}, u32[]{:S(2)}, u32[]{:S(2)}) %collective-permute-start.17) | collective-permute-done | bytes 524320 | tf_op jit(solution)/shard_map/ppermute | solution.py:308
  77.3 2.1 %collective-permute-start.18 = (bf16[1024,256]{1,0:T(8,128)(2,1)S(1)}, bf16[1024,256]{1,0:T(8,128)(2,1)S(1)}, u32[]{:S(2)}, u32[]{:S(2)}) collective-permute-start(bf16[1024,256]{1,0:T(8,128)(2,1)S(1)} %collective-permute-done.17.refs_8_), channel_id=1, source_target_pairs={{0,1},{1,0},{2,3},{3,2},{4,5},{5,4},{6,7},{7,6},{8,9},{9,8},{10,11... | collective-permute-start | bytes 1572872 | tf_op jit(solution)/shard_map/ppermute | solution.py:315
  79.7 1.1 collective-permute-start.20
  82.0 0.8 copy-done.12
  82.9 10.4 %shard_map.37 = (f32[256,2048]{1,0:T(8,128)}, f32[256,128]{1,0:T(8,128)}) custom-call(s32[21]{0:T(128)} %stack.87.where, bf16[1024,256]{1,0:T(8,128)(2,1)} %copy-done.2, bf16[1024,256]{1,0:T(8,128)(2,1)} %copy-done.9, bf16[1024,256]{1,0:T(8,128)(2,1)} %copy-done.6, bf16[1024,256]{1,0:T(8,128)(2,1)} %copy-done.11, bf16[1024,256]{1,0:T(8,128)(2,1)} %copy-done.5, ...), custom_call_target="tpu_custom_call" | custom-call | flops 2684354560 | bytes 10485760 | tf_op jit(solution)/shard_map/pallas_call | solution.py:205
  93.3 0.7 collective-permute-done.19.refs_0_.refs_10_
  94.0 1.2 collective-permute-start.21
  95.3 1.4 collective-permute-start.24
  97.6 0.7 copy-done.14
  98.3 7.3 %shard_map.38 = (f32[256,2048]{1,0:T(8,128)}, f32[256,128]{1,0:T(8,128)}) custom-call(s32[21]{0:T(128)} %stack.87.where, bf16[1024,256]{1,0:T(8,128)(2,1)} %copy-done.4, bf16[1024,256]{1,0:T(8,128)(2,1)} %copy-done.13, bf16[1024,256]{1,0:T(8,128)(2,1)} %copy-done.3, bf16[1024,256]{1,0:T(8,128)(2,1)} %copy-done.14, bf16[2048,4096]{1,0:T(8,128)(2,1)} %refs_4_.3, ...), custom_call_target="tpu_custom_call" | custom-call | flops 1073741824 | bytes 4194304 | tf_op jit(solution)/shard_map/pallas_call | solution.py:205
  106.3 1.3 collective-permute-done.25.refs_15_.refs_1_
  108.5 5.1 %shard_map.40 = (bf16[64,2048]{1,0:T(8,128)(2,1)}, bf16[64,2048]{1,0:T(8,128)(2,1)}, bf16[64,2048]{1,0:T(8,128)(2,1)}, bf16[64,2048]{1,0:T(8,128)(2,1)}) custom-call(s32[21]{0:T(128)} %stack.87.where, bf16[512,256]{1,0:T(8,128)(2,1)} %collective-permute-done.23.refs_14_.refs_0_, bf16[512,256]{1,0:T(8,128)(2,1)} %copy-done.16, bf16[512,256]{1,0:T(8,128)(2,1)} %copy-done.15, ...), custom_call_target="tpu_custom_call" | custom-call | flops 536870912 | bytes 2097152 | tf_op jit(solution)/shard_map/pallas_call | solution.py:205
  113.7 1.4 collective-permute-start.27
  115.1 2.6 %collective-permute-start.28 = (bf16[64,2048]{1,0:T(8,128)(2,1)}, bf16[64,2048]{1,0:T(8,128)(2,1)S(1)}, u32[]{:S(2)}, u32[]{:S(2)}) collective-permute-start(bf16[64,2048]{1,0:T(8,128)(2,1)} %get-tuple-element.61), channel_id=1, source_target_pairs={{0,9},{1,10},{2,11},{3,8},{4,13},{5,14},{6,15},{7,12},{8,1},{9,2},... | collective-permute-start | bytes 786440 | tf_op jit(solution)/shard_map/ppermute | solution.py:341
  117.6 1.2 collective-permute-start.29
  118.9 1.4 collective-permute-start.30
  120.3 21.4 %shard_map.39 = bf16[768,2048]{1,0:T(8,128)(2,1)} custom-call(s32[21]{0:T(128)} %stack.87.where, bf16[1024,256]{1,0:T(8,128)(2,1)} %copy-done.2, bf16[1024,256]{1,0:T(8,128)(2,1)} %copy-done.9, bf16[1024,256]{1,0:T(8,128)(2,1)} %copy-done.6, bf16[1024,256]{1,0:T(8,128)(2,1)} %copy-done.11, bf16[1024,256]{1,0:T(8,128)(2,1)} %copy-done.5, ...), custom_call_target="tpu_custom_call" | custom-call | flops 12884901888 | bytes 16777216 | tf_op jit(solution)/shard_map/pallas_call | solution.py:222
  141.7 2.4 %broadcast_in_dim.3 = bf16[64,32768]{1,0:T(8,128)(2,1)} broadcast(bf16[]{:T(256)} %constant.260.clone.1), dimensions={} | broadcast | bytes 4194306 | tf_op jit(solution)/shard_map/broadcast_in_dim | solution.py:325
  144.1 1.0 copy-done.1
  145.1 1.7 constant_dynamic-slice_fusion
  146.8 1.1 collective-permute-start.31
  147.8 21.0 %collective-permute-done.30 = bf16[64,2048]{1,0:T(8,128)(2,1)S(1)} collective-permute-done((bf16[64,2048]{1,0:T(8,128)(2,1)}, bf16[64,2048]{1,0:T(8,128)(2,1)S(1)}, u32[]{:S(2)}, u32[]{:S(2)}) %collective-permute-start.30) | collective-permute-done | bytes 262176 | tf_op jit(solution)/shard_map/ppermute | solution.py:341
  169.0 1.6 collective-permute-start.34
  170.6 2.4 %collective-permute-start.35 = (bf16[64,2048]{1,0:T(8,128)(2,1)}, bf16[64,2048]{1,0:T(8,128)(2,1)S(1)}, u32[]{:S(2)}, u32[]{:S(2)}) collective-permute-start(bf16[64,2048]{1,0:T(8,128)(2,1)} %get-tuple-element.74), channel_id=1, source_target_pairs={{0,13},{1,14},{2,15},{3,12},{4,1},{5,2},{6,3},{7,0},{8,5},{9,6},{1... | collective-permute-start | bytes 786440 | tf_op jit(solution)/shard_map/ppermute | solution.py:341
  173.8 0.7 constant_dynamic-update-slice_fusion.8
  174.5 0.7 constant_dynamic-update-slice_fusion.7
  175.2 0.7 constant_dynamic-update-slice_fusion.6
  175.9 0.7 constant_dynamic-update-slice_fusion.5
  176.6 0.7 constant_dynamic-update-slice_fusion.4
  177.4 5.7 %collective-permute-done.32 = bf16[64,2048]{1,0:T(8,128)(2,1)S(1)} collective-permute-done((bf16[64,2048]{1,0:T(8,128)(2,1)}, bf16[64,2048]{1,0:T(8,128)(2,1)S(1)}, u32[]{:S(2)}, u32[]{:S(2)}) %collective-permute-start.32) | collective-permute-done | bytes 262176 | tf_op jit(solution)/shard_map/ppermute | solution.py:341
  183.1 4.2 %collective-permute-start.38 = (bf16[64,2048]{1,0:T(8,128)(2,1)}, bf16[64,2048]{1,0:T(8,128)(2,1)S(1)}, u32[]{:S(2)}, u32[]{:S(2)}) collective-permute-start(bf16[64,2048]{1,0:T(8,128)(2,1)} %get-tuple-element.79), channel_id=1, source_target_pairs={{0,14},{1,15},{2,12},{3,13},{4,2},{5,3},{6,0},{7,1},{8,6},{9,7},{1... | collective-permute-start | bytes 786440 | tf_op jit(solution)/shard_map/ppermute | solution.py:341
  187.2 0.9 collective-permute-start.39
  188.1 5.7 %collective-permute-done.35 = bf16[64,2048]{1,0:T(8,128)(2,1)S(1)} collective-permute-done((bf16[64,2048]{1,0:T(8,128)(2,1)}, bf16[64,2048]{1,0:T(8,128)(2,1)S(1)}, u32[]{:S(2)}, u32[]{:S(2)}) %collective-permute-start.35) | collective-permute-done | bytes 262176 | tf_op jit(solution)/shard_map/ppermute | solution.py:341
  193.8 3.8 %collective-permute-start.41 = (bf16[64,2048]{1,0:T(8,128)(2,1)}, bf16[64,2048]{1,0:T(8,128)(2,1)S(1)}, u32[]{:S(2)}, u32[]{:S(2)}) collective-permute-start(bf16[64,2048]{1,0:T(8,128)(2,1)} %get-tuple-element.82), channel_id=1, source_target_pairs={{0,15},{1,12},{2,13},{3,14},{4,3},{5,0},{6,1},{7,2},{8,7},{9,4},{1... | collective-permute-start | bytes 786440 | tf_op jit(solution)/shard_map/ppermute | solution.py:341
  197.6 0.7 constant_dynamic-update-slice_fusion.3
  198.4 0.7 constant_dynamic-update-slice_fusion.2
  199.1 0.7 constant_dynamic-update-slice_fusion.1
  199.8 0.7 constant_dynamic-update-slice_fusion
  201.2 0.7 constant_dynamic-update-slice_fusion.13
  202.0 0.7 constant_dynamic-update-slice_fusion.12
  202.7 1.5 collective-permute-done.39
  204.2 0.7 constant_dynamic-update-slice_fusion.11
  204.9 1.7 collective-permute-done.40
  206.6 0.7 constant_dynamic-update-slice_fusion.10
  207.3 3.4 %collective-permute-done.41 = bf16[64,2048]{1,0:T(8,128)(2,1)S(1)} collective-permute-done((bf16[64,2048]{1,0:T(8,128)(2,1)}, bf16[64,2048]{1,0:T(8,128)(2,1)S(1)}, u32[]{:S(2)}, u32[]{:S(2)}) %collective-permute-start.41) | collective-permute-done | bytes 262176 | tf_op jit(solution)/shard_map/ppermute | solution.py:341
  210.8 0.7 constant_dynamic-update-slice_fusion.9
  (107 shorter events, 12.8 us)
Async XLA Ops:
  0.0 2.8 %copy-start = (bf16[2048,512]{1,0:T(8,128)(2,1)S(1)}, bf16[2048,512]{1,0:T(8,128)(2,1)}, u32[]{:S(2)}) copy-start(bf16[2048,512]{1,0:T(8,128)(2,1)} %param.4) | copy-start | bytes 6291460
  0.0 13.9 %collective-permute-start = (bf16[128,2048]{1,0:T(8,128)(2,1)}, bf16[128,2048]{1,0:T(8,128)(2,1)S(1)}, u32[]{:S(2)}, u32[]{:S(2)}) collective-permute-start(bf16[128,2048]{1,0:T(8,128)(2,1)} %param.3), channel_id=1, source_target_pairs={{0,4},{4,8},{8,12},{12,14},{14,10},{10,6},{6,2},{2,0},{1,5},{5,9},... | collective-permute-start | bytes 1572872 | tf_op jit(solution)/shard_map/ppermute | solution.py:282
  2.1 13.5 %collective-permute-start.4 = (bf16[128,2048]{1,0:T(8,128)(2,1)}, bf16[128,2048]{1,0:T(8,128)(2,1)S(1)}, u32[]{:S(2)}, u32[]{:S(2)}) collective-permute-start(bf16[128,2048]{1,0:T(8,128)(2,1)} %param.3), channel_id=1, source_target_pairs={{4,0},{8,4},{12,8},{14,12},{10,14},{6,10},{2,6},{0,2},{5,1},{9,5},... | collective-permute-start | bytes 1572872 | tf_op jit(solution)/shard_map/ppermute | solution.py:283
  13.9 12.2 %collective-permute-start.1 = (bf16[128,2048]{1,0:T(8,128)(2,1)S(1)}, bf16[128,2048]{1,0:T(8,128)(2,1)S(1)}, u32[]{:S(2)}, u32[]{:S(2)}) collective-permute-start(bf16[128,2048]{1,0:T(8,128)(2,1)S(1)} %collective-permute-done), channel_id=1, source_target_pairs={{0,4},{4,8},{8,12},{12,14},{14,10},{10,6},{6,2},{2,0},{1,5},{5,9},... | collective-permute-start | bytes 1572872 | tf_op jit(solution)/shard_map/ppermute | solution.py:282
  15.6 11.9 %collective-permute-start.5 = (bf16[128,2048]{1,0:T(8,128)(2,1)S(1)}, bf16[128,2048]{1,0:T(8,128)(2,1)S(1)}, u32[]{:S(2)}, u32[]{:S(2)}) collective-permute-start(bf16[128,2048]{1,0:T(8,128)(2,1)S(1)} %collective-permute-done.4), channel_id=1, source_target_pairs={{4,0},{8,4},{12,8},{14,12},{10,14},{6,10},{2,6},{0,2},{5,1},{9,5},... | collective-permute-start | bytes 1572872 | tf_op jit(solution)/shard_map/ppermute | solution.py:283
  26.1 11.3 %collective-permute-start.2 = (bf16[128,2048]{1,0:T(8,128)(2,1)S(1)}, bf16[128,2048]{1,0:T(8,128)(2,1)S(1)}, u32[]{:S(2)}, u32[]{:S(2)}) collective-permute-start(bf16[128,2048]{1,0:T(8,128)(2,1)S(1)} %collective-permute-done.1), channel_id=1, source_target_pairs={{0,4},{4,8},{8,12},{12,14},{14,10},{10,6},{6,2},{2,0},{1,5},{5,9},... | collective-permute-start | bytes 1572872 | tf_op jit(solution)/shard_map/ppermute | solution.py:282
  27.5 10.7 %collective-permute-start.6 = (bf16[128,2048]{1,0:T(8,128)(2,1)S(1)}, bf16[128,2048]{1,0:T(8,128)(2,1)S(1)}, u32[]{:S(2)}, u32[]{:S(2)}) collective-permute-start(bf16[128,2048]{1,0:T(8,128)(2,1)S(1)} %collective-permute-done.5), channel_id=1, source_target_pairs={{4,0},{8,4},{12,8},{14,12},{10,14},{6,10},{2,6},{0,2},{5,1},{9,5},... | collective-permute-start | bytes 1572872 | tf_op jit(solution)/shard_map/ppermute | solution.py:283
  28.6 11.5 %collective-permute-start.8 = (f32[1024,256]{1,0:T(8,128)S(1)}, f32[1024,256]{1,0:T(8,128)S(1)}, u32[]{:S(2)}, u32[]{:S(2)}) collective-permute-start(f32[1024,256]{1,0:T(8,128)S(1)} %get-tuple-element.101), channel_id=1, source_target_pairs={{0,1},{1,0},{2,3},{3,2},{4,5},{5,4},{6,7},{7,6},{8,9},{9,8},{10,11... | collective-permute-start | bytes 3145736 | tf_op jit(solution)/shard_map/ppermute | solution.py:295
  37.4 5.3 %collective-permute-start.3 = (bf16[64,2048]{1,0:T(8,128)(2,1)S(1)}, bf16[64,2048]{1,0:T(8,128)(2,1)S(1)}, u32[]{:S(2)}, u32[]{:S(2)}) collective-permute-start(bf16[64,2048]{1,0:T(8,128)(2,1)S(1)} %slice.28), channel_id=1, source_target_pairs={{0,4},{4,8},{8,12},{12,14},{14,10},{10,6},{6,2},{2,0},{1,5},{5,9},... | collective-permute-start | bytes 786440 | tf_op jit(solution)/shard_map/ppermute | solution.py:287
  38.2 6.1 %collective-permute-start.7 = (bf16[64,2048]{1,0:T(8,128)(2,1)S(1)}, bf16[64,2048]{1,0:T(8,128)(2,1)S(1)}, u32[]{:S(2)}, u32[]{:S(2)}) collective-permute-start(bf16[64,2048]{1,0:T(8,128)(2,1)S(1)} %slice.29), channel_id=1, source_target_pairs={{4,0},{8,4},{12,8},{14,12},{10,14},{6,10},{2,6},{0,2},{5,1},{9,5},... | collective-permute-start | bytes 786440 | tf_op jit(solution)/shard_map/ppermute | solution.py:288
  44.8 6.0 %collective-permute-start.9 = (f32[384,256]{1,0:T(8,128)S(1)}, f32[384,256]{1,0:T(8,128)}, u32[]{:S(2)}, u32[]{:S(2)}) collective-permute-start(f32[384,256]{1,0:T(8,128)S(1)} %pad_maximum_fusion), channel_id=1, source_target_pairs={{0,1},{1,0},{2,3},{3,2},{4,5},{5,4},{6,7},{7,6},{8,9},{9,8},{10,11... | collective-permute-start | bytes 1179656 | tf_op jit(solution)/shard_map/ppermute | solution.py:299
  51.9 30.9 %copy-start.2 = (bf16[1024,256]{1,0:T(8,128)(2,1)}, bf16[1024,256]{1,0:T(8,128)(2,1)S(1)}, u32[]{:S(2)}) copy-start(bf16[1024,256]{1,0:T(8,128)(2,1)S(1)} %slice_dynamic-update-slice_fusion.refs_0_) | copy-start | bytes 1572868
  51.9 13.2 %collective-permute-start.13 = (bf16[1024,256]{1,0:T(8,128)(2,1)S(1)}, bf16[1024,256]{1,0:T(8,128)(2,1)S(1)}, u32[]{:S(2)}, u32[]{:S(2)}) collective-permute-start(bf16[1024,256]{1,0:T(8,128)(2,1)S(1)} %slice_dynamic-update-slice_fusion.refs_0_), channel_id=1, source_target_pairs={{4,0},{8,4},{12,8},{14,12},{10,14},{6,10},{2,6},{0,2},{5,1},{9,5},... | collective-permute-start | bytes 1572872 | tf_op jit(solution)/shard_map/ppermute | solution.py:308
  52.2 13.1 %collective-permute-start.11 = (bf16[1024,256]{1,0:T(8,128)(2,1)S(1)}, bf16[1024,256]{1,0:T(8,128)(2,1)S(1)}, u32[]{:S(2)}, u32[]{:S(2)}) collective-permute-start(bf16[1024,256]{1,0:T(8,128)(2,1)S(1)} %slice_dynamic-update-slice_fusion.refs_0_), channel_id=1, source_target_pairs={{0,4},{4,8},{8,12},{12,14},{14,10},{10,6},{6,2},{2,0},{1,5},{5,9},... | collective-permute-start | bytes 1572872 | tf_op jit(solution)/shard_map/ppermute | solution.py:307
  65.1 17.7 %copy-start.5 = (bf16[1024,256]{1,0:T(8,128)(2,1)}, bf16[1024,256]{1,0:T(8,128)(2,1)S(1)}, u32[]{:S(2)}) copy-start(bf16[1024,256]{1,0:T(8,128)(2,1)S(1)} %collective-permute-done.13.refs_4_) | copy-start | bytes 1572868
  65.1 12.2 %collective-permute-start.17 = (bf16[1024,256]{1,0:T(8,128)(2,1)S(1)}, bf16[1024,256]{1,0:T(8,128)(2,1)S(1)}, u32[]{:S(2)}, u32[]{:S(2)}) collective-permute-start(bf16[1024,256]{1,0:T(8,128)(2,1)S(1)} %collective-permute-done.13.refs_4_), channel_id=1, source_target_pairs={{4,0},{8,4},{12,8},{14,12},{10,14},{6,10},{2,6},{0,2},{5,1},{9,5},... | collective-permute-start | bytes 1572872 | tf_op jit(solution)/shard_map/ppermute | solution.py:308
  65.4 17.5 %copy-start.6 = (bf16[1024,256]{1,0:T(8,128)(2,1)}, bf16[1024,256]{1,0:T(8,128)(2,1)S(1)}, u32[]{:S(2)}) copy-start(bf16[1024,256]{1,0:T(8,128)(2,1)S(1)} %collective-permute-done.11.refs_2_) | copy-start | bytes 1572868
  65.4 14.1 %collective-permute-start.15 = (bf16[1024,256]{1,0:T(8,128)(2,1)S(1)}, bf16[1024,256]{1,0:T(8,128)(2,1)S(1)}, u32[]{:S(2)}, u32[]{:S(2)}) collective-permute-start(bf16[1024,256]{1,0:T(8,128)(2,1)S(1)} %collective-permute-done.11.refs_2_), channel_id=1, source_target_pairs={{0,4},{4,8},{8,12},{12,14},{14,10},{10,6},{6,2},{2,0},{1,5},{5,9},... | collective-permute-start | bytes 1572872 | tf_op jit(solution)/shard_map/ppermute | solution.py:307
  66.6 13.1 %collective-permute-start.10 = (bf16[1024,256]{1,0:T(8,128)(2,1)S(1)}, bf16[1024,256]{1,0:T(8,128)(2,1)S(1)}, u32[]{:S(2)}, u32[]{:S(2)}) collective-permute-start(bf16[1024,256]{1,0:T(8,128)(2,1)S(1)} %slice_dynamic-update-slice_fusion.refs_0_), channel_id=1, source_target_pairs={{0,1},{1,0},{2,3},{3,2},{4,5},{5,4},{6,7},{7,6},{8,9},{9,8},{10,11... | collective-permute-start | bytes 1572872 | tf_op jit(solution)/shard_map/ppermute | solution.py:304
  68.3 12.5 %collective-permute-start.14 = (bf16[1024,256]{1,0:T(8,128)(2,1)S(1)}, bf16[1024,256]{1,0:T(8,128)(2,1)S(1)}, u32[]{:S(2)}, u32[]{:S(2)}) collective-permute-start(bf16[1024,256]{1,0:T(8,128)(2,1)S(1)} %collective-permute-done.13.refs_4_), channel_id=1, source_target_pairs={{0,1},{1,0},{2,3},{3,2},{4,5},{5,4},{6,7},{7,6},{8,9},{9,8},{10,11... | collective-permute-start | bytes 1572872 | tf_op jit(solution)/shard_map/ppermute | solution.py:315
  68.3 12.9 %collective-permute-start.12 = (bf16[1024,256]{1,0:T(8,128)(2,1)S(1)}, bf16[1024,256]{1,0:T(8,128)(2,1)S(1)}, u32[]{:S(2)}, u32[]{:S(2)}) collective-permute-start(bf16[1024,256]{1,0:T(8,128)(2,1)S(1)} %collective-permute-done.11.refs_2_), channel_id=1, source_target_pairs={{0,1},{1,0},{2,3},{3,2},{4,5},{5,4},{6,7},{7,6},{8,9},{9,8},{10,11... | collective-permute-start | bytes 1572872 | tf_op jit(solution)/shard_map/ppermute | solution.py:315
  77.3 5.5 %copy-start.7 = (bf16[1024,256]{1,0:T(8,128)(2,1)}, bf16[1024,256]{1,0:T(8,128)(2,1)S(1)}, u32[]{:S(2)}) copy-start(bf16[1024,256]{1,0:T(8,128)(2,1)S(1)} %collective-permute-done.17.refs_8_) | copy-start | bytes 1572868
  77.3 3.9 %collective-permute-start.18 = (bf16[1024,256]{1,0:T(8,128)(2,1)S(1)}, bf16[1024,256]{1,0:T(8,128)(2,1)S(1)}, u32[]{:S(2)}, u32[]{:S(2)}) collective-permute-start(bf16[1024,256]{1,0:T(8,128)(2,1)S(1)} %collective-permute-done.17.refs_8_), channel_id=1, source_target_pairs={{0,1},{1,0},{2,3},{3,2},{4,5},{5,4},{6,7},{7,6},{8,9},{9,8},{10,11... | collective-permute-start | bytes 1572872 | tf_op jit(solution)/shard_map/ppermute | solution.py:315
  79.4 3.4 %copy-start.8 = (bf16[1024,256]{1,0:T(8,128)(2,1)}, bf16[1024,256]{1,0:T(8,128)(2,1)S(1)}, u32[]{:S(2)}) copy-start(bf16[1024,256]{1,0:T(8,128)(2,1)S(1)} %collective-permute-done.15.refs_6_) | copy-start | bytes 1572868
  79.4 3.4 %collective-permute-start.16 = (bf16[1024,256]{1,0:T(8,128)(2,1)S(1)}, bf16[1024,256]{1,0:T(8,128)(2,1)}, u32[]{:S(2)}, u32[]{:S(2)}) collective-permute-start(bf16[1024,256]{1,0:T(8,128)(2,1)S(1)} %collective-permute-done.15.refs_6_), channel_id=1, source_target_pairs={{0,1},{1,0},{2,3},{3,2},{4,5},{5,4},{6,7},{7,6},{8,9},{9,8},{10,11... | collective-permute-start | bytes 1572872 | tf_op jit(solution)/shard_map/ppermute | solution.py:315
  79.7 1.5 copy-start.9
  79.7 13.6 %collective-permute-start.20 = (bf16[1024,256]{1,0:T(8,128)(2,1)S(1)}, bf16[1024,256]{1,0:T(8,128)(2,1)S(1)}, u32[]{:S(2)}, u32[]{:S(2)}) collective-permute-start(bf16[1024,256]{1,0:T(8,128)(2,1)S(1)} %collective-permute-done.17.refs_8_), channel_id=1, source_target_pairs={{4,0},{8,4},{12,8},{14,12},{10,14},{6,10},{2,6},{0,2},{5,1},{9,5},... | collective-permute-start | bytes 1572872 | tf_op jit(solution)/shard_map/ppermute | solution.py:308
  80.9 0.8 copy-start.10
  80.9 13.2 %collective-permute-start.19 = (bf16[1024,256]{1,0:T(8,128)(2,1)S(1)}, bf16[1024,256]{1,0:T(8,128)(2,1)S(1)}, u32[]{:S(2)}, u32[]{:S(2)}) collective-permute-start(bf16[1024,256]{1,0:T(8,128)(2,1)S(1)} %collective-permute-done.15.refs_6_), channel_id=1, source_target_pairs={{0,4},{4,8},{8,12},{12,14},{14,10},{10,6},{6,2},{2,0},{1,5},{5,9},... | collective-permute-start | bytes 1572872 | tf_op jit(solution)/shard_map/ppermute | solution.py:307
  81.2 0.8 copy-start.11
  82.0 0.8 copy-start.12
  93.3 4.2 %copy-start.3 = (bf16[1024,256]{1,0:T(8,128)(2,1)}, bf16[1024,256]{1,0:T(8,128)(2,1)S(1)}, u32[]{:S(2)}) copy-start(bf16[1024,256]{1,0:T(8,128)(2,1)S(1)} %collective-permute-done.20.refs_2_.refs_12_) | copy-start | bytes 1572868
  94.0 3.5 %copy-start.4 = (bf16[1024,256]{1,0:T(8,128)(2,1)}, bf16[1024,256]{1,0:T(8,128)(2,1)S(1)}, u32[]{:S(2)}) copy-start(bf16[1024,256]{1,0:T(8,128)(2,1)S(1)} %collective-permute-done.19.refs_0_.refs_10_) | copy-start | bytes 1572868
  94.0 2.7 %collective-permute-start.21 = (bf16[1024,256]{1,0:T(8,128)(2,1)S(1)}, bf16[1024,256]{1,0:T(8,128)(2,1)S(1)}, u32[]{:S(2)}, u32[]{:S(2)}) collective-permute-start(bf16[1024,256]{1,0:T(8,128)(2,1)S(1)} %collective-permute-done.19.refs_0_.refs_10_), channel_id=1, source_target_pairs={{0,1},{1,0},{2,3},{3,2},{4,5},{5,4},{6,7},{7,6},{8,9},{9,8},{10,11... | collective-permute-start | bytes 1572872 | tf_op jit(solution)/shard_map/ppermute | solution.py:315
  95.2 2.3 %collective-permute-start.22 = (bf16[1024,256]{1,0:T(8,128)(2,1)S(1)}, bf16[1024,256]{1,0:T(8,128)(2,1)S(1)}, u32[]{:S(2)}, u32[]{:S(2)}) collective-permute-start(bf16[1024,256]{1,0:T(8,128)(2,1)S(1)} %collective-permute-done.20.refs_2_.refs_12_), channel_id=1, source_target_pairs={{0,1},{1,0},{2,3},{3,2},{4,5},{5,4},{6,7},{7,6},{8,9},{9,8},{10,11... | collective-permute-start | bytes 1572872 | tf_op jit(solution)/shard_map/ppermute | solution.py:315
  95.3 10.4 %collective-permute-start.24 = (bf16[512,256]{1,0:T(8,128)(2,1)S(1)}, bf16[512,256]{1,0:T(8,128)(2,1)S(1)}, u32[]{:S(2)}, u32[]{:S(2)}) collective-permute-start(bf16[512,256]{1,0:T(8,128)(2,1)S(1)} %slice.27), channel_id=1, source_target_pairs={{4,0},{8,4},{12,8},{14,12},{10,14},{6,10},{2,6},{0,2},{5,1},{9,5},... | collective-permute-start | bytes 786440 | tf_op jit(solution)/shard_map/ppermute | solution.py:317
  96.6 9.0 %collective-permute-start.23 = (bf16[512,256]{1,0:T(8,128)(2,1)S(1)}, bf16[512,256]{1,0:T(8,128)(2,1)}, u32[]{:S(2)}, u32[]{:S(2)}) collective-permute-start(bf16[512,256]{1,0:T(8,128)(2,1)S(1)} %slice.26), channel_id=1, source_target_pairs={{0,4},{4,8},{8,12},{12,14},{14,10},{10,6},{6,2},{2,0},{1,5},{5,9},... | collective-permute-start | bytes 786440 | tf_op jit(solution)/shard_map/ppermute | solution.py:316
  96.8 0.8 copy-start.13
  97.5 0.8 copy-start.14
  105.6 2.2 %copy-start.15 = (bf16[512,256]{1,0:T(8,128)(2,1)}, bf16[512,256]{1,0:T(8,128)(2,1)S(1)}, u32[]{:S(2)}) copy-start(bf16[512,256]{1,0:T(8,128)(2,1)S(1)} %collective-permute-done.24.refs_16_.refs_2_) | copy-start | bytes 786436
  105.6 2.0 collective-permute-start.25
  106.2 1.5 collective-permute-start.26
  107.6 0.7 copy-start.16
  107.8 0.7 copy-start.17
  113.7 55.2 %collective-permute-start.27 = (bf16[64,2048]{1,0:T(8,128)(2,1)}, bf16[64,2048]{1,0:T(8,128)(2,1)S(1)}, u32[]{:S(2)}, u32[]{:S(2)}) collective-permute-start(bf16[64,2048]{1,0:T(8,128)(2,1)} %get-tuple-element.59), channel_id=1, source_target_pairs={{0,8},{1,9},{2,10},{3,11},{4,12},{5,13},{6,14},{7,15},{8,0},{9,1},... | collective-permute-start | bytes 786440 | tf_op jit(solution)/shard_map/ppermute | solution.py:341
  115.1 53.8 %collective-permute-start.28 = (bf16[64,2048]{1,0:T(8,128)(2,1)}, bf16[64,2048]{1,0:T(8,128)(2,1)S(1)}, u32[]{:S(2)}, u32[]{:S(2)}) collective-permute-start(bf16[64,2048]{1,0:T(8,128)(2,1)} %get-tuple-element.61), channel_id=1, source_target_pairs={{0,9},{1,10},{2,11},{3,8},{4,13},{5,14},{6,15},{7,12},{8,1},{9,2},... | collective-permute-start | bytes 786440 | tf_op jit(solution)/shard_map/ppermute | solution.py:341
  117.6 51.2 %collective-permute-start.29 = (bf16[64,2048]{1,0:T(8,128)(2,1)}, bf16[64,2048]{1,0:T(8,128)(2,1)S(1)}, u32[]{:S(2)}, u32[]{:S(2)}) collective-permute-start(bf16[64,2048]{1,0:T(8,128)(2,1)} %get-tuple-element.63), channel_id=1, source_target_pairs={{0,10},{1,11},{2,8},{3,9},{4,14},{5,15},{6,12},{7,13},{8,2},{9,3},... | collective-permute-start | bytes 786440 | tf_op jit(solution)/shard_map/ppermute | solution.py:341
  118.9 50.0 %collective-permute-start.30 = (bf16[64,2048]{1,0:T(8,128)(2,1)}, bf16[64,2048]{1,0:T(8,128)(2,1)S(1)}, u32[]{:S(2)}, u32[]{:S(2)}) collective-permute-start(bf16[64,2048]{1,0:T(8,128)(2,1)} %get-tuple-element.65), channel_id=1, source_target_pairs={{0,11},{1,8},{2,9},{3,10},{4,15},{5,12},{6,13},{7,14},{8,3},{9,0},... | collective-permute-start | bytes 786440 | tf_op jit(solution)/shard_map/ppermute | solution.py:341
  141.7 3.4 %copy-start.1 = (bf16[768,2048]{1,0:T(8,128)(2,1)S(1)}, bf16[768,2048]{1,0:T(8,128)(2,1)}, u32[]{:S(2)}) copy-start(bf16[768,2048]{1,0:T(8,128)(2,1)} %shard_map.39) | copy-start | bytes 9437188
  146.8 26.3 %collective-permute-start.31 = (bf16[64,2048]{1,0:T(8,128)(2,1)}, bf16[64,2048]{1,0:T(8,128)(2,1)S(1)}, u32[]{:S(2)}, u32[]{:S(2)}) collective-permute-start(bf16[64,2048]{1,0:T(8,128)(2,1)} %get-tuple-element.88), channel_id=1, source_target_pairs={{0,4},{1,5},{2,6},{3,7},{4,8},{5,9},{6,10},{7,11},{8,12},{9,13},{1... | collective-permute-start | bytes 786440 | tf_op jit(solution)/shard_map/ppermute | solution.py:341
  168.8 14.2 %collective-permute-start.32 = (bf16[64,2048]{1,0:T(8,128)(2,1)}, bf16[64,2048]{1,0:T(8,128)(2,1)S(1)}, u32[]{:S(2)}, u32[]{:S(2)}) collective-permute-start(bf16[64,2048]{1,0:T(8,128)(2,1)} %get-tuple-element.68), channel_id=1, source_target_pairs={{0,12},{1,13},{2,14},{3,15},{4,0},{5,1},{6,2},{7,3},{8,4},{9,5},{1... | collective-permute-start | bytes 786440 | tf_op jit(solution)/shard_map/ppermute | solution.py:341
  168.9 14.1 %collective-permute-start.33 = (bf16[64,2048]{1,0:T(8,128)(2,1)}, bf16[64,2048]{1,0:T(8,128)(2,1)S(1)}, u32[]{:S(2)}, u32[]{:S(2)}) collective-permute-start(bf16[64,2048]{1,0:T(8,128)(2,1)} %get-tuple-element.70), channel_id=1, source_target_pairs={{0,1},{1,2},{2,3},{3,0},{4,5},{5,6},{6,7},{7,4},{8,9},{9,10},{10,1... | collective-permute-start | bytes 786440 | tf_op jit(solution)/shard_map/ppermute | solution.py:341
  169.0 18.2 %collective-permute-start.34 = (bf16[64,2048]{1,0:T(8,128)(2,1)}, bf16[64,2048]{1,0:T(8,128)(2,1)S(1)}, u32[]{:S(2)}, u32[]{:S(2)}) collective-permute-start(bf16[64,2048]{1,0:T(8,128)(2,1)} %get-tuple-element.72), channel_id=1, source_target_pairs={{0,5},{1,6},{2,7},{3,4},{4,9},{5,10},{6,11},{7,8},{8,13},{9,14},{1... | collective-permute-start | bytes 786440 | tf_op jit(solution)/shard_map/ppermute | solution.py:341
  170.6 23.2 %collective-permute-start.35 = (bf16[64,2048]{1,0:T(8,128)(2,1)}, bf16[64,2048]{1,0:T(8,128)(2,1)S(1)}, u32[]{:S(2)}, u32[]{:S(2)}) collective-permute-start(bf16[64,2048]{1,0:T(8,128)(2,1)} %get-tuple-element.74), channel_id=1, source_target_pairs={{0,13},{1,14},{2,15},{3,12},{4,1},{5,2},{6,3},{7,0},{8,5},{9,6},{1... | collective-permute-start | bytes 786440 | tf_op jit(solution)/shard_map/ppermute | solution.py:341
  173.1 20.8 %collective-permute-start.36 = (bf16[64,2048]{1,0:T(8,128)(2,1)}, bf16[64,2048]{1,0:T(8,128)(2,1)S(1)}, u32[]{:S(2)}, u32[]{:S(2)}) collective-permute-start(bf16[64,2048]{1,0:T(8,128)(2,1)} %get-tuple-element.76), channel_id=1, source_target_pairs={{0,2},{1,3},{2,0},{3,1},{4,6},{5,7},{6,4},{7,5},{8,10},{9,11},{10,... | collective-permute-start | bytes 786440 | tf_op jit(solution)/shard_map/ppermute | solution.py:341
  183.0 18.2 %collective-permute-start.37 = (bf16[64,2048]{1,0:T(8,128)(2,1)}, bf16[64,2048]{1,0:T(8,128)(2,1)S(1)}, u32[]{:S(2)}, u32[]{:S(2)}) collective-permute-start(bf16[64,2048]{1,0:T(8,128)(2,1)} %get-tuple-element.78), channel_id=1, source_target_pairs={{0,6},{1,7},{2,4},{3,5},{4,10},{5,11},{6,8},{7,9},{8,14},{9,15},{1... | collective-permute-start | bytes 786440 | tf_op jit(solution)/shard_map/ppermute | solution.py:341
  183.1 18.9 %collective-permute-start.38 = (bf16[64,2048]{1,0:T(8,128)(2,1)}, bf16[64,2048]{1,0:T(8,128)(2,1)S(1)}, u32[]{:S(2)}, u32[]{:S(2)}) collective-permute-start(bf16[64,2048]{1,0:T(8,128)(2,1)} %get-tuple-element.79), channel_id=1, source_target_pairs={{0,14},{1,15},{2,12},{3,13},{4,2},{5,3},{6,0},{7,1},{8,6},{9,7},{1... | collective-permute-start | bytes 786440 | tf_op jit(solution)/shard_map/ppermute | solution.py:341
  187.2 17.0 %collective-permute-start.39 = (bf16[64,2048]{1,0:T(8,128)(2,1)}, bf16[64,2048]{1,0:T(8,128)(2,1)S(1)}, u32[]{:S(2)}, u32[]{:S(2)}) collective-permute-start(bf16[64,2048]{1,0:T(8,128)(2,1)} %get-tuple-element.80), channel_id=1, source_target_pairs={{0,3},{1,0},{2,1},{3,2},{4,7},{5,4},{6,5},{7,6},{8,11},{9,8},{10,9... | collective-permute-start | bytes 786440 | tf_op jit(solution)/shard_map/ppermute | solution.py:341
  193.8 12.8 %collective-permute-start.40 = (bf16[64,2048]{1,0:T(8,128)(2,1)}, bf16[64,2048]{1,0:T(8,128)(2,1)S(1)}, u32[]{:S(2)}, u32[]{:S(2)}) collective-permute-start(bf16[64,2048]{1,0:T(8,128)(2,1)} %get-tuple-element.81), channel_id=1, source_target_pairs={{0,7},{1,4},{2,5},{3,6},{4,11},{5,8},{6,9},{7,10},{8,15},{9,12},{1... | collective-permute-start | bytes 786440 | tf_op jit(solution)/shard_map/ppermute | solution.py:341
  193.8 16.9 %collective-permute-start.41 = (bf16[64,2048]{1,0:T(8,128)(2,1)}, bf16[64,2048]{1,0:T(8,128)(2,1)S(1)}, u32[]{:S(2)}, u32[]{:S(2)}) collective-permute-start(bf16[64,2048]{1,0:T(8,128)(2,1)} %get-tuple-element.82), channel_id=1, source_target_pairs={{0,15},{1,12},{2,13},{3,14},{4,3},{5,0},{6,1},{7,2},{8,7},{9,4},{1... | collective-permute-start | bytes 786440 | tf_op jit(solution)/shard_map/ppermute | solution.py:341

commit v7 on v6

--- a/solution.py
+++ b/solution.py
@@ -321,7 +321,8 @@
     far = [top, lax.ppermute(top, "feat", swap), bottom, lax.ppermute(bottom, "feat", swap)]
 
     first = group_part(far, table, len(near), devices, train_feats, span, owned, partial, last=True)
-    rest = group_scores(near, far, table, 1, groups - 1, train_feats, span)
+    second = group_scores(near, far, table, 1, 1, train_feats, span)
+    rest = group_scores(near, far, table, 2, groups - 2, train_feats, span)
     scores = jnp.zeros((owned, devices * columns), jnp.bfloat16)
     order = [(0, turn) for turn in range(group)]
     for turn in range(group):
@@ -332,12 +333,14 @@
         if number == 0:
             block = first[turn]
         else:
-            block = lax.dynamic_slice_in_dim(rest, (number - 1) * span + (at_place + turn) % group * owned, owned, 0)
+            tiles, offset = (second, 0) if number == 1 else (rest, (number - 2) * span)
+            block = lax.dynamic_slice_in_dim(tiles, offset + (at_place + turn) % group * owned, owned, 0)
         source = (at_group + groups - shift) % groups * group + (at_place + group - turn) % group
         if shift or turn:
             pairs = [(i, (i // group + shift) % groups * group + (i + turn) % group) for i in range(devices)]
             if len(going) >= IN_FLIGHT:
-                block, going[-IN_FLIGHT] = lax.optimization_barrier((block, going[-IN_FLIGHT]))
+                block, going[-IN_FLIGHT], behind = lax.optimization_barrier((block, going[-IN_FLIGHT], behind))
+            behind = block
             going.append(lax.ppermute(block, ("rows", "feat"), pairs))
             sources.append(source)
         else:

time: 212 us -> 210 us (level)
  local copies, waits for them, and re-layouts: 20.1 us -> 8.43 us
  Pallas kernels: 44.3 us -> 50 us
  waiting for transfers between devices: 92.9 us -> 97.3 us
    ppermute x6, waiting for transfers between devices: 25.9 us -> 45.2 us  [per_device(): forward = lax.ppermute(forward, 'rows', ahead)]
    ppermute x6, waiting for transfers between devices: 20.3 us -> 1.1 us  [per_device(): backward = lax.ppermute(backward, 'rows', back)]
    dynamic_update_slice x15, local copies, waits for them, and re-layouts: 10.8 us -> 1.05 us  [per_device(): scores = lax.dynamic_update_slice(scores, block, (0, source * columns))]
    pallas_call x1 -> x2, Pallas kernels: 21.4 us -> 27.1 us  [group_scores(): pl.pallas_call(functools.partial(tile_rows, owners, skip, tuple(range(tar...]
    ppermute x15, waiting for transfers between devices: 39.1 us -> 43.1 us  [per_device(): going.append(lax.ppermute(block, ('rows', 'feat'), pairs))]
    broadcast_in_dim x1, local copies, waits for them, and re-layouts: 2.41 us -> 0.28 us  [per_device(): scores = jnp.zeros((owned, devices * columns), jnp.bfloat16)]
    unnamed x36 -> x38, local copies, waits for them, and re-layouts: 4.15 us -> 4.41 us
  transfers between devices with their start and end apart: 42 -> 42, of which waited for: 19 -> 22; matrix products, arithmetic and copies ran while one was open for 9% -> 4% of each run, Pallas kernels for 18% -> 21%
where the time goes in v7:
time: 210 us; the launch traced here: 209 us
  waiting for transfers between devices  97.3 us (46%)
  Pallas kernels  50 us (24%)
  starting transfers between devices  47 us (22%)
  local copies, waits for them, and re-layouts  8.43 us (4%)
  matrix products  4.61 us (2%)
    ppermute x6, waiting for transfers between devices, per_device(): forward = lax.ppermute(forward, 'rows', ahead)  45.2 us
    ppermute x15, waiting for transfers between devices, per_device(): going.append(lax.ppermute(block, ('rows', 'feat'), pairs))  43.1 us
    pallas_call x2, Pallas kernels, group_scores(): pl.pallas_call(functools.partial(tile_rows, owners, skip, tuple(range(tar...  27.1 us
    pallas_call x3, Pallas kernels, group_part(): pl.pallas_call(functools.partial(some_columns, count, base, group_at, las...  22.9 us
    ppermute x15, starting transfers between devices, per_device(): going.append(lax.ppermute(block, ('rows', 'feat'), pairs))  19.4 us
    ppermute x6, starting transfers between devices, per_device(): forward = lax.ppermute(forward, 'rows', ahead)  8.15 us
    ppermute x6, starting transfers between devices, per_device(): near += [block, lax.ppermute(block, 'feat', swap)]  5.1 us
    dot_general x8, matrix products, product(): partial = jnp.dot(block, kernel, preferred_element_type=jnp.float32)  4.61 us
  transfers between devices with their start and end apart: 42, of which 22 were waited for; matrix products, arithmetic and copies ran while one was open for 4% of the time, Pallas kernels for 21%

profile of v7, /device:TPU:1, one launch (start us, length us, event | category | flops | bytes accessed | tf_op | source)
XLA Modules:
  0.0 209.1 jit_solution(10671527268725536804)
XLA Ops:
  0.0 2.1 %collective-permute-start = (bf16[128,2048]{1,0:T(8,128)(2,1)}, bf16[128,2048]{1,0:T(8,128)(2,1)S(1)}, u32[]{:S(2)}, u32[]{:S(2)}) collective-permute-start(bf16[128,2048]{1,0:T(8,128)(2,1)} %param.3), channel_id=1, source_target_pairs={{0,4},{4,8},{8,12},{12,14},{14,10},{10,6},{6,2},{2,0},{1,5},{5,9},... | collective-permute-start | bytes 1572872 | tf_op jit(solution)/shard_map/ppermute | solution.py:282
  2.1 0.7 stack.87.where
  2.8 1.5 fusion.6
  4.5 9.4 %collective-permute-done = bf16[128,2048]{1,0:T(8,128)(2,1)S(1)} collective-permute-done((bf16[128,2048]{1,0:T(8,128)(2,1)}, bf16[128,2048]{1,0:T(8,128)(2,1)S(1)}, u32[]{:S(2)}, u32[]{:S(2)}) %collective-permute-start) | collective-permute-done | bytes 524320 | tf_op jit(solution)/shard_map/ppermute | solution.py:282
  13.9 1.2 collective-permute-start.1
  16.4 9.7 %collective-permute-done.1 = bf16[128,2048]{1,0:T(8,128)(2,1)S(1)} collective-permute-done((bf16[128,2048]{1,0:T(8,128)(2,1)S(1)}, bf16[128,2048]{1,0:T(8,128)(2,1)S(1)}, u32[]{:S(2)}, u32[]{:S(2)}) %collective-permute-start.1) | collective-permute-done | bytes 524320 | tf_op jit(solution)/shard_map/ppermute | solution.py:282
  26.1 0.9 collective-permute-start.2
  27.5 0.6 collective-permute-start.6
  28.6 2.8 %collective-permute-start.8 = (f32[1024,256]{1,0:T(8,128)S(1)}, f32[1024,256]{1,0:T(8,128)S(1)}, u32[]{:S(2)}, u32[]{:S(2)}) collective-permute-start(f32[1024,256]{1,0:T(8,128)S(1)} %get-tuple-element.101), channel_id=1, source_target_pairs={{0,1},{1,0},{2,3},{3,2},{4,5},{5,4},{6,7},{7,6},{8,9},{9,8},{10,11... | collective-permute-start | bytes 3145736 | tf_op jit(solution)/shard_map/ppermute | solution.py:295
  31.4 6.0 %collective-permute-done.2 = bf16[128,2048]{1,0:T(8,128)(2,1)S(1)} collective-permute-done((bf16[128,2048]{1,0:T(8,128)(2,1)S(1)}, bf16[128,2048]{1,0:T(8,128)(2,1)S(1)}, u32[]{:S(2)}, u32[]{:S(2)}) %collective-permute-start.2) | collective-permute-done | bytes 524320 | tf_op jit(solution)/shard_map/ppermute | solution.py:282
  37.4 0.6 collective-permute-start.3
  38.2 1.0 collective-permute-start.7
  39.2 0.5 fusion.11
  40.3 2.4 %collective-permute-done.3 = bf16[64,2048]{1,0:T(8,128)(2,1)S(1)} collective-permute-done((bf16[64,2048]{1,0:T(8,128)(2,1)S(1)}, bf16[64,2048]{1,0:T(8,128)(2,1)S(1)}, u32[]{:S(2)}, u32[]{:S(2)}) %collective-permute-start.3) | collective-permute-done | bytes 262176 | tf_op jit(solution)/shard_map/ppermute | solution.py:287
  42.7 1.6 collective-permute-done.7
  44.8 4.5 %collective-permute-start.9 = (f32[384,256]{1,0:T(8,128)S(1)}, f32[384,256]{1,0:T(8,128)}, u32[]{:S(2)}, u32[]{:S(2)}) collective-permute-start(f32[384,256]{1,0:T(8,128)S(1)} %pad_maximum_fusion), channel_id=1, source_target_pairs={{0,1},{1,0},{2,3},{3,2},{4,5},{5,4},{6,7},{7,6},{8,9},{9,8},{10,11... | collective-permute-start | bytes 1179656 | tf_op jit(solution)/shard_map/ppermute | solution.py:299
  49.3 1.5 collective-permute-done.9
  50.8 1.0 fusion.4
  51.9 1.3 collective-permute-start.11
  53.4 11.7 %collective-permute-done.11.refs_2_ = bf16[1024,256]{1,0:T(8,128)(2,1)S(1)} collective-permute-done((bf16[1024,256]{1,0:T(8,128)(2,1)S(1)}, bf16[1024,256]{1,0:T(8,128)(2,1)S(1)}, u32[]{:S(2)}, u32[]{:S(2)}) %collective-permute-start.11) | collective-permute-done | bytes 524320 | tf_op jit(solution)/shard_map/ppermute | solution.py:307
  65.1 1.3 collective-permute-start.15
  66.6 1.8 collective-permute-start.10
  68.3 0.5 collective-permute-start.14
  68.8 8.5 %collective-permute-done.15.refs_6_ = bf16[1024,256]{1,0:T(8,128)(2,1)S(1)} collective-permute-done((bf16[1024,256]{1,0:T(8,128)(2,1)S(1)}, bf16[1024,256]{1,0:T(8,128)(2,1)S(1)}, u32[]{:S(2)}, u32[]{:S(2)}) %collective-permute-start.15) | collective-permute-done | bytes 524320 | tf_op jit(solution)/shard_map/ppermute | solution.py:307
  77.3 2.1 %collective-permute-start.16 = (bf16[1024,256]{1,0:T(8,128)(2,1)S(1)}, bf16[1024,256]{1,0:T(8,128)(2,1)S(1)}, u32[]{:S(2)}, u32[]{:S(2)}) collective-permute-start(bf16[1024,256]{1,0:T(8,128)(2,1)S(1)} %collective-permute-done.15.refs_6_), channel_id=1, source_target_pairs={{0,1},{1,0},{2,3},{3,2},{4,5},{5,4},{6,7},{7,6},{8,9},{9,8},{10,11... | collective-permute-start | bytes 1572872 | tf_op jit(solution)/shard_map/ppermute | solution.py:315
  79.4 1.3 collective-permute-start.18
  80.7 1.3 collective-permute-start.19
  82.2 0.6 copy-done.10
  83.0 0.8 copy-done.12
  83.9 10.4 %shard_map.37 = (f32[256,2048]{1,0:T(8,128)}, f32[256,128]{1,0:T(8,128)}) custom-call(s32[21]{0:T(128)} %stack.87.where, bf16[1024,256]{1,0:T(8,128)(2,1)} %copy-done.1, bf16[1024,256]{1,0:T(8,128)(2,1)} %copy-done.9, bf16[1024,256]{1,0:T(8,128)(2,1)} %copy-done.5, bf16[1024,256]{1,0:T(8,128)(2,1)} %copy-done.10, bf16[1024,256]{1,0:T(8,128)(2,1)} %copy-done.6, ...), custom_call_target="tpu_custom_call" | custom-call | flops 2684354560 | bytes 10485760 | tf_op jit(solution)/shard_map/pallas_call | solution.py:205
  94.3 0.9 collective-permute-done.20.refs_2_.refs_12_
  95.2 1.2 collective-permute-start.21
  96.4 1.3 collective-permute-start.23
  98.0 0.7 collective-permute-done.22.refs_3_.refs_13_
  98.8 0.7 copy-done.14
  99.5 7.3 %shard_map.38 = (f32[256,2048]{1,0:T(8,128)}, f32[256,128]{1,0:T(8,128)}) custom-call(s32[21]{0:T(128)} %stack.87.where, bf16[1024,256]{1,0:T(8,128)(2,1)} %copy-done.3, bf16[1024,256]{1,0:T(8,128)(2,1)} %copy-done.13, bf16[1024,256]{1,0:T(8,128)(2,1)} %copy-done.4, bf16[1024,256]{1,0:T(8,128)(2,1)} %copy-done.14, bf16[2048,4096]{1,0:T(8,128)(2,1)} %refs_18_.3, ...), custom_call_target="tpu_custom_call" | custom-call | flops 1073741824 | bytes 4194304 | tf_op jit(solution)/shard_map/pallas_call | solution.py:205
  106.8 0.6 collective-permute-start.25
  107.5 1.1 collective-permute-done.25.refs_15_.refs_1_
  108.6 0.6 collective-permute-done.26.refs_17_.refs_3_
  109.3 0.6 copy-done.18
  109.9 5.1 %shard_map.40 = (bf16[64,2048]{1,0:T(8,128)(2,1)}, bf16[64,2048]{1,0:T(8,128)(2,1)}, bf16[64,2048]{1,0:T(8,128)(2,1)}, bf16[64,2048]{1,0:T(8,128)(2,1)}) custom-call(s32[21]{0:T(128)} %stack.87.where, bf16[512,256]{1,0:T(8,128)(2,1)} %copy-done.16, bf16[512,256]{1,0:T(8,128)(2,1)} %copy-done.17, bf16[512,256]{1,0:T(8,128)(2,1)} %collective-permute-done.24.refs_16_.refs_2_, ...), custom_call_target="tpu_custom_call" | custom-call | flops 536870912 | bytes 2097152 | tf_op jit(solution)/shard_map/pallas_call | solution.py:205
  115.1 1.2 collective-permute-start.27
  116.3 1.7 collective-permute-start.28
  117.9 2.1 %collective-permute-start.29 = (bf16[64,2048]{1,0:T(8,128)(2,1)}, bf16[64,2048]{1,0:T(8,128)(2,1)S(1)}, u32[]{:S(2)}, u32[]{:S(2)}) collective-permute-start(bf16[64,2048]{1,0:T(8,128)(2,1)} %get-tuple-element.64), channel_id=1, source_target_pairs={{0,10},{1,11},{2,8},{3,9},{4,14},{5,15},{6,12},{7,13},{8,2},{9,3},... | collective-permute-start | bytes 786440 | tf_op jit(solution)/shard_map/ppermute | solution.py:344
  120.3 11.4 %shard_map.41 = bf16[256,2048]{1,0:T(8,128)(2,1)} custom-call(s32[21]{0:T(128)} %stack.87.where, bf16[1024,256]{1,0:T(8,128)(2,1)} %copy-done.1, bf16[1024,256]{1,0:T(8,128)(2,1)} %copy-done.9, bf16[1024,256]{1,0:T(8,128)(2,1)} %copy-done.5, bf16[1024,256]{1,0:T(8,128)(2,1)} %copy-done.10, bf16[1024,256]{1,0:T(8,128)(2,1)} %copy-done.6, ...), custom_call_target="tpu_custom_call" | custom-call | flops 4294967296 | bytes 16777216 | tf_op jit(solution)/shard_map/pallas_call | solution.py:222
  131.7 1.3 constant_dynamic-slice_fusion.1
  133.0 1.3 collective-permute-start.31
  134.3 15.7 %shard_map.39 = bf16[512,2048]{1,0:T(8,128)(2,1)} custom-call(s32[21]{0:T(128)} %stack.87.where, bf16[1024,256]{1,0:T(8,128)(2,1)} %copy-done.1, bf16[1024,256]{1,0:T(8,128)(2,1)} %copy-done.9, bf16[1024,256]{1,0:T(8,128)(2,1)} %copy-done.5, bf16[1024,256]{1,0:T(8,128)(2,1)} %copy-done.10, bf16[1024,256]{1,0:T(8,128)(2,1)} %copy-done.6, ...), custom_call_target="tpu_custom_call" | custom-call | flops 8589934592 | bytes 16777216 | tf_op jit(solution)/shard_map/pallas_call | solution.py:222
  150.3 1.3 copy-done.15
  151.9 3.0 %collective-permute-start.32 = (bf16[64,2048]{1,0:T(8,128)(2,1)S(1)}, bf16[64,2048]{1,0:T(8,128)(2,1)S(1)}, u32[]{:S(2)}, u32[]{:S(2)}) collective-permute-start(bf16[64,2048]{1,0:T(8,128)(2,1)S(1)} %get-tuple-element.62), channel_id=1, source_target_pairs={{0,12},{1,13},{2,14},{3,15},{4,0},{5,1},{6,2},{7,3},{8,4},{9,5},{1... | collective-permute-start | bytes 786440 | tf_op jit(solution)/shard_map/ppermute | solution.py:344
  154.9 4.2 %collective-permute-done.28 = bf16[64,2048]{1,0:T(8,128)(2,1)S(1)} collective-permute-done((bf16[64,2048]{1,0:T(8,128)(2,1)}, bf16[64,2048]{1,0:T(8,128)(2,1)S(1)}, u32[]{:S(2)}, u32[]{:S(2)}) %collective-permute-start.28) | collective-permute-done | bytes 262176 | tf_op jit(solution)/shard_map/ppermute | solution.py:344
  159.1 4.5 %collective-permute-done.29 = bf16[64,2048]{1,0:T(8,128)(2,1)S(1)} collective-permute-done((bf16[64,2048]{1,0:T(8,128)(2,1)}, bf16[64,2048]{1,0:T(8,128)(2,1)S(1)}, u32[]{:S(2)}, u32[]{:S(2)}) %collective-permute-start.29) | collective-permute-done | bytes 262176 | tf_op jit(solution)/shard_map/ppermute | solution.py:344
  163.6 11.3 %collective-permute-done.30 = bf16[64,2048]{1,0:T(8,128)(2,1)S(1)} collective-permute-done((bf16[64,2048]{1,0:T(8,128)(2,1)}, bf16[64,2048]{1,0:T(8,128)(2,1)S(1)}, u32[]{:S(2)}, u32[]{:S(2)}) %collective-permute-start.30) | collective-permute-done | bytes 262176 | tf_op jit(solution)/shard_map/ppermute | solution.py:344
  175.0 2.0 collective-permute-start.36
  177.2 3.5 %collective-permute-done.32 = bf16[64,2048]{1,0:T(8,128)(2,1)S(1)} collective-permute-done((bf16[64,2048]{1,0:T(8,128)(2,1)S(1)}, bf16[64,2048]{1,0:T(8,128)(2,1)S(1)}, u32[]{:S(2)}, u32[]{:S(2)}) %collective-permute-start.32) | collective-permute-done | bytes 262176 | tf_op jit(solution)/shard_map/ppermute | solution.py:344
  180.8 4.0 %collective-permute-start.38 = (bf16[64,2048]{1,0:T(8,128)(2,1)S(1)}, bf16[64,2048]{1,0:T(8,128)(2,1)S(1)}, u32[]{:S(2)}, u32[]{:S(2)}) collective-permute-start(bf16[64,2048]{1,0:T(8,128)(2,1)S(1)} %get-tuple-element.76), channel_id=1, source_target_pairs={{0,14},{1,15},{2,12},{3,13},{4,2},{5,3},{6,0},{7,1},{8,6},{9,7},{1... | collective-permute-start | bytes 786440 | tf_op jit(solution)/shard_map/ppermute | solution.py:344
  184.8 1.1 collective-permute-start.39
  186.0 6.1 %collective-permute-done.35 = bf16[64,2048]{1,0:T(8,128)(2,1)S(1)} collective-permute-done((bf16[64,2048]{1,0:T(8,128)(2,1)S(1)}, bf16[64,2048]{1,0:T(8,128)(2,1)S(1)}, u32[]{:S(2)}, u32[]{:S(2)}) %collective-permute-start.35) | collective-permute-done | bytes 262176 | tf_op jit(solution)/shard_map/ppermute | solution.py:344
  192.1 2.5 %collective-permute-start.41 = (bf16[64,2048]{1,0:T(8,128)(2,1)S(1)}, bf16[64,2048]{1,0:T(8,128)(2,1)S(1)}, u32[]{:S(2)}, u32[]{:S(2)}) collective-permute-start(bf16[64,2048]{1,0:T(8,128)(2,1)S(1)} %get-tuple-element.82), channel_id=1, source_target_pairs={{0,15},{1,12},{2,13},{3,14},{4,3},{5,0},{6,1},{7,2},{8,7},{9,4},{1... | collective-permute-start | bytes 786440 | tf_op jit(solution)/shard_map/ppermute | solution.py:344
  194.8 2.5 %collective-permute-done.38 = bf16[64,2048]{1,0:T(8,128)(2,1)S(1)} collective-permute-done((bf16[64,2048]{1,0:T(8,128)(2,1)S(1)}, bf16[64,2048]{1,0:T(8,128)(2,1)S(1)}, u32[]{:S(2)}, u32[]{:S(2)}) %collective-permute-start.38) | collective-permute-done | bytes 262176 | tf_op jit(solution)/shard_map/ppermute | solution.py:344
  197.3 4.2 %collective-permute-done.39 = bf16[64,2048]{1,0:T(8,128)(2,1)S(1)} collective-permute-done((bf16[64,2048]{1,0:T(8,128)(2,1)S(1)}, bf16[64,2048]{1,0:T(8,128)(2,1)S(1)}, u32[]{:S(2)}, u32[]{:S(2)}) %collective-permute-start.39) | collective-permute-done | bytes 262176 | tf_op jit(solution)/shard_map/ppermute | solution.py:344
  201.6 2.1 %collective-permute-done.40 = bf16[64,2048]{1,0:T(8,128)(2,1)S(1)} collective-permute-done((bf16[64,2048]{1,0:T(8,128)(2,1)S(1)}, bf16[64,2048]{1,0:T(8,128)(2,1)S(1)}, u32[]{:S(2)}, u32[]{:S(2)}) %collective-permute-start.40) | collective-permute-done | bytes 262176 | tf_op jit(solution)/shard_map/ppermute | solution.py:344
  203.7 4.6 %collective-permute-done.41 = bf16[64,2048]{1,0:T(8,128)(2,1)S(1)} collective-permute-done((bf16[64,2048]{1,0:T(8,128)(2,1)S(1)}, bf16[64,2048]{1,0:T(8,128)(2,1)S(1)}, u32[]{:S(2)}, u32[]{:S(2)}) %collective-permute-start.41) | collective-permute-done | bytes 262176 | tf_op jit(solution)/shard_map/ppermute | solution.py:344
  208.3 0.7 constant_dynamic-update-slice_fusion.9
  (111 shorter events, 6.4 us)
Async XLA Ops:
  0.0 2.8 %copy-start = (bf16[2048,512]{1,0:T(8,128)(2,1)S(1)}, bf16[2048,512]{1,0:T(8,128)(2,1)}, u32[]{:S(2)}) copy-start(bf16[2048,512]{1,0:T(8,128)(2,1)} %param.4) | copy-start | bytes 6291460
  0.0 13.9 %collective-permute-start = (bf16[128,2048]{1,0:T(8,128)(2,1)}, bf16[128,2048]{1,0:T(8,128)(2,1)S(1)}, u32[]{:S(2)}, u32[]{:S(2)}) collective-permute-start(bf16[128,2048]{1,0:T(8,128)(2,1)} %param.3), channel_id=1, source_target_pairs={{0,4},{4,8},{8,12},{12,14},{14,10},{10,6},{6,2},{2,0},{1,5},{5,9},... | collective-permute-start | bytes 1572872 | tf_op jit(solution)/shard_map/ppermute | solution.py:282
  2.1 13.5 %collective-permute-start.4 = (bf16[128,2048]{1,0:T(8,128)(2,1)}, bf16[128,2048]{1,0:T(8,128)(2,1)S(1)}, u32[]{:S(2)}, u32[]{:S(2)}) collective-permute-start(bf16[128,2048]{1,0:T(8,128)(2,1)} %param.3), channel_id=1, source_target_pairs={{4,0},{8,4},{12,8},{14,12},{10,14},{6,10},{2,6},{0,2},{5,1},{9,5},... | collective-permute-start | bytes 1572872 | tf_op jit(solution)/shard_map/ppermute | solution.py:283
  13.9 12.2 %collective-permute-start.1 = (bf16[128,2048]{1,0:T(8,128)(2,1)S(1)}, bf16[128,2048]{1,0:T(8,128)(2,1)S(1)}, u32[]{:S(2)}, u32[]{:S(2)}) collective-permute-start(bf16[128,2048]{1,0:T(8,128)(2,1)S(1)} %collective-permute-done), channel_id=1, source_target_pairs={{0,4},{4,8},{8,12},{12,14},{14,10},{10,6},{6,2},{2,0},{1,5},{5,9},... | collective-permute-start | bytes 1572872 | tf_op jit(solution)/shard_map/ppermute | solution.py:282
  15.6 11.9 %collective-permute-start.5 = (bf16[128,2048]{1,0:T(8,128)(2,1)S(1)}, bf16[128,2048]{1,0:T(8,128)(2,1)S(1)}, u32[]{:S(2)}, u32[]{:S(2)}) collective-permute-start(bf16[128,2048]{1,0:T(8,128)(2,1)S(1)} %collective-permute-done.4), channel_id=1, source_target_pairs={{4,0},{8,4},{12,8},{14,12},{10,14},{6,10},{2,6},{0,2},{5,1},{9,5},... | collective-permute-start | bytes 1572872 | tf_op jit(solution)/shard_map/ppermute | solution.py:283
  26.1 11.3 %collective-permute-start.2 = (bf16[128,2048]{1,0:T(8,128)(2,1)S(1)}, bf16[128,2048]{1,0:T(8,128)(2,1)S(1)}, u32[]{:S(2)}, u32[]{:S(2)}) collective-permute-start(bf16[128,2048]{1,0:T(8,128)(2,1)S(1)} %collective-permute-done.1), channel_id=1, source_target_pairs={{0,4},{4,8},{8,12},{12,14},{14,10},{10,6},{6,2},{2,0},{1,5},{5,9},... | collective-permute-start | bytes 1572872 | tf_op jit(solution)/shard_map/ppermute | solution.py:282
  27.5 10.7 %collective-permute-start.6 = (bf16[128,2048]{1,0:T(8,128)(2,1)S(1)}, bf16[128,2048]{1,0:T(8,128)(2,1)S(1)}, u32[]{:S(2)}, u32[]{:S(2)}) collective-permute-start(bf16[128,2048]{1,0:T(8,128)(2,1)S(1)} %collective-permute-done.5), channel_id=1, source_target_pairs={{4,0},{8,4},{12,8},{14,12},{10,14},{6,10},{2,6},{0,2},{5,1},{9,5},... | collective-permute-start | bytes 1572872 | tf_op jit(solution)/shard_map/ppermute | solution.py:283
  28.6 11.5 %collective-permute-start.8 = (f32[1024,256]{1,0:T(8,128)S(1)}, f32[1024,256]{1,0:T(8,128)S(1)}, u32[]{:S(2)}, u32[]{:S(2)}) collective-permute-start(f32[1024,256]{1,0:T(8,128)S(1)} %get-tuple-element.101), channel_id=1, source_target_pairs={{0,1},{1,0},{2,3},{3,2},{4,5},{5,4},{6,7},{7,6},{8,9},{9,8},{10,11... | collective-permute-start | bytes 3145736 | tf_op jit(solution)/shard_map/ppermute | solution.py:295
  37.4 5.3 %collective-permute-start.3 = (bf16[64,2048]{1,0:T(8,128)(2,1)S(1)}, bf16[64,2048]{1,0:T(8,128)(2,1)S(1)}, u32[]{:S(2)}, u32[]{:S(2)}) collective-permute-start(bf16[64,2048]{1,0:T(8,128)(2,1)S(1)} %slice.28), channel_id=1, source_target_pairs={{0,4},{4,8},{8,12},{12,14},{14,10},{10,6},{6,2},{2,0},{1,5},{5,9},... | collective-permute-start | bytes 786440 | tf_op jit(solution)/shard_map/ppermute | solution.py:287
  38.2 6.1 %collective-permute-start.7 = (bf16[64,2048]{1,0:T(8,128)(2,1)S(1)}, bf16[64,2048]{1,0:T(8,128)(2,1)S(1)}, u32[]{:S(2)}, u32[]{:S(2)}) collective-permute-start(bf16[64,2048]{1,0:T(8,128)(2,1)S(1)} %slice.29), channel_id=1, source_target_pairs={{4,0},{8,4},{12,8},{14,12},{10,14},{6,10},{2,6},{0,2},{5,1},{9,5},... | collective-permute-start | bytes 786440 | tf_op jit(solution)/shard_map/ppermute | solution.py:288
  44.8 6.0 %collective-permute-start.9 = (f32[384,256]{1,0:T(8,128)S(1)}, f32[384,256]{1,0:T(8,128)}, u32[]{:S(2)}, u32[]{:S(2)}) collective-permute-start(f32[384,256]{1,0:T(8,128)S(1)} %pad_maximum_fusion), channel_id=1, source_target_pairs={{0,1},{1,0},{2,3},{3,2},{4,5},{5,4},{6,7},{7,6},{8,9},{9,8},{10,11... | collective-permute-start | bytes 1179656 | tf_op jit(solution)/shard_map/ppermute | solution.py:299
  51.9 31.9 %copy-start.1 = (bf16[1024,256]{1,0:T(8,128)(2,1)}, bf16[1024,256]{1,0:T(8,128)(2,1)S(1)}, u32[]{:S(2)}) copy-start(bf16[1024,256]{1,0:T(8,128)(2,1)S(1)} %slice_dynamic-update-slice_fusion.refs_0_) | copy-start | bytes 1572868
  51.9 13.2 %collective-permute-start.11 = (bf16[1024,256]{1,0:T(8,128)(2,1)S(1)}, bf16[1024,256]{1,0:T(8,128)(2,1)S(1)}, u32[]{:S(2)}, u32[]{:S(2)}) collective-permute-start(bf16[1024,256]{1,0:T(8,128)(2,1)S(1)} %slice_dynamic-update-slice_fusion.refs_0_), channel_id=1, source_target_pairs={{0,4},{4,8},{8,12},{12,14},{14,10},{10,6},{6,2},{2,0},{1,5},{5,9},... | collective-permute-start | bytes 1572872 | tf_op jit(solution)/shard_map/ppermute | solution.py:307
  53.3 13.1 %collective-permute-start.13 = (bf16[1024,256]{1,0:T(8,128)(2,1)S(1)}, bf16[1024,256]{1,0:T(8,128)(2,1)S(1)}, u32[]{:S(2)}, u32[]{:S(2)}) collective-permute-start(bf16[1024,256]{1,0:T(8,128)(2,1)S(1)} %slice_dynamic-update-slice_fusion.refs_0_), channel_id=1, source_target_pairs={{4,0},{8,4},{12,8},{14,12},{10,14},{6,10},{2,6},{0,2},{5,1},{9,5},... | collective-permute-start | bytes 1572872 | tf_op jit(solution)/shard_map/ppermute | solution.py:308
  65.1 18.7 %copy-start.5 = (bf16[1024,256]{1,0:T(8,128)(2,1)}, bf16[1024,256]{1,0:T(8,128)(2,1)S(1)}, u32[]{:S(2)}) copy-start(bf16[1024,256]{1,0:T(8,128)(2,1)S(1)} %collective-permute-done.11.refs_2_) | copy-start | bytes 1572868
  65.1 12.2 %collective-permute-start.15 = (bf16[1024,256]{1,0:T(8,128)(2,1)S(1)}, bf16[1024,256]{1,0:T(8,128)(2,1)S(1)}, u32[]{:S(2)}, u32[]{:S(2)}) collective-permute-start(bf16[1024,256]{1,0:T(8,128)(2,1)S(1)} %collective-permute-done.11.refs_2_), channel_id=1, source_target_pairs={{0,4},{4,8},{8,12},{12,14},{14,10},{10,6},{6,2},{2,0},{1,5},{5,9},... | collective-permute-start | bytes 1572872 | tf_op jit(solution)/shard_map/ppermute | solution.py:307
  66.4 17.4 %copy-start.6 = (bf16[1024,256]{1,0:T(8,128)(2,1)}, bf16[1024,256]{1,0:T(8,128)(2,1)S(1)}, u32[]{:S(2)}) copy-start(bf16[1024,256]{1,0:T(8,128)(2,1)S(1)} %collective-permute-done.13.refs_4_) | copy-start | bytes 1572868
  66.4 13.0 %collective-permute-start.17 = (bf16[1024,256]{1,0:T(8,128)(2,1)S(1)}, bf16[1024,256]{1,0:T(8,128)(2,1)S(1)}, u32[]{:S(2)}, u32[]{:S(2)}) collective-permute-start(bf16[1024,256]{1,0:T(8,128)(2,1)S(1)} %collective-permute-done.13.refs_4_), channel_id=1, source_target_pairs={{4,0},{8,4},{12,8},{14,12},{10,14},{6,10},{2,6},{0,2},{5,1},{9,5},... | collective-permute-start | bytes 1572872 | tf_op jit(solution)/shard_map/ppermute | solution.py:308
  66.6 14.2 %collective-permute-start.10 = (bf16[1024,256]{1,0:T(8,128)(2,1)S(1)}, bf16[1024,256]{1,0:T(8,128)(2,1)S(1)}, u32[]{:S(2)}, u32[]{:S(2)}) collective-permute-start(bf16[1024,256]{1,0:T(8,128)(2,1)S(1)} %slice_dynamic-update-slice_fusion.refs_0_), channel_id=1, source_target_pairs={{0,1},{1,0},{2,3},{3,2},{4,5},{5,4},{6,7},{7,6},{8,9},{9,8},{10,11... | collective-permute-start | bytes 1572872 | tf_op jit(solution)/shard_map/ppermute | solution.py:304
  68.3 13.7 %collective-permute-start.12 = (bf16[1024,256]{1,0:T(8,128)(2,1)S(1)}, bf16[1024,256]{1,0:T(8,128)(2,1)S(1)}, u32[]{:S(2)}, u32[]{:S(2)}) collective-permute-start(bf16[1024,256]{1,0:T(8,128)(2,1)S(1)} %collective-permute-done.11.refs_2_), channel_id=1, source_target_pairs={{0,1},{1,0},{2,3},{3,2},{4,5},{5,4},{6,7},{7,6},{8,9},{9,8},{10,11... | collective-permute-start | bytes 1572872 | tf_op jit(solution)/shard_map/ppermute | solution.py:315
  68.3 13.9 %collective-permute-start.14 = (bf16[1024,256]{1,0:T(8,128)(2,1)S(1)}, bf16[1024,256]{1,0:T(8,128)(2,1)S(1)}, u32[]{:S(2)}, u32[]{:S(2)}) collective-permute-start(bf16[1024,256]{1,0:T(8,128)(2,1)S(1)} %collective-permute-done.13.refs_4_), channel_id=1, source_target_pairs={{0,1},{1,0},{2,3},{3,2},{4,5},{5,4},{6,7},{7,6},{8,9},{9,8},{10,11... | collective-permute-start | bytes 1572872 | tf_op jit(solution)/shard_map/ppermute | solution.py:315
  77.3 6.5 %copy-start.7 = (bf16[1024,256]{1,0:T(8,128)(2,1)}, bf16[1024,256]{1,0:T(8,128)(2,1)S(1)}, u32[]{:S(2)}) copy-start(bf16[1024,256]{1,0:T(8,128)(2,1)S(1)} %collective-permute-done.15.refs_6_) | copy-start | bytes 1572868
  77.3 4.9 %collective-permute-start.16 = (bf16[1024,256]{1,0:T(8,128)(2,1)S(1)}, bf16[1024,256]{1,0:T(8,128)(2,1)S(1)}, u32[]{:S(2)}, u32[]{:S(2)}) collective-permute-start(bf16[1024,256]{1,0:T(8,128)(2,1)S(1)} %collective-permute-done.15.refs_6_), channel_id=1, source_target_pairs={{0,1},{1,0},{2,3},{3,2},{4,5},{5,4},{6,7},{7,6},{8,9},{9,8},{10,11... | collective-permute-start | bytes 1572872 | tf_op jit(solution)/shard_map/ppermute | solution.py:315
  79.4 4.4 %copy-start.8 = (bf16[1024,256]{1,0:T(8,128)(2,1)}, bf16[1024,256]{1,0:T(8,128)(2,1)S(1)}, u32[]{:S(2)}) copy-start(bf16[1024,256]{1,0:T(8,128)(2,1)S(1)} %collective-permute-done.17.refs_8_) | copy-start | bytes 1572868
  79.4 4.4 %collective-permute-start.18 = (bf16[1024,256]{1,0:T(8,128)(2,1)S(1)}, bf16[1024,256]{1,0:T(8,128)(2,1)}, u32[]{:S(2)}, u32[]{:S(2)}) collective-permute-start(bf16[1024,256]{1,0:T(8,128)(2,1)S(1)} %collective-permute-done.17.refs_8_), channel_id=1, source_target_pairs={{0,1},{1,0},{2,3},{3,2},{4,5},{5,4},{6,7},{7,6},{8,9},{9,8},{10,11... | collective-permute-start | bytes 1572872 | tf_op jit(solution)/shard_map/ppermute | solution.py:315
  80.7 1.5 copy-start.9
  80.7 13.5 %collective-permute-start.19 = (bf16[1024,256]{1,0:T(8,128)(2,1)S(1)}, bf16[1024,256]{1,0:T(8,128)(2,1)S(1)}, u32[]{:S(2)}, u32[]{:S(2)}) collective-permute-start(bf16[1024,256]{1,0:T(8,128)(2,1)S(1)} %collective-permute-done.15.refs_6_), channel_id=1, source_target_pairs={{0,4},{4,8},{8,12},{12,14},{14,10},{10,6},{6,2},{2,0},{1,5},{5,9},... | collective-permute-start | bytes 1572872 | tf_op jit(solution)/shard_map/ppermute | solution.py:307
  82.0 0.8 copy-start.10
  82.0 13.2 %collective-permute-start.20 = (bf16[1024,256]{1,0:T(8,128)(2,1)S(1)}, bf16[1024,256]{1,0:T(8,128)(2,1)S(1)}, u32[]{:S(2)}, u32[]{:S(2)}) collective-permute-start(bf16[1024,256]{1,0:T(8,128)(2,1)S(1)} %collective-permute-done.17.refs_8_), channel_id=1, source_target_pairs={{4,0},{8,4},{12,8},{14,12},{10,14},{6,10},{2,6},{0,2},{5,1},{9,5},... | collective-permute-start | bytes 1572872 | tf_op jit(solution)/shard_map/ppermute | solution.py:308
  82.2 0.8 copy-start.11
  83.0 0.8 copy-start.12
  94.3 4.4 %copy-start.3 = (bf16[1024,256]{1,0:T(8,128)(2,1)}, bf16[1024,256]{1,0:T(8,128)(2,1)S(1)}, u32[]{:S(2)}) copy-start(bf16[1024,256]{1,0:T(8,128)(2,1)S(1)} %collective-permute-done.19.refs_0_.refs_10_) | copy-start | bytes 1572868
  95.2 3.5 %copy-start.4 = (bf16[1024,256]{1,0:T(8,128)(2,1)}, bf16[1024,256]{1,0:T(8,128)(2,1)S(1)}, u32[]{:S(2)}) copy-start(bf16[1024,256]{1,0:T(8,128)(2,1)S(1)} %collective-permute-done.20.refs_2_.refs_12_) | copy-start | bytes 1572868
  95.2 2.7 %collective-permute-start.21 = (bf16[1024,256]{1,0:T(8,128)(2,1)S(1)}, bf16[1024,256]{1,0:T(8,128)(2,1)S(1)}, u32[]{:S(2)}, u32[]{:S(2)}) collective-permute-start(bf16[1024,256]{1,0:T(8,128)(2,1)S(1)} %collective-permute-done.19.refs_0_.refs_10_), channel_id=1, source_target_pairs={{0,1},{1,0},{2,3},{3,2},{4,5},{5,4},{6,7},{7,6},{8,9},{9,8},{10,11... | collective-permute-start | bytes 1572872 | tf_op jit(solution)/shard_map/ppermute | solution.py:315
  96.4 2.3 %collective-permute-start.22 = (bf16[1024,256]{1,0:T(8,128)(2,1)S(1)}, bf16[1024,256]{1,0:T(8,128)(2,1)S(1)}, u32[]{:S(2)}, u32[]{:S(2)}) collective-permute-start(bf16[1024,256]{1,0:T(8,128)(2,1)S(1)} %collective-permute-done.20.refs_2_.refs_12_), channel_id=1, source_target_pairs={{0,1},{1,0},{2,3},{3,2},{4,5},{5,4},{6,7},{7,6},{8,9},{9,8},{10,11... | collective-permute-start | bytes 1572872 | tf_op jit(solution)/shard_map/ppermute | solution.py:315
  96.4 10.3 %collective-permute-start.23 = (bf16[512,256]{1,0:T(8,128)(2,1)S(1)}, bf16[512,256]{1,0:T(8,128)(2,1)S(1)}, u32[]{:S(2)}, u32[]{:S(2)}) collective-permute-start(bf16[512,256]{1,0:T(8,128)(2,1)S(1)} %slice.26), channel_id=1, source_target_pairs={{0,4},{4,8},{8,12},{12,14},{14,10},{10,6},{6,2},{2,0},{1,5},{5,9},... | collective-permute-start | bytes 786440 | tf_op jit(solution)/shard_map/ppermute | solution.py:316
  97.7 9.1 %collective-permute-start.24 = (bf16[512,256]{1,0:T(8,128)(2,1)S(1)}, bf16[512,256]{1,0:T(8,128)(2,1)}, u32[]{:S(2)}, u32[]{:S(2)}) collective-permute-start(bf16[512,256]{1,0:T(8,128)(2,1)S(1)} %slice.27), channel_id=1, source_target_pairs={{4,0},{8,4},{12,8},{14,12},{10,14},{6,10},{2,6},{0,2},{5,1},{9,5},... | collective-permute-start | bytes 786440 | tf_op jit(solution)/shard_map/ppermute | solution.py:317
  98.0 0.8 copy-start.13
  98.7 0.8 copy-start.14
  106.8 2.4 %copy-start.16 = (bf16[512,256]{1,0:T(8,128)(2,1)}, bf16[512,256]{1,0:T(8,128)(2,1)S(1)}, u32[]{:S(2)}) copy-start(bf16[512,256]{1,0:T(8,128)(2,1)S(1)} %collective-permute-done.23.refs_14_.refs_0_) | copy-start | bytes 786436
  106.8 1.8 collective-permute-start.25
  107.5 1.7 collective-permute-start.26
  108.6 0.7 copy-start.17
  109.2 0.7 copy-start.18
  115.1 36.8 %collective-permute-start.27 = (bf16[64,2048]{1,0:T(8,128)(2,1)}, bf16[64,2048]{1,0:T(8,128)(2,1)S(1)}, u32[]{:S(2)}, u32[]{:S(2)}) collective-permute-start(bf16[64,2048]{1,0:T(8,128)(2,1)} %get-tuple-element.59), channel_id=1, source_target_pairs={{0,8},{1,9},{2,10},{3,11},{4,12},{5,13},{6,14},{7,15},{8,0},{9,1},... | collective-permute-start | bytes 786440 | tf_op jit(solution)/shard_map/ppermute | solution.py:344
  116.3 42.9 %collective-permute-start.28 = (bf16[64,2048]{1,0:T(8,128)(2,1)}, bf16[64,2048]{1,0:T(8,128)(2,1)S(1)}, u32[]{:S(2)}, u32[]{:S(2)}) collective-permute-start(bf16[64,2048]{1,0:T(8,128)(2,1)} %get-tuple-element.61), channel_id=1, source_target_pairs={{0,9},{1,10},{2,11},{3,8},{4,13},{5,14},{6,15},{7,12},{8,1},{9,2},... | collective-permute-start | bytes 786440 | tf_op jit(solution)/shard_map/ppermute | solution.py:344
  117.9 45.7 %collective-permute-start.29 = (bf16[64,2048]{1,0:T(8,128)(2,1)}, bf16[64,2048]{1,0:T(8,128)(2,1)S(1)}, u32[]{:S(2)}, u32[]{:S(2)}) collective-permute-start(bf16[64,2048]{1,0:T(8,128)(2,1)} %get-tuple-element.64), channel_id=1, source_target_pairs={{0,10},{1,11},{2,8},{3,9},{4,14},{5,15},{6,12},{7,13},{8,2},{9,3},... | collective-permute-start | bytes 786440 | tf_op jit(solution)/shard_map/ppermute | solution.py:344
  120.1 54.9 %collective-permute-start.30 = (bf16[64,2048]{1,0:T(8,128)(2,1)}, bf16[64,2048]{1,0:T(8,128)(2,1)S(1)}, u32[]{:S(2)}, u32[]{:S(2)}) collective-permute-start(bf16[64,2048]{1,0:T(8,128)(2,1)} %get-tuple-element.67), channel_id=1, source_target_pairs={{0,11},{1,8},{2,9},{3,10},{4,15},{5,12},{6,13},{7,14},{8,3},{9,0},... | collective-permute-start | bytes 786440 | tf_op jit(solution)/shard_map/ppermute | solution.py:344
  133.0 42.0 %collective-permute-start.31 = (bf16[64,2048]{1,0:T(8,128)(2,1)S(1)}, bf16[64,2048]{1,0:T(8,128)(2,1)S(1)}, u32[]{:S(2)}, u32[]{:S(2)}) collective-permute-start(bf16[64,2048]{1,0:T(8,128)(2,1)S(1)} %get-tuple-element.94), channel_id=1, source_target_pairs={{0,4},{1,5},{2,6},{3,7},{4,8},{5,9},{6,10},{7,11},{8,12},{9,13},{1... | collective-permute-start | bytes 786440 | tf_op jit(solution)/shard_map/ppermute | solution.py:344
  150.0 1.6 copy-start.15
  151.9 28.8 %collective-permute-start.32 = (bf16[64,2048]{1,0:T(8,128)(2,1)S(1)}, bf16[64,2048]{1,0:T(8,128)(2,1)S(1)}, u32[]{:S(2)}, u32[]{:S(2)}) collective-permute-start(bf16[64,2048]{1,0:T(8,128)(2,1)S(1)} %get-tuple-element.62), channel_id=1, source_target_pairs={{0,12},{1,13},{2,14},{3,15},{4,0},{5,1},{6,2},{7,3},{8,4},{9,5},{1... | collective-permute-start | bytes 786440 | tf_op jit(solution)/shard_map/ppermute | solution.py:344
  159.1 21.7 %collective-permute-start.33 = (bf16[64,2048]{1,0:T(8,128)(2,1)S(1)}, bf16[64,2048]{1,0:T(8,128)(2,1)S(1)}, u32[]{:S(2)}, u32[]{:S(2)}) collective-permute-start(bf16[64,2048]{1,0:T(8,128)(2,1)S(1)} %get-tuple-element.65), channel_id=1, source_target_pairs={{0,1},{1,2},{2,3},{3,0},{4,5},{5,6},{6,7},{7,4},{8,9},{9,10},{10,1... | collective-permute-start | bytes 786440 | tf_op jit(solution)/shard_map/ppermute | solution.py:344
  163.6 21.2 %collective-permute-start.34 = (bf16[64,2048]{1,0:T(8,128)(2,1)S(1)}, bf16[64,2048]{1,0:T(8,128)(2,1)S(1)}, u32[]{:S(2)}, u32[]{:S(2)}) collective-permute-start(bf16[64,2048]{1,0:T(8,128)(2,1)S(1)} %get-tuple-element.68), channel_id=1, source_target_pairs={{0,5},{1,6},{2,7},{3,4},{4,9},{5,10},{6,11},{7,8},{8,13},{9,14},{1... | collective-permute-start | bytes 786440 | tf_op jit(solution)/shard_map/ppermute | solution.py:344
  175.0 17.1 %collective-permute-start.35 = (bf16[64,2048]{1,0:T(8,128)(2,1)S(1)}, bf16[64,2048]{1,0:T(8,128)(2,1)S(1)}, u32[]{:S(2)}, u32[]{:S(2)}) collective-permute-start(bf16[64,2048]{1,0:T(8,128)(2,1)S(1)} %get-tuple-element.70), channel_id=1, source_target_pairs={{0,13},{1,14},{2,15},{3,12},{4,1},{5,2},{6,3},{7,0},{8,5},{9,6},{1... | collective-permute-start | bytes 786440 | tf_op jit(solution)/shard_map/ppermute | solution.py:344
  175.0 17.1 %collective-permute-start.36 = (bf16[64,2048]{1,0:T(8,128)(2,1)S(1)}, bf16[64,2048]{1,0:T(8,128)(2,1)S(1)}, u32[]{:S(2)}, u32[]{:S(2)}) collective-permute-start(bf16[64,2048]{1,0:T(8,128)(2,1)S(1)} %get-tuple-element.72), channel_id=1, source_target_pairs={{0,2},{1,3},{2,0},{3,1},{4,6},{5,7},{6,4},{7,5},{8,10},{9,11},{10,... | collective-permute-start | bytes 786440 | tf_op jit(solution)/shard_map/ppermute | solution.py:344
  180.6 14.1 %collective-permute-start.37 = (bf16[64,2048]{1,0:T(8,128)(2,1)S(1)}, bf16[64,2048]{1,0:T(8,128)(2,1)S(1)}, u32[]{:S(2)}, u32[]{:S(2)}) collective-permute-start(bf16[64,2048]{1,0:T(8,128)(2,1)S(1)} %get-tuple-element.74), channel_id=1, source_target_pairs={{0,6},{1,7},{2,4},{3,5},{4,10},{5,11},{6,8},{7,9},{8,14},{9,15},{1... | collective-permute-start | bytes 786440 | tf_op jit(solution)/shard_map/ppermute | solution.py:344
  180.8 16.5 %collective-permute-start.38 = (bf16[64,2048]{1,0:T(8,128)(2,1)S(1)}, bf16[64,2048]{1,0:T(8,128)(2,1)S(1)}, u32[]{:S(2)}, u32[]{:S(2)}) collective-permute-start(bf16[64,2048]{1,0:T(8,128)(2,1)S(1)} %get-tuple-element.76), channel_id=1, source_target_pairs={{0,14},{1,15},{2,12},{3,13},{4,2},{5,3},{6,0},{7,1},{8,6},{9,7},{1... | collective-permute-start | bytes 786440 | tf_op jit(solution)/shard_map/ppermute | solution.py:344
  184.8 16.7 %collective-permute-start.39 = (bf16[64,2048]{1,0:T(8,128)(2,1)S(1)}, bf16[64,2048]{1,0:T(8,128)(2,1)S(1)}, u32[]{:S(2)}, u32[]{:S(2)}) collective-permute-start(bf16[64,2048]{1,0:T(8,128)(2,1)S(1)} %get-tuple-element.78), channel_id=1, source_target_pairs={{0,3},{1,0},{2,1},{3,2},{4,7},{5,4},{6,5},{7,6},{8,11},{9,8},{10,9... | collective-permute-start | bytes 786440 | tf_op jit(solution)/shard_map/ppermute | solution.py:344
  192.1 11.6 %collective-permute-start.40 = (bf16[64,2048]{1,0:T(8,128)(2,1)S(1)}, bf16[64,2048]{1,0:T(8,128)(2,1)S(1)}, u32[]{:S(2)}, u32[]{:S(2)}) collective-permute-start(bf16[64,2048]{1,0:T(8,128)(2,1)S(1)} %get-tuple-element.80), channel_id=1, source_target_pairs={{0,7},{1,4},{2,5},{3,6},{4,11},{5,8},{6,9},{7,10},{8,15},{9,12},{1... | collective-permute-start | bytes 786440 | tf_op jit(solution)/shard_map/ppermute | solution.py:344
  192.1 16.3 %collective-permute-start.41 = (bf16[64,2048]{1,0:T(8,128)(2,1)S(1)}, bf16[64,2048]{1,0:T(8,128)(2,1)S(1)}, u32[]{:S(2)}, u32[]{:S(2)}) collective-permute-start(bf16[64,2048]{1,0:T(8,128)(2,1)S(1)} %get-tuple-element.82), channel_id=1, source_target_pairs={{0,15},{1,12},{2,13},{3,14},{4,3},{5,0},{6,1},{7,2},{8,7},{9,4},{1... | collective-permute-start | bytes 786440 | tf_op jit(solution)/shard_map/ppermute | solution.py:344
  203.7 4.7 %copy-start.2 = (bf16[64,32768]{1,0:T(8,128)(2,1)}, bf16[64,32768]{1,0:T(8,128)(2,1)S(1)}, u32[]{:S(2)}) copy-start(bf16[64,32768]{1,0:T(8,128)(2,1)S(1)} %constant_dynamic-update-slice_fusion.10) | copy-start | bytes 12582916

commit v8 on v7

--- a/solution.py
+++ b/solution.py
@@ -182,7 +182,7 @@
     columns = train_feats.shape[0]
     count = len(pieces) // 2 if last else len(pieces)
     depth = count * pieces[0].shape[1]
-    tile = 512
+    tile = 1024
     group = span // owned
     anywhere, inside = pl.BlockSpec(memory_space=pl.ANY), pl.BlockSpec(memory_space=pltpu.VMEM)
     in_specs = [pl.BlockSpec(memory_space=pltpu.SMEM)] + [anywhere] * (len(pieces) + 1)

time: 210 us -> 209 us (level)
  Pallas kernels: 50 us -> 47.9 us
  transfers between devices with their start and end apart: 42 -> 42, of which waited for: 22 -> 24; matrix products, arithmetic and copies ran while one was open for 4% -> 4% of each run, Pallas kernels for 21% -> 21%
where the time goes in v8:
time: 209 us; the launch traced here: 208 us
  waiting for transfers between devices  98.4 us (47%)
  Pallas kernels  47.9 us (23%)
  starting transfers between devices  46.9 us (22%)
  local copies, waits for them, and re-layouts  8.43 us (4%)
  matrix products  4.61 us (2%)
    ppermute x6, waiting for transfers between devices, per_device(): forward = lax.ppermute(forward, 'rows', ahead)  46 us
    ppermute x15, waiting for transfers between devices, per_device(): going.append(lax.ppermute(block, ('rows', 'feat'), pairs))  43.4 us
    pallas_call x2, Pallas kernels, group_scores(): pl.pallas_call(functools.partial(tile_rows, owners, skip, tuple(range(tar...  27.1 us
    pallas_call x3, Pallas kernels, group_part(): pl.pallas_call(functools.partial(some_columns, count, base, group_at, las...  20.8 us
    ppermute x15, starting transfers between devices, per_device(): going.append(lax.ppermute(block, ('rows', 'feat'), pairs))  19.2 us
    ppermute x6, starting transfers between devices, per_device(): forward = lax.ppermute(forward, 'rows', ahead)  8.15 us
    ppermute x6, starting transfers between devices, per_device(): near += [block, lax.ppermute(block, 'feat', swap)]  5.1 us
    dot_general x8, matrix products, product(): partial = jnp.dot(block, kernel, preferred_element_type=jnp.float32)  4.61 us
  transfers between devices with their start and end apart: 42, of which 24 were waited for; matrix products, arithmetic and copies ran while one was open for 4% of the time, Pallas kernels for 21%

profile of v8, /device:TPU:1, one launch (start us, length us, event | category | flops | bytes accessed | tf_op | source)
XLA Modules:
  0.0 208.1 jit_solution(10823629442226712553)
XLA Ops:
  0.0 2.1 %collective-permute-start = (bf16[128,2048]{1,0:T(8,128)(2,1)}, bf16[128,2048]{1,0:T(8,128)(2,1)S(1)}, u32[]{:S(2)}, u32[]{:S(2)}) collective-permute-start(bf16[128,2048]{1,0:T(8,128)(2,1)} %param.3), channel_id=1, source_target_pairs={{0,4},{4,8},{8,12},{12,14},{14,10},{10,6},{6,2},{2,0},{1,5},{5,9},... | collective-permute-start | bytes 1572872 | tf_op jit(solution)/shard_map/ppermute | solution.py:282
  2.1 0.7 stack.87.where
  2.8 1.5 fusion.6
  4.5 9.4 %collective-permute-done = bf16[128,2048]{1,0:T(8,128)(2,1)S(1)} collective-permute-done((bf16[128,2048]{1,0:T(8,128)(2,1)}, bf16[128,2048]{1,0:T(8,128)(2,1)S(1)}, u32[]{:S(2)}, u32[]{:S(2)}) %collective-permute-start) | collective-permute-done | bytes 524320 | tf_op jit(solution)/shard_map/ppermute | solution.py:282
  13.9 1.2 collective-permute-start.1
  16.4 9.7 %collective-permute-done.1 = bf16[128,2048]{1,0:T(8,128)(2,1)S(1)} collective-permute-done((bf16[128,2048]{1,0:T(8,128)(2,1)S(1)}, bf16[128,2048]{1,0:T(8,128)(2,1)S(1)}, u32[]{:S(2)}, u32[]{:S(2)}) %collective-permute-start.1) | collective-permute-done | bytes 524320 | tf_op jit(solution)/shard_map/ppermute | solution.py:282
  26.1 0.9 collective-permute-start.2
  27.5 0.6 collective-permute-start.6
  28.6 2.8 %collective-permute-start.8 = (f32[1024,256]{1,0:T(8,128)S(1)}, f32[1024,256]{1,0:T(8,128)S(1)}, u32[]{:S(2)}, u32[]{:S(2)}) collective-permute-start(f32[1024,256]{1,0:T(8,128)S(1)} %get-tuple-element.101), channel_id=1, source_target_pairs={{0,1},{1,0},{2,3},{3,2},{4,5},{5,4},{6,7},{7,6},{8,9},{9,8},{10,11... | collective-permute-start | bytes 3145736 | tf_op jit(solution)/shard_map/ppermute | solution.py:295
  31.4 6.0 %collective-permute-done.2 = bf16[128,2048]{1,0:T(8,128)(2,1)S(1)} collective-permute-done((bf16[128,2048]{1,0:T(8,128)(2,1)S(1)}, bf16[128,2048]{1,0:T(8,128)(2,1)S(1)}, u32[]{:S(2)}, u32[]{:S(2)}) %collective-permute-start.2) | collective-permute-done | bytes 524320 | tf_op jit(solution)/shard_map/ppermute | solution.py:282
  37.4 0.6 collective-permute-start.3
  38.2 1.0 collective-permute-start.7
  40.3 2.4 %collective-permute-done.3 = bf16[64,2048]{1,0:T(8,128)(2,1)S(1)} collective-permute-done((bf16[64,2048]{1,0:T(8,128)(2,1)S(1)}, bf16[64,2048]{1,0:T(8,128)(2,1)S(1)}, u32[]{:S(2)}, u32[]{:S(2)}) %collective-permute-start.3) | collective-permute-done | bytes 262176 | tf_op jit(solution)/shard_map/ppermute | solution.py:287
  42.7 1.6 collective-permute-done.7
  44.8 4.5 %collective-permute-start.9 = (f32[384,256]{1,0:T(8,128)S(1)}, f32[384,256]{1,0:T(8,128)}, u32[]{:S(2)}, u32[]{:S(2)}) collective-permute-start(f32[384,256]{1,0:T(8,128)S(1)} %pad_maximum_fusion), channel_id=1, source_target_pairs={{0,1},{1,0},{2,3},{3,2},{4,5},{5,4},{6,7},{7,6},{8,9},{9,8},{10,11... | collective-permute-start | bytes 1179656 | tf_op jit(solution)/shard_map/ppermute | solution.py:299
  49.3 1.5 collective-permute-done.9
  50.8 1.0 fusion.4
  51.9 1.3 collective-permute-start.11
  53.4 11.7 %collective-permute-done.11.refs_2_ = bf16[1024,256]{1,0:T(8,128)(2,1)S(1)} collective-permute-done((bf16[1024,256]{1,0:T(8,128)(2,1)S(1)}, bf16[1024,256]{1,0:T(8,128)(2,1)S(1)}, u32[]{:S(2)}, u32[]{:S(2)}) %collective-permute-start.11) | collective-permute-done | bytes 524320 | tf_op jit(solution)/shard_map/ppermute | solution.py:307
  65.1 1.3 collective-permute-start.15
  66.6 1.8 collective-permute-start.10
  68.3 0.5 collective-permute-start.14
  68.8 8.5 %collective-permute-done.15.refs_6_ = bf16[1024,256]{1,0:T(8,128)(2,1)S(1)} collective-permute-done((bf16[1024,256]{1,0:T(8,128)(2,1)S(1)}, bf16[1024,256]{1,0:T(8,128)(2,1)S(1)}, u32[]{:S(2)}, u32[]{:S(2)}) %collective-permute-start.15) | collective-permute-done | bytes 524320 | tf_op jit(solution)/shard_map/ppermute | solution.py:307
  77.3 2.1 %collective-permute-start.16 = (bf16[1024,256]{1,0:T(8,128)(2,1)S(1)}, bf16[1024,256]{1,0:T(8,128)(2,1)S(1)}, u32[]{:S(2)}, u32[]{:S(2)}) collective-permute-start(bf16[1024,256]{1,0:T(8,128)(2,1)S(1)} %collective-permute-done.15.refs_6_), channel_id=1, source_target_pairs={{0,1},{1,0},{2,3},{3,2},{4,5},{5,4},{6,7},{7,6},{8,9},{9,8},{10,11... | collective-permute-start | bytes 1572872 | tf_op jit(solution)/shard_map/ppermute | solution.py:315
  79.4 1.3 collective-permute-start.18
  80.7 1.3 collective-permute-start.19
  82.2 0.6 copy-done.10
  83.0 0.8 copy-done.12
  83.9 9.6 %shard_map.37 = (f32[256,2048]{1,0:T(8,128)}, f32[256,128]{1,0:T(8,128)}) custom-call(s32[21]{0:T(128)} %stack.87.where, bf16[1024,256]{1,0:T(8,128)(2,1)} %copy-done.1, bf16[1024,256]{1,0:T(8,128)(2,1)} %copy-done.9, bf16[1024,256]{1,0:T(8,128)(2,1)} %copy-done.5, bf16[1024,256]{1,0:T(8,128)(2,1)} %copy-done.10, bf16[1024,256]{1,0:T(8,128)(2,1)} %copy-done.6, ...), custom_call_target="tpu_custom_call" | custom-call | flops 2684354560 | bytes 10485760 | tf_op jit(solution)/shard_map/pallas_call | solution.py:205
  93.5 0.8 collective-permute-done.19.refs_0_.refs_10_
  94.2 1.0 collective-permute-done.20.refs_2_.refs_12_
  95.2 1.2 collective-permute-start.21
  96.4 1.3 collective-permute-start.23
  98.0 0.7 collective-permute-done.22.refs_3_.refs_13_
  98.8 0.7 copy-done.14
  99.5 6.2 %shard_map.38 = (f32[256,2048]{1,0:T(8,128)}, f32[256,128]{1,0:T(8,128)}) custom-call(s32[21]{0:T(128)} %stack.87.where, bf16[1024,256]{1,0:T(8,128)(2,1)} %copy-done.3, bf16[1024,256]{1,0:T(8,128)(2,1)} %copy-done.13, bf16[1024,256]{1,0:T(8,128)(2,1)} %copy-done.4, bf16[1024,256]{1,0:T(8,128)(2,1)} %copy-done.14, bf16[2048,4096]{1,0:T(8,128)(2,1)} %refs_18_.3, ...), custom_call_target="tpu_custom_call" | custom-call | flops 1073741824 | bytes 4194304 | tf_op jit(solution)/shard_map/pallas_call | solution.py:205
  105.7 0.8 collective-permute-start.25
  106.6 1.5 collective-permute-done.25.refs_15_.refs_1_
  108.3 0.5 copy-done.17
  109.0 5.0 %shard_map.40 = (bf16[64,2048]{1,0:T(8,128)(2,1)}, bf16[64,2048]{1,0:T(8,128)(2,1)}, bf16[64,2048]{1,0:T(8,128)(2,1)}, bf16[64,2048]{1,0:T(8,128)(2,1)}) custom-call(s32[21]{0:T(128)} %stack.87.where, bf16[512,256]{1,0:T(8,128)(2,1)} %copy-done.16, bf16[512,256]{1,0:T(8,128)(2,1)} %copy-done.17, bf16[512,256]{1,0:T(8,128)(2,1)} %collective-permute-done.24.refs_16_.refs_2_, ...), custom_call_target="tpu_custom_call" | custom-call | flops 536870912 | bytes 2097152 | tf_op jit(solution)/shard_map/pallas_call | solution.py:205
  114.0 1.0 collective-permute-start.27
  115.0 1.9 collective-permute-start.28
  116.9 1.9 collective-permute-start.29
  118.8 0.5 collective-permute-start.30
  119.3 11.4 %shard_map.41 = bf16[256,2048]{1,0:T(8,128)(2,1)} custom-call(s32[21]{0:T(128)} %stack.87.where, bf16[1024,256]{1,0:T(8,128)(2,1)} %copy-done.1, bf16[1024,256]{1,0:T(8,128)(2,1)} %copy-done.9, bf16[1024,256]{1,0:T(8,128)(2,1)} %copy-done.5, bf16[1024,256]{1,0:T(8,128)(2,1)} %copy-done.10, bf16[1024,256]{1,0:T(8,128)(2,1)} %copy-done.6, ...), custom_call_target="tpu_custom_call" | custom-call | flops 4294967296 | bytes 16777216 | tf_op jit(solution)/shard_map/pallas_call | solution.py:222
  130.7 1.3 constant_dynamic-slice_fusion.1
  132.0 1.1 collective-permute-start.31
  133.1 15.7 %shard_map.39 = bf16[512,2048]{1,0:T(8,128)(2,1)} custom-call(s32[21]{0:T(128)} %stack.87.where, bf16[1024,256]{1,0:T(8,128)(2,1)} %copy-done.1, bf16[1024,256]{1,0:T(8,128)(2,1)} %copy-done.9, bf16[1024,256]{1,0:T(8,128)(2,1)} %copy-done.5, bf16[1024,256]{1,0:T(8,128)(2,1)} %copy-done.10, bf16[1024,256]{1,0:T(8,128)(2,1)} %copy-done.6, ...), custom_call_target="tpu_custom_call" | custom-call | flops 8589934592 | bytes 16777216 | tf_op jit(solution)/shard_map/pallas_call | solution.py:222
  149.1 1.3 copy-done.15
  150.8 2.9 %collective-permute-start.32 = (bf16[64,2048]{1,0:T(8,128)(2,1)S(1)}, bf16[64,2048]{1,0:T(8,128)(2,1)S(1)}, u32[]{:S(2)}, u32[]{:S(2)}) collective-permute-start(bf16[64,2048]{1,0:T(8,128)(2,1)S(1)} %get-tuple-element.62), channel_id=1, source_target_pairs={{0,12},{1,13},{2,14},{3,15},{4,0},{5,1},{6,2},{7,3},{8,4},{9,5},{1... | collective-permute-start | bytes 786440 | tf_op jit(solution)/shard_map/ppermute | solution.py:344
  153.7 4.3 %collective-permute-done.28 = bf16[64,2048]{1,0:T(8,128)(2,1)S(1)} collective-permute-done((bf16[64,2048]{1,0:T(8,128)(2,1)}, bf16[64,2048]{1,0:T(8,128)(2,1)S(1)}, u32[]{:S(2)}, u32[]{:S(2)}) %collective-permute-start.28) | collective-permute-done | bytes 262176 | tf_op jit(solution)/shard_map/ppermute | solution.py:344
  158.1 4.6 %collective-permute-done.29 = bf16[64,2048]{1,0:T(8,128)(2,1)S(1)} collective-permute-done((bf16[64,2048]{1,0:T(8,128)(2,1)}, bf16[64,2048]{1,0:T(8,128)(2,1)S(1)}, u32[]{:S(2)}, u32[]{:S(2)}) %collective-permute-start.29) | collective-permute-done | bytes 262176 | tf_op jit(solution)/shard_map/ppermute | solution.py:344
  162.6 11.3 %collective-permute-done.30 = bf16[64,2048]{1,0:T(8,128)(2,1)S(1)} collective-permute-done((bf16[64,2048]{1,0:T(8,128)(2,1)}, bf16[64,2048]{1,0:T(8,128)(2,1)S(1)}, u32[]{:S(2)}, u32[]{:S(2)}) %collective-permute-start.30) | collective-permute-done | bytes 262176 | tf_op jit(solution)/shard_map/ppermute | solution.py:344
  174.0 2.0 collective-permute-start.36
  176.1 3.5 %collective-permute-done.32 = bf16[64,2048]{1,0:T(8,128)(2,1)S(1)} collective-permute-done((bf16[64,2048]{1,0:T(8,128)(2,1)S(1)}, bf16[64,2048]{1,0:T(8,128)(2,1)S(1)}, u32[]{:S(2)}, u32[]{:S(2)}) %collective-permute-start.32) | collective-permute-done | bytes 262176 | tf_op jit(solution)/shard_map/ppermute | solution.py:344
  179.8 3.9 %collective-permute-start.38 = (bf16[64,2048]{1,0:T(8,128)(2,1)S(1)}, bf16[64,2048]{1,0:T(8,128)(2,1)S(1)}, u32[]{:S(2)}, u32[]{:S(2)}) collective-permute-start(bf16[64,2048]{1,0:T(8,128)(2,1)S(1)} %get-tuple-element.76), channel_id=1, source_target_pairs={{0,14},{1,15},{2,12},{3,13},{4,2},{5,3},{6,0},{7,1},{8,6},{9,7},{1... | collective-permute-start | bytes 786440 | tf_op jit(solution)/shard_map/ppermute | solution.py:344
  183.8 1.1 collective-permute-start.39
  184.9 6.1 %collective-permute-done.35 = bf16[64,2048]{1,0:T(8,128)(2,1)S(1)} collective-permute-done((bf16[64,2048]{1,0:T(8,128)(2,1)S(1)}, bf16[64,2048]{1,0:T(8,128)(2,1)S(1)}, u32[]{:S(2)}, u32[]{:S(2)}) %collective-permute-start.35) | collective-permute-done | bytes 262176 | tf_op jit(solution)/shard_map/ppermute | solution.py:344
  191.0 2.6 %collective-permute-start.41 = (bf16[64,2048]{1,0:T(8,128)(2,1)S(1)}, bf16[64,2048]{1,0:T(8,128)(2,1)S(1)}, u32[]{:S(2)}, u32[]{:S(2)}) collective-permute-start(bf16[64,2048]{1,0:T(8,128)(2,1)S(1)} %get-tuple-element.82), channel_id=1, source_target_pairs={{0,15},{1,12},{2,13},{3,14},{4,3},{5,0},{6,1},{7,2},{8,7},{9,4},{1... | collective-permute-start | bytes 786440 | tf_op jit(solution)/shard_map/ppermute | solution.py:344
  193.9 2.5 %collective-permute-done.38 = bf16[64,2048]{1,0:T(8,128)(2,1)S(1)} collective-permute-done((bf16[64,2048]{1,0:T(8,128)(2,1)S(1)}, bf16[64,2048]{1,0:T(8,128)(2,1)S(1)}, u32[]{:S(2)}, u32[]{:S(2)}) %collective-permute-start.38) | collective-permute-done | bytes 262176 | tf_op jit(solution)/shard_map/ppermute | solution.py:344
  196.3 4.2 %collective-permute-done.39 = bf16[64,2048]{1,0:T(8,128)(2,1)S(1)} collective-permute-done((bf16[64,2048]{1,0:T(8,128)(2,1)S(1)}, bf16[64,2048]{1,0:T(8,128)(2,1)S(1)}, u32[]{:S(2)}, u32[]{:S(2)}) %collective-permute-start.39) | collective-permute-done | bytes 262176 | tf_op jit(solution)/shard_map/ppermute | solution.py:344
  200.6 2.0 collective-permute-done.40
  202.7 4.7 %collective-permute-done.41 = bf16[64,2048]{1,0:T(8,128)(2,1)S(1)} collective-permute-done((bf16[64,2048]{1,0:T(8,128)(2,1)S(1)}, bf16[64,2048]{1,0:T(8,128)(2,1)S(1)}, u32[]{:S(2)}, u32[]{:S(2)}) %collective-permute-start.41) | collective-permute-done | bytes 262176 | tf_op jit(solution)/shard_map/ppermute | solution.py:344
  207.4 0.7 constant_dynamic-update-slice_fusion.9
  (111 shorter events, 7.1 us)
Async XLA Ops:
  0.0 2.8 %copy-start = (bf16[2048,512]{1,0:T(8,128)(2,1)S(1)}, bf16[2048,512]{1,0:T(8,128)(2,1)}, u32[]{:S(2)}) copy-start(bf16[2048,512]{1,0:T(8,128)(2,1)} %param.4) | copy-start | bytes 6291460
  0.0 13.9 %collective-permute-start = (bf16[128,2048]{1,0:T(8,128)(2,1)}, bf16[128,2048]{1,0:T(8,128)(2,1)S(1)}, u32[]{:S(2)}, u32[]{:S(2)}) collective-permute-start(bf16[128,2048]{1,0:T(8,128)(2,1)} %param.3), channel_id=1, source_target_pairs={{0,4},{4,8},{8,12},{12,14},{14,10},{10,6},{6,2},{2,0},{1,5},{5,9},... | collective-permute-start | bytes 1572872 | tf_op jit(solution)/shard_map/ppermute | solution.py:282
  2.1 13.5 %collective-permute-start.4 = (bf16[128,2048]{1,0:T(8,128)(2,1)}, bf16[128,2048]{1,0:T(8,128)(2,1)S(1)}, u32[]{:S(2)}, u32[]{:S(2)}) collective-permute-start(bf16[128,2048]{1,0:T(8,128)(2,1)} %param.3), channel_id=1, source_target_pairs={{4,0},{8,4},{12,8},{14,12},{10,14},{6,10},{2,6},{0,2},{5,1},{9,5},... | collective-permute-start | bytes 1572872 | tf_op jit(solution)/shard_map/ppermute | solution.py:283
  13.9 12.2 %collective-permute-start.1 = (bf16[128,2048]{1,0:T(8,128)(2,1)S(1)}, bf16[128,2048]{1,0:T(8,128)(2,1)S(1)}, u32[]{:S(2)}, u32[]{:S(2)}) collective-permute-start(bf16[128,2048]{1,0:T(8,128)(2,1)S(1)} %collective-permute-done), channel_id=1, source_target_pairs={{0,4},{4,8},{8,12},{12,14},{14,10},{10,6},{6,2},{2,0},{1,5},{5,9},... | collective-permute-start | bytes 1572872 | tf_op jit(solution)/shard_map/ppermute | solution.py:282
  15.6 11.9 %collective-permute-start.5 = (bf16[128,2048]{1,0:T(8,128)(2,1)S(1)}, bf16[128,2048]{1,0:T(8,128)(2,1)S(1)}, u32[]{:S(2)}, u32[]{:S(2)}) collective-permute-start(bf16[128,2048]{1,0:T(8,128)(2,1)S(1)} %collective-permute-done.4), channel_id=1, source_target_pairs={{4,0},{8,4},{12,8},{14,12},{10,14},{6,10},{2,6},{0,2},{5,1},{9,5},... | collective-permute-start | bytes 1572872 | tf_op jit(solution)/shard_map/ppermute | solution.py:283
  26.1 11.3 %collective-permute-start.2 = (bf16[128,2048]{1,0:T(8,128)(2,1)S(1)}, bf16[128,2048]{1,0:T(8,128)(2,1)S(1)}, u32[]{:S(2)}, u32[]{:S(2)}) collective-permute-start(bf16[128,2048]{1,0:T(8,128)(2,1)S(1)} %collective-permute-done.1), channel_id=1, source_target_pairs={{0,4},{4,8},{8,12},{12,14},{14,10},{10,6},{6,2},{2,0},{1,5},{5,9},... | collective-permute-start | bytes 1572872 | tf_op jit(solution)/shard_map/ppermute | solution.py:282
  27.5 10.7 %collective-permute-start.6 = (bf16[128,2048]{1,0:T(8,128)(2,1)S(1)}, bf16[128,2048]{1,0:T(8,128)(2,1)S(1)}, u32[]{:S(2)}, u32[]{:S(2)}) collective-permute-start(bf16[128,2048]{1,0:T(8,128)(2,1)S(1)} %collective-permute-done.5), channel_id=1, source_target_pairs={{4,0},{8,4},{12,8},{14,12},{10,14},{6,10},{2,6},{0,2},{5,1},{9,5},... | collective-permute-start | bytes 1572872 | tf_op jit(solution)/shard_map/ppermute | solution.py:283
  28.6 11.5 %collective-permute-start.8 = (f32[1024,256]{1,0:T(8,128)S(1)}, f32[1024,256]{1,0:T(8,128)S(1)}, u32[]{:S(2)}, u32[]{:S(2)}) collective-permute-start(f32[1024,256]{1,0:T(8,128)S(1)} %get-tuple-element.101), channel_id=1, source_target_pairs={{0,1},{1,0},{2,3},{3,2},{4,5},{5,4},{6,7},{7,6},{8,9},{9,8},{10,11... | collective-permute-start | bytes 3145736 | tf_op jit(solution)/shard_map/ppermute | solution.py:295
  37.4 5.3 %collective-permute-start.3 = (bf16[64,2048]{1,0:T(8,128)(2,1)S(1)}, bf16[64,2048]{1,0:T(8,128)(2,1)S(1)}, u32[]{:S(2)}, u32[]{:S(2)}) collective-permute-start(bf16[64,2048]{1,0:T(8,128)(2,1)S(1)} %slice.28), channel_id=1, source_target_pairs={{0,4},{4,8},{8,12},{12,14},{14,10},{10,6},{6,2},{2,0},{1,5},{5,9},... | collective-permute-start | bytes 786440 | tf_op jit(solution)/shard_map/ppermute | solution.py:287
  38.2 6.1 %collective-permute-start.7 = (bf16[64,2048]{1,0:T(8,128)(2,1)S(1)}, bf16[64,2048]{1,0:T(8,128)(2,1)S(1)}, u32[]{:S(2)}, u32[]{:S(2)}) collective-permute-start(bf16[64,2048]{1,0:T(8,128)(2,1)S(1)} %slice.29), channel_id=1, source_target_pairs={{4,0},{8,4},{12,8},{14,12},{10,14},{6,10},{2,6},{0,2},{5,1},{9,5},... | collective-permute-start | bytes 786440 | tf_op jit(solution)/shard_map/ppermute | solution.py:288
  44.8 6.0 %collective-permute-start.9 = (f32[384,256]{1,0:T(8,128)S(1)}, f32[384,256]{1,0:T(8,128)}, u32[]{:S(2)}, u32[]{:S(2)}) collective-permute-start(f32[384,256]{1,0:T(8,128)S(1)} %pad_maximum_fusion), channel_id=1, source_target_pairs={{0,1},{1,0},{2,3},{3,2},{4,5},{5,4},{6,7},{7,6},{8,9},{9,8},{10,11... | collective-permute-start | bytes 1179656 | tf_op jit(solution)/shard_map/ppermute | solution.py:299
  51.9 31.9 %copy-start.1 = (bf16[1024,256]{1,0:T(8,128)(2,1)}, bf16[1024,256]{1,0:T(8,128)(2,1)S(1)}, u32[]{:S(2)}) copy-start(bf16[1024,256]{1,0:T(8,128)(2,1)S(1)} %slice_dynamic-update-slice_fusion.refs_0_) | copy-start | bytes 1572868
  51.9 13.2 %collective-permute-start.11 = (bf16[1024,256]{1,0:T(8,128)(2,1)S(1)}, bf16[1024,256]{1,0:T(8,128)(2,1)S(1)}, u32[]{:S(2)}, u32[]{:S(2)}) collective-permute-start(bf16[1024,256]{1,0:T(8,128)(2,1)S(1)} %slice_dynamic-update-slice_fusion.refs_0_), channel_id=1, source_target_pairs={{0,4},{4,8},{8,12},{12,14},{14,10},{10,6},{6,2},{2,0},{1,5},{5,9},... | collective-permute-start | bytes 1572872 | tf_op jit(solution)/shard_map/ppermute | solution.py:307
  53.3 13.1 %collective-permute-start.13 = (bf16[1024,256]{1,0:T(8,128)(2,1)S(1)}, bf16[1024,256]{1,0:T(8,128)(2,1)S(1)}, u32[]{:S(2)}, u32[]{:S(2)}) collective-permute-start(bf16[1024,256]{1,0:T(8,128)(2,1)S(1)} %slice_dynamic-update-slice_fusion.refs_0_), channel_id=1, source_target_pairs={{4,0},{8,4},{12,8},{14,12},{10,14},{6,10},{2,6},{0,2},{5,1},{9,5},... | collective-permute-start | bytes 1572872 | tf_op jit(solution)/shard_map/ppermute | solution.py:308
  65.1 18.7 %copy-start.5 = (bf16[1024,256]{1,0:T(8,128)(2,1)}, bf16[1024,256]{1,0:T(8,128)(2,1)S(1)}, u32[]{:S(2)}) copy-start(bf16[1024,256]{1,0:T(8,128)(2,1)S(1)} %collective-permute-done.11.refs_2_) | copy-start | bytes 1572868
  65.1 12.2 %collective-permute-start.15 = (bf16[1024,256]{1,0:T(8,128)(2,1)S(1)}, bf16[1024,256]{1,0:T(8,128)(2,1)S(1)}, u32[]{:S(2)}, u32[]{:S(2)}) collective-permute-start(bf16[1024,256]{1,0:T(8,128)(2,1)S(1)} %collective-permute-done.11.refs_2_), channel_id=1, source_target_pairs={{0,4},{4,8},{8,12},{12,14},{14,10},{10,6},{6,2},{2,0},{1,5},{5,9},... | collective-permute-start | bytes 1572872 | tf_op jit(solution)/shard_map/ppermute | solution.py:307
  66.4 17.4 %copy-start.6 = (bf16[1024,256]{1,0:T(8,128)(2,1)}, bf16[1024,256]{1,0:T(8,128)(2,1)S(1)}, u32[]{:S(2)}) copy-start(bf16[1024,256]{1,0:T(8,128)(2,1)S(1)} %collective-permute-done.13.refs_4_) | copy-start | bytes 1572868
  66.4 13.0 %collective-permute-start.17 = (bf16[1024,256]{1,0:T(8,128)(2,1)S(1)}, bf16[1024,256]{1,0:T(8,128)(2,1)S(1)}, u32[]{:S(2)}, u32[]{:S(2)}) collective-permute-start(bf16[1024,256]{1,0:T(8,128)(2,1)S(1)} %collective-permute-done.13.refs_4_), channel_id=1, source_target_pairs={{4,0},{8,4},{12,8},{14,12},{10,14},{6,10},{2,6},{0,2},{5,1},{9,5},... | collective-permute-start | bytes 1572872 | tf_op jit(solution)/shard_map/ppermute | solution.py:308
  66.6 14.2 %collective-permute-start.10 = (bf16[1024,256]{1,0:T(8,128)(2,1)S(1)}, bf16[1024,256]{1,0:T(8,128)(2,1)S(1)}, u32[]{:S(2)}, u32[]{:S(2)}) collective-permute-start(bf16[1024,256]{1,0:T(8,128)(2,1)S(1)} %slice_dynamic-update-slice_fusion.refs_0_), channel_id=1, source_target_pairs={{0,1},{1,0},{2,3},{3,2},{4,5},{5,4},{6,7},{7,6},{8,9},{9,8},{10,11... | collective-permute-start | bytes 1572872 | tf_op jit(solution)/shard_map/ppermute | solution.py:304
  68.3 13.7 %collective-permute-start.12 = (bf16[1024,256]{1,0:T(8,128)(2,1)S(1)}, bf16[1024,256]{1,0:T(8,128)(2,1)S(1)}, u32[]{:S(2)}, u32[]{:S(2)}) collective-permute-start(bf16[1024,256]{1,0:T(8,128)(2,1)S(1)} %collective-permute-done.11.refs_2_), channel_id=1, source_target_pairs={{0,1},{1,0},{2,3},{3,2},{4,5},{5,4},{6,7},{7,6},{8,9},{9,8},{10,11... | collective-permute-start | bytes 1572872 | tf_op jit(solution)/shard_map/ppermute | solution.py:315
  68.3 13.9 %collective-permute-start.14 = (bf16[1024,256]{1,0:T(8,128)(2,1)S(1)}, bf16[1024,256]{1,0:T(8,128)(2,1)S(1)}, u32[]{:S(2)}, u32[]{:S(2)}) collective-permute-start(bf16[1024,256]{1,0:T(8,128)(2,1)S(1)} %collective-permute-done.13.refs_4_), channel_id=1, source_target_pairs={{0,1},{1,0},{2,3},{3,2},{4,5},{5,4},{6,7},{7,6},{8,9},{9,8},{10,11... | collective-permute-start | bytes 1572872 | tf_op jit(solution)/shard_map/ppermute | solution.py:315
  77.3 6.5 %copy-start.7 = (bf16[1024,256]{1,0:T(8,128)(2,1)}, bf16[1024,256]{1,0:T(8,128)(2,1)S(1)}, u32[]{:S(2)}) copy-start(bf16[1024,256]{1,0:T(8,128)(2,1)S(1)} %collective-permute-done.15.refs_6_) | copy-start | bytes 1572868
  77.3 4.9 %collective-permute-start.16 = (bf16[1024,256]{1,0:T(8,128)(2,1)S(1)}, bf16[1024,256]{1,0:T(8,128)(2,1)S(1)}, u32[]{:S(2)}, u32[]{:S(2)}) collective-permute-start(bf16[1024,256]{1,0:T(8,128)(2,1)S(1)} %collective-permute-done.15.refs_6_), channel_id=1, source_target_pairs={{0,1},{1,0},{2,3},{3,2},{4,5},{5,4},{6,7},{7,6},{8,9},{9,8},{10,11... | collective-permute-start | bytes 1572872 | tf_op jit(solution)/shard_map/ppermute | solution.py:315
  79.4 4.4 %copy-start.8 = (bf16[1024,256]{1,0:T(8,128)(2,1)}, bf16[1024,256]{1,0:T(8,128)(2,1)S(1)}, u32[]{:S(2)}) copy-start(bf16[1024,256]{1,0:T(8,128)(2,1)S(1)} %collective-permute-done.17.refs_8_) | copy-start | bytes 1572868
  79.4 4.4 %collective-permute-start.18 = (bf16[1024,256]{1,0:T(8,128)(2,1)S(1)}, bf16[1024,256]{1,0:T(8,128)(2,1)}, u32[]{:S(2)}, u32[]{:S(2)}) collective-permute-start(bf16[1024,256]{1,0:T(8,128)(2,1)S(1)} %collective-permute-done.17.refs_8_), channel_id=1, source_target_pairs={{0,1},{1,0},{2,3},{3,2},{4,5},{5,4},{6,7},{7,6},{8,9},{9,8},{10,11... | collective-permute-start | bytes 1572872 | tf_op jit(solution)/shard_map/ppermute | solution.py:315
  80.7 1.5 copy-start.9
  80.7 13.5 %collective-permute-start.19 = (bf16[1024,256]{1,0:T(8,128)(2,1)S(1)}, bf16[1024,256]{1,0:T(8,128)(2,1)S(1)}, u32[]{:S(2)}, u32[]{:S(2)}) collective-permute-start(bf16[1024,256]{1,0:T(8,128)(2,1)S(1)} %collective-permute-done.15.refs_6_), channel_id=1, source_target_pairs={{0,4},{4,8},{8,12},{12,14},{14,10},{10,6},{6,2},{2,0},{1,5},{5,9},... | collective-permute-start | bytes 1572872 | tf_op jit(solution)/shard_map/ppermute | solution.py:307
  82.0 0.8 copy-start.10
  82.0 13.2 %collective-permute-start.20 = (bf16[1024,256]{1,0:T(8,128)(2,1)S(1)}, bf16[1024,256]{1,0:T(8,128)(2,1)S(1)}, u32[]{:S(2)}, u32[]{:S(2)}) collective-permute-start(bf16[1024,256]{1,0:T(8,128)(2,1)S(1)} %collective-permute-done.17.refs_8_), channel_id=1, source_target_pairs={{4,0},{8,4},{12,8},{14,12},{10,14},{6,10},{2,6},{0,2},{5,1},{9,5},... | collective-permute-start | bytes 1572872 | tf_op jit(solution)/shard_map/ppermute | solution.py:308
  82.2 0.8 copy-start.11
  83.0 0.8 copy-start.12
  94.2 4.4 %copy-start.3 = (bf16[1024,256]{1,0:T(8,128)(2,1)}, bf16[1024,256]{1,0:T(8,128)(2,1)S(1)}, u32[]{:S(2)}) copy-start(bf16[1024,256]{1,0:T(8,128)(2,1)S(1)} %collective-permute-done.19.refs_0_.refs_10_) | copy-start | bytes 1572868
  95.2 3.5 %copy-start.4 = (bf16[1024,256]{1,0:T(8,128)(2,1)}, bf16[1024,256]{1,0:T(8,128)(2,1)S(1)}, u32[]{:S(2)}) copy-start(bf16[1024,256]{1,0:T(8,128)(2,1)S(1)} %collective-permute-done.20.refs_2_.refs_12_) | copy-start | bytes 1572868
  95.2 2.7 %collective-permute-start.21 = (bf16[1024,256]{1,0:T(8,128)(2,1)S(1)}, bf16[1024,256]{1,0:T(8,128)(2,1)S(1)}, u32[]{:S(2)}, u32[]{:S(2)}) collective-permute-start(bf16[1024,256]{1,0:T(8,128)(2,1)S(1)} %collective-permute-done.19.refs_0_.refs_10_), channel_id=1, source_target_pairs={{0,1},{1,0},{2,3},{3,2},{4,5},{5,4},{6,7},{7,6},{8,9},{9,8},{10,11... | collective-permute-start | bytes 1572872 | tf_op jit(solution)/shard_map/ppermute | solution.py:315
  96.4 2.3 %collective-permute-start.22 = (bf16[1024,256]{1,0:T(8,128)(2,1)S(1)}, bf16[1024,256]{1,0:T(8,128)(2,1)S(1)}, u32[]{:S(2)}, u32[]{:S(2)}) collective-permute-start(bf16[1024,256]{1,0:T(8,128)(2,1)S(1)} %collective-permute-done.20.refs_2_.refs_12_), channel_id=1, source_target_pairs={{0,1},{1,0},{2,3},{3,2},{4,5},{5,4},{6,7},{7,6},{8,9},{9,8},{10,11... | collective-permute-start | bytes 1572872 | tf_op jit(solution)/shard_map/ppermute | solution.py:315
  96.4 9.3 %collective-permute-start.23 = (bf16[512,256]{1,0:T(8,128)(2,1)S(1)}, bf16[512,256]{1,0:T(8,128)(2,1)S(1)}, u32[]{:S(2)}, u32[]{:S(2)}) collective-permute-start(bf16[512,256]{1,0:T(8,128)(2,1)S(1)} %slice.26), channel_id=1, source_target_pairs={{0,4},{4,8},{8,12},{12,14},{14,10},{10,6},{6,2},{2,0},{1,5},{5,9},... | collective-permute-start | bytes 786440 | tf_op jit(solution)/shard_map/ppermute | solution.py:316
  97.7 8.0 %collective-permute-start.24 = (bf16[512,256]{1,0:T(8,128)(2,1)S(1)}, bf16[512,256]{1,0:T(8,128)(2,1)}, u32[]{:S(2)}, u32[]{:S(2)}) collective-permute-start(bf16[512,256]{1,0:T(8,128)(2,1)S(1)} %slice.27), channel_id=1, source_target_pairs={{4,0},{8,4},{12,8},{14,12},{10,14},{6,10},{2,6},{0,2},{5,1},{9,5},... | collective-permute-start | bytes 786440 | tf_op jit(solution)/shard_map/ppermute | solution.py:317
  98.0 0.8 copy-start.13
  98.7 0.8 copy-start.14
  105.7 2.6 %copy-start.16 = (bf16[512,256]{1,0:T(8,128)(2,1)}, bf16[512,256]{1,0:T(8,128)(2,1)S(1)}, u32[]{:S(2)}) copy-start(bf16[512,256]{1,0:T(8,128)(2,1)S(1)} %collective-permute-done.23.refs_14_.refs_0_) | copy-start | bytes 786436
  105.7 2.3 %collective-permute-start.25 = (bf16[512,256]{1,0:T(8,128)(2,1)S(1)}, bf16[512,256]{1,0:T(8,128)(2,1)S(1)}, u32[]{:S(2)}, u32[]{:S(2)}) collective-permute-start(bf16[512,256]{1,0:T(8,128)(2,1)S(1)} %collective-permute-done.23.refs_14_.refs_0_), channel_id=1, source_target_pairs={{0,1},{1,0},{2,3},{3,2},{4,5},{5,4},{6,7},{7,6},{8,9},{9,8},{10,11... | collective-permute-start | bytes 786440 | tf_op jit(solution)/shard_map/ppermute | solution.py:321
  106.6 1.7 collective-permute-start.26
  108.1 0.7 copy-start.17
  108.3 0.7 copy-start.18
  114.0 36.8 %collective-permute-start.27 = (bf16[64,2048]{1,0:T(8,128)(2,1)}, bf16[64,2048]{1,0:T(8,128)(2,1)S(1)}, u32[]{:S(2)}, u32[]{:S(2)}) collective-permute-start(bf16[64,2048]{1,0:T(8,128)(2,1)} %get-tuple-element.59), channel_id=1, source_target_pairs={{0,8},{1,9},{2,10},{3,11},{4,12},{5,13},{6,14},{7,15},{8,0},{9,1},... | collective-permute-start | bytes 786440 | tf_op jit(solution)/shard_map/ppermute | solution.py:344
  115.0 43.0 %collective-permute-start.28 = (bf16[64,2048]{1,0:T(8,128)(2,1)}, bf16[64,2048]{1,0:T(8,128)(2,1)S(1)}, u32[]{:S(2)}, u32[]{:S(2)}) collective-permute-start(bf16[64,2048]{1,0:T(8,128)(2,1)} %get-tuple-element.61), channel_id=1, source_target_pairs={{0,9},{1,10},{2,11},{3,8},{4,13},{5,14},{6,15},{7,12},{8,1},{9,2},... | collective-permute-start | bytes 786440 | tf_op jit(solution)/shard_map/ppermute | solution.py:344
  116.9 45.7 %collective-permute-start.29 = (bf16[64,2048]{1,0:T(8,128)(2,1)}, bf16[64,2048]{1,0:T(8,128)(2,1)S(1)}, u32[]{:S(2)}, u32[]{:S(2)}) collective-permute-start(bf16[64,2048]{1,0:T(8,128)(2,1)} %get-tuple-element.64), channel_id=1, source_target_pairs={{0,10},{1,11},{2,8},{3,9},{4,14},{5,15},{6,12},{7,13},{8,2},{9,3},... | collective-permute-start | bytes 786440 | tf_op jit(solution)/shard_map/ppermute | solution.py:344
  118.8 55.1 %collective-permute-start.30 = (bf16[64,2048]{1,0:T(8,128)(2,1)}, bf16[64,2048]{1,0:T(8,128)(2,1)S(1)}, u32[]{:S(2)}, u32[]{:S(2)}) collective-permute-start(bf16[64,2048]{1,0:T(8,128)(2,1)} %get-tuple-element.67), channel_id=1, source_target_pairs={{0,11},{1,8},{2,9},{3,10},{4,15},{5,12},{6,13},{7,14},{8,3},{9,0},... | collective-permute-start | bytes 786440 | tf_op jit(solution)/shard_map/ppermute | solution.py:344
  132.0 42.0 %collective-permute-start.31 = (bf16[64,2048]{1,0:T(8,128)(2,1)S(1)}, bf16[64,2048]{1,0:T(8,128)(2,1)S(1)}, u32[]{:S(2)}, u32[]{:S(2)}) collective-permute-start(bf16[64,2048]{1,0:T(8,128)(2,1)S(1)} %get-tuple-element.94), channel_id=1, source_target_pairs={{0,4},{1,5},{2,6},{3,7},{4,8},{5,9},{6,10},{7,11},{8,12},{9,13},{1... | collective-permute-start | bytes 786440 | tf_op jit(solution)/shard_map/ppermute | solution.py:344
  148.8 1.6 copy-start.15
  150.8 28.8 %collective-permute-start.32 = (bf16[64,2048]{1,0:T(8,128)(2,1)S(1)}, bf16[64,2048]{1,0:T(8,128)(2,1)S(1)}, u32[]{:S(2)}, u32[]{:S(2)}) collective-permute-start(bf16[64,2048]{1,0:T(8,128)(2,1)S(1)} %get-tuple-element.62), channel_id=1, source_target_pairs={{0,12},{1,13},{2,14},{3,15},{4,0},{5,1},{6,2},{7,3},{8,4},{9,5},{1... | collective-permute-start | bytes 786440 | tf_op jit(solution)/shard_map/ppermute | solution.py:344
  158.0 21.8 %collective-permute-start.33 = (bf16[64,2048]{1,0:T(8,128)(2,1)S(1)}, bf16[64,2048]{1,0:T(8,128)(2,1)S(1)}, u32[]{:S(2)}, u32[]{:S(2)}) collective-permute-start(bf16[64,2048]{1,0:T(8,128)(2,1)S(1)} %get-tuple-element.65), channel_id=1, source_target_pairs={{0,1},{1,2},{2,3},{3,0},{4,5},{5,6},{6,7},{7,4},{8,9},{9,10},{10,1... | collective-permute-start | bytes 786440 | tf_op jit(solution)/shard_map/ppermute | solution.py:344
  162.6 21.1 %collective-permute-start.34 = (bf16[64,2048]{1,0:T(8,128)(2,1)S(1)}, bf16[64,2048]{1,0:T(8,128)(2,1)S(1)}, u32[]{:S(2)}, u32[]{:S(2)}) collective-permute-start(bf16[64,2048]{1,0:T(8,128)(2,1)S(1)} %get-tuple-element.68), channel_id=1, source_target_pairs={{0,5},{1,6},{2,7},{3,4},{4,9},{5,10},{6,11},{7,8},{8,13},{9,14},{1... | collective-permute-start | bytes 786440 | tf_op jit(solution)/shard_map/ppermute | solution.py:344
  174.0 17.1 %collective-permute-start.35 = (bf16[64,2048]{1,0:T(8,128)(2,1)S(1)}, bf16[64,2048]{1,0:T(8,128)(2,1)S(1)}, u32[]{:S(2)}, u32[]{:S(2)}) collective-permute-start(bf16[64,2048]{1,0:T(8,128)(2,1)S(1)} %get-tuple-element.70), channel_id=1, source_target_pairs={{0,13},{1,14},{2,15},{3,12},{4,1},{5,2},{6,3},{7,0},{8,5},{9,6},{1... | collective-permute-start | bytes 786440 | tf_op jit(solution)/shard_map/ppermute | solution.py:344
  174.0 17.1 %collective-permute-start.36 = (bf16[64,2048]{1,0:T(8,128)(2,1)S(1)}, bf16[64,2048]{1,0:T(8,128)(2,1)S(1)}, u32[]{:S(2)}, u32[]{:S(2)}) collective-permute-start(bf16[64,2048]{1,0:T(8,128)(2,1)S(1)} %get-tuple-element.72), channel_id=1, source_target_pairs={{0,2},{1,3},{2,0},{3,1},{4,6},{5,7},{6,4},{7,5},{8,10},{9,11},{10,... | collective-permute-start | bytes 786440 | tf_op jit(solution)/shard_map/ppermute | solution.py:344
  179.6 14.2 %collective-permute-start.37 = (bf16[64,2048]{1,0:T(8,128)(2,1)S(1)}, bf16[64,2048]{1,0:T(8,128)(2,1)S(1)}, u32[]{:S(2)}, u32[]{:S(2)}) collective-permute-start(bf16[64,2048]{1,0:T(8,128)(2,1)S(1)} %get-tuple-element.74), channel_id=1, source_target_pairs={{0,6},{1,7},{2,4},{3,5},{4,10},{5,11},{6,8},{7,9},{8,14},{9,15},{1... | collective-permute-start | bytes 786440 | tf_op jit(solution)/shard_map/ppermute | solution.py:344
  179.8 16.5 %collective-permute-start.38 = (bf16[64,2048]{1,0:T(8,128)(2,1)S(1)}, bf16[64,2048]{1,0:T(8,128)(2,1)S(1)}, u32[]{:S(2)}, u32[]{:S(2)}) collective-permute-start(bf16[64,2048]{1,0:T(8,128)(2,1)S(1)} %get-tuple-element.76), channel_id=1, source_target_pairs={{0,14},{1,15},{2,12},{3,13},{4,2},{5,3},{6,0},{7,1},{8,6},{9,7},{1... | collective-permute-start | bytes 786440 | tf_op jit(solution)/shard_map/ppermute | solution.py:344
  183.8 16.8 %collective-permute-start.39 = (bf16[64,2048]{1,0:T(8,128)(2,1)S(1)}, bf16[64,2048]{1,0:T(8,128)(2,1)S(1)}, u32[]{:S(2)}, u32[]{:S(2)}) collective-permute-start(bf16[64,2048]{1,0:T(8,128)(2,1)S(1)} %get-tuple-element.78), channel_id=1, source_target_pairs={{0,3},{1,0},{2,1},{3,2},{4,7},{5,4},{6,5},{7,6},{8,11},{9,8},{10,9... | collective-permute-start | bytes 786440 | tf_op jit(solution)/shard_map/ppermute | solution.py:344
  191.0 11.6 %collective-permute-start.40 = (bf16[64,2048]{1,0:T(8,128)(2,1)S(1)}, bf16[64,2048]{1,0:T(8,128)(2,1)S(1)}, u32[]{:S(2)}, u32[]{:S(2)}) collective-permute-start(bf16[64,2048]{1,0:T(8,128)(2,1)S(1)} %get-tuple-element.80), channel_id=1, source_target_pairs={{0,7},{1,4},{2,5},{3,6},{4,11},{5,8},{6,9},{7,10},{8,15},{9,12},{1... | collective-permute-start | bytes 786440 | tf_op jit(solution)/shard_map/ppermute | solution.py:344
  191.0 16.3 %collective-permute-start.41 = (bf16[64,2048]{1,0:T(8,128)(2,1)S(1)}, bf16[64,2048]{1,0:T(8,128)(2,1)S(1)}, u32[]{:S(2)}, u32[]{:S(2)}) collective-permute-start(bf16[64,2048]{1,0:T(8,128)(2,1)S(1)} %get-tuple-element.82), channel_id=1, source_target_pairs={{0,15},{1,12},{2,13},{3,14},{4,3},{5,0},{6,1},{7,2},{8,7},{9,4},{1... | collective-permute-start | bytes 786440 | tf_op jit(solution)/shard_map/ppermute | solution.py:344
  202.7 4.7 %copy-start.2 = (bf16[64,32768]{1,0:T(8,128)(2,1)}, bf16[64,32768]{1,0:T(8,128)(2,1)S(1)}, u32[]{:S(2)}) copy-start(bf16[64,32768]{1,0:T(8,128)(2,1)S(1)} %constant_dynamic-update-slice_fusion.10) | copy-start | bytes 12582916
